TPU v7x, 32 devices: a whole 2x2x4 slice. The times are simulated.
32 devices in a mesh: root: 4 (over x, core), col: 8 (over z, y).
Axes of the slice: x: 2, y: 2, z: 4, core: 2. Of those that a mesh axis runs over, the one named last changes fastest.
Arguments:
- coeffs: float32 [4, 3072, 3072], P('root', 'col'), may hold values from -6 to 6
- diagonal: float32 [3072, 3072], P('col'), may hold values from -1 to 1
- shift: float32 [4], P('root'), may hold values from -1 to 1
- rotation: float32 [4, 4], replicated, may hold values from -1 to 1, as said below
- string_blocks: bfloat16 [30720, 128], P('col'), may hold values from -0.15625 to 0.15625
- block_cols: int32 [24, 10], replicated, may hold values from 0 to 23, all different within a row
Outputs:
- filtered: float32 [4, 3072, 3072], P('root', 'col')
Inputs may be any that keep to these rules, and one draw needn't show every extreme that they name: `block_cols`: each row names 10 different block columns, and every block column is named by some row. rotation is an orthogonal matrix.
All inputs are finite; a program needn't handle non-finite values.
Results may differ from a plain program's by a relative error of at most 0.0003.
Values may be sent and summed in bfloat16 or wider, within the bound.
No kernel may reach another device: no remote copies, remote signals or barrier semaphores. Data moves between devices by JAX's collectives and lax.ppermute only.
A program may use at most 192 MiB of HBM per device.

v0:
```python
import jax
import jax.numpy as jnp
from jax import lax
from jax.sharding import PartitionSpec as P


def apply_blocks(matrix, operator_blocks, block_cols):
    height, breadth = matrix.shape
    nblocks, filled = block_cols.shape
    blocksize = breadth // nblocks
    grouped = matrix.reshape(height, nblocks, blocksize)
    picked = jnp.take(grouped, block_cols, axis=1)
    tiles = operator_blocks.reshape(nblocks, filled, blocksize, blocksize).astype(jnp.float32)
    result = jnp.einsum("rifk,ifjk->rij", picked, tiles, precision=lax.Precision.HIGHEST)
    return result.reshape(height, breadth)


def layout_pieces(stacked):
    count, height, breadth = stacked.shape
    groups = breadth // height
    return (
        stacked.reshape(count, height, groups, height)
        .transpose(0, 2, 1, 3)
        .reshape(count, groups, height * height)
    )


def layout_whole(moved, height):
    count = moved.shape[0]
    groups = moved.shape[1]
    return (
        moved.reshape(count, groups, height, height)
        .transpose(0, 3, 1, 2)
        .reshape(count, height, groups * height)
    )


def swap_layout(stacked):
    moved = lax.all_to_all(layout_pieces(stacked), "col", split_axis=1, concat_axis=1, tiled=True)
    return layout_whole(moved, stacked.shape[1])


def shards(coeffs, diagonal, shift, rotation, string_blocks, block_cols):
    start = coeffs[0]
    energy = shift[0]
    operator_blocks = lax.all_gather(string_blocks, "col", axis=0, tiled=True)

    def apply_local(matrix):
        return apply_blocks(matrix, operator_blocks, block_cols)

    def sigma_local(vector):
        turned = swap_layout(vector[None])[0]
        beta_turned = apply_local(turned)
        beta_part = swap_layout(beta_turned[None])[0]
        return apply_local(vector) + beta_part + diagonal * vector

    first = 0.5 * (sigma_local(start) - energy * start)
    second = sigma_local(first) - energy * first - start
    weights = lax.dynamic_index_in_dim(rotation, lax.axis_index("root"), 1, keepdims=False)
    terms = weights[:, None, None] * second[None]
    return lax.psum_scatter(terms, "root", scatter_dimension=0, tiled=True)


def solution(mesh):
    return jax.shard_map(
        shards,
        mesh=mesh,
        in_specs=(P("root", "col", None), P("col", None), P("root"), P(), P("col", None), P()),
        out_specs=P("root", "col", None),
        check_vma=False,
    )
```

profile of v0, /device:TPU:0, one launch (start us, length us, event | category | flops | bytes accessed | tf_op | source)
XLA Modules:
  0.0 973.0 jit_solution(14098955473341781873)
XLA Ops:
  6.5 0.7 all-gather.2.cloned.1.call-update
  7.3 4.8 copy.113
  12.1 8.9 reshape.49
  21.0 7.5 all-to-all-start
  28.6 0.1 reshape.99
  28.7 0.1 copy.71
  28.8 185.5 %all-to-all-done = f32[1,8,147456]{2,0,1:T(1,128)} async-done(((f32[1,8,147456]{2,0,1:T(1,128)}), f32[1,8,147456]{2,0,1:T(1,128)}, u32[]{:S(2)}, u32[]{:S(2)}) %all-to-all-start) | async-done | bytes 4718624 | tf_op jit(solution)/shard_map/all_to_all | solution.py:39
  214.2 15.4 %reduce.1 = f32[8,147456]{1,0:T(8,128)} reduce(f32[1,8,147456]{2,0,1:T(1,128)} %all-to-all-done, f32[]{:T(128)} %constant.25), dimensions={0}, to_apply=%all_to_all.12.reduce_sub_computation | reduce | bytes 9437188 | tf_op jit(solution)/shard_map/all_to_all | solution.py:39
  229.6 5.4 copy.112
  235.0 6.0 copy.79
  241.0 22.3 %gather_fusion.1 = f32[240,384,128]{2,1,0:T(8,128)} fusion(f32[384,24,128]{2,0,1:T(8,128)} %copy.79, s32[1024]{0:T(1024)S(1)} %pad_clamp_fusion), kind=kCustom, calls=%fused_computation.1.clone | custom fusion | bytes 94372800 | tf_op jit(solution)/shard_map/jit(_take)/gather | solution.py:12
  263.3 32.3 %fusion.4 = f32[24,384,128,1]{1,2,3,0:T(8,128)} fusion(bf16[24,10,128,128]{3,2,1,0:T(8,128)(2,1)} %bitcast.140, f32[24,10,384,128]{3,2,1,0:T(8,128)} %bitcast.136, pred[24,10]{1,0:T(8,128)(4,1)S(1)} %copy.71), kind=kOutput, calls=%fused_computation.8 | convolution fusion | flops 18131189760 | bytes 59769072 | tf_op jit(solution)/shard_map/rifk,ifjk->rij/dot_general | solution.py:14
  295.7 6.1 copy.80
  301.7 8.8 reshape.119
  310.5 9.3 all-to-all-start.1
  319.8 6.1 copy.73
  325.9 6.0 copy.75
  331.9 22.3 %gather_fusion = f32[240,384,128]{2,1,0:T(8,128)} fusion(f32[384,24,128]{2,0,1:T(8,128)} %copy.75, s32[1024]{0:T(1024)S(1)} %pad_clamp_fusion), kind=kCustom, calls=%fused_computation.clone | custom fusion | bytes 94372800 | tf_op jit(solution)/shard_map/jit(_take)/gather | solution.py:12
  354.9 6.0 copy.83
  360.9 32.4 %fusion.6 = f32[24,384,128,1]{1,2,3,0:T(8,128)} fusion(bf16[24,10,128,128]{3,2,1,0:T(8,128)(2,1)} %bitcast.141, f32[24,10,384,128]{3,2,1,0:T(8,128)} %bitcast.138, pred[24,10]{1,0:T(8,128)(4,1)S(1)} %copy.71), kind=kOutput, calls=%fused_computation.10 | convolution fusion | flops 18131189760 | bytes 59769072 | tf_op jit(solution)/shard_map/rifk,ifjk->rij/dot_general | solution.py:14
  393.3 30.4 %all-to-all-done.1 = f32[1,8,147456]{2,0,1:T(1,128)} async-done(((f32[1,8,147456]{2,0,1:T(1,128)}), f32[1,8,147456]{2,0,1:T(1,128)}, u32[]{:S(2)}, u32[]{:S(2)}) %all-to-all-start.1) | async-done | bytes 4718624 | tf_op jit(solution)/shard_map/all_to_all | solution.py:39
  423.7 15.3 %reduce.2 = f32[8,147456]{1,0:T(8,128)} reduce(f32[1,8,147456]{2,0,1:T(1,128)} %all-to-all-done.1, f32[]{:T(128)} %constant.25), dimensions={0}, to_apply=%all_to_all.13.reduce_sub_computation | reduce | bytes 9437188 | tf_op jit(solution)/shard_map/all_to_all | solution.py:39
  439.0 5.5 copy.111
  444.6 8.8 broadcast_multiply_fusion.1
  453.4 6.3 copy.87
  459.7 8.8 reshape.120
  468.4 108.6 %all_to_all.20 = f32[1,8,147456]{2,0,1:T(1,128)} all-to-all(f32[1,8,147456]{2,0,1:T(1,128)} %reshape.120), channel_id=1, replica_groups=mesh['root'=4,'col'=8] {'col'}, dimensions={1} | all-to-all | bytes 9437184 | tf_op jit(solution)/shard_map/all_to_all | solution.py:39
  577.0 15.3 %reduce.3 = f32[8,147456]{1,0:T(8,128)} reduce(f32[1,8,147456]{2,0,1:T(1,128)} %all_to_all.20, f32[]{:T(128)} %constant.25), dimensions={0}, to_apply=%all_to_all.14.reduce_sub_computation | reduce | bytes 9437188 | tf_op jit(solution)/shard_map/all_to_all | solution.py:39
  592.3 5.4 copy.110
  597.7 6.1 copy.90
  603.8 22.3 %gather_fusion.3 = f32[240,384,128]{2,1,0:T(8,128)} fusion(f32[384,24,128]{2,0,1:T(8,128)} %copy.90, s32[1024]{0:T(1024)S(1)} %pad_clamp_fusion), kind=kCustom, calls=%fused_computation.3.clone | custom fusion | bytes 94372800 | tf_op jit(solution)/shard_map/jit(_take)/gather | solution.py:12
  626.1 32.4 %fusion = f32[24,384,128,1]{1,2,3,0:T(8,128)} fusion(bf16[24,10,128,128]{3,2,1,0:T(8,128)(2,1)} %bitcast.142, f32[24,10,384,128]{3,2,1,0:T(8,128)} %bitcast.139, pred[24,10]{1,0:T(8,128)(4,1)S(1)} %copy.71), kind=kOutput, calls=%fused_computation.4 | convolution fusion | flops 18131189760 | bytes 59769072 | tf_op jit(solution)/shard_map/rifk,ifjk->rij/dot_general | solution.py:14
  658.4 6.1 copy.91
  664.5 8.8 reshape.121
  673.3 4.8 all-to-all-start.3
  678.1 0.2 dynamic-slice_reduce_fusion
  678.3 6.1 copy.85
  684.4 22.3 %gather_fusion.2 = f32[240,384,128]{2,1,0:T(8,128)} fusion(f32[384,24,128]{2,0,1:T(8,128)} %copy.85, s32[1024]{0:T(1024)S(1)} %pad_clamp_fusion), kind=kCustom, calls=%fused_computation.2.clone | custom fusion | bytes 94372800 | tf_op jit(solution)/shard_map/jit(_take)/gather | solution.py:12
  706.7 32.4 %fusion.2 = f32[24,384,128,1]{1,2,3,0:T(8,128)} fusion(bf16[24,10,128,128]{3,2,1,0:T(8,128)(2,1)} %bitcast.143, f32[24,10,384,128]{3,2,1,0:T(8,128)} %bitcast.137, pred[24,10]{1,0:T(8,128)(4,1)S(1)} %copy.71), kind=kOutput, calls=%fused_computation.6 | convolution fusion | flops 18131189760 | bytes 59769072 | tf_op jit(solution)/shard_map/rifk,ifjk->rij/dot_general | solution.py:14
  739.0 42.4 %all-to-all-done.3 = f32[1,8,147456]{2,0,1:T(1,128)} async-done(((f32[1,8,147456]{2,0,1:T(1,128)}), f32[1,8,147456]{2,0,1:T(1,128)}, u32[]{:S(2)}, u32[]{:S(2)}) %all-to-all-start.3) | async-done | bytes 4718624 | tf_op jit(solution)/shard_map/all_to_all | solution.py:39
  781.4 15.3 %reduce.4 = f32[8,147456]{1,0:T(8,128)} reduce(f32[1,8,147456]{2,0,1:T(1,128)} %all-to-all-done.3, f32[]{:T(128)} %constant.25), dimensions={0}, to_apply=%all_to_all.15.reduce_sub_computation | reduce | bytes 9437188 | tf_op jit(solution)/shard_map/all_to_all | solution.py:39
  796.7 3.4 copy.109
  800.1 0.2 slice-done.3
  800.3 1.4 copy-done.1
  801.8 7.7 fusion.22
  809.5 6.1 copy.94
  815.6 11.5 %broadcast_multiply_fusion = f32[4,384,3072]{2,1,0:T(8,128)} fusion(f32[384,3072]{1,0:T(8,128)} %copy.94, f32[4]{0:T(128)S(1)} %dynamic-slice_reduce_fusion), kind=kLoop, calls=%fused_computation.24 | loop fusion | flops 4718592 | bytes 23592976 | tf_op jit(solution)/shard_map/mul | solution.py:60
  827.1 138.6 %reduce-scatter.2.cloned.1.call-done = f32[1,384,3072]{2,1,0:T(8,128)} async-done(((f32[4,384,3072]{2,1,0:T(8,128)}), f32[1,384,3072]{2,1,0:T(8,128)}) %reduce-scatter.2.cloned.1.call-update) | async-done | bytes 4718608 | tf_op jit(solution)/shard_map/reduce_scatter | solution.py:61
  (22 shorter events, 0.2 us)
Async XLA Ops:
  6.5 671.6 %copy-start = (f32[4,4]{1,0:T(4,128)S(1)}, f32[4,4]{1,0:T(4,128)}, u32[]{:S(2)}) copy-start(f32[4,4]{1,0:T(4,128)} %param.11) | copy-start | bytes 196
  6.5 256.8 %all-gather.2.cloned.1.call-start = ((), (), s32[]{:S(2)}) async-start(), calls=%async_computation.5 | async-start | bytes 8847360 | tf_op jit(solution)/shard_map/all_gather | solution.py:46
  21.0 7.5 copy-start.2
  21.0 193.3 %all-to-all-start = ((f32[1,8,147456]{2,0,1:T(1,128)}), f32[1,8,147456]{2,0,1:T(1,128)}, u32[]{:S(2)}, u32[]{:S(2)}) async-start(f32[1,8,147456]{2,0,1:T(1,128)} %reshape.49), calls=%async_computation | async-start | bytes 9437184 | tf_op jit(solution)/shard_map/all_to_all | solution.py:39
  310.5 113.2 %all-to-all-start.1 = ((f32[1,8,147456]{2,0,1:T(1,128)}), f32[1,8,147456]{2,0,1:T(1,128)}, u32[]{:S(2)}, u32[]{:S(2)}) async-start(f32[1,8,147456]{2,0,1:T(1,128)} %reshape.119), calls=%async_computation.1 | async-start | bytes 9437184 | tf_op jit(solution)/shard_map/all_to_all | solution.py:39
  423.7 20.8 %slice-start = ((s8[4718592]{0:T(1024)(128)(4,1)}), s8[524288]{0:T(1024)(128)(4,1)S(1)}, s32[]{:S(2)}) async-start(s8[4718592]{0:T(1024)(128)(4,1)} %bitcast.145), calls=%async_computation.7 | async-start | bytes 1048576
  439.0 5.5 slice-start.1
  673.3 108.1 %all-to-all-start.3 = ((f32[1,8,147456]{2,0,1:T(1,128)}), f32[1,8,147456]{2,0,1:T(1,128)}, u32[]{:S(2)}, u32[]{:S(2)}) async-start(f32[1,8,147456]{2,0,1:T(1,128)} %reshape.121), calls=%async_computation.3 | async-start | bytes 9437184 | tf_op jit(solution)/shard_map/all_to_all | solution.py:39
  678.1 287.7 %reduce-scatter.2.cloned.1.call-start = ((), (), s32[]{:S(2)}) async-start(), calls=%async_computation.6 | async-start | bytes 23592960 | tf_op jit(solution)/shard_map/reduce_scatter | solution.py:61
  781.4 18.7 %slice-start.2 = ((s8[4718592]{0:T(1024)(128)(4,1)}), s8[524288]{0:T(1024)(128)(4,1)S(1)}, s32[]{:S(2)}) async-start(s8[4718592]{0:T(1024)(128)(4,1)} %bitcast.147), calls=%async_computation.9 | async-start | bytes 1048576
  796.7 3.6 slice-start.3
  796.7 5.0 copy-start.1
Sparse Core Ops, SparseCore 0:
  9.5 211.9 all-gather.1
  827.3 138.4 reduce-scatter.1
where the time goes:
time: 984 us; the launch traced here: 973 us
  waiting for transfers between devices  398 us (40%)
  local copies, waits for them, and re-layouts  212 us (22%)
  matrix products  129 us (13%)
  blocking collectives  109 us (11%)
  other arithmetic  89.4 us (9%)
  starting transfers between devices  21.6 us (2%)
  between operations  14.5 us (1%)
    all_to_all x3, waiting for transfers between devices, swap_layout(): lax.all_to_all(layout_pieces(stacked), 'col', split_axis=1, concat_axis=1...  258 us
    reduce_scatter x1, waiting for transfers between devices, shards(): return lax.psum_scatter(terms, 'root', scatter_dimension=0, tiled=True)  139 us
    dot_general x4, matrix products, apply_blocks(): jnp.einsum('rifk,ifjk->rij', picked, tiles, precision=lax.Precision.HIGHEST)  129 us
    all_to_all x1, blocking collectives, swap_layout(): lax.all_to_all(layout_pieces(stacked), 'col', split_axis=1, concat_axis=1...  109 us
    gather x4, local copies, waits for them, and re-layouts, apply_blocks(): picked = jnp.take(grouped, block_cols, axis=1)  89.2 us
    all_to_all x4, other arithmetic, swap_layout(): lax.all_to_all(layout_pieces(stacked), 'col', split_axis=1, concat_axis=1...  61.3 us
    reshape x4, local copies, waits for them, and re-layouts, layout_pieces(): return stacked.reshape(count, height, groups, height).transpose(0, 2, 1,...  35.3 us
    unnamed x20, local copies, waits for them, and re-layouts  33.5 us
  transfers between devices with their start and end apart: 5, of which 4 were waited for; matrix products, arithmetic and copies ran while one was open for 20% of the time, Pallas kernels for 0%

commit v1 on v0

v1 whole, which is shorter than its diff:
```python
import functools

import jax
import jax.numpy as jnp
from jax import lax
from jax.experimental import pallas as pl
from jax.experimental.pallas import tpu as pltpu
from jax.sharding import PartitionSpec as P

LANES = 128
PAD = 16
TOP = 32764.0
LIMIT = 56 * 1024 * 1024


def scale_of(mantissa, exponent):
    return mantissa * jnp.exp2(exponent - 7.0) * (1.0 / TOP)


def encode(piece):
    width = piece.shape[1]
    top = jnp.maximum(jnp.max(jnp.abs(piece), axis=0, keepdims=True), 1e-25)
    exponent = jnp.floor(jnp.log2(top))
    mantissa = jnp.floor(top * jnp.exp2(7.0 - exponent)) + 1.0
    codes = jnp.floor(piece * (1.0 / scale_of(mantissa, exponent)) + 0.5)
    codes = codes.astype(jnp.int32).astype(jnp.int16)
    row = lax.broadcasted_iota(jnp.int32, (PAD, width), 0)
    tail = jnp.where(row == 0, mantissa, jnp.where(row == 1, exponent, 0.0))
    return codes, tail.astype(jnp.int32).astype(jnp.int16)


def put(ref, index, piece):
    height = piece.shape[0]
    codes, tail = encode(piece)
    ref[index, pl.ds(0, height), :] = codes
    ref[index, pl.ds(height, PAD), :] = tail


def decode(coded):
    height = coded.shape[0] - PAD
    tail = coded[height:].astype(jnp.int32).astype(jnp.float32)
    codes = coded[:height].astype(jnp.int32).astype(jnp.float32)
    return codes * scale_of(tail[0:1], tail[1:2])


def split_into(halves, block, value):
    rows = value.shape[0]
    high = value.astype(jnp.bfloat16)
    halves[block, pl.ds(0, rows), :] = high
    low = value - high.astype(jnp.float32)
    halves[block, pl.ds(rows, rows), :] = low.astype(jnp.bfloat16)


def apply_row(halves, tiles, place, cols, block, fill, blk):
    rows = halves.shape[1] // 2
    total = jnp.zeros((2 * rows, blk), jnp.float32)
    for first in range(0, fill, 2):
        terms = range(first, min(first + 2, fill))
        left = [halves[cols[block, f]] for f in terms]
        right = [tiles[pl.ds((place * fill + f) * blk, blk), :] for f in terms]
        total += lax.dot_general(
            jnp.concatenate(left, axis=1),
            jnp.concatenate(right, axis=1),
            (((1,), (1,)), ((), ())),
            preferred_element_type=jnp.float32,
        )
    return total[:rows] + total[rows:]


def pack_kernel(v_ref, out_ref):
    put(out_ref, 0, v_ref[...].T)


def right_first_kernel(dims, cols, shift, v_ref, d_ref, tiles, w_ref, u_ref, halves, turned):
    nblk, fill, blk, per = dims
    step = pl.program_id(0)

    @pl.when(step == 0)
    def _():
        for b in range(nblk):
            split_into(halves, b, v_ref[:, b * blk : (b + 1) * blk])

    for t in range(per):
        lanes = slice(t * blk, (t + 1) * blk)
        block = step * per + t
        here = v_ref[:, pl.ds(pl.multiple_of(block * blk, blk), blk)]
        moved = apply_row(halves, tiles, t, cols, block, fill, blk)
        whole = moved + (d_ref[:, lanes] - shift[0, 0]) * here
        w_ref[:, lanes] = whole
        turned[lanes, :] = (moved + whole).T
    put(u_ref, 0, turned[...])


def left_first_kernel(dims, cols, tv_ref, tiles, y_ref, halves):
    nblk, fill, blk, per = dims
    step = pl.program_id(0)

    @pl.when(step == 0)
    def _():
        for p in range(nblk // per):
            value = decode(tv_ref[p])
            for t in range(per):
                split_into(halves, p * per + t, value[:, t * blk : (t + 1) * blk])

    for t in range(per):
        y_ref[:, t * blk : (t + 1) * blk] = apply_row(halves, tiles, t, cols, step * per + t, fill, blk)


def right_second_kernel(dims, cols, shift, w_ref, v_ref, d_ref, tiles, p_ref, halves):
    nblk, fill, blk, per = dims
    step = pl.program_id(0)

    @pl.when(step == 0)
    def _():
        for b in range(nblk):
            split_into(halves, b, w_ref[:, b * blk : (b + 1) * blk])

    for t in range(per):
        lanes = slice(t * blk, (t + 1) * blk)
        block = step * per + t
        here = w_ref[:, pl.ds(pl.multiple_of(block * blk, blk), blk)]
        moved = apply_row(halves, tiles, t, cols, block, fill, blk)
        p_ref[:, lanes] = 0.5 * (moved + (d_ref[:, lanes] - shift[0, 0]) * here) - v_ref[:, lanes]


def left_second_kernel(dims, cols, shift, tu_ref, y_ref, dt_ref, tiles, *rest):
    nblk, fill, blk, per = dims
    outs, halves, turned = rest[:-2], rest[-2], rest[-1]
    step = pl.program_id(0)
    slab = dt_ref.shape[2]

    @pl.when(step == 0)
    def _():
        for p in range(nblk // per):
            value = decode(tu_ref[p]) + y_ref[:, p * per * blk : (p + 1) * per * blk]
            for t in range(per):
                split_into(halves, p * per + t, value[:, t * blk : (t + 1) * blk])

    for t in range(per):
        lanes = slice(t * blk, (t + 1) * blk)
        block = step * per + t
        here = y_ref[:, pl.ds(pl.multiple_of(block * blk, blk), blk)]
        diagonal = [
            dt_ref[r, 0, :, lanes].astype(jnp.int32).astype(jnp.float32)
            for r in range(dt_ref.shape[0])
        ]
        diagonal = jnp.concatenate(diagonal, axis=0) * (1.0 / 32767.0)
        moved = apply_row(halves, tiles, t, cols, block, fill, blk)
        turned[lanes, :] = (moved + (diagonal - shift[0, 0]) * here).T
    width = turned.shape[1] // len(outs)
    for k, out in enumerate(outs):
        put(out, 0, turned[:, k * width : (k + 1) * width])


def second_kernel(z_ref, p_ref, out_ref):
    put(out_ref, 0, 0.5 * decode(z_ref[0]) + p_ref[...])


def rotate_kernel(chunks, weights, *refs):
    ins, out_ref = refs[:-1], refs[-1]
    members = len(ins) // chunks
    width = out_ref.shape[2] // chunks
    for k in range(chunks):
        total = jnp.zeros((out_ref.shape[1], width), jnp.float32)
        for m in range(members):
            total += weights[0, m] * decode(ins[k * members + m][0])
        out_ref[0, :, k * width : (k + 1) * width] = total


def smem():
    return pl.BlockSpec(memory_space=pltpu.SMEM)


def call(kernel, grid, in_specs, out_specs, out_shape, scratch, flops, moved):
    return pl.pallas_call(
        kernel,
        grid=(grid,),
        in_specs=in_specs,
        out_specs=out_specs,
        out_shape=out_shape,
        scratch_shapes=scratch,
        compiler_params=pltpu.CompilerParams(
            dimension_semantics=("arbitrary",), vmem_limit_bytes=LIMIT
        ),
        cost_estimate=pl.CostEstimate(flops=flops, bytes_accessed=moved, transcendentals=0),
    )


def blocked_shards(sizes, coeffs, diagonal, shift, rotation, string_blocks, block_cols):
    roots, groups = sizes
    start = coeffs[0]
    rows, strings = start.shape
    nblk, fill = block_cols.shape
    blk = strings // nblk
    width = strings // groups
    per = width // blk
    chunks = per
    dims = (nblk, fill, blk, per)
    energy = shift.reshape(1, 1)
    root = lax.axis_index("root")
    f32, i16 = jnp.float32, jnp.int16

    def swap(pieces):
        return lax.all_to_all(pieces, "col", split_axis=0, concat_axis=0, tiled=True)

    piece = pl.BlockSpec((rows, width), lambda q: (0, q))
    whole = pl.BlockSpec((rows, strings), lambda q: (0, 0), pipeline_mode=pl.Buffered(1))
    tall = pl.BlockSpec((width, strings), lambda q: (0, 0), pipeline_mode=pl.Buffered(1))
    coded = pl.BlockSpec((1, width + PAD, rows), lambda q: (q, 0, 0))
    all_coded = pl.BlockSpec((groups, width + PAD, rows), lambda q: (0, 0, 0), pipeline_mode=pl.Buffered(1))
    tile_spec = pl.BlockSpec((per * fill * blk, blk), lambda q: (q, 0))
    codes_shape = jax.ShapeDtypeStruct((groups, width + PAD, rows), i16)
    row_shape = jax.ShapeDtypeStruct((rows, strings), f32)
    row_halves = pltpu.VMEM((nblk, 2 * rows, blk), jnp.bfloat16)
    col_halves = pltpu.VMEM((nblk, 2 * width, blk), jnp.bfloat16)
    work = 2 * 2 * rows * strings * fill * blk
    size = 4 * rows * strings

    share = string_blocks.shape[0] // roots
    mine = lax.dynamic_slice_in_dim(string_blocks, root * share, share, 0)
    tiles = lax.all_gather(mine, ("col", "root"), axis=0, tiled=True)

    tv = call(pack_kernel, groups, [piece], coded, codes_shape, [], 0, size * 3 // 2)(start)
    tv = swap(tv)

    slab = width // roots
    codes = jnp.round(diagonal * 32767.0).astype(jnp.int32).astype(i16)
    codes = codes.reshape(rows, groups, roots, slab)
    codes = lax.dynamic_index_in_dim(codes, root, 2, keepdims=False)
    codes = swap(codes.transpose(1, 2, 0))
    turned_diagonal = lax.all_gather(codes, "root", axis=0, tiled=False)

    w, tu = call(
        functools.partial(right_first_kernel, dims),
        groups,
        [smem(), smem(), whole, piece, tile_spec],
        [piece, coded],
        [row_shape, codes_shape],
        [row_halves, pltpu.VMEM((width, rows), f32)],
        work,
        size * 4 + size // 2,
    )(block_cols, energy, start, diagonal, tiles)
    tu = swap(tu)

    y = call(
        functools.partial(left_first_kernel, dims),
        groups,
        [smem(), all_coded, tile_spec],
        pl.BlockSpec((width, width), lambda q: (0, q)),
        jax.ShapeDtypeStruct((width, strings), f32),
        [col_halves],
        work,
        size * 3,
    )(block_cols, tv, tiles)

    base = call(
        functools.partial(right_second_kernel, dims),
        groups,
        [smem(), smem(), whole, piece, piece, tile_spec],
        piece,
        row_shape,
        [row_halves],
        work,
        size * 5,
    )(block_cols, energy, w, start, diagonal, tiles)

    part = width // chunks
    chunk_coded = pl.BlockSpec((1, rows + PAD, part), lambda q: (q, 0, 0))
    chunk_shape = jax.ShapeDtypeStruct((groups, rows + PAD, part), i16)
    tz = call(
        functools.partial(left_second_kernel, dims),
        groups,
        [
            smem(),
            smem(),
            all_coded,
            tall,
            pl.BlockSpec((roots, 1, slab, rows), lambda q: (0, q, 0, 0)),
            tile_spec,
        ],
        [chunk_coded] * chunks,
        [chunk_shape] * chunks,
        [col_halves, pltpu.VMEM((rows, width), f32)],
        work,
        size * 4,
    )(block_cols, energy, tu, y, turned_diagonal, tiles)

    masks = [0]
    held = []
    for k in range(chunks):
        z = swap(tz[k])
        second = call(
            second_kernel,
            groups,
            [chunk_coded, pl.BlockSpec((rows, part), lambda q, k=k: (0, q * chunks + k))],
            chunk_coded,
            chunk_shape,
            [],
            0,
            size * 2 // chunks,
        )(z, base)
        have, masks, bit = [second], [0], roots // 2
        while bit:
            pairs = [(r, r ^ bit) for r in range(roots)]
            have = have + [lax.ppermute(h, "root", pairs) for h in have]
            masks = masks + [m ^ bit for m in masks]
            bit //= 2
        held += have
    weights = rotation[root][jnp.bitwise_xor(root, jnp.array(masks, jnp.int32))]
    return call(
        functools.partial(rotate_kernel, chunks),
        groups,
        [smem()] + [chunk_coded] * len(held),
        pl.BlockSpec((1, rows, width), lambda q: (0, 0, q)),
        jax.ShapeDtypeStruct((1, rows, strings), f32),
        [],
        0,
        size * 3,
    )(weights.reshape(1, -1), *held)


def plain_blocks(matrix, operator_blocks, block_cols):
    height, breadth = matrix.shape
    nblocks, filled = block_cols.shape
    blocksize = breadth // nblocks
    grouped = matrix.reshape(height, nblocks, blocksize)
    picked = jnp.take(grouped, block_cols, axis=1)
    tiles = operator_blocks.reshape(nblocks, filled, blocksize, blocksize).astype(jnp.float32)
    result = jnp.einsum("rifk,ifjk->rij", picked, tiles, precision=lax.Precision.HIGHEST)
    return result.reshape(height, breadth)


def plain_swap(matrix):
    height, breadth = matrix.shape
    pieces = matrix.reshape(height, breadth // height, height).transpose(1, 2, 0)
    moved = lax.all_to_all(pieces, "col", split_axis=0, concat_axis=0, tiled=True)
    return moved.transpose(1, 0, 2).reshape(height, breadth)


def plain_shards(coeffs, diagonal, shift, rotation, string_blocks, block_cols):
    start = coeffs[0]
    energy = shift[0]
    operator_blocks = lax.all_gather(string_blocks, "col", axis=0, tiled=True)

    def sigma(vector):
        beta = plain_swap(plain_blocks(plain_swap(vector), operator_blocks, block_cols))
        return plain_blocks(vector, operator_blocks, block_cols) + beta + diagonal * vector

    first = 0.5 * (sigma(start) - energy * start)
    second = sigma(first) - energy * first - start
    weights = lax.dynamic_index_in_dim(rotation, lax.axis_index("root"), 1, keepdims=False)
    terms = weights[:, None, None] * second[None]
    return lax.psum_scatter(terms, "root", scatter_dimension=0, tiled=True)


def solution(mesh):
    roots, groups = mesh.shape["root"], mesh.shape["col"]

    def shards(coeffs, diagonal, shift, rotation, string_blocks, block_cols):
        rows, strings = coeffs.shape[1:]
        blk = strings // block_cols.shape[0]
        width = strings // groups
        regular = blk % LANES == 0 and width % blk == 0 and rows == width
        regular = regular and roots & (roots - 1) == 0 and width % (16 * roots) == 0
        args = (coeffs, diagonal, shift, rotation, string_blocks, block_cols)
        if regular and string_blocks.shape[0] % (16 * roots) == 0:
            return blocked_shards((roots, groups), *args)
        return plain_shards(*args)

    return jax.shard_map(
        shards,
        mesh=mesh,
        in_specs=(P("root", "col", None), P("col", None), P("root"), P(), P("col", None), P()),
        out_specs=P("root", "col", None),
        check_vma=False,
    )
```

time: 984 us -> 390 us (0.40)
  waiting for transfers between devices: 398 us -> 155 us
  local copies, waits for them, and re-layouts: 212 us -> 12.2 us
  matrix products: 129 us -> 0 us
  Pallas kernels: 0 us -> 112 us
  other arithmetic: 89.4 us -> 2.84 us
  blocking collectives: 109 us -> 68.3 us
    all_to_all x3 -> x4, waiting for transfers between devices: 258 us -> 33.2 us  [swap(): lax.all_to_all(pieces, 'col', split_axis=0, concat_axis=0, tiled=True)]
    reduce_scatter x1 -> x0, waiting for transfers between devices: 139 us -> none  [shards(): return lax.psum_scatter(terms, 'root', scatter_dimension=0, tiled=True)]
    dot_general x4 -> x0, matrix products: 129 us -> none  [apply_blocks(): jnp.einsum('rifk,ifjk->rij', picked, tiles, precision=lax.Precision.HIGHEST)]
    pallas_call x0 -> x9, Pallas kernels: none -> 112 us  [the longest x1 21 us: blocked_shards(): call(functools.partial(left_second_kernel, dims), groups, [smem(), smem()...]
    gather x4 -> x1, local copies, waits for them, and re-layouts: 89.2 us -> 1.11 us  [blocked_shards(): weights = rotation[root][jnp.bitwise_xor(root, jnp.array(masks, jnp.int32))]]
    all_gather x1, waiting for transfers between devices: 0.01 us -> 82.1 us  [blocked_shards(): tiles = lax.all_gather(mine, ('col', 'root'), axis=0, tiled=True)]
    all_to_all x4 -> x0, other arithmetic: 61.3 us -> none  [swap_layout(): lax.all_to_all(layout_pieces(stacked), 'col', split_axis=1, concat_axis=1...]
    all_to_all x1 -> x2, blocking collectives: 109 us -> 50.7 us  [swap(): lax.all_to_all(pieces, 'col', split_axis=0, concat_axis=0, tiled=True)]
  transfers between devices with their start and end apart: 5 -> 14, of which waited for: 4 -> 7; matrix products, arithmetic and copies ran while one was open for 20% -> 3% of each run, Pallas kernels for 0% -> 21%
where the time goes in v1:
time: 390 us; the launch traced here: 388 us
  waiting for transfers between devices  155 us (40%)
  Pallas kernels  112 us (29%)
  blocking collectives  68.3 us (18%)
  starting transfers between devices  23 us (6%)
  between operations  14.2 us (4%)
  local copies, waits for them, and re-layouts  12.2 us (3%)
    all_gather x1, waiting for transfers between devices, blocked_shards(): tiles = lax.all_gather(mine, ('col', 'root'), axis=0, tiled=True)  82.1 us
    all_to_all x2, blocking collectives, swap(): lax.all_to_all(pieces, 'col', split_axis=0, concat_axis=0, tiled=True)  50.7 us
    ppermute x9, waiting for transfers between devices, blocked_shards(): have = have + [lax.ppermute(h, 'root', pairs) for h in have]  40 us
    all_to_all x4, waiting for transfers between devices, swap(): lax.all_to_all(pieces, 'col', split_axis=0, concat_axis=0, tiled=True)  33.2 us
    pallas_call x1, Pallas kernels, blocked_shards(): call(functools.partial(left_second_kernel, dims), groups, [smem(), smem()...  21 us
    pallas_call x1, Pallas kernels, blocked_shards(): call(functools.partial(right_first_kernel, dims), groups, [smem(), smem()...  20.1 us
    all_to_all x4, starting transfers between devices, swap(): lax.all_to_all(pieces, 'col', split_axis=0, concat_axis=0, tiled=True)  19.1 us
    pallas_call x1, Pallas kernels, blocked_shards(): call(functools.partial(right_second_kernel, dims), groups, [smem(), smem(...  19 us
  transfers between devices with their start and end apart: 14, of which 7 were waited for; matrix products, arithmetic and copies ran while one was open for 3% of the time, Pallas kernels for 21%

profile of v1, /device:TPU:0, one launch (start us, length us, event | category | flops | bytes accessed | tf_op | source)
XLA Modules:
  0.0 388.2 jit_solution(11145007678263356163)
XLA Ops:
  6.5 1.2 copy-done
  7.7 0.7 constant_dynamic-slice_fusion
  8.4 0.0 all-gather.4.cloned.1.call-update
  8.5 6.0 %copy.20 = f32[384,3072]{0,1:T(8,128)} copy(f32[384,3072]{1,0:T(8,128)} %d_ref.3) | data formatting | bytes 9437184 | tf_op args[1]
  14.5 2.8 convert_convert_fusion
  17.3 0.9 dynamic-slice_bitcast_fusion
  18.2 7.3 %all-to-all-start.2 = ((s16[8,96,384]{2,1,0:T(8,128)(2,1)}), s16[8,96,384]{2,1,0:T(8,128)(2,1)S(1)}, u32[]{:S(2)}, u32[]{:S(2)}) async-start(s16[8,96,384]{2,1,0:T(8,128)(2,1)} %dynamic-slice_bitcast_fusion), calls=%async_computation.2 | async-start | bytes 1179648 | tf_op jit(solution)/shard_map/all_to_all | solution.py:204
  25.5 7.6 %shard_map.74 = s16[8,400,384]{2,1,0:T(8,128)(2,1)} custom-call(f32[384,3072]{1,0:T(8,128)} %bitcast.14), custom_call_target="tpu_custom_call" | custom-call | bytes 7077888 | tf_op jit(solution)/shard_map/pallas_call | solution.py:223
  33.1 11.7 %all-to-all-done.2 = s16[8,96,384]{2,1,0:T(8,128)(2,1)S(1)} async-done(((s16[8,96,384]{2,1,0:T(8,128)(2,1)}), s16[8,96,384]{2,1,0:T(8,128)(2,1)S(1)}, u32[]{:S(2)}, u32[]{:S(2)}) %all-to-all-start.2) | async-done | bytes 589856 | tf_op jit(solution)/shard_map/all_to_all | solution.py:204
  44.8 3.6 all-to-all-start.1
  49.1 0.7 copy.21.cols
  49.8 82.1 %all-gather.4.cloned.1.call-done.tiles = bf16[30720,128]{1,0:T(8,128)(2,1)} async-done(((bf16[960,128]{1,0:T(8,128)(2,1)}), bf16[30720,128]{1,0:T(8,128)(2,1)}) %all-gather.4.cloned.1.call-update) | async-done | bytes 7864336 | tf_op jit(solution)/shard_map/all_gather | solution.py:221
  131.9 20.1 %shard_map.73 = (f32[384,3072]{1,0:T(8,128)}, s16[8,400,384]{2,1,0:T(8,128)(2,1)}) custom-call(s32[24,10]{1,0:T(8,128)} %copy.21.cols, f32[1,1]{1,0:T(1,128)} %bitcast.11.shift, f32[384,3072]{1,0:T(8,128)} %bitcast.15, f32[384,3072]{1,0:T(8,128)} %d_ref.3, bf16[30720,128]{1,0:T(8,128)(2,1)} %all-gather.4.cloned.1.call-done.tiles), custom_call_target="tpu_custom_call" | custom-call | flops 6039797760 | bytes 21233664 | tf_op jit(solution)/shard_map/pallas_call | solution.py:233
  152.0 0.0 all-to-all-done.1.tv_ref
  152.0 4.4 %all-to-all-start = ((s16[8,400,384]{2,1,0:T(8,128)(2,1)}), s16[8,400,384]{2,1,0:T(8,128)(2,1)}, u32[]{:S(2)}, u32[]{:S(2)}) async-start(s16[8,400,384]{2,1,0:T(8,128)(2,1)} %get-tuple-element.10), calls=%async_computation | async-start | bytes 4915200 | tf_op jit(solution)/shard_map/all_to_all | solution.py:204
  156.4 17.6 %all-gather.5 = s16[32,96,384]{2,1,0:T(8,128)(2,1)} all-gather(s16[8,96,384]{2,1,0:T(8,128)(2,1)S(1)} %all-to-all-done.2), channel_id=2, replica_groups=mesh['root'=4,'col'=8] {'root'}, dimensions={0}, use_global_device_ids=true | all-gather | bytes 2949120 | tf_op jit(solution)/shard_map/all_gather | solution.py:231
  174.0 17.5 %shard_map.75.y_ref = f32[384,3072]{1,0:T(8,128)} custom-call(s32[24,10]{1,0:T(8,128)} %copy.21.cols, s16[8,400,384]{2,1,0:T(8,128)(2,1)} %copy-done.4, bf16[30720,128]{1,0:T(8,128)(2,1)} %all-gather.4.cloned.1.call-done.tiles), custom_call_target="tpu_custom_call" | custom-call | flops 6039797760 | bytes 14155776 | tf_op jit(solution)/shard_map/pallas_call | solution.py:245
  191.6 21.5 %all-to-all-done.tu_ref = s16[8,400,384]{2,1,0:T(8,128)(2,1)} async-done(((s16[8,400,384]{2,1,0:T(8,128)(2,1)}), s16[8,400,384]{2,1,0:T(8,128)(2,1)}, u32[]{:S(2)}, u32[]{:S(2)}) %all-to-all-start) | async-done | bytes 2457632 | tf_op jit(solution)/shard_map/all_to_all | solution.py:204
  213.1 21.0 %shard_map.76 = (s16[8,400,128]{2,1,0:T(8,128)(2,1)}, s16[8,400,128]{2,1,0:T(8,128)(2,1)}, s16[8,400,128]{2,1,0:T(8,128)(2,1)}) custom-call(s32[24,10]{1,0:T(8,128)} %copy.21.cols, f32[1,1]{1,0:T(1,128)} %bitcast.12.shift, s16[8,400,384]{2,1,0:T(8,128)(2,1)} %all-to-all-done.tu_ref, f32[384,3072]{1,0:T(8,128)} %shard_map.75.y_ref, ...), custom_call_target="tpu_custom_call" | custom-call | flops 6039797760 | bytes 18874368 | tf_op jit(solution)/shard_map/pallas_call | solution.py:270
  234.0 25.7 %all_to_all.30.z_ref = s16[8,400,128]{2,1,0:T(8,128)(2,1)} all-to-all(s16[8,400,128]{2,1,0:T(8,128)(2,1)} %get-tuple-element.13), channel_id=1, replica_groups=mesh['root'=4,'col'=8] {'col'}, dimensions={0} | all-to-all | bytes 1638400 | tf_op jit(solution)/shard_map/all_to_all | solution.py:204
  259.7 25.0 %all_to_all.31.z_ref = s16[8,400,128]{2,1,0:T(8,128)(2,1)} all-to-all(s16[8,400,128]{2,1,0:T(8,128)(2,1)} %get-tuple-element.14), channel_id=1, replica_groups=mesh['root'=4,'col'=8] {'col'}, dimensions={0} | all-to-all | bytes 1638400 | tf_op jit(solution)/shard_map/all_to_all | solution.py:204
  284.7 3.7 all-to-all-start.3
  288.5 19.0 %shard_map.77.p_ref = f32[384,3072]{1,0:T(8,128)} custom-call(s32[24,10]{1,0:T(8,128)} %copy.21.cols, f32[1,1]{1,0:T(1,128)} %bitcast.13.shift, f32[384,3072]{1,0:T(8,128)} %get-tuple-element.12.w_ref, f32[384,3072]{1,0:T(8,128)} %bitcast.16, f32[384,3072]{1,0:T(8,128)} %d_ref.3, bf16[30720,128]{1,0:T(8,128)(2,1)} %all-gather.4.cloned.1.call-done.tiles), custom_call_target="tpu_custom_call" | custom-call | flops 6039797760 | bytes 23592960 | tf_op jit(solution)/shard_map/pallas_call | solution.py:256
  307.5 5.9 %shard_map.80.refs_8_ = s16[8,400,128]{2,1,0:T(8,128)(2,1)} custom-call(s16[8,400,128]{2,1,0:T(8,128)(2,1)} %all_to_all.31.z_ref, f32[384,3072]{1,0:T(8,128)} %shard_map.77.p_ref), custom_call_target="tpu_custom_call" | custom-call | bytes 3145728 | tf_op jit(solution)/shard_map/pallas_call | solution.py:292
  313.4 0.0 collective-permute-start.7
  313.4 1.4 collective-permute-start.6
  314.8 5.9 %shard_map.79.refs_4_ = s16[8,400,128]{2,1,0:T(8,128)(2,1)} custom-call(s16[8,400,128]{2,1,0:T(8,128)(2,1)} %all_to_all.30.z_ref, f32[384,3072]{1,0:T(8,128)} %shard_map.77.p_ref), custom_call_target="tpu_custom_call" | custom-call | bytes 3145728 | tf_op jit(solution)/shard_map/pallas_call | solution.py:292
  320.6 0.6 collective-permute-start.3
  321.3 0.0 all-to-all-done.3.z_ref
  321.3 0.9 copy-done.3
  322.2 5.9 %shard_map.78.refs_0_ = s16[8,400,128]{2,1,0:T(8,128)(2,1)} custom-call(s16[8,400,128]{2,1,0:T(8,128)(2,1)} %copy-done.3, f32[384,3072]{1,0:T(8,128)} %shard_map.77.p_ref), custom_call_target="tpu_custom_call" | custom-call | bytes 3145728 | tf_op jit(solution)/shard_map/pallas_call | solution.py:292
  328.0 1.4 collective-permute-start
  329.4 0.0 collective-permute-start.4
  329.4 0.0 collective-permute-done.7.refs_10_
  329.5 0.5 collective-permute-start.1
  329.9 4.7 %collective-permute-done.6.refs_9_ = s16[8,400,128]{2,1,0:T(8,128)(2,1)S(1)} collective-permute-done((s16[8,400,128]{2,1,0:T(8,128)(2,1)}, s16[8,400,128]{2,1,0:T(8,128)(2,1)S(1)}, u32[]{:S(2)}, u32[]{:S(2)}) %collective-permute-start.6) | collective-permute-done | bytes 819232 | tf_op jit(solution)/shard_map/ppermute | solution.py:305
  334.6 0.0 collective-permute-start.8
  334.6 17.7 %collective-permute-done.3.refs_5_ = s16[8,400,128]{2,1,0:T(8,128)(2,1)} collective-permute-done((s16[8,400,128]{2,1,0:T(8,128)(2,1)}, s16[8,400,128]{2,1,0:T(8,128)(2,1)}, u32[]{:S(2)}, u32[]{:S(2)}) %collective-permute-start.3) | collective-permute-done | bytes 819232 | tf_op jit(solution)/shard_map/ppermute | solution.py:305
  352.3 0.0 collective-permute-start.5
  352.3 17.1 %collective-permute-done.refs_1_ = s16[8,400,128]{2,1,0:T(8,128)(2,1)S(1)} collective-permute-done((s16[8,400,128]{2,1,0:T(8,128)(2,1)}, s16[8,400,128]{2,1,0:T(8,128)(2,1)S(1)}, u32[]{:S(2)}, u32[]{:S(2)}) %collective-permute-start) | collective-permute-done | bytes 819232 | tf_op jit(solution)/shard_map/ppermute | solution.py:305
  369.3 0.0 collective-permute-start.2
  369.3 0.7 fusion
  370.1 1.1 gather_fusion
  371.2 0.0 collective-permute-done.4.refs_6_
  371.2 0.0 collective-permute-done.1.refs_2_
  371.2 0.0 collective-permute-done.8.refs_11_
  371.2 0.6 collective-permute-done.2.refs_3_
  371.8 9.6 %shard_map.81 = f32[1,384,3072]{2,1,0:T(8,128)} custom-call(f32[1,4]{1,0:T(1,128)} %bitcast.19, s16[8,400,128]{2,1,0:T(8,128)(2,1)} %shard_map.78.refs_0_, s16[8,400,128]{2,1,0:T(8,128)(2,1)} %copy-done.7, s16[8,400,128]{2,1,0:T(8,128)(2,1)} %collective-permute-done.1.refs_2_, s16[8,400,128]{2,1,0:T(8,128)(2,1)} %collective-permute-done.2.refs_3_, ...), custom_call_target="tpu_custom_call" | custom-call | bytes 14155776 | tf_op jit(solution)/shard_map/pallas_call | solution.py:310
  (22 shorter events, 0.1 us)
Async XLA Ops:
  6.5 1.2 copy-start
  6.5 125.4 %all-gather.4.cloned.1.call-start = ((), (), s32[]{:S(2)}) async-start(), calls=%async_computation.6 | async-start | bytes 8110080 | tf_op jit(solution)/shard_map/all_gather | solution.py:221
  18.2 26.6 %all-to-all-start.2 = ((s16[8,96,384]{2,1,0:T(8,128)(2,1)}), s16[8,96,384]{2,1,0:T(8,128)(2,1)S(1)}, u32[]{:S(2)}, u32[]{:S(2)}) async-start(s16[8,96,384]{2,1,0:T(8,128)(2,1)} %dynamic-slice_bitcast_fusion), calls=%async_computation.2 | async-start | bytes 1179648 | tf_op jit(solution)/shard_map/all_to_all | solution.py:204
  25.5 23.6 %copy-start.8 = (s32[24,10]{0,1:T(8,128)S(1)}, s32[24,10]{0,1:T(8,128)}, u32[]{:S(2)}) copy-start(s32[24,10]{0,1:T(8,128)} %param.12) | copy-start | bytes 2884
  44.8 107.2 %all-to-all-start.1 = ((s16[8,400,384]{2,1,0:T(8,128)(2,1)}), s16[8,400,384]{2,1,0:T(8,128)(2,1)S(1)}, u32[]{:S(2)}, u32[]{:S(2)}) async-start(s16[8,400,384]{2,1,0:T(8,128)(2,1)} %shard_map.74), calls=%async_computation.1 | async-start | bytes 4915200 | tf_op jit(solution)/shard_map/all_to_all | solution.py:204
  152.0 22.1 %copy-start.4 = (s16[8,400,384]{2,1,0:T(8,128)(2,1)}, s16[8,400,384]{2,1,0:T(8,128)(2,1)S(1)}, u32[]{:S(2)}) copy-start(s16[8,400,384]{2,1,0:T(8,128)(2,1)S(1)} %all-to-all-done.1.tv_ref) | copy-start | bytes 7372804
  152.0 61.1 %all-to-all-start = ((s16[8,400,384]{2,1,0:T(8,128)(2,1)}), s16[8,400,384]{2,1,0:T(8,128)(2,1)}, u32[]{:S(2)}, u32[]{:S(2)}) async-start(s16[8,400,384]{2,1,0:T(8,128)(2,1)} %get-tuple-element.10), calls=%async_computation | async-start | bytes 4915200 | tf_op jit(solution)/shard_map/all_to_all | solution.py:204
  284.7 36.5 %all-to-all-start.3 = ((s16[8,400,128]{2,1,0:T(8,128)(2,1)}), s16[8,400,128]{2,1,0:T(8,128)(2,1)S(1)}, u32[]{:S(2)}, u32[]{:S(2)}) async-start(s16[8,400,128]{2,1,0:T(8,128)(2,1)} %get-tuple-element.11), calls=%async_computation.3 | async-start | bytes 1638400 | tf_op jit(solution)/shard_map/all_to_all | solution.py:204
  313.4 16.1 %collective-permute-start.7 = (s16[8,400,128]{2,1,0:T(8,128)(2,1)}, s16[8,400,128]{2,1,0:T(8,128)(2,1)S(1)}, u32[]{:S(2)}, u32[]{:S(2)}) collective-permute-start(s16[8,400,128]{2,1,0:T(8,128)(2,1)} %shard_map.80.refs_8_), channel_id=1, source_target_pairs={{0,8},{8,0},{16,24},{24,16},{1,9},{9,1},{17,25},{25,17},{2,10},{10... | collective-permute-start | bytes 2457608 | tf_op jit(solution)/shard_map/ppermute | solution.py:305
  313.4 21.3 %collective-permute-start.6 = (s16[8,400,128]{2,1,0:T(8,128)(2,1)}, s16[8,400,128]{2,1,0:T(8,128)(2,1)S(1)}, u32[]{:S(2)}, u32[]{:S(2)}) collective-permute-start(s16[8,400,128]{2,1,0:T(8,128)(2,1)} %shard_map.80.refs_8_), channel_id=1, source_target_pairs={{0,16},{8,24},{16,0},{24,8},{1,17},{9,25},{17,1},{25,9},{2,18},{10... | collective-permute-start | bytes 2457608 | tf_op jit(solution)/shard_map/ppermute | solution.py:305
  320.6 8.8 %copy-start.2 = (s16[8,400,128]{2,1,0:T(8,128)(2,1)S(1)}, s16[8,400,128]{2,1,0:T(8,128)(2,1)}, u32[]{:S(2)}) copy-start(s16[8,400,128]{2,1,0:T(8,128)(2,1)} %shard_map.79.refs_4_) | copy-start | bytes 2457604
  320.6 49.4 %copy-start.9 = (s32[4]{0:T(128)S(1)}, s32[4]{0:T(128)}, u32[]{:S(2)}) copy-start(s32[4]{0:T(128)} %constant.6.clone) | copy-start | bytes 52
  320.6 31.6 %collective-permute-start.3 = (s16[8,400,128]{2,1,0:T(8,128)(2,1)}, s16[8,400,128]{2,1,0:T(8,128)(2,1)}, u32[]{:S(2)}, u32[]{:S(2)}) collective-permute-start(s16[8,400,128]{2,1,0:T(8,128)(2,1)} %shard_map.79.refs_4_), channel_id=1, source_target_pairs={{0,16},{8,24},{16,0},{24,8},{1,17},{9,25},{17,1},{25,9},{2,18},{10... | collective-permute-start | bytes 2457608 | tf_op jit(solution)/shard_map/ppermute | solution.py:305
  321.3 0.9 copy-start.3
  328.0 41.3 %collective-permute-start = (s16[8,400,128]{2,1,0:T(8,128)(2,1)}, s16[8,400,128]{2,1,0:T(8,128)(2,1)S(1)}, u32[]{:S(2)}, u32[]{:S(2)}) collective-permute-start(s16[8,400,128]{2,1,0:T(8,128)(2,1)} %shard_map.78.refs_0_), channel_id=1, source_target_pairs={{0,16},{8,24},{16,0},{24,8},{1,17},{9,25},{17,1},{25,9},{2,18},{10... | collective-permute-start | bytes 2457608 | tf_op jit(solution)/shard_map/ppermute | solution.py:305
  329.4 41.7 %collective-permute-start.4 = (s16[8,400,128]{2,1,0:T(8,128)(2,1)S(1)}, s16[8,400,128]{2,1,0:T(8,128)(2,1)}, u32[]{:S(2)}, u32[]{:S(2)}) collective-permute-start(s16[8,400,128]{2,1,0:T(8,128)(2,1)S(1)} %copy-done.2), channel_id=1, source_target_pairs={{0,8},{8,0},{16,24},{24,16},{1,9},{9,1},{17,25},{25,17},{2,10},{10... | collective-permute-start | bytes 2457608 | tf_op jit(solution)/shard_map/ppermute | solution.py:305
  329.4 42.4 %copy-start.5 = (s16[8,400,128]{2,1,0:T(8,128)(2,1)}, s16[8,400,128]{2,1,0:T(8,128)(2,1)S(1)}, u32[]{:S(2)}) copy-start(s16[8,400,128]{2,1,0:T(8,128)(2,1)S(1)} %collective-permute-done.7.refs_10_) | copy-start | bytes 2457604
  329.5 41.7 %collective-permute-start.1 = (s16[8,400,128]{2,1,0:T(8,128)(2,1)}, s16[8,400,128]{2,1,0:T(8,128)(2,1)}, u32[]{:S(2)}, u32[]{:S(2)}) collective-permute-start(s16[8,400,128]{2,1,0:T(8,128)(2,1)} %shard_map.78.refs_0_), channel_id=1, source_target_pairs={{0,8},{8,0},{16,24},{24,16},{1,9},{9,1},{17,25},{25,17},{2,10},{10... | collective-permute-start | bytes 2457608 | tf_op jit(solution)/shard_map/ppermute | solution.py:305
  334.6 37.2 %copy-start.6 = (s16[8,400,128]{2,1,0:T(8,128)(2,1)}, s16[8,400,128]{2,1,0:T(8,128)(2,1)S(1)}, u32[]{:S(2)}) copy-start(s16[8,400,128]{2,1,0:T(8,128)(2,1)S(1)} %collective-permute-done.6.refs_9_) | copy-start | bytes 2457604
  334.6 36.6 %collective-permute-start.8 = (s16[8,400,128]{2,1,0:T(8,128)(2,1)S(1)}, s16[8,400,128]{2,1,0:T(8,128)(2,1)}, u32[]{:S(2)}, u32[]{:S(2)}) collective-permute-start(s16[8,400,128]{2,1,0:T(8,128)(2,1)S(1)} %collective-permute-done.6.refs_9_), channel_id=1, source_target_pairs={{0,8},{8,0},{16,24},{24,16},{1,9},{9,1},{17,25},{25,17},{2,10},{10... | collective-permute-start | bytes 2457608 | tf_op jit(solution)/shard_map/ppermute | solution.py:305
  352.3 18.9 %collective-permute-start.5 = (s16[8,400,128]{2,1,0:T(8,128)(2,1)}, s16[8,400,128]{2,1,0:T(8,128)(2,1)}, u32[]{:S(2)}, u32[]{:S(2)}) collective-permute-start(s16[8,400,128]{2,1,0:T(8,128)(2,1)} %collective-permute-done.3.refs_5_), channel_id=1, source_target_pairs={{0,8},{8,0},{16,24},{24,16},{1,9},{9,1},{17,25},{25,17},{2,10},{10... | collective-permute-start | bytes 2457608 | tf_op jit(solution)/shard_map/ppermute | solution.py:305
  369.3 1.8 copy-start.7
  369.3 2.5 collective-permute-start.2
  371.8 9.6 %copy-start.1 = (bf16[3840,128]{1,0:T(8,128)(2,1)S(1)}, bf16[3840,128]{1,0:T(8,128)(2,1)}, u32[]{:S(2)}) copy-start(bf16[3840,128]{1,0:T(8,128)(2,1)} %param.11) | copy-start | bytes 2949124
Sparse Core Ops, SparseCore 0:
  10.3 121.5 all-gather.3

commit v2 on v1

--- a/solution.py
+++ b/solution.py
@@ -36,11 +36,14 @@
     ref[index, pl.ds(height, PAD), :] = tail
 
 
-def decode(coded):
-    height = coded.shape[0] - PAD
-    tail = coded[height:].astype(jnp.int32).astype(jnp.float32)
-    codes = coded[:height].astype(jnp.int32).astype(jnp.float32)
-    return codes * scale_of(tail[0:1], tail[1:2])
+def decode(codes, tail):
+    tail = tail.astype(jnp.int32).astype(jnp.float32)
+    return codes.astype(jnp.int32).astype(jnp.float32) * scale_of(tail[0:1], tail[1:2])
+
+
+def take(ref, index):
+    height = ref.shape[1] - PAD
+    return decode(ref[index, pl.ds(0, height), :], ref[index, pl.ds(height, PAD), :])
 
 
 def split_into(halves, block, value):
@@ -71,20 +74,33 @@
     put(out_ref, 0, v_ref[...].T)
 
 
-def right_first_kernel(dims, cols, shift, v_ref, d_ref, tiles, w_ref, u_ref, halves, turned):
+def right_first_kernel(dims, cols, shift, place, v_ref, d_ref, own, *rest):
     nblk, fill, blk, per = dims
+    shards, (w_ref, u_ref, tiles_ref, halves, turned, tiles) = rest[:-6], rest[-6:]
     step = pl.program_id(0)
+    size = own.shape[0]
 
     @pl.when(step == 0)
     def _():
         for b in range(nblk):
             split_into(halves, b, v_ref[:, b * blk : (b + 1) * blk])
-
+        tiles[pl.ds(pl.multiple_of(place[0, 0] * size, size), size), :] = own[...]
+
+        @pl.loop(0, size // blk)
+        def _(b):
+            for k, shard in enumerate(shards):
+                share = shard.shape[1]
+                base = place[0, 1 + k] * size + place[1, 1 + k] * share
+                at = pl.multiple_of(base + b * blk, share)
+                tiles[pl.ds(at, share), :] = shard[b]
+
+    here_tiles = tiles.at[pl.ds(pl.multiple_of(step * size, size), size), :]
+    tiles_ref[...] = here_tiles[...]
     for t in range(per):
         lanes = slice(t * blk, (t + 1) * blk)
         block = step * per + t
         here = v_ref[:, pl.ds(pl.multiple_of(block * blk, blk), blk)]
-        moved = apply_row(halves, tiles, t, cols, block, fill, blk)
+        moved = apply_row(halves, here_tiles, t, cols, block, fill, blk)
         whole = moved + (d_ref[:, lanes] - shift[0, 0]) * here
         w_ref[:, lanes] = whole
         turned[lanes, :] = (moved + whole).T
@@ -98,7 +114,7 @@
     @pl.when(step == 0)
     def _():
         for p in range(nblk // per):
-            value = decode(tv_ref[p])
+            value = take(tv_ref, p)
             for t in range(per):
                 split_into(halves, p * per + t, value[:, t * blk : (t + 1) * blk])
 
@@ -106,7 +122,7 @@
         y_ref[:, t * blk : (t + 1) * blk] = apply_row(halves, tiles, t, cols, step * per + t, fill, blk)
 
 
-def right_second_kernel(dims, cols, shift, w_ref, v_ref, d_ref, tiles, p_ref, halves):
+def right_second_kernel(dims, cols, shift, w_ref, v_ref, d_ref, tiles, p_ref, halves, part):
     nblk, fill, blk, per = dims
     step = pl.program_id(0)
 
@@ -120,22 +136,24 @@
         block = step * per + t
         here = w_ref[:, pl.ds(pl.multiple_of(block * blk, blk), blk)]
         moved = apply_row(halves, tiles, t, cols, block, fill, blk)
-        p_ref[:, lanes] = 0.5 * (moved + (d_ref[:, lanes] - shift[0, 0]) * here) - v_ref[:, lanes]
-
-
-def left_second_kernel(dims, cols, shift, tu_ref, y_ref, dt_ref, tiles, *rest):
+        part[:, lanes] = 0.5 * (moved + (d_ref[:, lanes] - shift[0, 0]) * here) - v_ref[:, lanes]
+    put(p_ref, 0, part[...])
+
+
+def left_second_kernel(dims, chunk, cols, shift, tu_ref, tail_ref, y_ref, dt_ref, tiles, after, out, halves):
     nblk, fill, blk, per = dims
-    outs, halves, turned = rest[:-2], rest[-2], rest[-1]
+    del after
     step = pl.program_id(0)
-    slab = dt_ref.shape[2]
+    part = y_ref.shape[0]
 
     @pl.when(step == 0)
     def _():
         for p in range(nblk // per):
-            value = decode(tu_ref[p]) + y_ref[:, p * per * blk : (p + 1) * per * blk]
+            value = decode(tu_ref[p], tail_ref[p]) + y_ref[:, p * per * blk : (p + 1) * per * blk]
             for t in range(per):
                 split_into(halves, p * per + t, value[:, t * blk : (t + 1) * blk])
 
+    done = []
     for t in range(per):
         lanes = slice(t * blk, (t + 1) * blk)
         block = step * per + t
@@ -144,34 +162,33 @@
             dt_ref[r, 0, :, lanes].astype(jnp.int32).astype(jnp.float32)
             for r in range(dt_ref.shape[0])
         ]
-        diagonal = jnp.concatenate(diagonal, axis=0) * (1.0 / 32767.0)
+        diagonal = jnp.concatenate(diagonal, axis=0)[chunk * part : (chunk + 1) * part]
         moved = apply_row(halves, tiles, t, cols, block, fill, blk)
-        turned[lanes, :] = (moved + (diagonal - shift[0, 0]) * here).T
-    width = turned.shape[1] // len(outs)
-    for k, out in enumerate(outs):
-        put(out, 0, turned[:, k * width : (k + 1) * width])
-
-
-def second_kernel(z_ref, p_ref, out_ref):
-    put(out_ref, 0, 0.5 * decode(z_ref[0]) + p_ref[...])
-
-
-def rotate_kernel(chunks, weights, *refs):
+        done.append((0.5 * (moved + (diagonal * (1.0 / 32767.0) - shift[0, 0]) * here)).T)
+    put(out, 0, jnp.concatenate(done, axis=0))
+
+
+def rotate_kernel(weights, *refs):
     ins, out_ref = refs[:-1], refs[-1]
-    members = len(ins) // chunks
-    width = out_ref.shape[2] // chunks
-    for k in range(chunks):
-        total = jnp.zeros((out_ref.shape[1], width), jnp.float32)
-        for m in range(members):
-            total += weights[0, m] * decode(ins[k * members + m][0])
-        out_ref[0, :, k * width : (k + 1) * width] = total
+    total = weights[0, 0] * take(ins[0], 0)
+    for m in range(1, len(ins)):
+        total += weights[0, m] * take(ins[m], 0)
+    out_ref[0] = total
+
+
+def finish_kernel(weights, base_ref, *refs):
+    ins, out_ref = refs[:-1], refs[-1]
+    total = base_ref[0]
+    for m in range(len(ins)):
+        total += weights[0, m] * take(ins[m], 0)
+    out_ref[0] = total
 
 
 def smem():
     return pl.BlockSpec(memory_space=pltpu.SMEM)
 
 
-def call(kernel, grid, in_specs, out_specs, out_shape, scratch, flops, moved):
+def call(kernel, grid, in_specs, out_specs, out_shape, scratch, flops, moved, aliases={}):
     return pl.pallas_call(
         kernel,
         grid=(grid,),
@@ -179,6 +196,7 @@
         out_specs=out_specs,
         out_shape=out_shape,
         scratch_shapes=scratch,
+        input_output_aliases=aliases,
         compiler_params=pltpu.CompilerParams(
             dimension_semantics=("arbitrary",), vmem_limit_bytes=LIMIT
         ),
@@ -205,7 +223,6 @@
 
     piece = pl.BlockSpec((rows, width), lambda q: (0, q))
     whole = pl.BlockSpec((rows, strings), lambda q: (0, 0), pipeline_mode=pl.Buffered(1))
-    tall = pl.BlockSpec((width, strings), lambda q: (0, 0), pipeline_mode=pl.Buffered(1))
     coded = pl.BlockSpec((1, width + PAD, rows), lambda q: (q, 0, 0))
     all_coded = pl.BlockSpec((groups, width + PAD, rows), lambda q: (0, 0, 0), pipeline_mode=pl.Buffered(1))
     tile_spec = pl.BlockSpec((per * fill * blk, blk), lambda q: (q, 0))
@@ -216,31 +233,81 @@
     work = 2 * 2 * rows * strings * fill * blk
     size = 4 * rows * strings
 
-    share = string_blocks.shape[0] // roots
-    mine = lax.dynamic_slice_in_dim(string_blocks, root * share, share, 0)
-    tiles = lax.all_gather(mine, ("col", "root"), axis=0, tiled=True)
+    def exchange(value):
+        have, bit = [value], roots // 2
+        while bit:
+            pairs = [(r, r ^ bit) for r in range(roots)]
+            have = have + [lax.ppermute(h, "root", pairs) for h in have]
+            bit //= 2
+        return have
+
+    masks, bit = [0], roots // 2
+    while bit:
+        masks = masks + [m ^ bit for m in masks]
+        bit //= 2
+    far = jnp.bitwise_xor(root, jnp.array(masks, jnp.int32))
+
+    ring = list(range(0, groups, 2)) + list(range(1, groups, 2))[::-1]
+    spot = jnp.array([ring.index(c) for c in range(groups)], jnp.int32)[lax.axis_index("col")]
+    share = blk // roots
+    mine = string_blocks.reshape(-1, blk, blk)
+    mine = lax.dynamic_slice_in_dim(mine, root * share, share, 1)
+    shards, owners, forth, back = [], [0], mine, mine
+    for hop in range(1, groups // 2 + 1):
+        for way in (1, -1) if 2 * hop < groups else (1,):
+            pairs = [(ring[s], ring[(s + way) % groups]) for s in range(groups)]
+            moved = lax.ppermute(forth if way == 1 else back, "col", pairs)
+            forth, back = (moved, back) if way == 1 else (forth, moved)
+            shards += exchange(moved)
+            owners += [-way * hop] * roots
+    place = jnp.array(ring, jnp.int32)[(spot + jnp.array(owners, jnp.int32)) % groups]
+    place = jnp.stack([place, jnp.concatenate([far[:1]] + [far] * (groups - 1))])
 
     tv = call(pack_kernel, groups, [piece], coded, codes_shape, [], 0, size * 3 // 2)(start)
+    diagonal_later, tv = lax.optimization_barrier((diagonal, tv))
     tv = swap(tv)
 
     slab = width // roots
-    codes = jnp.round(diagonal * 32767.0).astype(jnp.int32).astype(i16)
+    codes = jnp.round(diagonal_later * 32767.0).astype(jnp.int32).astype(i16)
     codes = codes.reshape(rows, groups, roots, slab)
     codes = lax.dynamic_index_in_dim(codes, root, 2, keepdims=False)
     codes = swap(codes.transpose(1, 2, 0))
     turned_diagonal = lax.all_gather(codes, "root", axis=0, tiled=False)
 
-    w, tu = call(
+    once = pl.Buffered(1)
+    shard_spec = pl.BlockSpec(mine.shape, lambda q: (0, 0, 0), pipeline_mode=once)
+    w, tu, tiles = call(
         functools.partial(right_first_kernel, dims),
         groups,
-        [smem(), smem(), whole, piece, tile_spec],
-        [piece, coded],
-        [row_shape, codes_shape],
-        [row_halves, pltpu.VMEM((width, rows), f32)],
+        [smem(), smem(), smem(), whole, piece]
+        + [pl.BlockSpec(string_blocks.shape, lambda q: (0, 0), pipeline_mode=once)]
+        + [shard_spec] * len(shards),
+        [piece, coded, tile_spec],
+        [
+            row_shape,
+            codes_shape,
+            jax.ShapeDtypeStruct((nblk * fill * blk, blk), string_blocks.dtype),
+        ],
+        [
+            row_halves,
+            pltpu.VMEM((width, rows), f32),
+            pltpu.VMEM((nblk * fill * blk, blk), string_blocks.dtype),
+        ],
         work,
-        size * 4 + size // 2,
-    )(block_cols, energy, start, diagonal, tiles)
+        size * 6,
+    )(block_cols, energy, place, start, diagonal, string_blocks, *shards)
     tu = swap(tu)
+
+    base = call(
+        functools.partial(right_second_kernel, dims),
+        groups,
+        [smem(), smem(), whole, piece, piece, tile_spec],
+        pl.BlockSpec((1, rows + PAD, width), lambda q: (q, 0, 0)),
+        jax.ShapeDtypeStruct((groups, rows + PAD, width), i16),
+        [row_halves, pltpu.VMEM((rows, width), f32)],
+        work,
+        size * 5,
+    )(block_cols, energy, w, start, diagonal, tiles)
 
     y = call(
         functools.partial(left_first_kernel, dims),
@@ -253,70 +320,53 @@
         size * 3,
     )(block_cols, tv, tiles)
 
-    base = call(
-        functools.partial(right_second_kernel, dims),
+    weights = rotation[root][far].reshape(1, -1)
+    out = call(
+        rotate_kernel,
         groups,
-        [smem(), smem(), whole, piece, piece, tile_spec],
-        piece,
-        row_shape,
-        [row_halves],
-        work,
-        size * 5,
-    )(block_cols, energy, w, start, diagonal, tiles)
-
-    part = width // chunks
-    chunk_coded = pl.BlockSpec((1, rows + PAD, part), lambda q: (q, 0, 0))
-    chunk_shape = jax.ShapeDtypeStruct((groups, rows + PAD, part), i16)
-    tz = call(
-        functools.partial(left_second_kernel, dims),
-        groups,
-        [
-            smem(),
-            smem(),
-            all_coded,
-            tall,
-            pl.BlockSpec((roots, 1, slab, rows), lambda q: (0, q, 0, 0)),
-            tile_spec,
-        ],
-        [chunk_coded] * chunks,
-        [chunk_shape] * chunks,
-        [col_halves, pltpu.VMEM((rows, width), f32)],
-        work,
-        size * 4,
-    )(block_cols, energy, tu, y, turned_diagonal, tiles)
-
-    masks = [0]
-    held = []
-    for k in range(chunks):
-        z = swap(tz[k])
-        second = call(
-            second_kernel,
-            groups,
-            [chunk_coded, pl.BlockSpec((rows, part), lambda q, k=k: (0, q * chunks + k))],
-            chunk_coded,
-            chunk_shape,
-            [],
-            0,
-            size * 2 // chunks,
-        )(z, base)
-        have, masks, bit = [second], [0], roots // 2
-        while bit:
-            pairs = [(r, r ^ bit) for r in range(roots)]
-            have = have + [lax.ppermute(h, "root", pairs) for h in have]
-            masks = masks + [m ^ bit for m in masks]
-            bit //= 2
-        held += have
-    weights = rotation[root][jnp.bitwise_xor(root, jnp.array(masks, jnp.int32))]
-    return call(
-        functools.partial(rotate_kernel, chunks),
-        groups,
-        [smem()] + [chunk_coded] * len(held),
+        [smem()] + [pl.BlockSpec((1, rows + PAD, width), lambda q: (q, 0, 0))] * roots,
         pl.BlockSpec((1, rows, width), lambda q: (0, 0, q)),
         jax.ShapeDtypeStruct((1, rows, strings), f32),
         [],
         0,
         size * 3,
-    )(weights.reshape(1, -1), *held)
+    )(weights, *exchange(base))
+
+    part = width // chunks
+    chunk_coded = pl.BlockSpec((1, rows + PAD, part), lambda q: (q, 0, 0))
+    for k in range(chunks):
+        z = call(
+            functools.partial(left_second_kernel, dims, k),
+            groups,
+            [
+                smem(),
+                smem(),
+                pl.BlockSpec((groups, part, rows), lambda q, k=k: (0, k, 0), pipeline_mode=once),
+                pl.BlockSpec((groups, PAD, rows), lambda q: (0, width // PAD, 0), pipeline_mode=once),
+                pl.BlockSpec((part, strings), lambda q, k=k: (k, 0), pipeline_mode=once),
+                pl.BlockSpec((roots, 1, slab, rows), lambda q: (0, q, 0, 0)),
+                tile_spec,
+                pl.BlockSpec(memory_space=pl.ANY),
+            ],
+            chunk_coded,
+            jax.ShapeDtypeStruct((groups, rows + PAD, part), i16),
+            [pltpu.VMEM((nblk, 2 * part, blk), jnp.bfloat16)],
+            work // chunks,
+            size * 4 // chunks,
+        )(block_cols, energy, tu, tu, y, turned_diagonal, tiles, base)
+        slot = pl.BlockSpec((1, rows, part), lambda q, k=k: (0, 0, q * chunks + k))
+        out = call(
+            finish_kernel,
+            groups,
+            [smem(), slot] + [chunk_coded] * roots,
+            slot,
+            jax.ShapeDtypeStruct((1, rows, strings), f32),
+            [],
+            0,
+            size * 3 // chunks,
+            {1: 0},
+        )(weights, out, *exchange(swap(z)))
+    return out
 
 
 def plain_blocks(matrix, operator_blocks, block_cols):
@@ -362,8 +412,9 @@
         width = strings // groups
         regular = blk % LANES == 0 and width % blk == 0 and rows == width
         regular = regular and roots & (roots - 1) == 0 and width % (16 * roots) == 0
+        regular = regular and groups % 2 == 0 and blk % (16 * roots) == 0
         args = (coeffs, diagonal, shift, rotation, string_blocks, block_cols)
-        if regular and string_blocks.shape[0] % (16 * roots) == 0:
+        if regular:
             return blocked_shards((roots, groups), *args)
         return plain_shards(*args)
 

time: 390 us -> 418 us (1.072)
  starting transfers between devices: 23 us -> 76.1 us
  blocking collectives: 68.3 us -> 41.4 us
  Pallas kernels: 112 us -> 135 us
  between operations: 14.2 us -> 0.99 us
  waiting for transfers between devices: 155 us -> 142 us
    all_gather x1 -> x0, waiting for transfers between devices: 82.1 us -> none  [blocked_shards(): tiles = lax.all_gather(mine, ('col', 'root'), axis=0, tiled=True)]
    ppermute x9 -> x40, waiting for transfers between devices: 40 us -> 113 us  [the longest x33 76.2 us: exchange(): have = have + [lax.ppermute(h, 'root', pairs) for h in have]]
    ppermute x9 -> x40, starting transfers between devices: 3.93 us -> 52.6 us  [the longest x7 35.6 us: blocked_shards(): moved = lax.ppermute(forth if way == 1 else back, 'col', pairs)]
    all_to_all x2 -> x1, blocking collectives: 50.7 us -> 23.6 us  [swap(): lax.all_to_all(pieces, 'col', split_axis=0, concat_axis=0, tiled=True)]
    pallas_call x5 -> x7, Pallas kernels: 48.2 us -> 64.3 us  [the longest x3 35.3 us: blocked_shards(): call(functools.partial(left_second_kernel, dims, k), groups, [smem(), sme...]
    pallas_call x1, Pallas kernels: 20.1 us -> 26.1 us  [blocked_shards(): call(functools.partial(right_first_kernel, dims), groups, [smem(), smem()...]
    optimization_barrier x0 -> x1, local copies, waits for them, and re-layouts: none -> 6.04 us  [blocked_shards(): diagonal_later, tv = lax.optimization_barrier((diagonal, tv))]
    all_to_all x4 -> x5, starting transfers between devices: 19.1 us -> 23.5 us  [swap(): lax.all_to_all(pieces, 'col', split_axis=0, concat_axis=0, tiled=True)]
  transfers between devices with their start and end apart: 14 -> 45, of which waited for: 7 -> 16; matrix products, arithmetic and copies ran while one was open for 3% -> 1% of each run, Pallas kernels for 21% -> 26%
where the time goes in v2:
time: 418 us; the launch traced here: 416 us
  waiting for transfers between devices  142 us (34%)
  Pallas kernels  135 us (32%)
  starting transfers between devices  76.1 us (18%)
  blocking collectives  41.4 us (10%)
  local copies, waits for them, and re-layouts  15.1 us (4%)
    ppermute x33, waiting for transfers between devices, exchange(): have = have + [lax.ppermute(h, 'root', pairs) for h in have]  76.2 us
    ppermute x7, waiting for transfers between devices, blocked_shards(): moved = lax.ppermute(forth if way == 1 else back, 'col', pairs)  37.1 us
    ppermute x7, starting transfers between devices, blocked_shards(): moved = lax.ppermute(forth if way == 1 else back, 'col', pairs)  35.6 us
    pallas_call x3, Pallas kernels, blocked_shards(): call(functools.partial(left_second_kernel, dims, k), groups, [smem(), sme...  35.3 us
    all_to_all x5, waiting for transfers between devices, swap(): lax.all_to_all(pieces, 'col', split_axis=0, concat_axis=0, tiled=True)  29.3 us
    pallas_call x1, Pallas kernels, blocked_shards(): call(functools.partial(right_first_kernel, dims), groups, [smem(), smem()...  26.1 us
    all_to_all x1, blocking collectives, swap(): lax.all_to_all(pieces, 'col', split_axis=0, concat_axis=0, tiled=True)  23.6 us
    all_to_all x5, starting transfers between devices, swap(): lax.all_to_all(pieces, 'col', split_axis=0, concat_axis=0, tiled=True)  23.5 us
  transfers between devices with their start and end apart: 45, of which 16 were waited for; matrix products, arithmetic and copies ran while one was open for 1% of the time, Pallas kernels for 26%

profile of v2, /device:TPU:0, one launch (start us, length us, event | category | flops | bytes accessed | tf_op | source)
XLA Modules:
  0.0 415.6 jit_solution(5652020170785349681)
XLA Ops:
  0.0 7.5 %shard_map.103 = s16[8,400,384]{2,1,0:T(8,128)(2,1)} custom-call(f32[384,3072]{1,0:T(8,128)} %bitcast.24), custom_call_target="tpu_custom_call" | custom-call | bytes 7077888 | tf_op jit(solution)/shard_map/pallas_call | solution.py:266
  7.6 6.0 %copy.31 = f32[384,3072]{0,1:T(8,128)} copy(f32[384,3072]{1,0:T(8,128)} %d_ref.3) | data formatting | bytes 9437184 | tf_op jit(solution)/shard_map/optimization_barrier | solution.py:267
  13.6 2.8 convert_convert_fusion
  16.6 23.6 %all_to_all.30 = s16[8,96,384]{2,1,0:T(8,128)(2,1)S(1)} all-to-all(s16[8,96,384]{2,1,0:T(8,128)(2,1)S(1)} %dynamic-slice_bitcast_fusion), channel_id=1, replica_groups=mesh['root'=4,'col'=8] {'col'}, dimensions={0} | all-to-all | bytes 1179648 | tf_op jit(solution)/shard_map/all_to_all | solution.py:222
  40.2 3.6 all-to-all-start.1
  44.8 2.0 collective-permute-start.4
  46.9 31.7 %collective-permute-done.4.rest_4_ = bf16[30,32,128]{2,1,0:T(8,128)(2,1)S(1)} collective-permute-done((bf16[30,32,128]{2,1,0:T(8,128)(2,1)S(1)}, bf16[30,32,128]{2,1,0:T(8,128)(2,1)S(1)}, u32[]{:S(2)}, u32[]{:S(2)}) %collective-permute-start.4) | collective-permute-done | bytes 245792 | tf_op jit(solution)/shard_map/ppermute | solution.py:259
  78.6 11.5 %collective-permute-start.12 = (bf16[30,32,128]{2,1,0:T(8,128)(2,1)S(1)}, bf16[30,32,128]{2,1,0:T(8,128)(2,1)S(1)}, u32[]{:S(2)}, u32[]{:S(2)}) collective-permute-start(bf16[30,32,128]{2,1,0:T(8,128)(2,1)S(1)} %collective-permute-done.4.rest_4_), channel_id=1, source_target_pairs={{0,1},{2,0},{4,2},{6,4},{7,6},{5,7},{3,5},{1,3},{8,9},{10,8},{12,1... | collective-permute-start | bytes 737288 | tf_op jit(solution)/shard_map/ppermute | solution.py:259
  90.1 1.5 collective-permute-start.5
  91.6 14.8 %collective-permute-start.8 = (bf16[30,32,128]{2,1,0:T(8,128)(2,1)S(1)}, bf16[30,32,128]{2,1,0:T(8,128)(2,1)S(1)}, u32[]{:S(2)}, u32[]{:S(2)}) collective-permute-start(bf16[30,32,128]{2,1,0:T(8,128)(2,1)S(1)} %collective-permute-done.rest_0_), channel_id=1, source_target_pairs={{0,2},{2,4},{4,6},{6,7},{7,5},{5,3},{3,1},{1,0},{8,10},{10,12},{12... | collective-permute-start | bytes 737288 | tf_op jit(solution)/shard_map/ppermute | solution.py:259
  106.4 2.6 collective-permute-done.12.rest_12_
  109.0 1.5 collective-permute-start.1
  112.7 3.1 collective-permute-done.1.rest_1_
  115.8 4.1 collective-permute-start.16
  119.9 1.6 collective-permute-start.9
  122.1 1.7 collective-permute-done.16.rest_16_
  123.8 2.4 collective-permute-start.24
  126.2 1.5 collective-permute-start.21
  129.4 1.6 collective-permute-start.17
  131.1 1.5 collective-permute-start.25
  133.2 1.7 collective-permute-done.21.rest_21_
  135.5 4.7 %collective-permute-done.17.rest_17_ = bf16[30,32,128]{2,1,0:T(8,128)(2,1)} collective-permute-done((bf16[30,32,128]{2,1,0:T(8,128)(2,1)}, bf16[30,32,128]{2,1,0:T(8,128)(2,1)}, u32[]{:S(2)}, u32[]{:S(2)}) %collective-permute-start.17) | collective-permute-done | bytes 245792 | tf_op jit(solution)/shard_map/ppermute | solution.py:240
  140.2 4.0 collective-permute-done.25.rest_25_
  147.6 26.1 %shard_map.100 = (f32[384,3072]{1,0:T(8,128)}, s16[8,400,384]{2,1,0:T(8,128)(2,1)}, bf16[30720,128]{1,0:T(8,128)(2,1)}) custom-call(s32[24,10]{1,0:T(8,128)} %copy.29.cols, f32[1,1]{1,0:T(1,128)} %bitcast.16.shift, s32[2,29]{1,0:T(2,128)} %pad_add_fusion.place, f32[384,3072]{1,0:T(8,128)} %bitcast.25, f32[384,3072]{1,0:T(8,128)} %d_ref.3, ...), custom_call_target="tpu_custom_call" | custom-call | flops 6039797760 | bytes 28311552 | tf_op jit(solution)/shard_map/pallas_call | solution.py:279
  173.7 1.4 copy-done.5
  175.2 5.3 %all-to-all-start = ((s16[8,400,384]{2,1,0:T(8,128)(2,1)}), s16[8,400,384]{2,1,0:T(8,128)(2,1)S(1)}, u32[]{:S(2)}, u32[]{:S(2)}) async-start(s16[8,400,384]{2,1,0:T(8,128)(2,1)} %get-tuple-element.12), calls=%async_computation | async-start | bytes 4915200 | tf_op jit(solution)/shard_map/all_to_all | solution.py:222
  180.5 17.8 %all-gather.2 = s16[32,96,384]{2,1,0:T(8,128)(2,1)} all-gather(s16[8,96,384]{2,1,0:T(8,128)(2,1)S(1)} %all_to_all.30), channel_id=2, replica_groups=mesh['root'=4,'col'=8] {'root'}, dimensions={0}, use_global_device_ids=true | all-gather | bytes 2949120 | tf_op jit(solution)/shard_map/all_gather | solution.py:275
  198.2 20.0 %shard_map.101.refs_0_.after = s16[8,400,384]{2,1,0:T(8,128)(2,1)} custom-call(s32[24,10]{1,0:T(8,128)} %copy.29.cols, f32[1,1]{1,0:T(1,128)} %bitcast.17.shift, f32[384,3072]{1,0:T(8,128)} %get-tuple-element.10.w_ref, f32[384,3072]{1,0:T(8,128)} %bitcast.26, f32[384,3072]{1,0:T(8,128)} %d_ref.3, bf16[30720,128]{1,0:T(8,128)(2,1)} %get-tuple-element.11.tiles), custom_call_target="tpu_custom_call" | custom-call | flops 6039797760 | bytes 23592960 | tf_op jit(solution)/shard_map/pallas_call | solution.py:301
  218.2 17.5 %shard_map.104.y_ref = f32[384,3072]{1,0:T(8,128)} custom-call(s32[24,10]{1,0:T(8,128)} %copy.29.cols, s16[8,400,384]{2,1,0:T(8,128)(2,1)} %copy-done.5, bf16[30720,128]{1,0:T(8,128)(2,1)} %get-tuple-element.11.tiles), custom_call_target="tpu_custom_call" | custom-call | flops 6039797760 | bytes 14155776 | tf_op jit(solution)/shard_map/pallas_call | solution.py:312
  235.7 1.4 all-to-all-done.tu_ref.tail_ref
  237.1 1.4 copy-done.2
  238.5 11.7 %shard_map.105 = s16[8,400,128]{2,1,0:T(8,128)(2,1)} custom-call(s32[24,10]{1,0:T(8,128)} %copy.29.cols, f32[1,1]{1,0:T(1,128)} %bitcast.18.shift, s16[8,400,384]{2,1,0:T(8,128)(2,1)} %copy-done.2, s16[8,400,384]{2,1,0:T(8,128)(2,1)} %copy-done.2, f32[384,3072]{1,0:T(8,128)} %shard_map.104.y_ref, s16[4,8,96,384]{3,2,1,0:T(8,128)(2,1)} %bitcast.21, ...), custom_call_target="tpu_custom_call" | custom-call | flops 2013265920 | bytes 6291456 | tf_op jit(solution)/shard_map/pallas_call | solution.py:338
  250.2 4.6 %all-to-all-start.3 = ((s16[8,400,128]{2,1,0:T(8,128)(2,1)}), s16[8,400,128]{2,1,0:T(8,128)(2,1)S(1)}, u32[]{:S(2)}, u32[]{:S(2)}) async-start(s16[8,400,128]{2,1,0:T(8,128)(2,1)} %shard_map.105), calls=%async_computation.3 | async-start | bytes 1638400 | tf_op jit(solution)/shard_map/all_to_all | solution.py:222
  256.1 11.8 %shard_map.107 = s16[8,400,128]{2,1,0:T(8,128)(2,1)} custom-call(s32[24,10]{1,0:T(8,128)} %copy.29.cols, f32[1,1]{1,0:T(1,128)} %bitcast.19.shift, s16[8,400,384]{2,1,0:T(8,128)(2,1)} %copy-done.2, s16[8,400,384]{2,1,0:T(8,128)(2,1)} %copy-done.2, f32[384,3072]{1,0:T(8,128)} %shard_map.104.y_ref, s16[4,8,96,384]{3,2,1,0:T(8,128)(2,1)} %bitcast.22, ...), custom_call_target="tpu_custom_call" | custom-call | flops 2013265920 | bytes 6291456 | tf_op jit(solution)/shard_map/pallas_call | solution.py:338
  267.9 8.3 %all-to-all-done.3.refs_0_ = s16[8,400,128]{2,1,0:T(8,128)(2,1)S(1)} async-done(((s16[8,400,128]{2,1,0:T(8,128)(2,1)}), s16[8,400,128]{2,1,0:T(8,128)(2,1)S(1)}, u32[]{:S(2)}, u32[]{:S(2)}) %all-to-all-start.3) | async-done | bytes 819232 | tf_op jit(solution)/shard_map/all_to_all | solution.py:222
  276.2 4.2 %all-to-all-start.4 = ((s16[8,400,128]{2,1,0:T(8,128)(2,1)}), s16[8,400,128]{2,1,0:T(8,128)(2,1)}, u32[]{:S(2)}, u32[]{:S(2)}) async-start(s16[8,400,128]{2,1,0:T(8,128)(2,1)} %shard_map.107), calls=%async_computation.4 | async-start | bytes 1638400 | tf_op jit(solution)/shard_map/all_to_all | solution.py:222
  280.5 30.0 %collective-permute-done.28.refs_1_ = s16[8,400,384]{2,1,0:T(8,128)(2,1)} collective-permute-done((s16[8,400,384]{2,1,0:T(8,128)(2,1)}, s16[8,400,384]{2,1,0:T(8,128)(2,1)}, u32[]{:S(2)}, u32[]{:S(2)}) %collective-permute-start.28) | collective-permute-done | bytes 2457632 | tf_op jit(solution)/shard_map/ppermute | solution.py:240
  310.5 11.7 %shard_map.109 = s16[8,400,128]{2,1,0:T(8,128)(2,1)} custom-call(s32[24,10]{1,0:T(8,128)} %copy.29.cols, f32[1,1]{1,0:T(1,128)} %bitcast.20.shift, s16[8,400,384]{2,1,0:T(8,128)(2,1)} %copy-done.2, s16[8,400,384]{2,1,0:T(8,128)(2,1)} %copy-done.2, f32[384,3072]{1,0:T(8,128)} %shard_map.104.y_ref, s16[4,8,96,384]{3,2,1,0:T(8,128)(2,1)} %bitcast.23, ...), custom_call_target="tpu_custom_call" | custom-call | flops 2013265920 | bytes 6291456 | tf_op jit(solution)/shard_map/pallas_call | solution.py:338
  322.2 5.7 %all-to-all-start.5 = ((s16[8,400,128]{2,1,0:T(8,128)(2,1)}), s16[8,400,128]{2,1,0:T(8,128)(2,1)}, u32[]{:S(2)}, u32[]{:S(2)}) async-start(s16[8,400,128]{2,1,0:T(8,128)(2,1)} %shard_map.109), calls=%async_computation.5 | async-start | bytes 1638400 | tf_op jit(solution)/shard_map/all_to_all | solution.py:222
  328.0 1.2 collective-permute-start.31
  330.0 19.6 %all-to-all-done.5.refs_0_ = s16[8,400,128]{2,1,0:T(8,128)(2,1)} async-done(((s16[8,400,128]{2,1,0:T(8,128)(2,1)}), s16[8,400,128]{2,1,0:T(8,128)(2,1)}, u32[]{:S(2)}, u32[]{:S(2)}) %all-to-all-start.5) | async-done | bytes 819232 | tf_op jit(solution)/shard_map/all_to_all | solution.py:222
  349.6 1.2 collective-permute-start.37
  351.3 15.4 %collective-permute-done.34.refs_1_ = s16[8,400,128]{2,1,0:T(8,128)(2,1)} collective-permute-done((s16[8,400,128]{2,1,0:T(8,128)(2,1)}, s16[8,400,128]{2,1,0:T(8,128)(2,1)}, u32[]{:S(2)}, u32[]{:S(2)}) %collective-permute-start.34) | collective-permute-done | bytes 819232 | tf_op jit(solution)/shard_map/ppermute | solution.py:240
  367.2 16.2 %collective-permute-done.37.refs_1_ = s16[8,400,128]{2,1,0:T(8,128)(2,1)S(1)} collective-permute-done((s16[8,400,128]{2,1,0:T(8,128)(2,1)}, s16[8,400,128]{2,1,0:T(8,128)(2,1)S(1)}, u32[]{:S(2)}, u32[]{:S(2)}) %collective-permute-start.37) | collective-permute-done | bytes 819232 | tf_op jit(solution)/shard_map/ppermute | solution.py:240
  384.6 9.1 %shard_map.102.base_ref = f32[1,384,3072]{2,1,0:T(8,128)} custom-call(f32[1,4]{1,0:T(1,128)} %bitcast.30, s16[8,400,384]{2,1,0:T(8,128)(2,1)} %shard_map.101.refs_0_.after, s16[8,400,384]{2,1,0:T(8,128)(2,1)} %collective-permute-done.28.refs_1_, s16[8,400,384]{2,1,0:T(8,128)(2,1)} %collective-permute-done.29.refs_2_, ...), custom_call_target="tpu_custom_call" | custom-call | bytes 14155776 | tf_op jit(solution)/shard_map/pallas_call | solution.py:324
  393.7 6.7 %shard_map.106.base_ref = f32[1,384,3072]{2,1,0:T(8,128)} custom-call(f32[1,4]{1,0:T(1,128)} %bitcast.31, f32[1,384,3072]{2,1,0:T(8,128)} %shard_map.102.base_ref, s16[8,400,128]{2,1,0:T(8,128)(2,1)} %copy-done.4, s16[8,400,128]{2,1,0:T(8,128)(2,1)} %collective-permute-done.31.refs_1_, ...), custom_call_target="tpu_custom_call", output_to_operand_aliasing={{}: (1, {})} | custom-call | bytes 4718592 | tf_op jit(solution)/shard_map/pallas_call | solution.py:358
  401.3 6.6 %shard_map.108.base_ref = f32[1,384,3072]{2,1,0:T(8,128)} custom-call(f32[1,4]{1,0:T(1,128)} %bitcast.32, f32[1,384,3072]{2,1,0:T(8,128)} %shard_map.106.base_ref, s16[8,400,128]{2,1,0:T(8,128)(2,1)} %all-to-all-done.4.refs_0_, s16[8,400,128]{2,1,0:T(8,128)(2,1)} %collective-permute-done.34.refs_1_, ...), custom_call_target="tpu_custom_call", output_to_operand_aliasing={{}: (1, {})} | custom-call | bytes 4718592 | tf_op jit(solution)/shard_map/pallas_call | solution.py:358
  408.9 6.6 %shard_map.110 = f32[1,384,3072]{2,1,0:T(8,128)} custom-call(f32[1,4]{1,0:T(1,128)} %bitcast.33, f32[1,384,3072]{2,1,0:T(8,128)} %shard_map.108.base_ref, s16[8,400,128]{2,1,0:T(8,128)(2,1)} %all-to-all-done.5.refs_0_, s16[8,400,128]{2,1,0:T(8,128)(2,1)} %copy-done.6, s16[8,400,128]{2,1,0:T(8,128)(2,1)} %copy-done.8, ...), custom_call_target="tpu_custom_call", output_to_operand_aliasing={{}: (1, {})} | custom-call | bytes 4718592 | tf_op jit(solution)/shard_map/pallas_call | solution.py:358
  (124 shorter events, 15.9 us)
Async XLA Ops:
  0.0 383.4 %copy-start = (f32[4,4]{1,0:T(4,128)S(1)}, f32[4,4]{1,0:T(4,128)}, u32[]{:S(2)}) copy-start(f32[4,4]{1,0:T(4,128)} %param.13) | copy-start | bytes 196
  16.5 129.2 %copy-start.9 = (s32[24,10]{0,1:T(8,128)S(1)}, s32[24,10]{0,1:T(8,128)}, u32[]{:S(2)}) copy-start(s32[24,10]{0,1:T(8,128)} %param.15) | copy-start | bytes 2884
  16.5 129.8 %copy-start.1 = (s32[8]{0:T(128)S(1)}, s32[8]{0:T(128)}, u32[]{:S(2)}) copy-start(s32[8]{0:T(128)} %constant.50.clone) | copy-start | bytes 100
  40.2 133.5 %all-to-all-start.1 = ((s16[8,400,384]{2,1,0:T(8,128)(2,1)}), s16[8,400,384]{2,1,0:T(8,128)(2,1)S(1)}, u32[]{:S(2)}, u32[]{:S(2)}) async-start(s16[8,400,384]{2,1,0:T(8,128)(2,1)} %shard_map.103), calls=%async_computation.1 | async-start | bytes 4915200 | tf_op jit(solution)/shard_map/all_to_all | solution.py:222
  44.8 33.8 %collective-permute-start.4 = (bf16[30,32,128]{2,1,0:T(8,128)(2,1)S(1)}, bf16[30,32,128]{2,1,0:T(8,128)(2,1)S(1)}, u32[]{:S(2)}, u32[]{:S(2)}) collective-permute-start(bf16[30,32,128]{2,1,0:T(8,128)(2,1)S(1)} %constant_dynamic-slice_fusion), channel_id=1, source_target_pairs={{0,1},{2,0},{4,2},{6,4},{7,6},{5,7},{3,5},{1,3},{8,9},{10,8},{12,1... | collective-permute-start | bytes 737288 | tf_op jit(solution)/shard_map/ppermute | solution.py:259
  46.8 44.8 %collective-permute-start = (bf16[30,32,128]{2,1,0:T(8,128)(2,1)S(1)}, bf16[30,32,128]{2,1,0:T(8,128)(2,1)S(1)}, u32[]{:S(2)}, u32[]{:S(2)}) collective-permute-start(bf16[30,32,128]{2,1,0:T(8,128)(2,1)S(1)} %constant_dynamic-slice_fusion), channel_id=1, source_target_pairs={{0,2},{2,4},{4,6},{6,7},{7,5},{5,3},{3,1},{1,0},{8,10},{10,12},{12... | collective-permute-start | bytes 737288 | tf_op jit(solution)/shard_map/ppermute | solution.py:259
  78.6 30.4 %collective-permute-start.12 = (bf16[30,32,128]{2,1,0:T(8,128)(2,1)S(1)}, bf16[30,32,128]{2,1,0:T(8,128)(2,1)S(1)}, u32[]{:S(2)}, u32[]{:S(2)}) collective-permute-start(bf16[30,32,128]{2,1,0:T(8,128)(2,1)S(1)} %collective-permute-done.4.rest_4_), channel_id=1, source_target_pairs={{0,1},{2,0},{4,2},{6,4},{7,6},{5,7},{3,5},{1,3},{8,9},{10,8},{12,1... | collective-permute-start | bytes 737288 | tf_op jit(solution)/shard_map/ppermute | solution.py:259
  90.1 20.4 %collective-permute-start.6 = (bf16[30,32,128]{2,1,0:T(8,128)(2,1)S(1)}, bf16[30,32,128]{2,1,0:T(8,128)(2,1)S(1)}, u32[]{:S(2)}, u32[]{:S(2)}) collective-permute-start(bf16[30,32,128]{2,1,0:T(8,128)(2,1)S(1)} %collective-permute-done.4.rest_4_), channel_id=1, source_target_pairs={{0,8},{8,0},{16,24},{24,16},{1,9},{9,1},{17,25},{25,17},{2,10},{10... | collective-permute-start | bytes 737288 | tf_op jit(solution)/shard_map/ppermute | solution.py:240
  90.1 21.1 %collective-permute-start.5 = (bf16[30,32,128]{2,1,0:T(8,128)(2,1)S(1)}, bf16[30,32,128]{2,1,0:T(8,128)(2,1)S(1)}, u32[]{:S(2)}, u32[]{:S(2)}) collective-permute-start(bf16[30,32,128]{2,1,0:T(8,128)(2,1)S(1)} %collective-permute-done.4.rest_4_), channel_id=1, source_target_pairs={{0,16},{8,24},{16,0},{24,8},{1,17},{9,25},{17,1},{25,9},{2,18},{10... | collective-permute-start | bytes 737288 | tf_op jit(solution)/shard_map/ppermute | solution.py:240
  91.6 20.6 %collective-permute-start.8 = (bf16[30,32,128]{2,1,0:T(8,128)(2,1)S(1)}, bf16[30,32,128]{2,1,0:T(8,128)(2,1)S(1)}, u32[]{:S(2)}, u32[]{:S(2)}) collective-permute-start(bf16[30,32,128]{2,1,0:T(8,128)(2,1)S(1)} %collective-permute-done.rest_0_), channel_id=1, source_target_pairs={{0,2},{2,4},{4,6},{6,7},{7,5},{5,3},{3,1},{1,0},{8,10},{10,12},{12... | collective-permute-start | bytes 737288 | tf_op jit(solution)/shard_map/ppermute | solution.py:259
  106.4 6.4 %collective-permute-start.2 = (bf16[30,32,128]{2,1,0:T(8,128)(2,1)S(1)}, bf16[30,32,128]{2,1,0:T(8,128)(2,1)S(1)}, u32[]{:S(2)}, u32[]{:S(2)}) collective-permute-start(bf16[30,32,128]{2,1,0:T(8,128)(2,1)S(1)} %collective-permute-done.rest_0_), channel_id=1, source_target_pairs={{0,8},{8,0},{16,24},{24,16},{1,9},{9,1},{17,25},{25,17},{2,10},{10... | collective-permute-start | bytes 737288 | tf_op jit(solution)/shard_map/ppermute | solution.py:240
  109.0 6.8 %collective-permute-start.1 = (bf16[30,32,128]{2,1,0:T(8,128)(2,1)S(1)}, bf16[30,32,128]{2,1,0:T(8,128)(2,1)S(1)}, u32[]{:S(2)}, u32[]{:S(2)}) collective-permute-start(bf16[30,32,128]{2,1,0:T(8,128)(2,1)S(1)} %collective-permute-done.rest_0_), channel_id=1, source_target_pairs={{0,16},{8,24},{16,0},{24,8},{1,17},{9,25},{17,1},{25,9},{2,18},{10... | collective-permute-start | bytes 737288 | tf_op jit(solution)/shard_map/ppermute | solution.py:240
  110.5 9.4 %collective-permute-start.20 = (bf16[30,32,128]{2,1,0:T(8,128)(2,1)S(1)}, bf16[30,32,128]{2,1,0:T(8,128)(2,1)}, u32[]{:S(2)}, u32[]{:S(2)}) collective-permute-start(bf16[30,32,128]{2,1,0:T(8,128)(2,1)S(1)} %collective-permute-done.12.rest_12_), channel_id=1, source_target_pairs={{0,1},{2,0},{4,2},{6,4},{7,6},{5,7},{3,5},{1,3},{8,9},{10,8},{12,1... | collective-permute-start | bytes 737288 | tf_op jit(solution)/shard_map/ppermute | solution.py:259
  111.2 8.7 %collective-permute-start.14 = (bf16[30,32,128]{2,1,0:T(8,128)(2,1)S(1)}, bf16[30,32,128]{2,1,0:T(8,128)(2,1)S(1)}, u32[]{:S(2)}, u32[]{:S(2)}) collective-permute-start(bf16[30,32,128]{2,1,0:T(8,128)(2,1)S(1)} %collective-permute-done.12.rest_12_), channel_id=1, source_target_pairs={{0,8},{8,0},{16,24},{24,16},{1,9},{9,1},{17,25},{25,17},{2,10},{10... | collective-permute-start | bytes 737288 | tf_op jit(solution)/shard_map/ppermute | solution.py:240
  112.2 9.3 %collective-permute-start.13 = (bf16[30,32,128]{2,1,0:T(8,128)(2,1)S(1)}, bf16[30,32,128]{2,1,0:T(8,128)(2,1)}, u32[]{:S(2)}, u32[]{:S(2)}) collective-permute-start(bf16[30,32,128]{2,1,0:T(8,128)(2,1)S(1)} %collective-permute-done.12.rest_12_), channel_id=1, source_target_pairs={{0,16},{8,24},{16,0},{24,8},{1,17},{9,25},{17,1},{25,9},{2,18},{10... | collective-permute-start | bytes 737288 | tf_op jit(solution)/shard_map/ppermute | solution.py:240
  112.7 8.9 %collective-permute-start.7 = (bf16[30,32,128]{2,1,0:T(8,128)(2,1)S(1)}, bf16[30,32,128]{2,1,0:T(8,128)(2,1)S(1)}, u32[]{:S(2)}, u32[]{:S(2)}) collective-permute-start(bf16[30,32,128]{2,1,0:T(8,128)(2,1)S(1)} %collective-permute-done.5.rest_5_), channel_id=1, source_target_pairs={{0,8},{8,0},{16,24},{24,16},{1,9},{9,1},{17,25},{25,17},{2,10},{10... | collective-permute-start | bytes 737288 | tf_op jit(solution)/shard_map/ppermute | solution.py:240
  115.8 8.0 %collective-permute-start.16 = (bf16[30,32,128]{2,1,0:T(8,128)(2,1)S(1)}, bf16[30,32,128]{2,1,0:T(8,128)(2,1)}, u32[]{:S(2)}, u32[]{:S(2)}) collective-permute-start(bf16[30,32,128]{2,1,0:T(8,128)(2,1)S(1)} %collective-permute-done.8.rest_8_), channel_id=1, source_target_pairs={{0,2},{2,4},{4,6},{6,7},{7,5},{5,3},{3,1},{1,0},{8,10},{10,12},{12... | collective-permute-start | bytes 737288 | tf_op jit(solution)/shard_map/ppermute | solution.py:259
  119.9 6.3 %collective-permute-start.10 = (bf16[30,32,128]{2,1,0:T(8,128)(2,1)S(1)}, bf16[30,32,128]{2,1,0:T(8,128)(2,1)S(1)}, u32[]{:S(2)}, u32[]{:S(2)}) collective-permute-start(bf16[30,32,128]{2,1,0:T(8,128)(2,1)S(1)} %collective-permute-done.8.rest_8_), channel_id=1, source_target_pairs={{0,8},{8,0},{16,24},{24,16},{1,9},{9,1},{17,25},{25,17},{2,10},{10... | collective-permute-start | bytes 737288 | tf_op jit(solution)/shard_map/ppermute | solution.py:240
  119.9 8.8 %collective-permute-start.9 = (bf16[30,32,128]{2,1,0:T(8,128)(2,1)S(1)}, bf16[30,32,128]{2,1,0:T(8,128)(2,1)S(1)}, u32[]{:S(2)}, u32[]{:S(2)}) collective-permute-start(bf16[30,32,128]{2,1,0:T(8,128)(2,1)S(1)} %collective-permute-done.8.rest_8_), channel_id=1, source_target_pairs={{0,16},{8,24},{16,0},{24,8},{1,17},{9,25},{17,1},{25,9},{2,18},{10... | collective-permute-start | bytes 737288 | tf_op jit(solution)/shard_map/ppermute | solution.py:240
  121.5 7.3 %collective-permute-start.3 = (bf16[30,32,128]{2,1,0:T(8,128)(2,1)S(1)}, bf16[30,32,128]{2,1,0:T(8,128)(2,1)S(1)}, u32[]{:S(2)}, u32[]{:S(2)}) collective-permute-start(bf16[30,32,128]{2,1,0:T(8,128)(2,1)S(1)} %collective-permute-done.1.rest_1_), channel_id=1, source_target_pairs={{0,8},{8,0},{16,24},{24,16},{1,9},{9,1},{17,25},{25,17},{2,10},{10... | collective-permute-start | bytes 737288 | tf_op jit(solution)/shard_map/ppermute | solution.py:240
  121.7 7.7 %collective-permute-start.22 = (bf16[30,32,128]{2,1,0:T(8,128)(2,1)}, bf16[30,32,128]{2,1,0:T(8,128)(2,1)S(1)}, u32[]{:S(2)}, u32[]{:S(2)}) collective-permute-start(bf16[30,32,128]{2,1,0:T(8,128)(2,1)} %collective-permute-done.20.rest_20_), channel_id=1, source_target_pairs={{0,8},{8,0},{16,24},{24,16},{1,9},{9,1},{17,25},{25,17},{2,10},{10... | collective-permute-start | bytes 737288 | tf_op jit(solution)/shard_map/ppermute | solution.py:240
  123.8 7.3 %collective-permute-start.24 = (bf16[30,32,128]{2,1,0:T(8,128)(2,1)}, bf16[30,32,128]{2,1,0:T(8,128)(2,1)}, u32[]{:S(2)}, u32[]{:S(2)}) collective-permute-start(bf16[30,32,128]{2,1,0:T(8,128)(2,1)} %collective-permute-done.16.rest_16_), channel_id=1, source_target_pairs={{0,2},{2,4},{4,6},{6,7},{7,5},{5,3},{3,1},{1,0},{8,10},{10,12},{12... | collective-permute-start | bytes 737288 | tf_op jit(solution)/shard_map/ppermute | solution.py:259
  126.2 8.7 %collective-permute-start.21 = (bf16[30,32,128]{2,1,0:T(8,128)(2,1)}, bf16[30,32,128]{2,1,0:T(8,128)(2,1)}, u32[]{:S(2)}, u32[]{:S(2)}) collective-permute-start(bf16[30,32,128]{2,1,0:T(8,128)(2,1)} %collective-permute-done.20.rest_20_), channel_id=1, source_target_pairs={{0,16},{8,24},{16,0},{24,8},{1,17},{9,25},{17,1},{25,9},{2,18},{10... | collective-permute-start | bytes 737288 | tf_op jit(solution)/shard_map/ppermute | solution.py:240
  128.7 6.1 %collective-permute-start.15 = (bf16[30,32,128]{2,1,0:T(8,128)(2,1)}, bf16[30,32,128]{2,1,0:T(8,128)(2,1)}, u32[]{:S(2)}, u32[]{:S(2)}) collective-permute-start(bf16[30,32,128]{2,1,0:T(8,128)(2,1)} %collective-permute-done.13.rest_13_), channel_id=1, source_target_pairs={{0,8},{8,0},{16,24},{24,16},{1,9},{9,1},{17,25},{25,17},{2,10},{10... | collective-permute-start | bytes 737288 | tf_op jit(solution)/shard_map/ppermute | solution.py:240
  128.8 6.6 %collective-permute-start.18 = (bf16[30,32,128]{2,1,0:T(8,128)(2,1)}, bf16[30,32,128]{2,1,0:T(8,128)(2,1)}, u32[]{:S(2)}, u32[]{:S(2)}) collective-permute-start(bf16[30,32,128]{2,1,0:T(8,128)(2,1)} %collective-permute-done.16.rest_16_), channel_id=1, source_target_pairs={{0,8},{8,0},{16,24},{24,16},{1,9},{9,1},{17,25},{25,17},{2,10},{10... | collective-permute-start | bytes 737288 | tf_op jit(solution)/shard_map/ppermute | solution.py:240
  129.4 10.8 %collective-permute-start.17 = (bf16[30,32,128]{2,1,0:T(8,128)(2,1)}, bf16[30,32,128]{2,1,0:T(8,128)(2,1)}, u32[]{:S(2)}, u32[]{:S(2)}) collective-permute-start(bf16[30,32,128]{2,1,0:T(8,128)(2,1)} %collective-permute-done.16.rest_16_), channel_id=1, source_target_pairs={{0,16},{8,24},{16,0},{24,8},{1,17},{9,25},{17,1},{25,9},{2,18},{10... | collective-permute-start | bytes 737288 | tf_op jit(solution)/shard_map/ppermute | solution.py:240
  131.1 13.1 %collective-permute-start.25 = (bf16[30,32,128]{2,1,0:T(8,128)(2,1)}, bf16[30,32,128]{2,1,0:T(8,128)(2,1)}, u32[]{:S(2)}, u32[]{:S(2)}) collective-permute-start(bf16[30,32,128]{2,1,0:T(8,128)(2,1)} %collective-permute-done.24.rest_24_), channel_id=1, source_target_pairs={{0,16},{8,24},{16,0},{24,8},{1,17},{9,25},{17,1},{25,9},{2,18},{10... | collective-permute-start | bytes 737288 | tf_op jit(solution)/shard_map/ppermute | solution.py:240
  134.9 12.7 %collective-permute-start.11 = (bf16[30,32,128]{2,1,0:T(8,128)(2,1)}, bf16[30,32,128]{2,1,0:T(8,128)(2,1)}, u32[]{:S(2)}, u32[]{:S(2)}) collective-permute-start(bf16[30,32,128]{2,1,0:T(8,128)(2,1)} %copy-done.22), channel_id=1, source_target_pairs={{0,8},{8,0},{16,24},{24,16},{1,9},{9,1},{17,25},{25,17},{2,10},{10... | collective-permute-start | bytes 737288 | tf_op jit(solution)/shard_map/ppermute | solution.py:240
  134.9 12.7 %collective-permute-start.26 = (bf16[30,32,128]{2,1,0:T(8,128)(2,1)}, bf16[30,32,128]{2,1,0:T(8,128)(2,1)}, u32[]{:S(2)}, u32[]{:S(2)}) collective-permute-start(bf16[30,32,128]{2,1,0:T(8,128)(2,1)} %collective-permute-done.24.rest_24_), channel_id=1, source_target_pairs={{0,8},{8,0},{16,24},{24,16},{1,9},{9,1},{17,25},{25,17},{2,10},{10... | collective-permute-start | bytes 737288 | tf_op jit(solution)/shard_map/ppermute | solution.py:240
  135.4 12.2 %collective-permute-start.23 = (bf16[30,32,128]{2,1,0:T(8,128)(2,1)}, bf16[30,32,128]{2,1,0:T(8,128)(2,1)}, u32[]{:S(2)}, u32[]{:S(2)}) collective-permute-start(bf16[30,32,128]{2,1,0:T(8,128)(2,1)} %collective-permute-done.21.rest_21_), channel_id=1, source_target_pairs={{0,8},{8,0},{16,24},{24,16},{1,9},{9,1},{17,25},{25,17},{2,10},{10... | collective-permute-start | bytes 737288 | tf_op jit(solution)/shard_map/ppermute | solution.py:240
  140.2 7.4 %collective-permute-start.19 = (bf16[30,32,128]{2,1,0:T(8,128)(2,1)}, bf16[30,32,128]{2,1,0:T(8,128)(2,1)}, u32[]{:S(2)}, u32[]{:S(2)}) collective-permute-start(bf16[30,32,128]{2,1,0:T(8,128)(2,1)} %collective-permute-done.17.rest_17_), channel_id=1, source_target_pairs={{0,8},{8,0},{16,24},{24,16},{1,9},{9,1},{17,25},{25,17},{2,10},{10... | collective-permute-start | bytes 737288 | tf_op jit(solution)/shard_map/ppermute | solution.py:240
  144.2 3.4 collective-permute-start.27
  175.2 61.9 %all-to-all-start = ((s16[8,400,384]{2,1,0:T(8,128)(2,1)}), s16[8,400,384]{2,1,0:T(8,128)(2,1)S(1)}, u32[]{:S(2)}, u32[]{:S(2)}) async-start(s16[8,400,384]{2,1,0:T(8,128)(2,1)} %get-tuple-element.12), calls=%async_computation | async-start | bytes 4915200 | tf_op jit(solution)/shard_map/all_to_all | solution.py:222
  250.2 26.0 %all-to-all-start.3 = ((s16[8,400,128]{2,1,0:T(8,128)(2,1)}), s16[8,400,128]{2,1,0:T(8,128)(2,1)S(1)}, u32[]{:S(2)}, u32[]{:S(2)}) async-start(s16[8,400,128]{2,1,0:T(8,128)(2,1)} %shard_map.105), calls=%async_computation.3 | async-start | bytes 1638400 | tf_op jit(solution)/shard_map/all_to_all | solution.py:222
  254.9 55.6 %collective-permute-start.28 = (s16[8,400,384]{2,1,0:T(8,128)(2,1)}, s16[8,400,384]{2,1,0:T(8,128)(2,1)}, u32[]{:S(2)}, u32[]{:S(2)}) collective-permute-start(s16[8,400,384]{2,1,0:T(8,128)(2,1)} %shard_map.101.refs_0_.after), channel_id=1, source_target_pairs={{0,16},{8,24},{16,0},{24,8},{1,17},{9,25},{17,1},{25,9},{2,18},{10... | collective-permute-start | bytes 7372808 | tf_op jit(solution)/shard_map/ppermute | solution.py:240
  276.2 46.0 %all-to-all-start.4 = ((s16[8,400,128]{2,1,0:T(8,128)(2,1)}), s16[8,400,128]{2,1,0:T(8,128)(2,1)}, u32[]{:S(2)}, u32[]{:S(2)}) async-start(s16[8,400,128]{2,1,0:T(8,128)(2,1)} %shard_map.107), calls=%async_computation.4 | async-start | bytes 1638400 | tf_op jit(solution)/shard_map/all_to_all | solution.py:222
  280.4 49.5 %collective-permute-start.29 = (s16[8,400,384]{2,1,0:T(8,128)(2,1)S(1)}, s16[8,400,384]{2,1,0:T(8,128)(2,1)}, u32[]{:S(2)}, u32[]{:S(2)}) collective-permute-start(s16[8,400,384]{2,1,0:T(8,128)(2,1)S(1)} %copy-done.3), channel_id=1, source_target_pairs={{0,8},{8,0},{16,24},{24,16},{1,9},{9,1},{17,25},{25,17},{2,10},{10... | collective-permute-start | bytes 7372808 | tf_op jit(solution)/shard_map/ppermute | solution.py:240
  310.5 40.3 %collective-permute-start.30 = (s16[8,400,384]{2,1,0:T(8,128)(2,1)}, s16[8,400,384]{2,1,0:T(8,128)(2,1)}, u32[]{:S(2)}, u32[]{:S(2)}) collective-permute-start(s16[8,400,384]{2,1,0:T(8,128)(2,1)} %collective-permute-done.28.refs_1_), channel_id=1, source_target_pairs={{0,8},{8,0},{16,24},{24,16},{1,9},{9,1},{17,25},{25,17},{2,10},{10... | collective-permute-start | bytes 7372808 | tf_op jit(solution)/shard_map/ppermute | solution.py:240
  322.2 27.3 %all-to-all-start.5 = ((s16[8,400,128]{2,1,0:T(8,128)(2,1)}), s16[8,400,128]{2,1,0:T(8,128)(2,1)}, u32[]{:S(2)}, u32[]{:S(2)}) async-start(s16[8,400,128]{2,1,0:T(8,128)(2,1)} %shard_map.109), calls=%async_computation.5 | async-start | bytes 1638400 | tf_op jit(solution)/shard_map/all_to_all | solution.py:222
  328.0 22.8 %collective-permute-start.31 = (s16[8,400,128]{2,1,0:T(8,128)(2,1)S(1)}, s16[8,400,128]{2,1,0:T(8,128)(2,1)}, u32[]{:S(2)}, u32[]{:S(2)}) collective-permute-start(s16[8,400,128]{2,1,0:T(8,128)(2,1)S(1)} %all-to-all-done.3.refs_0_), channel_id=1, source_target_pairs={{0,16},{8,24},{16,0},{24,8},{1,17},{9,25},{17,1},{25,9},{2,18},{10... | collective-permute-start | bytes 2457608 | tf_op jit(solution)/shard_map/ppermute | solution.py:240
  329.2 37.5 %collective-permute-start.34 = (s16[8,400,128]{2,1,0:T(8,128)(2,1)}, s16[8,400,128]{2,1,0:T(8,128)(2,1)}, u32[]{:S(2)}, u32[]{:S(2)}) collective-permute-start(s16[8,400,128]{2,1,0:T(8,128)(2,1)} %all-to-all-done.4.refs_0_), channel_id=1, source_target_pairs={{0,16},{8,24},{16,0},{24,8},{1,17},{9,25},{17,1},{25,9},{2,18},{10... | collective-permute-start | bytes 2457608 | tf_op jit(solution)/shard_map/ppermute | solution.py:240
  330.0 36.7 %collective-permute-start.32 = (s16[8,400,128]{2,1,0:T(8,128)(2,1)S(1)}, s16[8,400,128]{2,1,0:T(8,128)(2,1)}, u32[]{:S(2)}, u32[]{:S(2)}) collective-permute-start(s16[8,400,128]{2,1,0:T(8,128)(2,1)S(1)} %all-to-all-done.3.refs_0_), channel_id=1, source_target_pairs={{0,8},{8,0},{16,24},{24,16},{1,9},{9,1},{17,25},{25,17},{2,10},{10... | collective-permute-start | bytes 2457608 | tf_op jit(solution)/shard_map/ppermute | solution.py:240
  349.6 33.9 %collective-permute-start.37 = (s16[8,400,128]{2,1,0:T(8,128)(2,1)}, s16[8,400,128]{2,1,0:T(8,128)(2,1)S(1)}, u32[]{:S(2)}, u32[]{:S(2)}) collective-permute-start(s16[8,400,128]{2,1,0:T(8,128)(2,1)} %all-to-all-done.5.refs_0_), channel_id=1, source_target_pairs={{0,16},{8,24},{16,0},{24,8},{1,17},{9,25},{17,1},{25,9},{2,18},{10... | collective-permute-start | bytes 2457608 | tf_op jit(solution)/shard_map/ppermute | solution.py:240
  350.8 49.6 %collective-permute-start.35 = (s16[8,400,128]{2,1,0:T(8,128)(2,1)}, s16[8,400,128]{2,1,0:T(8,128)(2,1)S(1)}, u32[]{:S(2)}, u32[]{:S(2)}) collective-permute-start(s16[8,400,128]{2,1,0:T(8,128)(2,1)} %all-to-all-done.4.refs_0_), channel_id=1, source_target_pairs={{0,8},{8,0},{16,24},{24,16},{1,9},{9,1},{17,25},{25,17},{2,10},{10... | collective-permute-start | bytes 2457608 | tf_op jit(solution)/shard_map/ppermute | solution.py:240
  350.8 42.9 %collective-permute-start.33 = (s16[8,400,128]{2,1,0:T(8,128)(2,1)}, s16[8,400,128]{2,1,0:T(8,128)(2,1)}, u32[]{:S(2)}, u32[]{:S(2)}) collective-permute-start(s16[8,400,128]{2,1,0:T(8,128)(2,1)} %collective-permute-done.31.refs_1_), channel_id=1, source_target_pairs={{0,8},{8,0},{16,24},{24,16},{1,9},{9,1},{17,25},{25,17},{2,10},{10... | collective-permute-start | bytes 2457608 | tf_op jit(solution)/shard_map/ppermute | solution.py:240
  366.7 33.7 %collective-permute-start.36 = (s16[8,400,128]{2,1,0:T(8,128)(2,1)}, s16[8,400,128]{2,1,0:T(8,128)(2,1)}, u32[]{:S(2)}, u32[]{:S(2)}) collective-permute-start(s16[8,400,128]{2,1,0:T(8,128)(2,1)} %collective-permute-done.34.refs_1_), channel_id=1, source_target_pairs={{0,8},{8,0},{16,24},{24,16},{1,9},{9,1},{17,25},{25,17},{2,10},{10... | collective-permute-start | bytes 2457608 | tf_op jit(solution)/shard_map/ppermute | solution.py:240
  366.7 41.3 %collective-permute-start.38 = (s16[8,400,128]{2,1,0:T(8,128)(2,1)}, s16[8,400,128]{2,1,0:T(8,128)(2,1)S(1)}, u32[]{:S(2)}, u32[]{:S(2)}) collective-permute-start(s16[8,400,128]{2,1,0:T(8,128)(2,1)} %all-to-all-done.5.refs_0_), channel_id=1, source_target_pairs={{0,8},{8,0},{16,24},{24,16},{1,9},{9,1},{17,25},{25,17},{2,10},{10... | collective-permute-start | bytes 2457608 | tf_op jit(solution)/shard_map/ppermute | solution.py:240
  383.4 24.6 %collective-permute-start.39 = (s16[8,400,128]{2,1,0:T(8,128)(2,1)S(1)}, s16[8,400,128]{2,1,0:T(8,128)(2,1)}, u32[]{:S(2)}, u32[]{:S(2)}) collective-permute-start(s16[8,400,128]{2,1,0:T(8,128)(2,1)S(1)} %collective-permute-done.37.refs_1_), channel_id=1, source_target_pairs={{0,8},{8,0},{16,24},{24,16},{1,9},{9,1},{17,25},{25,17},{2,10},{10... | collective-permute-start | bytes 2457608 | tf_op jit(solution)/shard_map/ppermute | solution.py:240
  (24 other events, 635.2 us)

commit v3 on v2

--- a/solution.py
+++ b/solution.py
@@ -70,37 +70,37 @@
     return total[:rows] + total[rows:]
 
 
-def pack_kernel(v_ref, out_ref):
+def pack_kernel(far, v_ref, d_ref, out_ref, turned):
     put(out_ref, 0, v_ref[...].T)
-
-
-def right_first_kernel(dims, cols, shift, place, v_ref, d_ref, own, *rest):
+    turned[...] = d_ref[...].T
+    width, rows = turned.shape
+    slab = out_ref.shape[1] - width - PAD
+    here = turned[pl.ds(pl.multiple_of(far[0, 0] * slab, slab), slab), :]
+    codes = jnp.floor(here * 32767.0 + 0.5)
+    out_ref[0, pl.ds(width + PAD, slab), :] = codes.astype(jnp.int32).astype(jnp.int16)
+
+
+def right_first_kernel(dims, cols, shift, far, v_ref, d_ref, *rest):
     nblk, fill, blk, per = dims
-    shards, (w_ref, u_ref, tiles_ref, halves, turned, tiles) = rest[:-6], rest[-6:]
+    shares, (w_ref, u_ref, tiles, halves, turned) = rest[:-5], rest[-5:]
     step = pl.program_id(0)
-    size = own.shape[0]
 
     @pl.when(step == 0)
     def _():
         for b in range(nblk):
             split_into(halves, b, v_ref[:, b * blk : (b + 1) * blk])
-        tiles[pl.ds(pl.multiple_of(place[0, 0] * size, size), size), :] = own[...]
-
-        @pl.loop(0, size // blk)
-        def _(b):
-            for k, shard in enumerate(shards):
-                share = shard.shape[1]
-                base = place[0, 1 + k] * size + place[1, 1 + k] * share
-                at = pl.multiple_of(base + b * blk, share)
-                tiles[pl.ds(at, share), :] = shard[b]
-
-    here_tiles = tiles.at[pl.ds(pl.multiple_of(step * size, size), size), :]
-    tiles_ref[...] = here_tiles[...]
+
+    roots = far.shape[1]
+    for n, share in enumerate(shares):
+        count, height = share.shape[:2]
+        for b in range(count):
+            at = ((n // roots) * count + b) * blk + far[0, n % roots] * height
+            tiles[pl.ds(pl.multiple_of(at, height), height), :] = share[b]
     for t in range(per):
         lanes = slice(t * blk, (t + 1) * blk)
         block = step * per + t
         here = v_ref[:, pl.ds(pl.multiple_of(block * blk, blk), blk)]
-        moved = apply_row(halves, here_tiles, t, cols, block, fill, blk)
+        moved = apply_row(halves, tiles, t, cols, block, fill, blk)
         whole = moved + (d_ref[:, lanes] - shift[0, 0]) * here
         w_ref[:, lanes] = whole
         turned[lanes, :] = (moved + whole).T
@@ -140,9 +140,9 @@
     put(p_ref, 0, part[...])
 
 
-def left_second_kernel(dims, chunk, cols, shift, tu_ref, tail_ref, y_ref, dt_ref, tiles, after, out, halves):
+def left_second_kernel(dims, chunk, cols, shift, far, tu_ref, tail_ref, y_ref, tiles, *rest):
     nblk, fill, blk, per = dims
-    del after
+    slabs, (_, out, halves, turned) = rest[:-4], rest[-4:]
     step = pl.program_id(0)
     part = y_ref.shape[0]
 
@@ -153,16 +153,15 @@
             for t in range(per):
                 split_into(halves, p * per + t, value[:, t * blk : (t + 1) * blk])
 
+    for m, slab in enumerate(slabs):
+        height = slab.shape[1]
+        at = pl.multiple_of(far[0, m] * height, height)
+        turned[pl.ds(at, height), :] = slab[0].astype(jnp.int32).astype(jnp.float32)
     done = []
     for t in range(per):
-        lanes = slice(t * blk, (t + 1) * blk)
         block = step * per + t
         here = y_ref[:, pl.ds(pl.multiple_of(block * blk, blk), blk)]
-        diagonal = [
-            dt_ref[r, 0, :, lanes].astype(jnp.int32).astype(jnp.float32)
-            for r in range(dt_ref.shape[0])
-        ]
-        diagonal = jnp.concatenate(diagonal, axis=0)[chunk * part : (chunk + 1) * part]
+        diagonal = turned[chunk * part : (chunk + 1) * part, t * blk : (t + 1) * blk]
         moved = apply_row(halves, tiles, t, cols, block, fill, blk)
         done.append((0.5 * (moved + (diagonal * (1.0 / 32767.0) - shift[0, 0]) * here)).T)
     put(out, 0, jnp.concatenate(done, axis=0))
@@ -233,11 +232,14 @@
     work = 2 * 2 * rows * strings * fill * blk
     size = 4 * rows * strings
 
-    def exchange(value):
+    def exchange(value, late=None):
         have, bit = [value], roots // 2
         while bit:
             pairs = [(r, r ^ bit) for r in range(roots)]
             have = have + [lax.ppermute(h, "root", pairs) for h in have]
+            if late is not None:
+                have = list(lax.optimization_barrier(tuple(have) + (late,)))[:-1]
+                late = None
             bit //= 2
         return have
 
@@ -246,57 +248,52 @@
         masks = masks + [m ^ bit for m in masks]
         bit //= 2
     far = jnp.bitwise_xor(root, jnp.array(masks, jnp.int32))
-
-    ring = list(range(0, groups, 2)) + list(range(1, groups, 2))[::-1]
-    spot = jnp.array([ring.index(c) for c in range(groups)], jnp.int32)[lax.axis_index("col")]
+    weights = rotation[root][far].reshape(1, -1)
+    far = far.reshape(1, -1)
+
     share = blk // roots
-    mine = string_blocks.reshape(-1, blk, blk)
+    local = string_blocks.shape[0] // blk
+    parts = 2 if local % 2 == 0 else 1
+    count = local // parts
+    mine = string_blocks.reshape(local, blk, blk)
     mine = lax.dynamic_slice_in_dim(mine, root * share, share, 1)
-    shards, owners, forth, back = [], [0], mine, mine
-    for hop in range(1, groups // 2 + 1):
-        for way in (1, -1) if 2 * hop < groups else (1,):
-            pairs = [(ring[s], ring[(s + way) % groups]) for s in range(groups)]
-            moved = lax.ppermute(forth if way == 1 else back, "col", pairs)
-            forth, back = (moved, back) if way == 1 else (forth, moved)
-            shards += exchange(moved)
-            owners += [-way * hop] * roots
-    place = jnp.array(ring, jnp.int32)[(spot + jnp.array(owners, jnp.int32)) % groups]
-    place = jnp.stack([place, jnp.concatenate([far[:1]] + [far] * (groups - 1))])
-
-    tv = call(pack_kernel, groups, [piece], coded, codes_shape, [], 0, size * 3 // 2)(start)
-    diagonal_later, tv = lax.optimization_barrier((diagonal, tv))
+    shares = []
+    for n in range(parts):
+        shares += exchange(lax.all_gather(mine[n * count : (n + 1) * count], "col", axis=0, tiled=True))
+
+    slab = width // roots
+    height = width + PAD + slab
+    tv = call(
+        pack_kernel,
+        groups,
+        [smem(), piece, piece],
+        pl.BlockSpec((1, height, rows), lambda q: (q, 0, 0)),
+        jax.ShapeDtypeStruct((groups, height, rows), i16),
+        [pltpu.VMEM((width, rows), f32)],
+        0,
+        size * 3,
+    )(far, start, diagonal)
     tv = swap(tv)
 
-    slab = width // roots
-    codes = jnp.round(diagonal_later * 32767.0).astype(jnp.int32).astype(i16)
-    codes = codes.reshape(rows, groups, roots, slab)
-    codes = lax.dynamic_index_in_dim(codes, root, 2, keepdims=False)
-    codes = swap(codes.transpose(1, 2, 0))
-    turned_diagonal = lax.all_gather(codes, "root", axis=0, tiled=False)
-
     once = pl.Buffered(1)
-    shard_spec = pl.BlockSpec(mine.shape, lambda q: (0, 0, 0), pipeline_mode=once)
+    share_spec = pl.BlockSpec((count, share, blk), lambda q: (q, 0, 0))
     w, tu, tiles = call(
         functools.partial(right_first_kernel, dims),
         groups,
         [smem(), smem(), smem(), whole, piece]
-        + [pl.BlockSpec(string_blocks.shape, lambda q: (0, 0), pipeline_mode=once)]
-        + [shard_spec] * len(shards),
+        + [share_spec] * len(shares),
         [piece, coded, tile_spec],
         [
             row_shape,
             codes_shape,
             jax.ShapeDtypeStruct((nblk * fill * blk, blk), string_blocks.dtype),
         ],
-        [
-            row_halves,
-            pltpu.VMEM((width, rows), f32),
-            pltpu.VMEM((nblk * fill * blk, blk), string_blocks.dtype),
-        ],
+        [row_halves, pltpu.VMEM((width, rows), f32)],
         work,
         size * 6,
-    )(block_cols, energy, place, start, diagonal, string_blocks, *shards)
+    )(block_cols, energy, far, start, diagonal, *shares)
     tu = swap(tu)
+    slabs = exchange(tv[:, width + PAD :])
 
     base = call(
         functools.partial(right_second_kernel, dims),
@@ -320,7 +317,32 @@
         size * 3,
     )(block_cols, tv, tiles)
 
-    weights = rotation[root][far].reshape(1, -1)
+    part = width // chunks
+    chunk_coded = pl.BlockSpec((1, rows + PAD, part), lambda q: (q, 0, 0))
+    turned = []
+    for k in range(chunks):
+        z = call(
+            functools.partial(left_second_kernel, dims, k),
+            groups,
+            [
+                smem(),
+                smem(),
+                smem(),
+                pl.BlockSpec((groups, part, rows), lambda q, k=k: (0, k, 0), pipeline_mode=once),
+                pl.BlockSpec((groups, PAD, rows), lambda q: (0, width // PAD, 0), pipeline_mode=once),
+                pl.BlockSpec((part, strings), lambda q, k=k: (k, 0), pipeline_mode=once),
+                tile_spec,
+            ]
+            + [pl.BlockSpec((1, slab, rows), lambda q: (q, 0, 0))] * roots
+            + [pl.BlockSpec(memory_space=pl.ANY)],
+            chunk_coded,
+            jax.ShapeDtypeStruct((groups, rows + PAD, part), i16),
+            [pltpu.VMEM((nblk, 2 * part, blk), jnp.bfloat16), pltpu.VMEM((width, rows), f32)],
+            work // chunks,
+            size * 4 // chunks,
+        )(block_cols, energy, far, tu, tu, y, tiles, *slabs, base)
+        turned.append(z)
+
     out = call(
         rotate_kernel,
         groups,
@@ -330,30 +352,12 @@
         [],
         0,
         size * 3,
-    )(weights, *exchange(base))
-
-    part = width // chunks
-    chunk_coded = pl.BlockSpec((1, rows + PAD, part), lambda q: (q, 0, 0))
+    )(weights, *exchange(base, turned[-1]))
+
     for k in range(chunks):
-        z = call(
-            functools.partial(left_second_kernel, dims, k),
-            groups,
-            [
-                smem(),
-                smem(),
-                pl.BlockSpec((groups, part, rows), lambda q, k=k: (0, k, 0), pipeline_mode=once),
-                pl.BlockSpec((groups, PAD, rows), lambda q: (0, width // PAD, 0), pipeline_mode=once),
-                pl.BlockSpec((part, strings), lambda q, k=k: (k, 0), pipeline_mode=once),
-                pl.BlockSpec((roots, 1, slab, rows), lambda q: (0, q, 0, 0)),
-                tile_spec,
-                pl.BlockSpec(memory_space=pl.ANY),
-            ],
-            chunk_coded,
-            jax.ShapeDtypeStruct((groups, rows + PAD, part), i16),
-            [pltpu.VMEM((nblk, 2 * part, blk), jnp.bfloat16)],
-            work // chunks,
-            size * 4 // chunks,
-        )(block_cols, energy, tu, tu, y, turned_diagonal, tiles, base)
+        back, late = swap(turned[k]), None
+        if k == chunks - 1:
+            late = out
         slot = pl.BlockSpec((1, rows, part), lambda q, k=k: (0, 0, q * chunks + k))
         out = call(
             finish_kernel,
@@ -365,7 +369,7 @@
             0,
             size * 3 // chunks,
             {1: 0},
-        )(weights, out, *exchange(swap(z)))
+        )(weights, out, *exchange(back, late))
     return out
 
 

time: 418 us -> 392 us (0.938)
  blocking collectives: 41.4 us -> 127 us
  waiting for transfers between devices: 142 us -> 86.8 us
  starting transfers between devices: 76.1 us -> 32.6 us
  local copies, waits for them, and re-layouts: 15.1 us -> 9.31 us
    all_gather x1 -> x2, blocking collectives: 17.8 us -> 127 us  [blocked_shards(): lax.all_gather(mine[n * count:(n + 1) * count], 'col', axis=0, tiled=True)]
    ppermute x7 -> x0, waiting for transfers between devices: 37.1 us -> none  [blocked_shards(): moved = lax.ppermute(forth if way == 1 else back, 'col', pairs)]
    ppermute x7 -> x0, starting transfers between devices: 35.6 us -> none  [blocked_shards(): moved = lax.ppermute(forth if way == 1 else back, 'col', pairs)]
    all_to_all x1 -> x0, blocking collectives: 23.6 us -> none  [swap(): lax.all_to_all(pieces, 'col', split_axis=0, concat_axis=0, tiled=True)]
    all_to_all x5, waiting for transfers between devices: 29.3 us -> 19.4 us  [swap(): lax.all_to_all(pieces, 'col', split_axis=0, concat_axis=0, tiled=True)]
    ppermute x33 -> x21, waiting for transfers between devices: 76.2 us -> 67.4 us  [exchange(): have = have + [lax.ppermute(h, 'root', pairs) for h in have]]
    ppermute x33 -> x21, starting transfers between devices: 17 us -> 8.82 us  [exchange(): have = have + [lax.ppermute(h, 'root', pairs) for h in have]]
    optimization_barrier x1 -> x0, local copies, waits for them, and re-layouts: 6.04 us -> none  [blocked_shards(): diagonal_later, tv = lax.optimization_barrier((diagonal, tv))]
  transfers between devices with their start and end apart: 45 -> 26, of which waited for: 16 -> 10; matrix products, arithmetic and copies ran while one was open for 1% -> 1% of each run, Pallas kernels for 26% -> 30%
where the time goes in v3:
time: 392 us; the launch traced here: 390 us
  Pallas kernels  133 us (34%)
  blocking collectives  127 us (32%)
  waiting for transfers between devices  86.8 us (22%)
  starting transfers between devices  32.6 us (8%)
  local copies, waits for them, and re-layouts  9.31 us (2%)
    all_gather x2, blocking collectives, blocked_shards(): lax.all_gather(mine[n * count:(n + 1) * count], 'col', axis=0, tiled=True)  127 us
    ppermute x21, waiting for transfers between devices, exchange(): have = have + [lax.ppermute(h, 'root', pairs) for h in have]  67.4 us
    pallas_call x3, Pallas kernels, blocked_shards(): call(functools.partial(left_second_kernel, dims, k), groups, [smem(), sme...  35.1 us
    all_to_all x5, starting transfers between devices, swap(): lax.all_to_all(pieces, 'col', split_axis=0, concat_axis=0, tiled=True)  23.8 us
    pallas_call x1, Pallas kernels, blocked_shards(): call(functools.partial(right_first_kernel, dims), groups, [smem(), smem()...  22.1 us
    pallas_call x1, Pallas kernels, blocked_shards(): call(functools.partial(right_second_kernel, dims), groups, [smem(), smem(...  20 us
    pallas_call x3, Pallas kernels, blocked_shards(): call(finish_kernel, groups, [smem(), slot] + [chunk_coded] * roots, slot,...  19.9 us
    all_to_all x5, waiting for transfers between devices, swap(): lax.all_to_all(pieces, 'col', split_axis=0, concat_axis=0, tiled=True)  19.4 us
  transfers between devices with their start and end apart: 26, of which 10 were waited for; matrix products, arithmetic and copies ran while one was open for 1% of the time, Pallas kernels for 30%

profile of v3, /device:TPU:0, one launch (start us, length us, event | category | flops | bytes accessed | tf_op | source)
XLA Modules:
  0.0 390.4 jit_solution(15871931074356631217)
XLA Ops:
  0.0 1.2 xor_bitcast_fusion
  1.2 8.8 %shard_map.75 = s16[8,496,384]{2,1,0:T(8,128)(2,1)} custom-call(s32[1,4]{1,0:T(1,128)} %get-tuple-element.21.far, f32[384,3072]{1,0:T(8,128)} %bitcast.13, f32[384,3072]{1,0:T(8,128)} %d_ref.5), custom_call_target="tpu_custom_call" | custom-call | bytes 14155776 | tf_op jit(solution)/shard_map/pallas_call | solution.py:266
  10.0 7.4 %all-to-all-start.1 = ((s16[8,496,384]{2,1,0:T(8,128)(2,1)}), s16[8,496,384]{2,1,0:T(8,128)(2,1)S(1)}, u32[]{:S(2)}, u32[]{:S(2)}) async-start(s16[8,496,384]{2,1,0:T(8,128)(2,1)} %shard_map.75), calls=%async_computation.1 | async-start | bytes 6094848 | tf_op jit(solution)/shard_map/all_to_all | solution.py:221
  17.4 1.0 constant_dynamic-slice_fusion.1
  18.4 92.3 %all_gather.6.rest_0_ = bf16[120,32,128]{2,1,0:T(8,128)(2,1)} all-gather(bf16[15,32,128]{2,1,0:T(8,128)(2,1)S(1)} %get-tuple-element.20), channel_id=1, replica_groups=mesh['root'=4,'col'=8] {'col'}, dimensions={0}, use_global_device_ids=true | all-gather | bytes 1105920 | tf_op jit(solution)/shard_map/all_gather | solution.py:262
  110.6 1.5 collective-permute-start
  112.1 34.8 %all_gather.7.rest_4_ = bf16[120,32,128]{2,1,0:T(8,128)(2,1)} all-gather(bf16[15,32,128]{2,1,0:T(8,128)(2,1)S(1)} %get-tuple-element.19), channel_id=1, replica_groups=mesh['root'=4,'col'=8] {'col'}, dimensions={0}, use_global_device_ids=true | all-gather | bytes 1105920 | tf_op jit(solution)/shard_map/all_gather | solution.py:262
  146.9 0.5 collective-permute-start.3
  147.4 0.5 collective-permute-start.4
  147.9 13.4 %collective-permute-done.3.rest_5_ = bf16[120,32,128]{2,1,0:T(8,128)(2,1)} collective-permute-done((bf16[120,32,128]{2,1,0:T(8,128)(2,1)}, bf16[120,32,128]{2,1,0:T(8,128)(2,1)}, u32[]{:S(2)}, u32[]{:S(2)}) %collective-permute-start.3) | collective-permute-done | bytes 983072 | tf_op jit(solution)/shard_map/ppermute | solution.py:239
  161.3 0.7 copy.24.cols
  162.7 1.5 collective-permute-done.5.rest_7_
  164.2 22.1 %shard_map.73 = (f32[384,3072]{1,0:T(8,128)}, s16[8,400,384]{2,1,0:T(8,128)(2,1)}, bf16[30720,128]{1,0:T(8,128)(2,1)}) custom-call(s32[24,10]{1,0:T(8,128)} %copy.24.cols, f32[1,1]{1,0:T(1,128)} %bitcast.8.shift, s32[1,4]{1,0:T(1,128)} %get-tuple-element.21.far, f32[384,3072]{1,0:T(8,128)} %bitcast.14, f32[384,3072]{1,0:T(8,128)} %d_ref.5, ...), custom_call_target="tpu_custom_call" | custom-call | flops 6039797760 | bytes 28311552 | tf_op jit(solution)/shard_map/pallas_call | solution.py:280
  186.3 1.7 copy-done.4
  188.0 3.8 all-to-all-start
  191.8 1.1 slice.14.rest_0_
  193.0 0.5 collective-permute-start.7
  193.5 14.8 %collective-permute-done.7.rest_1_ = s16[8,96,384]{2,1,0:T(8,128)(2,1)} collective-permute-done((s16[8,96,384]{2,1,0:T(8,128)(2,1)S(1)}, s16[8,96,384]{2,1,0:T(8,128)(2,1)}, u32[]{:S(2)}, u32[]{:S(2)}) %collective-permute-start.7) | collective-permute-done | bytes 589856 | tf_op jit(solution)/shard_map/ppermute | solution.py:239
  208.3 20.0 %shard_map.74.rest_4_.refs_0_ = s16[8,400,384]{2,1,0:T(8,128)(2,1)} custom-call(s32[24,10]{1,0:T(8,128)} %copy.24.cols, f32[1,1]{1,0:T(1,128)} %bitcast.9.shift, f32[384,3072]{1,0:T(8,128)} %get-tuple-element.12.w_ref, f32[384,3072]{1,0:T(8,128)} %bitcast.15, f32[384,3072]{1,0:T(8,128)} %d_ref.5, bf16[30720,128]{1,0:T(8,128)(2,1)} %get-tuple-element.13.tiles), custom_call_target="tpu_custom_call" | custom-call | flops 6039797760 | bytes 23592960 | tf_op jit(solution)/shard_map/pallas_call | solution.py:298
  228.3 0.5 collective-permute-start.6
  228.8 17.6 %shard_map.76.y_ref = f32[384,3072]{1,0:T(8,128)} custom-call(s32[24,10]{1,0:T(8,128)} %copy.24.cols, s16[8,496,384]{2,1,0:T(8,128)(2,1)} %copy-done.4, bf16[30720,128]{1,0:T(8,128)(2,1)} %get-tuple-element.13.tiles), custom_call_target="tpu_custom_call" | custom-call | flops 6039797760 | bytes 14155776 | tf_op jit(solution)/shard_map/pallas_call | solution.py:309
  246.4 1.7 all-to-all-done.tu_ref.tail_ref
  248.1 1.5 copy-done.1
  249.6 11.7 %shard_map.81 = s16[8,400,128]{2,1,0:T(8,128)(2,1)} custom-call(s32[24,10]{1,0:T(8,128)} %copy.24.cols, f32[1,1]{1,0:T(1,128)} %bitcast.12.shift, s32[1,4]{1,0:T(1,128)} %get-tuple-element.21.far, s16[8,400,384]{2,1,0:T(8,128)(2,1)} %copy-done.1, s16[8,400,384]{2,1,0:T(8,128)(2,1)} %copy-done.1, f32[384,3072]{1,0:T(8,128)} %shard_map.76.y_ref, ...), custom_call_target="tpu_custom_call" | custom-call | flops 2013265920 | bytes 6291456 | tf_op jit(solution)/shard_map/pallas_call | solution.py:324
  261.3 3.9 %all-to-all-start.3 = ((s16[8,400,128]{2,1,0:T(8,128)(2,1)}), s16[8,400,128]{2,1,0:T(8,128)(2,1)S(1)}, u32[]{:S(2)}, u32[]{:S(2)}) async-start(s16[8,400,128]{2,1,0:T(8,128)(2,1)} %shard_map.81), calls=%async_computation.3 | async-start | bytes 1638400 | tf_op jit(solution)/shard_map/all_to_all | solution.py:221
  265.2 11.7 %shard_map.79 = s16[8,400,128]{2,1,0:T(8,128)(2,1)} custom-call(s32[24,10]{1,0:T(8,128)} %copy.24.cols, f32[1,1]{1,0:T(1,128)} %bitcast.11.shift, s32[1,4]{1,0:T(1,128)} %get-tuple-element.21.far, s16[8,400,384]{2,1,0:T(8,128)(2,1)} %copy-done.1, s16[8,400,384]{2,1,0:T(8,128)(2,1)} %copy-done.1, f32[384,3072]{1,0:T(8,128)} %shard_map.76.y_ref, ...), custom_call_target="tpu_custom_call" | custom-call | flops 2013265920 | bytes 6291456 | tf_op jit(solution)/shard_map/pallas_call | solution.py:324
  276.9 9.6 %all-to-all-done.3.refs_0_ = s16[8,400,128]{2,1,0:T(8,128)(2,1)S(1)} async-done(((s16[8,400,128]{2,1,0:T(8,128)(2,1)}), s16[8,400,128]{2,1,0:T(8,128)(2,1)S(1)}, u32[]{:S(2)}, u32[]{:S(2)}) %all-to-all-start.3) | async-done | bytes 819232 | tf_op jit(solution)/shard_map/all_to_all | solution.py:221
  286.5 4.4 %all-to-all-start.2 = ((s16[8,400,128]{2,1,0:T(8,128)(2,1)}), s16[8,400,128]{2,1,0:T(8,128)(2,1)}, u32[]{:S(2)}, u32[]{:S(2)}) async-start(s16[8,400,128]{2,1,0:T(8,128)(2,1)} %shard_map.79), calls=%async_computation.2 | async-start | bytes 1638400 | tf_op jit(solution)/shard_map/all_to_all | solution.py:221
  290.9 11.8 %shard_map.77 = s16[8,400,128]{2,1,0:T(8,128)(2,1)} custom-call(s32[24,10]{1,0:T(8,128)} %copy.24.cols, f32[1,1]{1,0:T(1,128)} %bitcast.10.shift, s32[1,4]{1,0:T(1,128)} %get-tuple-element.21.far, s16[8,400,384]{2,1,0:T(8,128)(2,1)} %copy-done.1, s16[8,400,384]{2,1,0:T(8,128)(2,1)} %copy-done.1, f32[384,3072]{1,0:T(8,128)} %shard_map.76.y_ref, ...), custom_call_target="tpu_custom_call" | custom-call | flops 2013265920 | bytes 6291456 | tf_op jit(solution)/shard_map/pallas_call | solution.py:324
  302.8 0.5 collective-permute-start.11
  303.3 8.1 %all-to-all-done.2.refs_0_ = s16[8,400,128]{2,1,0:T(8,128)(2,1)} async-done(((s16[8,400,128]{2,1,0:T(8,128)(2,1)}), s16[8,400,128]{2,1,0:T(8,128)(2,1)}, u32[]{:S(2)}, u32[]{:S(2)}) %all-to-all-start.2) | async-done | bytes 819232 | tf_op jit(solution)/shard_map/all_to_all | solution.py:221
  311.4 4.2 %all-to-all-start.4 = ((s16[8,400,128]{2,1,0:T(8,128)(2,1)}), s16[8,400,128]{2,1,0:T(8,128)(2,1)}, u32[]{:S(2)}, u32[]{:S(2)}) async-start(s16[8,400,128]{2,1,0:T(8,128)(2,1)} %shard_map.77), calls=%async_computation.4 | async-start | bytes 1638400 | tf_op jit(solution)/shard_map/all_to_all | solution.py:221
  315.6 1.6 collective-permute-start.15
  317.2 0.5 collective-permute-start.12
  317.7 19.3 %collective-permute-done.15.refs_1_ = s16[8,400,128]{2,1,0:T(8,128)(2,1)} collective-permute-done((s16[8,400,128]{2,1,0:T(8,128)(2,1)S(1)}, s16[8,400,128]{2,1,0:T(8,128)(2,1)}, u32[]{:S(2)}, u32[]{:S(2)}) %collective-permute-start.15) | collective-permute-done | bytes 819232 | tf_op jit(solution)/shard_map/ppermute | solution.py:239
  337.0 15.4 %collective-permute-done.12.refs_1_ = s16[8,400,128]{2,1,0:T(8,128)(2,1)} collective-permute-done((s16[8,400,128]{2,1,0:T(8,128)(2,1)}, s16[8,400,128]{2,1,0:T(8,128)(2,1)}, u32[]{:S(2)}, u32[]{:S(2)}) %collective-permute-start.12) | collective-permute-done | bytes 819232 | tf_op jit(solution)/shard_map/ppermute | solution.py:239
  352.4 0.5 collective-permute-start.17
  352.9 1.5 collective-permute-start.18
  354.4 1.1 gather_fusion
  355.6 9.1 %shard_map.78.base_ref = f32[1,384,3072]{2,1,0:T(8,128)} custom-call(f32[1,4]{1,0:T(1,128)} %bitcast.17, s16[8,400,384]{2,1,0:T(8,128)(2,1)} %shard_map.74.rest_4_.refs_0_, s16[8,400,384]{2,1,0:T(8,128)(2,1)} %collective-permute-done.6.refs_1_, s16[8,400,384]{2,1,0:T(8,128)(2,1)} %collective-permute-done.10.refs_2_, ...), custom_call_target="tpu_custom_call" | custom-call | bytes 14155776 | tf_op jit(solution)/shard_map/pallas_call | solution.py:346
  364.7 6.7 %shard_map.80.base_ref = f32[1,384,3072]{2,1,0:T(8,128)} custom-call(f32[1,4]{1,0:T(1,128)} %bitcast.18, f32[1,384,3072]{2,1,0:T(8,128)} %shard_map.78.base_ref, s16[8,400,128]{2,1,0:T(8,128)(2,1)} %all-to-all-done.2.refs_0_, s16[8,400,128]{2,1,0:T(8,128)(2,1)} %collective-permute-done.12.refs_1_, ...), custom_call_target="tpu_custom_call", output_to_operand_aliasing={{}: (1, {})} | custom-call | bytes 4718592 | tf_op jit(solution)/shard_map/pallas_call | solution.py:362
  371.4 0.9 copy-done.7
  372.3 6.6 %shard_map.82.base_ref = f32[1,384,3072]{2,1,0:T(8,128)} custom-call(f32[1,4]{1,0:T(1,128)} %bitcast.19, f32[1,384,3072]{2,1,0:T(8,128)} %shard_map.80.base_ref, s16[8,400,128]{2,1,0:T(8,128)(2,1)} %copy-done.5, s16[8,400,128]{2,1,0:T(8,128)(2,1)} %collective-permute-done.15.refs_1_, ...), custom_call_target="tpu_custom_call", output_to_operand_aliasing={{}: (1, {})} | custom-call | bytes 4718592 | tf_op jit(solution)/shard_map/pallas_call | solution.py:362
  379.0 0.5 collective-permute-start.20
  379.5 2.4 collective-permute-done.19.refs_2_
  381.9 0.6 collective-permute-done.20.refs_3_
  382.9 0.9 copy-done.9
  383.8 6.6 %shard_map.83 = f32[1,384,3072]{2,1,0:T(8,128)} custom-call(f32[1,4]{1,0:T(1,128)} %bitcast.20, f32[1,384,3072]{2,1,0:T(8,128)} %shard_map.82.base_ref, s16[8,400,128]{2,1,0:T(8,128)(2,1)} %all-to-all-done.4.refs_0_, s16[8,400,128]{2,1,0:T(8,128)(2,1)} %copy-done.6, s16[8,400,128]{2,1,0:T(8,128)(2,1)} %copy-done.8, ...), custom_call_target="tpu_custom_call", output_to_operand_aliasing={{}: (1, {})} | custom-call | bytes 4718592 | tf_op jit(solution)/shard_map/pallas_call | solution.py:362
  (46 shorter events, 0.6 us)
Async XLA Ops:
  0.0 354.4 %copy-start = (f32[4,4]{1,0:T(4,128)S(1)}, f32[4,4]{1,0:T(4,128)}, u32[]{:S(2)}) copy-start(f32[4,4]{1,0:T(4,128)} %param.10) | copy-start | bytes 196
  10.0 151.4 %copy-start.10 = (s32[24,10]{0,1:T(8,128)S(1)}, s32[24,10]{0,1:T(8,128)}, u32[]{:S(2)}) copy-start(s32[24,10]{0,1:T(8,128)} %param.12) | copy-start | bytes 2884
  10.0 176.3 %all-to-all-start.1 = ((s16[8,496,384]{2,1,0:T(8,128)(2,1)}), s16[8,496,384]{2,1,0:T(8,128)(2,1)S(1)}, u32[]{:S(2)}, u32[]{:S(2)}) async-start(s16[8,496,384]{2,1,0:T(8,128)(2,1)} %shard_map.75), calls=%async_computation.1 | async-start | bytes 6094848 | tf_op jit(solution)/shard_map/all_to_all | solution.py:221
  110.6 37.3 %collective-permute-start = (bf16[120,32,128]{2,1,0:T(8,128)(2,1)}, bf16[120,32,128]{2,1,0:T(8,128)(2,1)}, u32[]{:S(2)}, u32[]{:S(2)}) collective-permute-start(bf16[120,32,128]{2,1,0:T(8,128)(2,1)} %all_gather.6.rest_0_), channel_id=1, source_target_pairs={{0,16},{8,24},{16,0},{24,8},{1,17},{9,25},{17,1},{25,9},{2,18},{10... | collective-permute-start | bytes 2949128 | tf_op jit(solution)/shard_map/ppermute | solution.py:239
  146.9 14.4 %collective-permute-start.3 = (bf16[120,32,128]{2,1,0:T(8,128)(2,1)}, bf16[120,32,128]{2,1,0:T(8,128)(2,1)}, u32[]{:S(2)}, u32[]{:S(2)}) collective-permute-start(bf16[120,32,128]{2,1,0:T(8,128)(2,1)} %all_gather.7.rest_4_), channel_id=1, source_target_pairs={{0,16},{8,24},{16,0},{24,8},{1,17},{9,25},{17,1},{25,9},{2,18},{10... | collective-permute-start | bytes 2949128 | tf_op jit(solution)/shard_map/ppermute | solution.py:239
  147.4 15.3 %collective-permute-start.1 = (bf16[120,32,128]{2,1,0:T(8,128)(2,1)}, bf16[120,32,128]{2,1,0:T(8,128)(2,1)}, u32[]{:S(2)}, u32[]{:S(2)}) collective-permute-start(bf16[120,32,128]{2,1,0:T(8,128)(2,1)} %all_gather.6.rest_0_), channel_id=1, source_target_pairs={{0,8},{8,0},{16,24},{24,16},{1,9},{9,1},{17,25},{25,17},{2,10},{10... | collective-permute-start | bytes 2949128 | tf_op jit(solution)/shard_map/ppermute | solution.py:239
  147.4 15.3 %collective-permute-start.4 = (bf16[120,32,128]{2,1,0:T(8,128)(2,1)}, bf16[120,32,128]{2,1,0:T(8,128)(2,1)}, u32[]{:S(2)}, u32[]{:S(2)}) collective-permute-start(bf16[120,32,128]{2,1,0:T(8,128)(2,1)} %all_gather.7.rest_4_), channel_id=1, source_target_pairs={{0,8},{8,0},{16,24},{24,16},{1,9},{9,1},{17,25},{25,17},{2,10},{10... | collective-permute-start | bytes 2949128 | tf_op jit(solution)/shard_map/ppermute | solution.py:239
  147.9 14.8 %collective-permute-start.2 = (bf16[120,32,128]{2,1,0:T(8,128)(2,1)}, bf16[120,32,128]{2,1,0:T(8,128)(2,1)}, u32[]{:S(2)}, u32[]{:S(2)}) collective-permute-start(bf16[120,32,128]{2,1,0:T(8,128)(2,1)} %collective-permute-done.rest_1_), channel_id=1, source_target_pairs={{0,8},{8,0},{16,24},{24,16},{1,9},{9,1},{17,25},{25,17},{2,10},{10... | collective-permute-start | bytes 2949128 | tf_op jit(solution)/shard_map/ppermute | solution.py:239
  161.3 2.9 collective-permute-start.5
  186.3 1.7 copy-start.4
  188.0 60.1 %all-to-all-start = ((s16[8,400,384]{2,1,0:T(8,128)(2,1)}), s16[8,400,384]{2,1,0:T(8,128)(2,1)S(1)}, u32[]{:S(2)}, u32[]{:S(2)}) async-start(s16[8,400,384]{2,1,0:T(8,128)(2,1)} %get-tuple-element.14), calls=%async_computation | async-start | bytes 4915200 | tf_op jit(solution)/shard_map/all_to_all | solution.py:221
  193.0 35.4 %copy-start.3 = (s16[8,96,384]{2,1,0:T(8,128)(2,1)}, s16[8,96,384]{2,1,0:T(8,128)(2,1)S(1)}, u32[]{:S(2)}) copy-start(s16[8,96,384]{2,1,0:T(8,128)(2,1)S(1)} %slice.14.rest_0_) | copy-start | bytes 1769476
  193.0 15.4 %collective-permute-start.7 = (s16[8,96,384]{2,1,0:T(8,128)(2,1)S(1)}, s16[8,96,384]{2,1,0:T(8,128)(2,1)}, u32[]{:S(2)}, u32[]{:S(2)}) collective-permute-start(s16[8,96,384]{2,1,0:T(8,128)(2,1)S(1)} %slice.14.rest_0_), channel_id=1, source_target_pairs={{0,16},{8,24},{16,0},{24,8},{1,17},{9,25},{17,1},{25,9},{2,18},{10... | collective-permute-start | bytes 1769480 | tf_op jit(solution)/shard_map/ppermute | solution.py:239
  193.5 52.9 %collective-permute-start.8 = (s16[8,96,384]{2,1,0:T(8,128)(2,1)S(1)}, s16[8,96,384]{2,1,0:T(8,128)(2,1)}, u32[]{:S(2)}, u32[]{:S(2)}) collective-permute-start(s16[8,96,384]{2,1,0:T(8,128)(2,1)S(1)} %slice.14.rest_0_), channel_id=1, source_target_pairs={{0,8},{8,0},{16,24},{24,16},{1,9},{9,1},{17,25},{25,17},{2,10},{10... | collective-permute-start | bytes 1769480 | tf_op jit(solution)/shard_map/ppermute | solution.py:239
  208.3 39.8 %collective-permute-start.9 = (s16[8,96,384]{2,1,0:T(8,128)(2,1)}, s16[8,96,384]{2,1,0:T(8,128)(2,1)}, u32[]{:S(2)}, u32[]{:S(2)}) collective-permute-start(s16[8,96,384]{2,1,0:T(8,128)(2,1)} %collective-permute-done.7.rest_1_), channel_id=1, source_target_pairs={{0,8},{8,0},{16,24},{24,16},{1,9},{9,1},{17,25},{25,17},{2,10},{10... | collective-permute-start | bytes 1769480 | tf_op jit(solution)/shard_map/ppermute | solution.py:239
  228.3 74.4 %collective-permute-start.6 = (s16[8,400,384]{2,1,0:T(8,128)(2,1)}, s16[8,400,384]{2,1,0:T(8,128)(2,1)}, u32[]{:S(2)}, u32[]{:S(2)}) collective-permute-start(s16[8,400,384]{2,1,0:T(8,128)(2,1)} %shard_map.74.rest_4_.refs_0_), channel_id=1, source_target_pairs={{0,16},{8,24},{16,0},{24,8},{1,17},{9,25},{17,1},{25,9},{2,18},{10... | collective-permute-start | bytes 7372808 | tf_op jit(solution)/shard_map/ppermute | solution.py:239
  248.1 1.5 copy-start.1
  261.3 25.2 %all-to-all-start.3 = ((s16[8,400,128]{2,1,0:T(8,128)(2,1)}), s16[8,400,128]{2,1,0:T(8,128)(2,1)S(1)}, u32[]{:S(2)}, u32[]{:S(2)}) async-start(s16[8,400,128]{2,1,0:T(8,128)(2,1)} %shard_map.81), calls=%async_computation.3 | async-start | bytes 1638400 | tf_op jit(solution)/shard_map/all_to_all | solution.py:221
  286.5 31.3 %copy-start.5 = (s16[8,400,128]{2,1,0:T(8,128)(2,1)}, s16[8,400,128]{2,1,0:T(8,128)(2,1)S(1)}, u32[]{:S(2)}) copy-start(s16[8,400,128]{2,1,0:T(8,128)(2,1)S(1)} %all-to-all-done.3.refs_0_) | copy-start | bytes 2457604
  286.5 24.9 %all-to-all-start.2 = ((s16[8,400,128]{2,1,0:T(8,128)(2,1)}), s16[8,400,128]{2,1,0:T(8,128)(2,1)}, u32[]{:S(2)}, u32[]{:S(2)}) async-start(s16[8,400,128]{2,1,0:T(8,128)(2,1)} %shard_map.79), calls=%async_computation.2 | async-start | bytes 1638400 | tf_op jit(solution)/shard_map/all_to_all | solution.py:221
  290.9 11.8 %copy-start.2 = (s16[8,400,384]{2,1,0:T(8,128)(2,1)S(1)}, s16[8,400,384]{2,1,0:T(8,128)(2,1)}, u32[]{:S(2)}) copy-start(s16[8,400,384]{2,1,0:T(8,128)(2,1)} %shard_map.74.rest_4_.refs_0_) | copy-start | bytes 7372804
  302.7 49.7 %collective-permute-start.10 = (s16[8,400,384]{2,1,0:T(8,128)(2,1)S(1)}, s16[8,400,384]{2,1,0:T(8,128)(2,1)}, u32[]{:S(2)}, u32[]{:S(2)}) collective-permute-start(s16[8,400,384]{2,1,0:T(8,128)(2,1)S(1)} %copy-done.2), channel_id=1, source_target_pairs={{0,8},{8,0},{16,24},{24,16},{1,9},{9,1},{17,25},{25,17},{2,10},{10... | collective-permute-start | bytes 7372808 | tf_op jit(solution)/shard_map/ppermute | solution.py:239
  302.8 50.1 %collective-permute-start.11 = (s16[8,400,384]{2,1,0:T(8,128)(2,1)}, s16[8,400,384]{2,1,0:T(8,128)(2,1)}, u32[]{:S(2)}, u32[]{:S(2)}) collective-permute-start(s16[8,400,384]{2,1,0:T(8,128)(2,1)} %collective-permute-done.6.refs_1_), channel_id=1, source_target_pairs={{0,8},{8,0},{16,24},{24,16},{1,9},{9,1},{17,25},{25,17},{2,10},{10... | collective-permute-start | bytes 7372808 | tf_op jit(solution)/shard_map/ppermute | solution.py:239
  311.4 41.5 %all-to-all-start.4 = ((s16[8,400,128]{2,1,0:T(8,128)(2,1)}), s16[8,400,128]{2,1,0:T(8,128)(2,1)}, u32[]{:S(2)}, u32[]{:S(2)}) async-start(s16[8,400,128]{2,1,0:T(8,128)(2,1)} %shard_map.77), calls=%async_computation.4 | async-start | bytes 1638400 | tf_op jit(solution)/shard_map/all_to_all | solution.py:221
  315.6 21.4 %collective-permute-start.15 = (s16[8,400,128]{2,1,0:T(8,128)(2,1)S(1)}, s16[8,400,128]{2,1,0:T(8,128)(2,1)}, u32[]{:S(2)}, u32[]{:S(2)}) collective-permute-start(s16[8,400,128]{2,1,0:T(8,128)(2,1)S(1)} %all-to-all-done.3.refs_0_), channel_id=1, source_target_pairs={{0,16},{8,24},{16,0},{24,8},{1,17},{9,25},{17,1},{25,9},{2,18},{10... | collective-permute-start | bytes 2457608 | tf_op jit(solution)/shard_map/ppermute | solution.py:239
  317.2 35.2 %collective-permute-start.12 = (s16[8,400,128]{2,1,0:T(8,128)(2,1)}, s16[8,400,128]{2,1,0:T(8,128)(2,1)}, u32[]{:S(2)}, u32[]{:S(2)}) collective-permute-start(s16[8,400,128]{2,1,0:T(8,128)(2,1)} %all-to-all-done.2.refs_0_), channel_id=1, source_target_pairs={{0,16},{8,24},{16,0},{24,8},{1,17},{9,25},{17,1},{25,9},{2,18},{10... | collective-permute-start | bytes 2457608 | tf_op jit(solution)/shard_map/ppermute | solution.py:239
  317.7 53.7 %collective-permute-start.16 = (s16[8,400,128]{2,1,0:T(8,128)(2,1)S(1)}, s16[8,400,128]{2,1,0:T(8,128)(2,1)}, u32[]{:S(2)}, u32[]{:S(2)}) collective-permute-start(s16[8,400,128]{2,1,0:T(8,128)(2,1)S(1)} %all-to-all-done.3.refs_0_), channel_id=1, source_target_pairs={{0,8},{8,0},{16,24},{24,16},{1,9},{9,1},{17,25},{25,17},{2,10},{10... | collective-permute-start | bytes 2457608 | tf_op jit(solution)/shard_map/ppermute | solution.py:239
  337.0 27.8 %collective-permute-start.13 = (s16[8,400,128]{2,1,0:T(8,128)(2,1)}, s16[8,400,128]{2,1,0:T(8,128)(2,1)}, u32[]{:S(2)}, u32[]{:S(2)}) collective-permute-start(s16[8,400,128]{2,1,0:T(8,128)(2,1)} %all-to-all-done.2.refs_0_), channel_id=1, source_target_pairs={{0,8},{8,0},{16,24},{24,16},{1,9},{9,1},{17,25},{25,17},{2,10},{10... | collective-permute-start | bytes 2457608 | tf_op jit(solution)/shard_map/ppermute | solution.py:239
  352.4 12.3 %collective-permute-start.14 = (s16[8,400,128]{2,1,0:T(8,128)(2,1)}, s16[8,400,128]{2,1,0:T(8,128)(2,1)}, u32[]{:S(2)}, u32[]{:S(2)}) collective-permute-start(s16[8,400,128]{2,1,0:T(8,128)(2,1)} %collective-permute-done.12.refs_1_), channel_id=1, source_target_pairs={{0,8},{8,0},{16,24},{24,16},{1,9},{9,1},{17,25},{25,17},{2,10},{10... | collective-permute-start | bytes 2457608 | tf_op jit(solution)/shard_map/ppermute | solution.py:239
  352.4 19.0 %collective-permute-start.17 = (s16[8,400,128]{2,1,0:T(8,128)(2,1)}, s16[8,400,128]{2,1,0:T(8,128)(2,1)S(1)}, u32[]{:S(2)}, u32[]{:S(2)}) collective-permute-start(s16[8,400,128]{2,1,0:T(8,128)(2,1)} %collective-permute-done.15.refs_1_), channel_id=1, source_target_pairs={{0,8},{8,0},{16,24},{24,16},{1,9},{9,1},{17,25},{25,17},{2,10},{10... | collective-permute-start | bytes 2457608 | tf_op jit(solution)/shard_map/ppermute | solution.py:239
  352.9 26.0 %collective-permute-start.18 = (s16[8,400,128]{2,1,0:T(8,128)(2,1)}, s16[8,400,128]{2,1,0:T(8,128)(2,1)S(1)}, u32[]{:S(2)}, u32[]{:S(2)}) collective-permute-start(s16[8,400,128]{2,1,0:T(8,128)(2,1)} %all-to-all-done.4.refs_0_), channel_id=1, source_target_pairs={{0,16},{8,24},{16,0},{24,8},{1,17},{9,25},{17,1},{25,9},{2,18},{10... | collective-permute-start | bytes 2457608 | tf_op jit(solution)/shard_map/ppermute | solution.py:239
  371.4 0.9 copy-start.7
  378.9 3.6 copy-start.6
  378.9 3.0 collective-permute-start.19
  379.0 3.5 collective-permute-start.20
  381.9 0.9 copy-start.8
  382.8 0.9 copy-start.9

commit v4 on v3

--- a/solution.py
+++ b/solution.py
@@ -80,27 +80,33 @@
     out_ref[0, pl.ds(width + PAD, slab), :] = codes.astype(jnp.int32).astype(jnp.int16)
 
 
-def right_first_kernel(dims, cols, shift, far, v_ref, d_ref, *rest):
+def right_first_kernel(dims, cols, shift, place, v_ref, d_ref, own, *rest):
     nblk, fill, blk, per = dims
-    shares, (w_ref, u_ref, tiles, halves, turned) = rest[:-5], rest[-5:]
+    shards, (w_ref, u_ref, tiles_ref, halves, turned, tiles) = rest[:-6], rest[-6:]
     step = pl.program_id(0)
+    size = own.shape[0]
 
     @pl.when(step == 0)
     def _():
         for b in range(nblk):
             split_into(halves, b, v_ref[:, b * blk : (b + 1) * blk])
-
-    roots = far.shape[1]
-    for n, share in enumerate(shares):
-        count, height = share.shape[:2]
-        for b in range(count):
-            at = ((n // roots) * count + b) * blk + far[0, n % roots] * height
-            tiles[pl.ds(pl.multiple_of(at, height), height), :] = share[b]
+        tiles[pl.ds(pl.multiple_of(place[0, 0] * size, size), size), :] = own[...]
+
+        @pl.loop(0, size // blk)
+        def _(b):
+            for k, shard in enumerate(shards):
+                share = shard.shape[1]
+                base = place[0, 1 + k] * size + place[1, 1 + k] * share
+                at = pl.multiple_of(base + b * blk, share)
+                tiles[pl.ds(at, share), :] = shard[b]
+
+    here_tiles = tiles.at[pl.ds(pl.multiple_of(step * size, size), size), :]
+    tiles_ref[...] = here_tiles[...]
     for t in range(per):
         lanes = slice(t * blk, (t + 1) * blk)
         block = step * per + t
         here = v_ref[:, pl.ds(pl.multiple_of(block * blk, blk), blk)]
-        moved = apply_row(halves, tiles, t, cols, block, fill, blk)
+        moved = apply_row(halves, here_tiles, t, cols, block, fill, blk)
         whole = moved + (d_ref[:, lanes] - shift[0, 0]) * here
         w_ref[:, lanes] = whole
         turned[lanes, :] = (moved + whole).T
@@ -122,7 +128,7 @@
         y_ref[:, t * blk : (t + 1) * blk] = apply_row(halves, tiles, t, cols, step * per + t, fill, blk)
 
 
-def right_second_kernel(dims, cols, shift, w_ref, v_ref, d_ref, tiles, p_ref, halves, part):
+def right_second_kernel(dims, cols, shift, w_ref, v_ref, d_ref, tiles, p_ref, halves):
     nblk, fill, blk, per = dims
     step = pl.program_id(0)
 
@@ -136,8 +142,7 @@
         block = step * per + t
         here = w_ref[:, pl.ds(pl.multiple_of(block * blk, blk), blk)]
         moved = apply_row(halves, tiles, t, cols, block, fill, blk)
-        part[:, lanes] = 0.5 * (moved + (d_ref[:, lanes] - shift[0, 0]) * here) - v_ref[:, lanes]
-    put(p_ref, 0, part[...])
+        p_ref[:, lanes] = 0.5 * (moved + (d_ref[:, lanes] - shift[0, 0]) * here) - v_ref[:, lanes]
 
 
 def left_second_kernel(dims, chunk, cols, shift, far, tu_ref, tail_ref, y_ref, tiles, *rest):
@@ -167,18 +172,14 @@
     put(out, 0, jnp.concatenate(done, axis=0))
 
 
-def rotate_kernel(weights, *refs):
-    ins, out_ref = refs[:-1], refs[-1]
+def second_kernel(z_ref, p_ref, out_ref):
+    put(out_ref, 0, take(z_ref, 0) + p_ref[...])
+
+
+def rotate_kernel(aliased, weights, *refs):
+    ins, out_ref = refs[aliased:-1], refs[-1]
     total = weights[0, 0] * take(ins[0], 0)
     for m in range(1, len(ins)):
-        total += weights[0, m] * take(ins[m], 0)
-    out_ref[0] = total
-
-
-def finish_kernel(weights, base_ref, *refs):
-    ins, out_ref = refs[:-1], refs[-1]
-    total = base_ref[0]
-    for m in range(len(ins)):
         total += weights[0, m] * take(ins[m], 0)
     out_ref[0] = total
 
@@ -251,15 +252,25 @@
     weights = rotation[root][far].reshape(1, -1)
     far = far.reshape(1, -1)
 
+    ring = list(range(0, groups, 2)) + list(range(1, groups, 2))[::-1]
+    spot = jnp.array([ring.index(c) for c in range(groups)], jnp.int32)[lax.axis_index("col")]
     share = blk // roots
-    local = string_blocks.shape[0] // blk
-    parts = 2 if local % 2 == 0 else 1
-    count = local // parts
-    mine = string_blocks.reshape(local, blk, blk)
+    mine = string_blocks.reshape(-1, blk, blk)
     mine = lax.dynamic_slice_in_dim(mine, root * share, share, 1)
-    shares = []
-    for n in range(parts):
-        shares += exchange(lax.all_gather(mine[n * count : (n + 1) * count], "col", axis=0, tiled=True))
+    shards, owners, forth, back = [], [0], mine, mine
+    started = start, diagonal
+    for hop in range(1, groups // 2 + 1):
+        both = 2 * hop < groups
+        for way in (1, -1) if both else (1,):
+            pairs = [(ring[s], ring[(s + way) % groups]) for s in range(groups)]
+            moved = lax.ppermute(forth if way == 1 else back, "col", pairs)
+            forth, back = (moved, back) if way == 1 else (forth, moved)
+            shards += exchange(moved)
+            owners += [-way * hop] * roots
+        if hop == 1:
+            started = lax.optimization_barrier((start, diagonal, forth, back))[:2]
+    place = jnp.array(ring, jnp.int32)[(spot + jnp.array(owners, jnp.int32)) % groups]
+    place = jnp.stack([place, jnp.concatenate([far[0, :1]] + [far[0]] * (groups - 1))])
 
     slab = width // roots
     height = width + PAD + slab
@@ -272,36 +283,40 @@
         [pltpu.VMEM((width, rows), f32)],
         0,
         size * 3,
-    )(far, start, diagonal)
-    tv = swap(tv)
+    )(far, *started)
+    tv = swap(lax.optimization_barrier((tv, forth, back))[0])
 
     once = pl.Buffered(1)
-    share_spec = pl.BlockSpec((count, share, blk), lambda q: (q, 0, 0))
+    shard_spec = pl.BlockSpec(mine.shape, lambda q: (0, 0, 0), pipeline_mode=once)
     w, tu, tiles = call(
         functools.partial(right_first_kernel, dims),
         groups,
         [smem(), smem(), smem(), whole, piece]
-        + [share_spec] * len(shares),
+        + [pl.BlockSpec(string_blocks.shape, lambda q: (0, 0), pipeline_mode=once)]
+        + [shard_spec] * len(shards),
         [piece, coded, tile_spec],
         [
             row_shape,
             codes_shape,
             jax.ShapeDtypeStruct((nblk * fill * blk, blk), string_blocks.dtype),
         ],
-        [row_halves, pltpu.VMEM((width, rows), f32)],
+        [
+            row_halves,
+            pltpu.VMEM((width, rows), f32),
+            pltpu.VMEM((nblk * fill * blk, blk), string_blocks.dtype),
+        ],
         work,
         size * 6,
-    )(block_cols, energy, far, start, diagonal, *shares)
+    )(block_cols, energy, place, start, diagonal, string_blocks, *shards)
     tu = swap(tu)
-    slabs = exchange(tv[:, width + PAD :])
 
     base = call(
         functools.partial(right_second_kernel, dims),
         groups,
         [smem(), smem(), whole, piece, piece, tile_spec],
-        pl.BlockSpec((1, rows + PAD, width), lambda q: (q, 0, 0)),
-        jax.ShapeDtypeStruct((groups, rows + PAD, width), i16),
-        [row_halves, pltpu.VMEM((rows, width), f32)],
+        piece,
+        row_shape,
+        [row_halves],
         work,
         size * 5,
     )(block_cols, energy, w, start, diagonal, tiles)
@@ -317,6 +332,7 @@
         size * 3,
     )(block_cols, tv, tiles)
 
+    slabs = exchange(tv[:, width + PAD :], y)
     part = width // chunks
     chunk_coded = pl.BlockSpec((1, rows + PAD, part), lambda q: (q, 0, 0))
     turned = []
@@ -343,34 +359,38 @@
         )(block_cols, energy, far, tu, tu, y, tiles, *slabs, base)
         turned.append(z)
 
-    out = call(
-        rotate_kernel,
-        groups,
-        [smem()] + [pl.BlockSpec((1, rows + PAD, width), lambda q: (q, 0, 0))] * roots,
-        pl.BlockSpec((1, rows, width), lambda q: (0, 0, q)),
-        jax.ShapeDtypeStruct((1, rows, strings), f32),
-        [],
-        0,
-        size * 3,
-    )(weights, *exchange(base, turned[-1]))
-
+    seconds = []
     for k in range(chunks):
-        back, late = swap(turned[k]), None
-        if k == chunks - 1:
-            late = out
-        slot = pl.BlockSpec((1, rows, part), lambda q, k=k: (0, 0, q * chunks + k))
-        out = call(
-            finish_kernel,
+        slot = pl.BlockSpec((rows, part), lambda q, k=k: (0, q * chunks + k))
+        second = call(
+            second_kernel,
             groups,
-            [smem(), slot] + [chunk_coded] * roots,
-            slot,
-            jax.ShapeDtypeStruct((1, rows, strings), f32),
+            [chunk_coded, slot],
+            chunk_coded,
+            jax.ShapeDtypeStruct((groups, rows + PAD, part), i16),
             [],
             0,
-            size * 3 // chunks,
-            {1: 0},
-        )(weights, out, *exchange(back, late))
-    return out
+            size * 2 // chunks,
+        )(swap(turned[k]), base)
+        seconds.append(second)
+    out = []
+    for k in range(chunks):
+        late = seconds[-1] if k < chunks - 1 else out[0] if out else None
+        slot = pl.BlockSpec((1, rows, part), lambda q, k=k: (0, 0, q * chunks + k))
+        out = [
+            call(
+                functools.partial(rotate_kernel, len(out)),
+                groups,
+                [smem()] + [pl.BlockSpec(memory_space=pl.ANY)] * len(out) + [chunk_coded] * roots,
+                slot,
+                jax.ShapeDtypeStruct((1, rows, strings), f32),
+                [],
+                0,
+                size * 3 // chunks,
+                {1: 0} if out else {},
+            )(weights, *out, *exchange(seconds[k], late))
+        ]
+    return out[0]
 
 
 def plain_blocks(matrix, operator_blocks, block_cols):

time: 392 us -> 319 us (0.81)
  blocking collectives: 127 us -> 0 us
  waiting for transfers between devices: 86.8 us -> 109 us
  starting transfers between devices: 32.6 us -> 48.3 us
  Pallas kernels: 133 us -> 144 us
    all_gather x2 -> x0, blocking collectives: 127 us -> none  [blocked_shards(): lax.all_gather(mine[n * count:(n + 1) * count], 'col', axis=0, tiled=True)]
    all_to_all x5, waiting for transfers between devices: 19.4 us -> 42.6 us  [swap(): lax.all_to_all(pieces, 'col', split_axis=0, concat_axis=0, tiled=True)]
    ppermute x21 -> x33, waiting for transfers between devices: 67.4 us -> 51.6 us  [exchange(): have = have + [lax.ppermute(h, 'root', pairs) for h in have]]
    ppermute x0 -> x7, waiting for transfers between devices: none -> 15.3 us  [blocked_shards(): moved = lax.ppermute(forth if way == 1 else back, 'col', pairs)]
    ppermute x0 -> x7, starting transfers between devices: none -> 8.94 us  [blocked_shards(): moved = lax.ppermute(forth if way == 1 else back, 'col', pairs)]
    ppermute x21 -> x33, starting transfers between devices: 8.82 us -> 17.7 us  [exchange(): have = have + [lax.ppermute(h, 'root', pairs) for h in have]]
    pallas_call x4 -> x6, Pallas kernels: 29.1 us -> 36.7 us  [the longest x3 19.2 us: blocked_shards(): call(functools.partial(rotate_kernel, len(out)), groups, [smem()] + [pl.B...]
    pallas_call x1, Pallas kernels: 22.1 us -> 26.1 us  [blocked_shards(): call(functools.partial(right_first_kernel, dims), groups, [smem(), smem()...]
  transfers between devices with their start and end apart: 26 -> 45, of which waited for: 10 -> 18; matrix products, arithmetic and copies ran while one was open for 1% -> 2% of each run, Pallas kernels for 30% -> 40%
where the time goes in v4:
time: 319 us; the launch traced here: 316 us
  Pallas kernels  144 us (45%)
  waiting for transfers between devices  109 us (34%)
  starting transfers between devices  48.3 us (15%)
  local copies, waits for them, and re-layouts  11.6 us (4%)
    ppermute x33, waiting for transfers between devices, exchange(): have = have + [lax.ppermute(h, 'root', pairs) for h in have]  51.6 us
    all_to_all x5, waiting for transfers between devices, swap(): lax.all_to_all(pieces, 'col', split_axis=0, concat_axis=0, tiled=True)  42.6 us
    pallas_call x3, Pallas kernels, blocked_shards(): call(functools.partial(left_second_kernel, dims, k), groups, [smem(), sme...  35 us
    pallas_call x1, Pallas kernels, blocked_shards(): call(functools.partial(right_first_kernel, dims), groups, [smem(), smem()...  26.1 us
    all_to_all x5, starting transfers between devices, swap(): lax.all_to_all(pieces, 'col', split_axis=0, concat_axis=0, tiled=True)  21.6 us
    pallas_call x1, Pallas kernels, blocked_shards(): call(functools.partial(right_second_kernel, dims), groups, [smem(), smem(...  19.3 us
    pallas_call x3, Pallas kernels, blocked_shards(): call(functools.partial(rotate_kernel, len(out)), groups, [smem()] + [pl.B...  19.2 us
    ppermute x33, starting transfers between devices, exchange(): have = have + [lax.ppermute(h, 'root', pairs) for h in have]  17.7 us
  transfers between devices with their start and end apart: 45, of which 18 were waited for; matrix products, arithmetic and copies ran while one was open for 2% of the time, Pallas kernels for 40%

profile of v4, /device:TPU:0, one launch (start us, length us, event | category | flops | bytes accessed | tf_op | source)
XLA Modules:
  0.0 316.2 jit_solution(3105833013392459928)
XLA Ops:
  1.0 3.1 collective-permute-start
  4.1 5.9 %collective-permute-done.rest_0_ = bf16[30,32,128]{2,1,0:T(8,128)(2,1)S(1)} collective-permute-done((bf16[30,32,128]{2,1,0:T(8,128)(2,1)S(1)}, bf16[30,32,128]{2,1,0:T(8,128)(2,1)S(1)}, u32[]{:S(2)}, u32[]{:S(2)}) %collective-permute-start) | collective-permute-done | bytes 245792 | tf_op jit(solution)/shard_map/ppermute | solution.py:266
  10.0 1.8 collective-permute-start.8
  12.0 5.1 %collective-permute-done.8.rest_8_ = bf16[30,32,128]{2,1,0:T(8,128)(2,1)S(1)} collective-permute-done((bf16[30,32,128]{2,1,0:T(8,128)(2,1)S(1)}, bf16[30,32,128]{2,1,0:T(8,128)(2,1)S(1)}, u32[]{:S(2)}, u32[]{:S(2)}) %collective-permute-start.8) | collective-permute-done | bytes 245792 | tf_op jit(solution)/shard_map/ppermute | solution.py:266
  17.1 1.5 collective-permute-start.16
  19.1 4.3 %collective-permute-done.16.rest_16_ = bf16[30,32,128]{2,1,0:T(8,128)(2,1)S(1)} collective-permute-done((bf16[30,32,128]{2,1,0:T(8,128)(2,1)S(1)}, bf16[30,32,128]{2,1,0:T(8,128)(2,1)S(1)}, u32[]{:S(2)}, u32[]{:S(2)}) %collective-permute-start.16) | collective-permute-done | bytes 245792 | tf_op jit(solution)/shard_map/ppermute | solution.py:266
  23.4 1.8 collective-permute-start.24
  26.4 8.8 %shard_map.101 = s16[8,496,384]{2,1,0:T(8,128)(2,1)} custom-call(s32[1,4]{1,0:T(1,128)} %get-tuple-element.34.far, f32[384,3072]{1,0:T(8,128)} %bitcast.18, f32[384,3072]{1,0:T(8,128)} %d_ref.4), custom_call_target="tpu_custom_call" | custom-call | bytes 14155776 | tf_op jit(solution)/shard_map/pallas_call | solution.py:277
  36.0 4.8 %all-to-all-start.1 = ((s16[8,496,384]{2,1,0:T(8,128)(2,1)}), s16[8,496,384]{2,1,0:T(8,128)(2,1)S(1)}, u32[]{:S(2)}, u32[]{:S(2)}) async-start(s16[8,496,384]{2,1,0:T(8,128)(2,1)} %shard_map.101), calls=%async_computation.1 | async-start | bytes 6094848 | tf_op jit(solution)/shard_map/all_to_all | solution.py:222
  40.8 1.6 collective-permute-start.5
  43.1 1.5 collective-permute-start.13
  44.6 5.2 %collective-permute-done.5.rest_5_ = bf16[30,32,128]{2,1,0:T(8,128)(2,1)S(1)} collective-permute-done((bf16[30,32,128]{2,1,0:T(8,128)(2,1)}, bf16[30,32,128]{2,1,0:T(8,128)(2,1)S(1)}, u32[]{:S(2)}, u32[]{:S(2)}) %collective-permute-start.5) | collective-permute-done | bytes 245792 | tf_op jit(solution)/shard_map/ppermute | solution.py:240
  50.4 4.7 %collective-permute-done.1.rest_1_ = bf16[30,32,128]{2,1,0:T(8,128)(2,1)S(1)} collective-permute-done((bf16[30,32,128]{2,1,0:T(8,128)(2,1)S(1)}, bf16[30,32,128]{2,1,0:T(8,128)(2,1)S(1)}, u32[]{:S(2)}, u32[]{:S(2)}) %collective-permute-start.1) | collective-permute-done | bytes 245792 | tf_op jit(solution)/shard_map/ppermute | solution.py:240
  55.1 1.5 collective-permute-start.9
  56.7 3.8 %collective-permute-done.13.rest_13_ = bf16[30,32,128]{2,1,0:T(8,128)(2,1)} collective-permute-done((bf16[30,32,128]{2,1,0:T(8,128)(2,1)}, bf16[30,32,128]{2,1,0:T(8,128)(2,1)}, u32[]{:S(2)}, u32[]{:S(2)}) %collective-permute-start.13) | collective-permute-done | bytes 245792 | tf_op jit(solution)/shard_map/ppermute | solution.py:240
  60.5 1.6 collective-permute-start.21
  62.4 3.3 %collective-permute-done.9.rest_9_ = bf16[30,32,128]{2,1,0:T(8,128)(2,1)S(1)} collective-permute-done((bf16[30,32,128]{2,1,0:T(8,128)(2,1)}, bf16[30,32,128]{2,1,0:T(8,128)(2,1)S(1)}, u32[]{:S(2)}, u32[]{:S(2)}) %collective-permute-start.9) | collective-permute-done | bytes 245792 | tf_op jit(solution)/shard_map/ppermute | solution.py:240
  65.7 1.6 collective-permute-start.17
  69.2 1.9 collective-permute-done.21.rest_21_
  71.6 4.7 %collective-permute-done.17.rest_17_ = bf16[30,32,128]{2,1,0:T(8,128)(2,1)} collective-permute-done((bf16[30,32,128]{2,1,0:T(8,128)(2,1)}, bf16[30,32,128]{2,1,0:T(8,128)(2,1)}, u32[]{:S(2)}, u32[]{:S(2)}) %collective-permute-start.17) | collective-permute-done | bytes 245792 | tf_op jit(solution)/shard_map/ppermute | solution.py:240
  76.3 4.8 %collective-permute-done.25.rest_25_ = bf16[30,32,128]{2,1,0:T(8,128)(2,1)} collective-permute-done((bf16[30,32,128]{2,1,0:T(8,128)(2,1)}, bf16[30,32,128]{2,1,0:T(8,128)(2,1)}, u32[]{:S(2)}, u32[]{:S(2)}) %collective-permute-start.25) | collective-permute-done | bytes 245792 | tf_op jit(solution)/shard_map/ppermute | solution.py:240
  84.6 26.1 %shard_map.100 = (f32[384,3072]{1,0:T(8,128)}, s16[8,400,384]{2,1,0:T(8,128)(2,1)}, bf16[30720,128]{1,0:T(8,128)(2,1)}) custom-call(s32[24,10]{1,0:T(8,128)} %copy.22.cols, f32[1,1]{1,0:T(1,128)} %bitcast.13.shift, s32[2,29]{1,0:T(2,128)} %pad_add_fusion.place, f32[384,3072]{1,0:T(8,128)} %bitcast.19, f32[384,3072]{1,0:T(8,128)} %d_ref.4, ...), custom_call_target="tpu_custom_call" | custom-call | flops 6039797760 | bytes 28311552 | tf_op jit(solution)/shard_map/pallas_call | solution.py:291
  110.7 1.6 copy-done.4
  112.3 6.0 %all-to-all-start = ((s16[8,400,384]{2,1,0:T(8,128)(2,1)}), s16[8,400,384]{2,1,0:T(8,128)(2,1)S(1)}, u32[]{:S(2)}, u32[]{:S(2)}) async-start(s16[8,400,384]{2,1,0:T(8,128)(2,1)} %get-tuple-element.19), calls=%async_computation | async-start | bytes 4915200 | tf_op jit(solution)/shard_map/all_to_all | solution.py:222
  119.4 1.6 collective-permute-start.28
  121.0 17.6 %shard_map.102.y_ref = f32[384,3072]{1,0:T(8,128)} custom-call(s32[24,10]{1,0:T(8,128)} %copy.22.cols, s16[8,496,384]{2,1,0:T(8,128)(2,1)} %copy-done.4, bf16[30720,128]{1,0:T(8,128)(2,1)} %get-tuple-element.23.tiles), custom_call_target="tpu_custom_call" | custom-call | flops 6039797760 | bytes 14155776 | tf_op jit(solution)/shard_map/pallas_call | solution.py:324
  139.2 19.3 %shard_map.103.rest_4_.p_ref = f32[384,3072]{1,0:T(8,128)} custom-call(s32[24,10]{1,0:T(8,128)} %copy.22.cols, f32[1,1]{1,0:T(1,128)} %bitcast.14.shift, f32[384,3072]{1,0:T(8,128)} %get-tuple-element.26.w_ref, f32[384,3072]{1,0:T(8,128)} %bitcast.20, f32[384,3072]{1,0:T(8,128)} %d_ref.4, bf16[30720,128]{1,0:T(8,128)(2,1)} %get-tuple-element.23.tiles), custom_call_target="tpu_custom_call" | custom-call | flops 6039797760 | bytes 23592960 | tf_op jit(solution)/shard_map/pallas_call | solution.py:313
  158.5 16.5 %all-to-all-done.tu_ref.tail_ref = s16[8,400,384]{2,1,0:T(8,128)(2,1)S(1)} async-done(((s16[8,400,384]{2,1,0:T(8,128)(2,1)}), s16[8,400,384]{2,1,0:T(8,128)(2,1)S(1)}, u32[]{:S(2)}, u32[]{:S(2)}) %all-to-all-start) | async-done | bytes 2457632 | tf_op jit(solution)/shard_map/all_to_all | solution.py:222
  176.3 11.6 %shard_map.109 = s16[8,400,128]{2,1,0:T(8,128)(2,1)} custom-call(s32[24,10]{1,0:T(8,128)} %copy.22.cols, f32[1,1]{1,0:T(1,128)} %bitcast.17.shift, s32[1,4]{1,0:T(1,128)} %get-tuple-element.34.far, s16[8,400,384]{2,1,0:T(8,128)(2,1)} %copy-done.2, s16[8,400,384]{2,1,0:T(8,128)(2,1)} %copy-done.2, f32[384,3072]{1,0:T(8,128)} %shard_map.102.y_ref, ...), custom_call_target="tpu_custom_call" | custom-call | flops 2013265920 | bytes 6291456 | tf_op jit(solution)/shard_map/pallas_call | solution.py:340
  188.0 3.6 %all-to-all-start.4 = ((s16[8,400,128]{2,1,0:T(8,128)(2,1)}), s16[8,400,128]{2,1,0:T(8,128)(2,1)S(1)}, u32[]{:S(2)}, u32[]{:S(2)}) async-start(s16[8,400,128]{2,1,0:T(8,128)(2,1)} %shard_map.109), calls=%async_computation.4 | async-start | bytes 1638400 | tf_op jit(solution)/shard_map/all_to_all | solution.py:222
  191.6 11.7 %shard_map.104 = s16[8,400,128]{2,1,0:T(8,128)(2,1)} custom-call(s32[24,10]{1,0:T(8,128)} %copy.22.cols, f32[1,1]{1,0:T(1,128)} %bitcast.15.shift, s32[1,4]{1,0:T(1,128)} %get-tuple-element.34.far, s16[8,400,384]{2,1,0:T(8,128)(2,1)} %copy-done.2, s16[8,400,384]{2,1,0:T(8,128)(2,1)} %copy-done.2, f32[384,3072]{1,0:T(8,128)} %shard_map.102.y_ref, ...), custom_call_target="tpu_custom_call" | custom-call | flops 2013265920 | bytes 6291456 | tf_op jit(solution)/shard_map/pallas_call | solution.py:340
  203.3 9.4 %all-to-all-done.4.z_ref = s16[8,400,128]{2,1,0:T(8,128)(2,1)S(1)} async-done(((s16[8,400,128]{2,1,0:T(8,128)(2,1)}), s16[8,400,128]{2,1,0:T(8,128)(2,1)S(1)}, u32[]{:S(2)}, u32[]{:S(2)}) %all-to-all-start.4) | async-done | bytes 819232 | tf_op jit(solution)/shard_map/all_to_all | solution.py:222
  212.7 3.6 %all-to-all-start.2 = ((s16[8,400,128]{2,1,0:T(8,128)(2,1)}), s16[8,400,128]{2,1,0:T(8,128)(2,1)S(1)}, u32[]{:S(2)}, u32[]{:S(2)}) async-start(s16[8,400,128]{2,1,0:T(8,128)(2,1)} %shard_map.104), calls=%async_computation.2 | async-start | bytes 1638400 | tf_op jit(solution)/shard_map/all_to_all | solution.py:222
  216.3 11.7 %shard_map.106 = s16[8,400,128]{2,1,0:T(8,128)(2,1)} custom-call(s32[24,10]{1,0:T(8,128)} %copy.22.cols, f32[1,1]{1,0:T(1,128)} %bitcast.16.shift, s32[1,4]{1,0:T(1,128)} %get-tuple-element.34.far, s16[8,400,384]{2,1,0:T(8,128)(2,1)} %copy-done.2, s16[8,400,384]{2,1,0:T(8,128)(2,1)} %copy-done.2, f32[384,3072]{1,0:T(8,128)} %shard_map.102.y_ref, ...), custom_call_target="tpu_custom_call" | custom-call | flops 2013265920 | bytes 6291456 | tf_op jit(solution)/shard_map/pallas_call | solution.py:340
  228.0 9.4 %all-to-all-done.2.z_ref = s16[8,400,128]{2,1,0:T(8,128)(2,1)S(1)} async-done(((s16[8,400,128]{2,1,0:T(8,128)(2,1)}), s16[8,400,128]{2,1,0:T(8,128)(2,1)S(1)}, u32[]{:S(2)}, u32[]{:S(2)}) %all-to-all-start.2) | async-done | bytes 819232 | tf_op jit(solution)/shard_map/all_to_all | solution.py:222
  237.4 3.6 %all-to-all-start.3 = ((s16[8,400,128]{2,1,0:T(8,128)(2,1)}), s16[8,400,128]{2,1,0:T(8,128)(2,1)S(1)}, u32[]{:S(2)}, u32[]{:S(2)}) async-start(s16[8,400,128]{2,1,0:T(8,128)(2,1)} %shard_map.106), calls=%async_computation.3 | async-start | bytes 1638400 | tf_op jit(solution)/shard_map/all_to_all | solution.py:222
  240.9 5.9 %shard_map.105.refs_0_ = s16[8,400,128]{2,1,0:T(8,128)(2,1)} custom-call(s16[8,400,128]{2,1,0:T(8,128)(2,1)} %copy-done.8, f32[384,3072]{1,0:T(8,128)} %shard_map.103.rest_4_.p_ref), custom_call_target="tpu_custom_call" | custom-call | bytes 3145728 | tf_op jit(solution)/shard_map/pallas_call | solution.py:365
  246.8 1.5 collective-permute-start.31
  248.3 5.9 %shard_map.110.refs_1_ = s16[8,400,128]{2,1,0:T(8,128)(2,1)} custom-call(s16[8,400,128]{2,1,0:T(8,128)(2,1)} %copy-done.7, f32[384,3072]{1,0:T(8,128)} %shard_map.103.rest_4_.p_ref), custom_call_target="tpu_custom_call" | custom-call | bytes 3145728 | tf_op jit(solution)/shard_map/pallas_call | solution.py:365
  254.7 7.3 %all-to-all-done.3.z_ref = s16[8,400,128]{2,1,0:T(8,128)(2,1)S(1)} async-done(((s16[8,400,128]{2,1,0:T(8,128)(2,1)}), s16[8,400,128]{2,1,0:T(8,128)(2,1)S(1)}, u32[]{:S(2)}, u32[]{:S(2)}) %all-to-all-start.3) | async-done | bytes 819232 | tf_op jit(solution)/shard_map/all_to_all | solution.py:222
  262.9 5.9 %shard_map.107.refs_1_ = s16[8,400,128]{2,1,0:T(8,128)(2,1)} custom-call(s16[8,400,128]{2,1,0:T(8,128)(2,1)} %copy-done.9, f32[384,3072]{1,0:T(8,128)} %shard_map.103.rest_4_.p_ref), custom_call_target="tpu_custom_call" | custom-call | bytes 3145728 | tf_op jit(solution)/shard_map/pallas_call | solution.py:365
  269.3 15.2 %collective-permute-done.34.refs_2_ = s16[8,400,128]{2,1,0:T(8,128)(2,1)} collective-permute-done((s16[8,400,128]{2,1,0:T(8,128)(2,1)}, s16[8,400,128]{2,1,0:T(8,128)(2,1)}, u32[]{:S(2)}, u32[]{:S(2)}) %collective-permute-start.34) | collective-permute-done | bytes 819232 | tf_op jit(solution)/shard_map/ppermute | solution.py:240
  285.1 1.5 collective-permute-start.37
  287.7 6.4 %shard_map.108.refs_0_ = f32[1,384,3072]{2,1,0:T(8,128)} custom-call(f32[1,4]{1,0:T(1,128)} %bitcast.23, s16[8,400,128]{2,1,0:T(8,128)(2,1)} %shard_map.105.refs_0_, s16[8,400,128]{2,1,0:T(8,128)(2,1)} %collective-permute-done.31.refs_1_, s16[8,400,128]{2,1,0:T(8,128)(2,1)} %collective-permute-done.32.refs_2_, ...), custom_call_target="tpu_custom_call" | custom-call | bytes 4718592 | tf_op jit(solution)/shard_map/pallas_call | solution.py:381
  294.1 6.4 %shard_map.111.refs_0_ = f32[1,384,3072]{2,1,0:T(8,128)} custom-call(f32[1,4]{1,0:T(1,128)} %bitcast.24, f32[1,384,3072]{2,1,0:T(8,128)} %shard_map.108.refs_0_, s16[8,400,128]{2,1,0:T(8,128)(2,1)} %shard_map.110.refs_1_, s16[8,400,128]{2,1,0:T(8,128)(2,1)} %collective-permute-done.34.refs_2_, ...), custom_call_target="tpu_custom_call", output_to_operand_aliasing={{}: (1, {})} | custom-call | bytes 4718592 | tf_op jit(solution)/shard_map/pallas_call | solution.py:381
  300.5 4.9 %collective-permute-done.37.refs_2_ = s16[8,400,128]{2,1,0:T(8,128)(2,1)S(1)} collective-permute-done((s16[8,400,128]{2,1,0:T(8,128)(2,1)}, s16[8,400,128]{2,1,0:T(8,128)(2,1)S(1)}, u32[]{:S(2)}, u32[]{:S(2)}) %collective-permute-start.37) | collective-permute-done | bytes 819232 | tf_op jit(solution)/shard_map/ppermute | solution.py:240
  305.9 1.8 collective-permute-done.38.refs_3_
  309.8 6.4 %shard_map.112 = f32[1,384,3072]{2,1,0:T(8,128)} custom-call(f32[1,4]{1,0:T(1,128)} %bitcast.25, f32[1,384,3072]{2,1,0:T(8,128)} %shard_map.111.refs_0_, s16[8,400,128]{2,1,0:T(8,128)(2,1)} %shard_map.107.refs_1_, s16[8,400,128]{2,1,0:T(8,128)(2,1)} %copy-done.11, s16[8,400,128]{2,1,0:T(8,128)(2,1)} %copy-done.12, ...), custom_call_target="tpu_custom_call", output_to_operand_aliasing={{}: (1, {})} | custom-call | bytes 4718592 | tf_op jit(solution)/shard_map/pallas_call | solution.py:381
  (136 shorter events, 20.0 us)
Async XLA Ops:
  0.0 286.6 %copy-start = (f32[4,4]{1,0:T(4,128)S(1)}, f32[4,4]{1,0:T(4,128)}, u32[]{:S(2)}) copy-start(f32[4,4]{1,0:T(4,128)} %param.13) | copy-start | bytes 196
  1.0 9.0 %collective-permute-start = (bf16[30,32,128]{2,1,0:T(8,128)(2,1)S(1)}, bf16[30,32,128]{2,1,0:T(8,128)(2,1)S(1)}, u32[]{:S(2)}, u32[]{:S(2)}) collective-permute-start(bf16[30,32,128]{2,1,0:T(8,128)(2,1)S(1)} %constant_dynamic-slice_fusion), channel_id=1, source_target_pairs={{0,2},{2,4},{4,6},{6,7},{7,5},{5,3},{3,1},{1,0},{8,10},{10,12},{12... | collective-permute-start | bytes 737288 | tf_op jit(solution)/shard_map/ppermute | solution.py:266
  4.1 7.7 %collective-permute-start.4 = (bf16[30,32,128]{2,1,0:T(8,128)(2,1)S(1)}, bf16[30,32,128]{2,1,0:T(8,128)(2,1)S(1)}, u32[]{:S(2)}, u32[]{:S(2)}) collective-permute-start(bf16[30,32,128]{2,1,0:T(8,128)(2,1)S(1)} %constant_dynamic-slice_fusion), channel_id=1, source_target_pairs={{0,1},{2,0},{4,2},{6,4},{7,6},{5,7},{3,5},{1,3},{8,9},{10,8},{12,1... | collective-permute-start | bytes 737288 | tf_op jit(solution)/shard_map/ppermute | solution.py:266
  10.0 7.1 %collective-permute-start.8 = (bf16[30,32,128]{2,1,0:T(8,128)(2,1)S(1)}, bf16[30,32,128]{2,1,0:T(8,128)(2,1)S(1)}, u32[]{:S(2)}, u32[]{:S(2)}) collective-permute-start(bf16[30,32,128]{2,1,0:T(8,128)(2,1)S(1)} %collective-permute-done.rest_0_), channel_id=1, source_target_pairs={{0,2},{2,4},{4,6},{6,7},{7,5},{5,3},{3,1},{1,0},{8,10},{10,12},{12... | collective-permute-start | bytes 737288 | tf_op jit(solution)/shard_map/ppermute | solution.py:266
  11.8 6.8 %collective-permute-start.12 = (bf16[30,32,128]{2,1,0:T(8,128)(2,1)S(1)}, bf16[30,32,128]{2,1,0:T(8,128)(2,1)S(1)}, u32[]{:S(2)}, u32[]{:S(2)}) collective-permute-start(bf16[30,32,128]{2,1,0:T(8,128)(2,1)S(1)} %collective-permute-done.4.rest_4_), channel_id=1, source_target_pairs={{0,1},{2,0},{4,2},{6,4},{7,6},{5,7},{3,5},{1,3},{8,9},{10,8},{12,1... | collective-permute-start | bytes 737288 | tf_op jit(solution)/shard_map/ppermute | solution.py:266
  17.1 6.3 %collective-permute-start.16 = (bf16[30,32,128]{2,1,0:T(8,128)(2,1)S(1)}, bf16[30,32,128]{2,1,0:T(8,128)(2,1)S(1)}, u32[]{:S(2)}, u32[]{:S(2)}) collective-permute-start(bf16[30,32,128]{2,1,0:T(8,128)(2,1)S(1)} %collective-permute-done.8.rest_8_), channel_id=1, source_target_pairs={{0,2},{2,4},{4,6},{6,7},{7,5},{5,3},{3,1},{1,0},{8,10},{10,12},{12... | collective-permute-start | bytes 737288 | tf_op jit(solution)/shard_map/ppermute | solution.py:266
  18.6 16.7 %collective-permute-start.20 = (bf16[30,32,128]{2,1,0:T(8,128)(2,1)S(1)}, bf16[30,32,128]{2,1,0:T(8,128)(2,1)S(1)}, u32[]{:S(2)}, u32[]{:S(2)}) collective-permute-start(bf16[30,32,128]{2,1,0:T(8,128)(2,1)S(1)} %collective-permute-done.12.rest_12_), channel_id=1, source_target_pairs={{0,1},{2,0},{4,2},{6,4},{7,6},{5,7},{3,5},{1,3},{8,9},{10,8},{12,1... | collective-permute-start | bytes 737288 | tf_op jit(solution)/shard_map/ppermute | solution.py:266
  23.4 12.6 %collective-permute-start.24 = (bf16[30,32,128]{2,1,0:T(8,128)(2,1)S(1)}, bf16[30,32,128]{2,1,0:T(8,128)(2,1)}, u32[]{:S(2)}, u32[]{:S(2)}) collective-permute-start(bf16[30,32,128]{2,1,0:T(8,128)(2,1)S(1)} %collective-permute-done.16.rest_16_), channel_id=1, source_target_pairs={{0,2},{2,4},{4,6},{6,7},{7,5},{5,3},{3,1},{1,0},{8,10},{10,12},{12... | collective-permute-start | bytes 737288 | tf_op jit(solution)/shard_map/ppermute | solution.py:266
  35.2 47.8 %copy-start.14 = (s32[1,4]{1,0:T(1,128)S(1)}, s32[1,4]{1,0:T(1,128)}, u32[]{:S(2)}) copy-start(s32[1,4]{1,0:T(1,128)} %get-tuple-element.34.far) | copy-start | bytes 52
  35.3 48.0 %copy-start.1 = (s32[8]{0:T(128)S(1)}, s32[8]{0:T(128)}, u32[]{:S(2)}) copy-start(s32[8]{0:T(128)} %constant.44.clone) | copy-start | bytes 100
  36.0 74.7 %all-to-all-start.1 = ((s16[8,496,384]{2,1,0:T(8,128)(2,1)}), s16[8,496,384]{2,1,0:T(8,128)(2,1)S(1)}, u32[]{:S(2)}, u32[]{:S(2)}) async-start(s16[8,496,384]{2,1,0:T(8,128)(2,1)} %shard_map.101), calls=%async_computation.1 | async-start | bytes 6094848 | tf_op jit(solution)/shard_map/all_to_all | solution.py:222
  40.8 2.3 collective-permute-start.6
  40.8 9.0 %collective-permute-start.5 = (bf16[30,32,128]{2,1,0:T(8,128)(2,1)}, bf16[30,32,128]{2,1,0:T(8,128)(2,1)S(1)}, u32[]{:S(2)}, u32[]{:S(2)}) collective-permute-start(bf16[30,32,128]{2,1,0:T(8,128)(2,1)} %copy-done.17), channel_id=1, source_target_pairs={{0,16},{8,24},{16,0},{24,8},{1,17},{9,25},{17,1},{25,9},{2,18},{10... | collective-permute-start | bytes 737288 | tf_op jit(solution)/shard_map/ppermute | solution.py:240
  42.4 7.5 %collective-permute-start.2 = (bf16[30,32,128]{2,1,0:T(8,128)(2,1)S(1)}, bf16[30,32,128]{2,1,0:T(8,128)(2,1)S(1)}, u32[]{:S(2)}, u32[]{:S(2)}) collective-permute-start(bf16[30,32,128]{2,1,0:T(8,128)(2,1)S(1)} %collective-permute-done.rest_0_), channel_id=1, source_target_pairs={{0,8},{8,0},{16,24},{24,16},{1,9},{9,1},{17,25},{25,17},{2,10},{10... | collective-permute-start | bytes 737288 | tf_op jit(solution)/shard_map/ppermute | solution.py:240
  42.5 12.6 %collective-permute-start.1 = (bf16[30,32,128]{2,1,0:T(8,128)(2,1)S(1)}, bf16[30,32,128]{2,1,0:T(8,128)(2,1)S(1)}, u32[]{:S(2)}, u32[]{:S(2)}) collective-permute-start(bf16[30,32,128]{2,1,0:T(8,128)(2,1)S(1)} %collective-permute-done.rest_0_), channel_id=1, source_target_pairs={{0,16},{8,24},{16,0},{24,8},{1,17},{9,25},{17,1},{25,9},{2,18},{10... | collective-permute-start | bytes 737288 | tf_op jit(solution)/shard_map/ppermute | solution.py:240
  43.1 13.6 %collective-permute-start.14 = (bf16[30,32,128]{2,1,0:T(8,128)(2,1)}, bf16[30,32,128]{2,1,0:T(8,128)(2,1)S(1)}, u32[]{:S(2)}, u32[]{:S(2)}) collective-permute-start(bf16[30,32,128]{2,1,0:T(8,128)(2,1)} %copy-done.19), channel_id=1, source_target_pairs={{0,8},{8,0},{16,24},{24,16},{1,9},{9,1},{17,25},{25,17},{2,10},{10... | collective-permute-start | bytes 737288 | tf_op jit(solution)/shard_map/ppermute | solution.py:240
  43.1 17.3 %collective-permute-start.13 = (bf16[30,32,128]{2,1,0:T(8,128)(2,1)}, bf16[30,32,128]{2,1,0:T(8,128)(2,1)}, u32[]{:S(2)}, u32[]{:S(2)}) collective-permute-start(bf16[30,32,128]{2,1,0:T(8,128)(2,1)} %copy-done.19), channel_id=1, source_target_pairs={{0,16},{8,24},{16,0},{24,8},{1,17},{9,25},{17,1},{25,9},{2,18},{10... | collective-permute-start | bytes 737288 | tf_op jit(solution)/shard_map/ppermute | solution.py:240
  49.9 10.6 %collective-permute-start.7 = (bf16[30,32,128]{2,1,0:T(8,128)(2,1)S(1)}, bf16[30,32,128]{2,1,0:T(8,128)(2,1)S(1)}, u32[]{:S(2)}, u32[]{:S(2)}) collective-permute-start(bf16[30,32,128]{2,1,0:T(8,128)(2,1)S(1)} %collective-permute-done.5.rest_5_), channel_id=1, source_target_pairs={{0,8},{8,0},{16,24},{24,16},{1,9},{9,1},{17,25},{25,17},{2,10},{10... | collective-permute-start | bytes 737288 | tf_op jit(solution)/shard_map/ppermute | solution.py:240
  49.9 12.2 %collective-permute-start.10 = (bf16[30,32,128]{2,1,0:T(8,128)(2,1)}, bf16[30,32,128]{2,1,0:T(8,128)(2,1)S(1)}, u32[]{:S(2)}, u32[]{:S(2)}) collective-permute-start(bf16[30,32,128]{2,1,0:T(8,128)(2,1)} %copy-done.18), channel_id=1, source_target_pairs={{0,8},{8,0},{16,24},{24,16},{1,9},{9,1},{17,25},{25,17},{2,10},{10... | collective-permute-start | bytes 737288 | tf_op jit(solution)/shard_map/ppermute | solution.py:240
  55.1 10.5 %collective-permute-start.9 = (bf16[30,32,128]{2,1,0:T(8,128)(2,1)}, bf16[30,32,128]{2,1,0:T(8,128)(2,1)S(1)}, u32[]{:S(2)}, u32[]{:S(2)}) collective-permute-start(bf16[30,32,128]{2,1,0:T(8,128)(2,1)} %copy-done.18), channel_id=1, source_target_pairs={{0,16},{8,24},{16,0},{24,8},{1,17},{9,25},{17,1},{25,9},{2,18},{10... | collective-permute-start | bytes 737288 | tf_op jit(solution)/shard_map/ppermute | solution.py:240
  56.6 9.0 %collective-permute-start.3 = (bf16[30,32,128]{2,1,0:T(8,128)(2,1)S(1)}, bf16[30,32,128]{2,1,0:T(8,128)(2,1)S(1)}, u32[]{:S(2)}, u32[]{:S(2)}) collective-permute-start(bf16[30,32,128]{2,1,0:T(8,128)(2,1)S(1)} %collective-permute-done.1.rest_1_), channel_id=1, source_target_pairs={{0,8},{8,0},{16,24},{24,16},{1,9},{9,1},{17,25},{25,17},{2,10},{10... | collective-permute-start | bytes 737288 | tf_op jit(solution)/shard_map/ppermute | solution.py:240
  60.5 6.8 %collective-permute-start.22 = (bf16[30,32,128]{2,1,0:T(8,128)(2,1)}, bf16[30,32,128]{2,1,0:T(8,128)(2,1)S(1)}, u32[]{:S(2)}, u32[]{:S(2)}) collective-permute-start(bf16[30,32,128]{2,1,0:T(8,128)(2,1)} %copy-done.21), channel_id=1, source_target_pairs={{0,8},{8,0},{16,24},{24,16},{1,9},{9,1},{17,25},{25,17},{2,10},{10... | collective-permute-start | bytes 737288 | tf_op jit(solution)/shard_map/ppermute | solution.py:240
  60.5 10.5 %collective-permute-start.21 = (bf16[30,32,128]{2,1,0:T(8,128)(2,1)}, bf16[30,32,128]{2,1,0:T(8,128)(2,1)}, u32[]{:S(2)}, u32[]{:S(2)}) collective-permute-start(bf16[30,32,128]{2,1,0:T(8,128)(2,1)} %copy-done.21), channel_id=1, source_target_pairs={{0,16},{8,24},{16,0},{24,8},{1,17},{9,25},{17,1},{25,9},{2,18},{10... | collective-permute-start | bytes 737288 | tf_op jit(solution)/shard_map/ppermute | solution.py:240
  62.1 8.9 %collective-permute-start.15 = (bf16[30,32,128]{2,1,0:T(8,128)(2,1)}, bf16[30,32,128]{2,1,0:T(8,128)(2,1)}, u32[]{:S(2)}, u32[]{:S(2)}) collective-permute-start(bf16[30,32,128]{2,1,0:T(8,128)(2,1)} %collective-permute-done.13.rest_13_), channel_id=1, source_target_pairs={{0,8},{8,0},{16,24},{24,16},{1,9},{9,1},{17,25},{25,17},{2,10},{10... | collective-permute-start | bytes 737288 | tf_op jit(solution)/shard_map/ppermute | solution.py:240
  65.7 5.9 %collective-permute-start.18 = (bf16[30,32,128]{2,1,0:T(8,128)(2,1)}, bf16[30,32,128]{2,1,0:T(8,128)(2,1)}, u32[]{:S(2)}, u32[]{:S(2)}) collective-permute-start(bf16[30,32,128]{2,1,0:T(8,128)(2,1)} %copy-done.20), channel_id=1, source_target_pairs={{0,8},{8,0},{16,24},{24,16},{1,9},{9,1},{17,25},{25,17},{2,10},{10... | collective-permute-start | bytes 737288 | tf_op jit(solution)/shard_map/ppermute | solution.py:240
  65.7 10.6 %collective-permute-start.17 = (bf16[30,32,128]{2,1,0:T(8,128)(2,1)}, bf16[30,32,128]{2,1,0:T(8,128)(2,1)}, u32[]{:S(2)}, u32[]{:S(2)}) collective-permute-start(bf16[30,32,128]{2,1,0:T(8,128)(2,1)} %copy-done.20), channel_id=1, source_target_pairs={{0,16},{8,24},{16,0},{24,8},{1,17},{9,25},{17,1},{25,9},{2,18},{10... | collective-permute-start | bytes 737288 | tf_op jit(solution)/shard_map/ppermute | solution.py:240
  68.0 13.1 %collective-permute-start.25 = (bf16[30,32,128]{2,1,0:T(8,128)(2,1)}, bf16[30,32,128]{2,1,0:T(8,128)(2,1)}, u32[]{:S(2)}, u32[]{:S(2)}) collective-permute-start(bf16[30,32,128]{2,1,0:T(8,128)(2,1)} %collective-permute-done.24.rest_24_), channel_id=1, source_target_pairs={{0,16},{8,24},{16,0},{24,8},{1,17},{9,25},{17,1},{25,9},{2,18},{10... | collective-permute-start | bytes 737288 | tf_op jit(solution)/shard_map/ppermute | solution.py:240
  71.0 13.5 %collective-permute-start.11 = (bf16[30,32,128]{2,1,0:T(8,128)(2,1)S(1)}, bf16[30,32,128]{2,1,0:T(8,128)(2,1)}, u32[]{:S(2)}, u32[]{:S(2)}) collective-permute-start(bf16[30,32,128]{2,1,0:T(8,128)(2,1)S(1)} %collective-permute-done.9.rest_9_), channel_id=1, source_target_pairs={{0,8},{8,0},{16,24},{24,16},{1,9},{9,1},{17,25},{25,17},{2,10},{10... | collective-permute-start | bytes 737288 | tf_op jit(solution)/shard_map/ppermute | solution.py:240
  71.0 13.5 %collective-permute-start.26 = (bf16[30,32,128]{2,1,0:T(8,128)(2,1)}, bf16[30,32,128]{2,1,0:T(8,128)(2,1)}, u32[]{:S(2)}, u32[]{:S(2)}) collective-permute-start(bf16[30,32,128]{2,1,0:T(8,128)(2,1)} %collective-permute-done.24.rest_24_), channel_id=1, source_target_pairs={{0,8},{8,0},{16,24},{24,16},{1,9},{9,1},{17,25},{25,17},{2,10},{10... | collective-permute-start | bytes 737288 | tf_op jit(solution)/shard_map/ppermute | solution.py:240
  71.5 13.0 %collective-permute-start.23 = (bf16[30,32,128]{2,1,0:T(8,128)(2,1)}, bf16[30,32,128]{2,1,0:T(8,128)(2,1)}, u32[]{:S(2)}, u32[]{:S(2)}) collective-permute-start(bf16[30,32,128]{2,1,0:T(8,128)(2,1)} %collective-permute-done.21.rest_21_), channel_id=1, source_target_pairs={{0,8},{8,0},{16,24},{24,16},{1,9},{9,1},{17,25},{25,17},{2,10},{10... | collective-permute-start | bytes 737288 | tf_op jit(solution)/shard_map/ppermute | solution.py:240
  76.3 8.3 %collective-permute-start.19 = (bf16[30,32,128]{2,1,0:T(8,128)(2,1)}, bf16[30,32,128]{2,1,0:T(8,128)(2,1)}, u32[]{:S(2)}, u32[]{:S(2)}) collective-permute-start(bf16[30,32,128]{2,1,0:T(8,128)(2,1)} %collective-permute-done.17.rest_17_), channel_id=1, source_target_pairs={{0,8},{8,0},{16,24},{24,16},{1,9},{9,1},{17,25},{25,17},{2,10},{10... | collective-permute-start | bytes 737288 | tf_op jit(solution)/shard_map/ppermute | solution.py:240
  81.1 3.5 %collective-permute-start.27 = (bf16[30,32,128]{2,1,0:T(8,128)(2,1)}, bf16[30,32,128]{2,1,0:T(8,128)(2,1)}, u32[]{:S(2)}, u32[]{:S(2)}) collective-permute-start(bf16[30,32,128]{2,1,0:T(8,128)(2,1)} %collective-permute-done.25.rest_25_), channel_id=1, source_target_pairs={{0,8},{8,0},{16,24},{24,16},{1,9},{9,1},{17,25},{25,17},{2,10},{10... | collective-permute-start | bytes 737288 | tf_op jit(solution)/shard_map/ppermute | solution.py:240
  112.3 62.6 %all-to-all-start = ((s16[8,400,384]{2,1,0:T(8,128)(2,1)}), s16[8,400,384]{2,1,0:T(8,128)(2,1)S(1)}, u32[]{:S(2)}, u32[]{:S(2)}) async-start(s16[8,400,384]{2,1,0:T(8,128)(2,1)} %get-tuple-element.19), calls=%async_computation | async-start | bytes 4915200 | tf_op jit(solution)/shard_map/all_to_all | solution.py:222
  119.4 19.2 %collective-permute-start.28 = (s16[8,96,384]{2,1,0:T(8,128)(2,1)S(1)}, s16[8,96,384]{2,1,0:T(8,128)(2,1)}, u32[]{:S(2)}, u32[]{:S(2)}) collective-permute-start(s16[8,96,384]{2,1,0:T(8,128)(2,1)S(1)} %slice.12.rest_0_), channel_id=1, source_target_pairs={{0,16},{8,24},{16,0},{24,8},{1,17},{9,25},{17,1},{25,9},{2,18},{10... | collective-permute-start | bytes 1769480 | tf_op jit(solution)/shard_map/ppermute | solution.py:240
  138.6 36.3 %collective-permute-start.29 = (s16[8,96,384]{2,1,0:T(8,128)(2,1)S(1)}, s16[8,96,384]{2,1,0:T(8,128)(2,1)}, u32[]{:S(2)}, u32[]{:S(2)}) collective-permute-start(s16[8,96,384]{2,1,0:T(8,128)(2,1)S(1)} %slice.12.rest_0_), channel_id=1, source_target_pairs={{0,8},{8,0},{16,24},{24,16},{1,9},{9,1},{17,25},{25,17},{2,10},{10... | collective-permute-start | bytes 1769480 | tf_op jit(solution)/shard_map/ppermute | solution.py:240
  138.7 36.2 %collective-permute-start.30 = (s16[8,96,384]{2,1,0:T(8,128)(2,1)}, s16[8,96,384]{2,1,0:T(8,128)(2,1)}, u32[]{:S(2)}, u32[]{:S(2)}) collective-permute-start(s16[8,96,384]{2,1,0:T(8,128)(2,1)} %collective-permute-done.28.rest_1_), channel_id=1, source_target_pairs={{0,8},{8,0},{16,24},{24,16},{1,9},{9,1},{17,25},{25,17},{2,10},{10... | collective-permute-start | bytes 1769480 | tf_op jit(solution)/shard_map/ppermute | solution.py:240
  188.0 24.7 %all-to-all-start.4 = ((s16[8,400,128]{2,1,0:T(8,128)(2,1)}), s16[8,400,128]{2,1,0:T(8,128)(2,1)S(1)}, u32[]{:S(2)}, u32[]{:S(2)}) async-start(s16[8,400,128]{2,1,0:T(8,128)(2,1)} %shard_map.109), calls=%async_computation.4 | async-start | bytes 1638400 | tf_op jit(solution)/shard_map/all_to_all | solution.py:222
  212.7 24.6 %all-to-all-start.2 = ((s16[8,400,128]{2,1,0:T(8,128)(2,1)}), s16[8,400,128]{2,1,0:T(8,128)(2,1)S(1)}, u32[]{:S(2)}, u32[]{:S(2)}) async-start(s16[8,400,128]{2,1,0:T(8,128)(2,1)} %shard_map.104), calls=%async_computation.2 | async-start | bytes 1638400 | tf_op jit(solution)/shard_map/all_to_all | solution.py:222
  237.4 24.6 %all-to-all-start.3 = ((s16[8,400,128]{2,1,0:T(8,128)(2,1)}), s16[8,400,128]{2,1,0:T(8,128)(2,1)S(1)}, u32[]{:S(2)}, u32[]{:S(2)}) async-start(s16[8,400,128]{2,1,0:T(8,128)(2,1)} %shard_map.106), calls=%async_computation.3 | async-start | bytes 1638400 | tf_op jit(solution)/shard_map/all_to_all | solution.py:222
  246.8 21.9 %collective-permute-start.31 = (s16[8,400,128]{2,1,0:T(8,128)(2,1)}, s16[8,400,128]{2,1,0:T(8,128)(2,1)}, u32[]{:S(2)}, u32[]{:S(2)}) collective-permute-start(s16[8,400,128]{2,1,0:T(8,128)(2,1)} %shard_map.105.refs_0_), channel_id=1, source_target_pairs={{0,16},{8,24},{16,0},{24,8},{1,17},{9,25},{17,1},{25,9},{2,18},{10... | collective-permute-start | bytes 2457608 | tf_op jit(solution)/shard_map/ppermute | solution.py:240
  254.1 30.4 %collective-permute-start.34 = (s16[8,400,128]{2,1,0:T(8,128)(2,1)}, s16[8,400,128]{2,1,0:T(8,128)(2,1)}, u32[]{:S(2)}, u32[]{:S(2)}) collective-permute-start(s16[8,400,128]{2,1,0:T(8,128)(2,1)} %shard_map.110.refs_1_), channel_id=1, source_target_pairs={{0,16},{8,24},{16,0},{24,8},{1,17},{9,25},{17,1},{25,9},{2,18},{10... | collective-permute-start | bytes 2457608 | tf_op jit(solution)/shard_map/ppermute | solution.py:240
  268.7 19.0 %collective-permute-start.32 = (s16[8,400,128]{2,1,0:T(8,128)(2,1)S(1)}, s16[8,400,128]{2,1,0:T(8,128)(2,1)}, u32[]{:S(2)}, u32[]{:S(2)}) collective-permute-start(s16[8,400,128]{2,1,0:T(8,128)(2,1)S(1)} %copy-done.10), channel_id=1, source_target_pairs={{0,8},{8,0},{16,24},{24,16},{1,9},{9,1},{17,25},{25,17},{2,10},{10... | collective-permute-start | bytes 2457608 | tf_op jit(solution)/shard_map/ppermute | solution.py:240
  268.8 18.9 %collective-permute-start.33 = (s16[8,400,128]{2,1,0:T(8,128)(2,1)}, s16[8,400,128]{2,1,0:T(8,128)(2,1)}, u32[]{:S(2)}, u32[]{:S(2)}) collective-permute-start(s16[8,400,128]{2,1,0:T(8,128)(2,1)} %collective-permute-done.31.refs_1_), channel_id=1, source_target_pairs={{0,8},{8,0},{16,24},{24,16},{1,9},{9,1},{17,25},{25,17},{2,10},{10... | collective-permute-start | bytes 2457608 | tf_op jit(solution)/shard_map/ppermute | solution.py:240
  284.6 9.5 %collective-permute-start.35 = (s16[8,400,128]{2,1,0:T(8,128)(2,1)S(1)}, s16[8,400,128]{2,1,0:T(8,128)(2,1)}, u32[]{:S(2)}, u32[]{:S(2)}) collective-permute-start(s16[8,400,128]{2,1,0:T(8,128)(2,1)S(1)} %copy-done.6), channel_id=1, source_target_pairs={{0,8},{8,0},{16,24},{24,16},{1,9},{9,1},{17,25},{25,17},{2,10},{10... | collective-permute-start | bytes 2457608 | tf_op jit(solution)/shard_map/ppermute | solution.py:240
  284.6 9.5 %collective-permute-start.36 = (s16[8,400,128]{2,1,0:T(8,128)(2,1)}, s16[8,400,128]{2,1,0:T(8,128)(2,1)}, u32[]{:S(2)}, u32[]{:S(2)}) collective-permute-start(s16[8,400,128]{2,1,0:T(8,128)(2,1)} %collective-permute-done.34.refs_2_), channel_id=1, source_target_pairs={{0,8},{8,0},{16,24},{24,16},{1,9},{9,1},{17,25},{25,17},{2,10},{10... | collective-permute-start | bytes 2457608 | tf_op jit(solution)/shard_map/ppermute | solution.py:240
  285.1 20.4 %collective-permute-start.37 = (s16[8,400,128]{2,1,0:T(8,128)(2,1)}, s16[8,400,128]{2,1,0:T(8,128)(2,1)S(1)}, u32[]{:S(2)}, u32[]{:S(2)}) collective-permute-start(s16[8,400,128]{2,1,0:T(8,128)(2,1)} %shard_map.107.refs_1_), channel_id=1, source_target_pairs={{0,16},{8,24},{16,0},{24,8},{1,17},{9,25},{17,1},{25,9},{2,18},{10... | collective-permute-start | bytes 2457608 | tf_op jit(solution)/shard_map/ppermute | solution.py:240
  305.4 2.3 collective-permute-start.38
  305.4 3.5 %collective-permute-start.39 = (s16[8,400,128]{2,1,0:T(8,128)(2,1)S(1)}, s16[8,400,128]{2,1,0:T(8,128)(2,1)S(1)}, u32[]{:S(2)}, u32[]{:S(2)}) collective-permute-start(s16[8,400,128]{2,1,0:T(8,128)(2,1)S(1)} %collective-permute-done.37.refs_2_), channel_id=1, source_target_pairs={{0,8},{8,0},{16,24},{24,16},{1,9},{9,1},{17,25},{25,17},{2,10},{10... | collective-permute-start | bytes 2457608 | tf_op jit(solution)/shard_map/ppermute | solution.py:240
  (31 other events, 388.4 us)

commit v5 on v4

--- a/solution.py
+++ b/solution.py
@@ -60,22 +60,23 @@
     for first in range(0, fill, 2):
         terms = range(first, min(first + 2, fill))
         left = [halves[cols[block, f]] for f in terms]
-        right = [tiles[pl.ds((place * fill + f) * blk, blk), :] for f in terms]
+        right = tiles[pl.ds((place * fill + first) * blk, len(left) * blk), :]
         total += lax.dot_general(
             jnp.concatenate(left, axis=1),
-            jnp.concatenate(right, axis=1),
-            (((1,), (1,)), ((), ())),
+            right,
+            (((1,), (0,)), ((), ())),
             preferred_element_type=jnp.float32,
         )
     return total[:rows] + total[rows:]
 
 
-def pack_kernel(far, v_ref, d_ref, out_ref, turned):
+def pack_kernel(cols, place, v_ref, d_ref, out_ref, turned):
+    del cols
     put(out_ref, 0, v_ref[...].T)
     turned[...] = d_ref[...].T
     width, rows = turned.shape
     slab = out_ref.shape[1] - width - PAD
-    here = turned[pl.ds(pl.multiple_of(far[0, 0] * slab, slab), slab), :]
+    here = turned[pl.ds(pl.multiple_of(place[1, 0] * slab, slab), slab), :]
     codes = jnp.floor(here * 32767.0 + 0.5)
     out_ref[0, pl.ds(width + PAD, slab), :] = codes.astype(jnp.int32).astype(jnp.int16)
 
@@ -128,8 +129,9 @@
         y_ref[:, t * blk : (t + 1) * blk] = apply_row(halves, tiles, t, cols, step * per + t, fill, blk)
 
 
-def right_second_kernel(dims, cols, shift, w_ref, v_ref, d_ref, tiles, p_ref, halves):
+def right_second_kernel(dims, cols, shift, w_ref, v_ref, d_ref, tiles, *rest):
     nblk, fill, blk, per = dims
+    outs, halves = rest[:-1], rest[-1]
     step = pl.program_id(0)
 
     @pl.when(step == 0)
@@ -142,7 +144,7 @@
         block = step * per + t
         here = w_ref[:, pl.ds(pl.multiple_of(block * blk, blk), blk)]
         moved = apply_row(halves, tiles, t, cols, block, fill, blk)
-        p_ref[:, lanes] = 0.5 * (moved + (d_ref[:, lanes] - shift[0, 0]) * here) - v_ref[:, lanes]
+        outs[t][...] = 0.5 * (moved + (d_ref[:, lanes] - shift[0, 0]) * here) - v_ref[:, lanes]
 
 
 def left_second_kernel(dims, chunk, cols, shift, far, tu_ref, tail_ref, y_ref, tiles, *rest):
@@ -172,8 +174,11 @@
     put(out, 0, jnp.concatenate(done, axis=0))
 
 
-def second_kernel(z_ref, p_ref, out_ref):
-    put(out_ref, 0, take(z_ref, 0) + p_ref[...])
+def second_kernel(weights, z_ref, p_ref, out_ref):
+    del weights
+    part = z_ref.shape[2]
+    for n in range(z_ref.shape[0]):
+        put(out_ref, n, take(z_ref, n) + p_ref[:, n * part : (n + 1) * part])
 
 
 def rotate_kernel(aliased, weights, *refs):
@@ -255,36 +260,43 @@
     ring = list(range(0, groups, 2)) + list(range(1, groups, 2))[::-1]
     spot = jnp.array([ring.index(c) for c in range(groups)], jnp.int32)[lax.axis_index("col")]
     share = blk // roots
-    mine = string_blocks.reshape(-1, blk, blk)
-    mine = lax.dynamic_slice_in_dim(mine, root * share, share, 1)
-    shards, owners, forth, back = [], [0], mine, mine
-    started = start, diagonal
+    owners = [0]
     for hop in range(1, groups // 2 + 1):
-        both = 2 * hop < groups
-        for way in (1, -1) if both else (1,):
+        owners += [-hop] * roots + ([hop] * roots if 2 * hop < groups else [])
+    place = jnp.array(ring, jnp.int32)[(spot + jnp.array(owners, jnp.int32)) % groups]
+    place = jnp.stack([place, jnp.concatenate([far[0, :1]] + [far[0]] * (groups - 1))])
+
+    slab = width // roots
+    height = width + PAD + slab
+
+    def pack(start, diagonal):
+        return call(
+            pack_kernel,
+            groups,
+            [smem(), smem(), piece, piece],
+            pl.BlockSpec((1, height, rows), lambda q: (q, 0, 0)),
+            jax.ShapeDtypeStruct((groups, height, rows), i16),
+            [pltpu.VMEM((width, rows), f32)],
+            0,
+            size * 3,
+        )(block_cols, place, start, diagonal)
+
+    own = jnp.swapaxes(string_blocks.reshape(-1, blk, blk), 1, 2)
+    mine = lax.dynamic_slice_in_dim(own, root * share, share, 1)
+    shards, crossed, tv, forth, back = [], [], None, mine, mine
+    for hop in range(1, groups // 2 + 1):
+        if hop == 3:
+            forth, back = lax.optimization_barrier((forth, back, tv, *crossed[:2]))[:2]
+        for way in (1, -1) if 2 * hop < groups else (1,):
             pairs = [(ring[s], ring[(s + way) % groups]) for s in range(groups)]
             moved = lax.ppermute(forth if way == 1 else back, "col", pairs)
             forth, back = (moved, back) if way == 1 else (forth, moved)
             shards += exchange(moved)
-            owners += [-way * hop] * roots
+            crossed.append(shards[1 - roots])
         if hop == 1:
-            started = lax.optimization_barrier((start, diagonal, forth, back))[:2]
-    place = jnp.array(ring, jnp.int32)[(spot + jnp.array(owners, jnp.int32)) % groups]
-    place = jnp.stack([place, jnp.concatenate([far[0, :1]] + [far[0]] * (groups - 1))])
-
-    slab = width // roots
-    height = width + PAD + slab
-    tv = call(
-        pack_kernel,
-        groups,
-        [smem(), piece, piece],
-        pl.BlockSpec((1, height, rows), lambda q: (q, 0, 0)),
-        jax.ShapeDtypeStruct((groups, height, rows), i16),
-        [pltpu.VMEM((width, rows), f32)],
-        0,
-        size * 3,
-    )(far, *started)
-    tv = swap(lax.optimization_barrier((tv, forth, back))[0])
+            tv = pack(*lax.optimization_barrier((start, diagonal, forth, back))[:2])
+    tv = swap(lax.optimization_barrier((tv, forth, back, *crossed[2:4]))[0])
+    own = own.reshape(string_blocks.shape)
 
     once = pl.Buffered(1)
     shard_spec = pl.BlockSpec(mine.shape, lambda q: (0, 0, 0), pipeline_mode=once)
@@ -307,15 +319,15 @@
         ],
         work,
         size * 6,
-    )(block_cols, energy, place, start, diagonal, string_blocks, *shards)
+    )(block_cols, energy, place, start, diagonal, own, *shards)
     tu = swap(tu)
 
     base = call(
         functools.partial(right_second_kernel, dims),
         groups,
         [smem(), smem(), whole, piece, piece, tile_spec],
-        piece,
-        row_shape,
+        [pl.BlockSpec((rows, blk), lambda q: (0, q))] * chunks,
+        [jax.ShapeDtypeStruct((rows, groups * blk), f32)] * chunks,
         [row_halves],
         work,
         size * 5,
@@ -335,7 +347,9 @@
     slabs = exchange(tv[:, width + PAD :], y)
     part = width // chunks
     chunk_coded = pl.BlockSpec((1, rows + PAD, part), lambda q: (q, 0, 0))
-    turned = []
+    many = 4 if groups % 4 == 0 else 1
+    many_coded = pl.BlockSpec((many, rows + PAD, part), lambda q: (q, 0, 0))
+    seconds = []
     for k in range(chunks):
         z = call(
             functools.partial(left_second_kernel, dims, k),
@@ -356,26 +370,21 @@
             [pltpu.VMEM((nblk, 2 * part, blk), jnp.bfloat16), pltpu.VMEM((width, rows), f32)],
             work // chunks,
             size * 4 // chunks,
-        )(block_cols, energy, far, tu, tu, y, tiles, *slabs, base)
-        turned.append(z)
-
-    seconds = []
-    for k in range(chunks):
-        slot = pl.BlockSpec((rows, part), lambda q, k=k: (0, q * chunks + k))
+        )(block_cols, energy, far, tu, tu, y, tiles, *slabs, base[0] if k < 2 else seconds[k - 2])
         second = call(
             second_kernel,
-            groups,
-            [chunk_coded, slot],
-            chunk_coded,
+            groups // many,
+            [smem(), many_coded, pl.BlockSpec((rows, many * part), lambda q: (0, q))],
+            many_coded,
             jax.ShapeDtypeStruct((groups, rows + PAD, part), i16),
             [],
             0,
             size * 2 // chunks,
-        )(swap(turned[k]), base)
+        )(weights, swap(z), base[k])
         seconds.append(second)
     out = []
     for k in range(chunks):
-        late = seconds[-1] if k < chunks - 1 else out[0] if out else None
+        late = seconds[k + 1] if k < chunks - 1 else out[0] if out else None
         slot = pl.BlockSpec((1, rows, part), lambda q, k=k: (0, 0, q * chunks + k))
         out = [
             call(

time: 319 us -> 312 us (0.978)
  Pallas kernels: 144 us -> 134 us
  local copies, waits for them, and re-layouts: 11.6 us -> 20 us
  waiting for transfers between devices: 109 us -> 104 us
    pallas_call x4, Pallas kernels: 26.4 us -> 17.1 us  [the longest x1 8.76 us: pack(): call(pack_kernel, groups, [smem(), smem(), piece, piece], pl.BlockSpec((1...]
    ppermute x7, waiting for transfers between devices: 15.3 us -> 6.47 us  [blocked_shards(): moved = lax.ppermute(forth if way == 1 else back, 'col', pairs)]
    unnamed x69 -> x72, local copies, waits for them, and re-layouts: 6.95 us -> 11.1 us
  transfers between devices with their start and end apart: 45 -> 45, of which waited for: 18 -> 18; matrix products, arithmetic and copies ran while one was open for 2% -> 4% of each run, Pallas kernels for 40% -> 37%
where the time goes in v5:
time: 312 us; the launch traced here: 310 us
  Pallas kernels  134 us (43%)
  waiting for transfers between devices  104 us (33%)
  starting transfers between devices  47.8 us (15%)
  local copies, waits for them, and re-layouts  20 us (6%)
    ppermute x33, waiting for transfers between devices, exchange(): have = have + [lax.ppermute(h, 'root', pairs) for h in have]  52.5 us
    all_to_all x5, waiting for transfers between devices, swap(): lax.all_to_all(pieces, 'col', split_axis=0, concat_axis=0, tiled=True)  45.3 us
    pallas_call x3, Pallas kernels, blocked_shards(): call(functools.partial(left_second_kernel, dims, k), groups, [smem(), sme...  35 us
    pallas_call x1, Pallas kernels, blocked_shards(): call(functools.partial(right_first_kernel, dims), groups, [smem(), smem()...  26 us
    all_to_all x5, starting transfers between devices, swap(): lax.all_to_all(pieces, 'col', split_axis=0, concat_axis=0, tiled=True)  20.7 us
    pallas_call x1, Pallas kernels, blocked_shards(): call(functools.partial(right_second_kernel, dims), groups, [smem(), smem(...  19.1 us
    pallas_call x3, Pallas kernels, blocked_shards(): call(functools.partial(rotate_kernel, len(out)), groups, [smem()] + [pl.B...  19.1 us
    ppermute x33, starting transfers between devices, exchange(): have = have + [lax.ppermute(h, 'root', pairs) for h in have]  17.6 us
  transfers between devices with their start and end apart: 45, of which 18 were waited for; matrix products, arithmetic and copies ran while one was open for 4% of the time, Pallas kernels for 37%

profile of v5, /device:TPU:0, one launch (start us, length us, event | category | flops | bytes accessed | tf_op | source)
XLA Modules:
  0.0 309.6 jit_solution(4729961799020428824)
XLA Ops:
  0.0 1.6 constant_dynamic-slice_fusion
  1.9 3.1 collective-permute-start
  6.9 4.0 %collective-permute-done.rest_0_ = bf16[30,32,128]{2,1,0:T(8,128)(2,1)S(1)} collective-permute-done((bf16[30,32,128]{2,1,0:T(8,128)(2,1)S(1)}, bf16[30,32,128]{2,1,0:T(8,128)(2,1)S(1)}, u32[]{:S(2)}, u32[]{:S(2)}) %collective-permute-start) | collective-permute-done | bytes 245792 | tf_op jit(solution)/shard_map/ppermute | solution.py:292
  10.9 1.8 collective-permute-start.8
  12.7 1.5 collective-permute-start.1
  19.7 8.8 %shard_map.100 = s16[8,496,384]{2,1,0:T(8,128)(2,1)} custom-call(s32[24,10]{1,0:T(8,128)} %copy.26.cols, s32[2,29]{1,0:T(2,128)} %pad_add_fusion.place, f32[384,3072]{1,0:T(8,128)} %bitcast.22, f32[384,3072]{1,0:T(8,128)} %d_ref.4), custom_call_target="tpu_custom_call" | custom-call | bytes 14155776 | tf_op jit(solution)/shard_map/pallas_call | solution.py:273
  28.5 1.8 collective-permute-start.16
  30.6 1.7 collective-permute-start.9
  32.6 2.5 collective-permute-done.16.rest_16_
  35.1 2.1 collective-permute-start.24
  37.2 1.5 collective-permute-done.9.rest_9_
  38.7 2.6 collective-permute-done.13.rest_13_
  42.1 6.2 %all-to-all-start.1 = ((s16[8,496,384]{2,1,0:T(8,128)(2,1)}), s16[8,496,384]{2,1,0:T(8,128)(2,1)S(1)}, u32[]{:S(2)}, u32[]{:S(2)}) async-start(s16[8,496,384]{2,1,0:T(8,128)(2,1)} %shard_map.100), calls=%async_computation.1 | async-start | bytes 6094848 | tf_op jit(solution)/shard_map/all_to_all | solution.py:227
  50.6 1.5 collective-permute-start.17
  54.1 5.5 %collective-permute-done.17.rest_17_ = bf16[30,32,128]{2,1,0:T(8,128)(2,1)S(1)} collective-permute-done((bf16[30,32,128]{2,1,0:T(8,128)(2,1)}, bf16[30,32,128]{2,1,0:T(8,128)(2,1)S(1)}, u32[]{:S(2)}, u32[]{:S(2)}) %collective-permute-start.17) | collective-permute-done | bytes 245792 | tf_op jit(solution)/shard_map/ppermute | solution.py:245
  59.7 1.5 collective-permute-start.25
  61.1 3.9 %collective-permute-done.21.rest_21_ = bf16[30,32,128]{2,1,0:T(8,128)(2,1)} collective-permute-done((bf16[30,32,128]{2,1,0:T(8,128)(2,1)}, bf16[30,32,128]{2,1,0:T(8,128)(2,1)}, u32[]{:S(2)}, u32[]{:S(2)}) %collective-permute-start.21) | collective-permute-done | bytes 245792 | tf_op jit(solution)/shard_map/ppermute | solution.py:245
  66.9 2.5 collective-permute-done.25.rest_25_
  70.1 2.3 copy.20
  72.5 26.0 %shard_map.101 = (f32[384,3072]{1,0:T(8,128)}, s16[8,400,384]{2,1,0:T(8,128)(2,1)}, bf16[30720,128]{1,0:T(8,128)(2,1)}) custom-call(s32[24,10]{1,0:T(8,128)} %copy.26.cols, f32[1,1]{1,0:T(1,128)} %bitcast.17.shift, s32[2,29]{1,0:T(2,128)} %pad_add_fusion.place, f32[384,3072]{1,0:T(8,128)} %bitcast.23, f32[384,3072]{1,0:T(8,128)} %d_ref.4, ...), custom_call_target="tpu_custom_call" | custom-call | flops 6039797760 | bytes 28311552 | tf_op jit(solution)/shard_map/pallas_call | solution.py:303
  98.5 14.7 %all-to-all-done.1.tv_ref = s16[8,496,384]{2,1,0:T(8,128)(2,1)S(1)} async-done(((s16[8,496,384]{2,1,0:T(8,128)(2,1)}), s16[8,496,384]{2,1,0:T(8,128)(2,1)S(1)}, u32[]{:S(2)}, u32[]{:S(2)}) %all-to-all-start.1) | async-done | bytes 3047456 | tf_op jit(solution)/shard_map/all_to_all | solution.py:227
  113.3 1.6 copy-done.4
  114.9 3.8 %all-to-all-start = ((s16[8,400,384]{2,1,0:T(8,128)(2,1)}), s16[8,400,384]{2,1,0:T(8,128)(2,1)S(1)}, u32[]{:S(2)}, u32[]{:S(2)}) async-start(s16[8,400,384]{2,1,0:T(8,128)(2,1)} %get-tuple-element.28), calls=%async_computation | async-start | bytes 4915200 | tf_op jit(solution)/shard_map/all_to_all | solution.py:227
  119.8 1.6 collective-permute-start.28
  121.4 17.6 %shard_map.102.y_ref = f32[384,3072]{1,0:T(8,128)} custom-call(s32[24,10]{1,0:T(8,128)} %copy.26.cols, s16[8,496,384]{2,1,0:T(8,128)(2,1)} %copy-done.4, bf16[30720,128]{1,0:T(8,128)(2,1)} %get-tuple-element.30.tiles), custom_call_target="tpu_custom_call" | custom-call | flops 6039797760 | bytes 14155776 | tf_op jit(solution)/shard_map/pallas_call | solution.py:336
  139.6 19.1 %shard_map.103 = (f32[384,1024]{1,0:T(8,128)}, f32[384,1024]{1,0:T(8,128)}, f32[384,1024]{1,0:T(8,128)}) custom-call(s32[24,10]{1,0:T(8,128)} %copy.26.cols, f32[1,1]{1,0:T(1,128)} %bitcast.18.shift, f32[384,3072]{1,0:T(8,128)} %get-tuple-element.33.w_ref, f32[384,3072]{1,0:T(8,128)} %bitcast.24, f32[384,3072]{1,0:T(8,128)} %d_ref.4, ...), custom_call_target="tpu_custom_call" | custom-call | flops 6039797760 | bytes 23592960 | tf_op jit(solution)/shard_map/pallas_call | solution.py:325
  158.7 15.8 %all-to-all-done.tu_ref.tail_ref = s16[8,400,384]{2,1,0:T(8,128)(2,1)S(1)} async-done(((s16[8,400,384]{2,1,0:T(8,128)(2,1)}), s16[8,400,384]{2,1,0:T(8,128)(2,1)S(1)}, u32[]{:S(2)}, u32[]{:S(2)}) %all-to-all-start) | async-done | bytes 2457632 | tf_op jit(solution)/shard_map/all_to_all | solution.py:227
  174.5 1.4 copy-done.1
  176.0 11.6 %shard_map.104 = s16[8,400,128]{2,1,0:T(8,128)(2,1)} custom-call(s32[24,10]{1,0:T(8,128)} %copy.26.cols, f32[1,1]{1,0:T(1,128)} %bitcast.19.shift, s32[1,4]{1,0:T(1,128)} %copy-done.16, s16[8,400,384]{2,1,0:T(8,128)(2,1)} %copy-done.1, s16[8,400,384]{2,1,0:T(8,128)(2,1)} %copy-done.1, f32[384,3072]{1,0:T(8,128)} %shard_map.102.y_ref, ...), custom_call_target="tpu_custom_call" | custom-call | flops 2013265920 | bytes 6291456 | tf_op jit(solution)/shard_map/pallas_call | solution.py:354
  187.6 3.5 %all-to-all-start.2 = ((s16[8,400,128]{2,1,0:T(8,128)(2,1)}), s16[8,400,128]{2,1,0:T(8,128)(2,1)S(1)}, u32[]{:S(2)}, u32[]{:S(2)}) async-start(s16[8,400,128]{2,1,0:T(8,128)(2,1)} %shard_map.104), calls=%async_computation.2 | async-start | bytes 1638400 | tf_op jit(solution)/shard_map/all_to_all | solution.py:227
  191.1 11.7 %shard_map.106 = s16[8,400,128]{2,1,0:T(8,128)(2,1)} custom-call(s32[24,10]{1,0:T(8,128)} %copy.26.cols, f32[1,1]{1,0:T(1,128)} %bitcast.20.shift, s32[1,4]{1,0:T(1,128)} %copy-done.16, s16[8,400,384]{2,1,0:T(8,128)(2,1)} %copy-done.1, s16[8,400,384]{2,1,0:T(8,128)(2,1)} %copy-done.1, f32[384,3072]{1,0:T(8,128)} %shard_map.102.y_ref, ...), custom_call_target="tpu_custom_call" | custom-call | flops 2013265920 | bytes 6291456 | tf_op jit(solution)/shard_map/pallas_call | solution.py:354
  202.8 9.4 %all-to-all-done.2.z_ref = s16[8,400,128]{2,1,0:T(8,128)(2,1)S(1)} async-done(((s16[8,400,128]{2,1,0:T(8,128)(2,1)}), s16[8,400,128]{2,1,0:T(8,128)(2,1)S(1)}, u32[]{:S(2)}, u32[]{:S(2)}) %all-to-all-start.2) | async-done | bytes 819232 | tf_op jit(solution)/shard_map/all_to_all | solution.py:227
  212.2 3.6 %all-to-all-start.3 = ((s16[8,400,128]{2,1,0:T(8,128)(2,1)}), s16[8,400,128]{2,1,0:T(8,128)(2,1)S(1)}, u32[]{:S(2)}, u32[]{:S(2)}) async-start(s16[8,400,128]{2,1,0:T(8,128)(2,1)} %shard_map.106), calls=%async_computation.3 | async-start | bytes 1638400 | tf_op jit(solution)/shard_map/all_to_all | solution.py:227
  217.0 2.8 shard_map.105.refs_0_.rest_4_
  219.8 11.7 %shard_map.109 = s16[8,400,128]{2,1,0:T(8,128)(2,1)} custom-call(s32[24,10]{1,0:T(8,128)} %copy.26.cols, f32[1,1]{1,0:T(1,128)} %bitcast.21.shift, s32[1,4]{1,0:T(1,128)} %copy-done.16, s16[8,400,384]{2,1,0:T(8,128)(2,1)} %copy-done.1, s16[8,400,384]{2,1,0:T(8,128)(2,1)} %copy-done.1, f32[384,3072]{1,0:T(8,128)} %shard_map.102.y_ref, ...), custom_call_target="tpu_custom_call" | custom-call | flops 2013265920 | bytes 6291456 | tf_op jit(solution)/shard_map/pallas_call | solution.py:354
  231.5 5.4 %all-to-all-done.3.z_ref = s16[8,400,128]{2,1,0:T(8,128)(2,1)S(1)} async-done(((s16[8,400,128]{2,1,0:T(8,128)(2,1)}), s16[8,400,128]{2,1,0:T(8,128)(2,1)S(1)}, u32[]{:S(2)}, u32[]{:S(2)}) %all-to-all-start.3) | async-done | bytes 819232 | tf_op jit(solution)/shard_map/all_to_all | solution.py:227
  236.8 3.6 %all-to-all-start.4 = ((s16[8,400,128]{2,1,0:T(8,128)(2,1)}), s16[8,400,128]{2,1,0:T(8,128)(2,1)S(1)}, u32[]{:S(2)}, u32[]{:S(2)}) async-start(s16[8,400,128]{2,1,0:T(8,128)(2,1)} %shard_map.109), calls=%async_computation.4 | async-start | bytes 1638400 | tf_op jit(solution)/shard_map/all_to_all | solution.py:227
  240.4 1.6 collective-permute-start.31
  242.0 2.8 shard_map.107.refs_1_
  245.2 16.4 %collective-permute-done.31.refs_1_ = s16[8,400,128]{2,1,0:T(8,128)(2,1)S(1)} collective-permute-done((s16[8,400,128]{2,1,0:T(8,128)(2,1)S(1)}, s16[8,400,128]{2,1,0:T(8,128)(2,1)S(1)}, u32[]{:S(2)}, u32[]{:S(2)}) %collective-permute-start.31) | collective-permute-done | bytes 819232 | tf_op jit(solution)/shard_map/ppermute | solution.py:245
  263.0 2.8 shard_map.110.refs_1_
  265.8 12.1 %collective-permute-done.34.refs_2_ = s16[8,400,128]{2,1,0:T(8,128)(2,1)S(1)} collective-permute-done((s16[8,400,128]{2,1,0:T(8,128)(2,1)}, s16[8,400,128]{2,1,0:T(8,128)(2,1)S(1)}, u32[]{:S(2)}, u32[]{:S(2)}) %collective-permute-start.34) | collective-permute-done | bytes 819232 | tf_op jit(solution)/shard_map/ppermute | solution.py:245
  278.4 1.5 collective-permute-start.37
  279.9 6.4 %shard_map.108.refs_0_ = f32[1,384,3072]{2,1,0:T(8,128)} custom-call(f32[1,4]{1,0:T(1,128)} %bitcast.33, s16[8,400,128]{2,1,0:T(8,128)(2,1)} %shard_map.105.refs_0_.rest_4_, s16[8,400,128]{2,1,0:T(8,128)(2,1)} %copy-done.15, s16[8,400,128]{2,1,0:T(8,128)(2,1)} %collective-permute-done.32.refs_2_, s16[8,400,128]{2,1,0:T(8,128)(2,1)} %collective-permute-done.33.refs_3_), custom_call_target="tpu_custom_call" | custom-call | bytes 4718592 | tf_op jit(solution)/shard_map/pallas_call | solution.py:390
  288.1 6.4 %shard_map.111.refs_0_ = f32[1,384,3072]{2,1,0:T(8,128)} custom-call(f32[1,4]{1,0:T(1,128)} %bitcast.34, f32[1,384,3072]{2,1,0:T(8,128)} %shard_map.108.refs_0_, s16[8,400,128]{2,1,0:T(8,128)(2,1)} %shard_map.107.refs_1_, s16[8,400,128]{2,1,0:T(8,128)(2,1)} %copy-done.9, s16[8,400,128]{2,1,0:T(8,128)(2,1)} %copy-done.11, ...), custom_call_target="tpu_custom_call", output_to_operand_aliasing={{}: (1, {})} | custom-call | bytes 4718592 | tf_op jit(solution)/shard_map/pallas_call | solution.py:390
  294.5 4.3 %collective-permute-done.37.refs_2_ = s16[8,400,128]{2,1,0:T(8,128)(2,1)S(1)} collective-permute-done((s16[8,400,128]{2,1,0:T(8,128)(2,1)}, s16[8,400,128]{2,1,0:T(8,128)(2,1)S(1)}, u32[]{:S(2)}, u32[]{:S(2)}) %collective-permute-start.37) | collective-permute-done | bytes 819232 | tf_op jit(solution)/shard_map/ppermute | solution.py:245
  299.3 1.8 collective-permute-done.38.refs_3_
  303.2 6.4 %shard_map.112 = f32[1,384,3072]{2,1,0:T(8,128)} custom-call(f32[1,4]{1,0:T(1,128)} %bitcast.35, f32[1,384,3072]{2,1,0:T(8,128)} %shard_map.111.refs_0_, s16[8,400,128]{2,1,0:T(8,128)(2,1)} %shard_map.110.refs_1_, s16[8,400,128]{2,1,0:T(8,128)(2,1)} %copy-done.10, s16[8,400,128]{2,1,0:T(8,128)(2,1)} %copy-done.13, ...), custom_call_target="tpu_custom_call", output_to_operand_aliasing={{}: (1, {})} | custom-call | bytes 4718592 | tf_op jit(solution)/shard_map/pallas_call | solution.py:390
  (140 shorter events, 25.0 us)
Async XLA Ops:
  0.0 215.8 %copy-start = (f32[4,4]{1,0:T(4,128)S(1)}, f32[4,4]{1,0:T(4,128)}, u32[]{:S(2)}) copy-start(f32[4,4]{1,0:T(4,128)} %param.13) | copy-start | bytes 196
  1.9 9.0 %collective-permute-start = (bf16[30,32,128]{2,1,0:T(8,128)(2,1)S(1)}, bf16[30,32,128]{2,1,0:T(8,128)(2,1)S(1)}, u32[]{:S(2)}, u32[]{:S(2)}) collective-permute-start(bf16[30,32,128]{2,1,0:T(8,128)(2,1)S(1)} %bitcast.28), channel_id=1, source_target_pairs={{0,2},{2,4},{4,6},{6,7},{7,5},{5,3},{3,1},{1,0},{8,10},{10,12},{12... | collective-permute-start | bytes 737288 | tf_op jit(solution)/shard_map/ppermute | solution.py:292
  5.0 9.2 %collective-permute-start.4 = (bf16[30,32,128]{2,1,0:T(8,128)(2,1)S(1)}, bf16[30,32,128]{2,1,0:T(8,128)(2,1)S(1)}, u32[]{:S(2)}, u32[]{:S(2)}) collective-permute-start(bf16[30,32,128]{2,1,0:T(8,128)(2,1)S(1)} %bitcast.29), channel_id=1, source_target_pairs={{0,1},{2,0},{4,2},{6,4},{7,6},{5,7},{3,5},{1,3},{8,9},{10,8},{12,1... | collective-permute-start | bytes 737288 | tf_op jit(solution)/shard_map/ppermute | solution.py:292
  10.9 37.4 %copy-start.17 = (bf16[30,32,128]{2,1,0:T(8,128)(2,1)}, bf16[30,32,128]{2,1,0:T(8,128)(2,1)S(1)}, u32[]{:S(2)}) copy-start(bf16[30,32,128]{2,1,0:T(8,128)(2,1)S(1)} %collective-permute-done.rest_0_) | copy-start | bytes 737284
  10.9 17.5 %collective-permute-start.8 = (bf16[30,32,128]{2,1,0:T(8,128)(2,1)S(1)}, bf16[30,32,128]{2,1,0:T(8,128)(2,1)S(1)}, u32[]{:S(2)}, u32[]{:S(2)}) collective-permute-start(bf16[30,32,128]{2,1,0:T(8,128)(2,1)S(1)} %collective-permute-done.rest_0_), channel_id=1, source_target_pairs={{0,2},{2,4},{4,6},{6,7},{7,5},{5,3},{3,1},{1,0},{8,10},{10,12},{12... | collective-permute-start | bytes 737288 | tf_op jit(solution)/shard_map/ppermute | solution.py:292
  12.7 15.8 %collective-permute-start.1 = (bf16[30,32,128]{2,1,0:T(8,128)(2,1)S(1)}, bf16[30,32,128]{2,1,0:T(8,128)(2,1)S(1)}, u32[]{:S(2)}, u32[]{:S(2)}) collective-permute-start(bf16[30,32,128]{2,1,0:T(8,128)(2,1)S(1)} %collective-permute-done.rest_0_), channel_id=1, source_target_pairs={{0,16},{8,24},{16,0},{24,8},{1,17},{9,25},{17,1},{25,9},{2,18},{10... | collective-permute-start | bytes 737288 | tf_op jit(solution)/shard_map/ppermute | solution.py:245
  14.2 34.2 %copy-start.18 = (bf16[30,32,128]{2,1,0:T(8,128)(2,1)}, bf16[30,32,128]{2,1,0:T(8,128)(2,1)S(1)}, u32[]{:S(2)}) copy-start(bf16[30,32,128]{2,1,0:T(8,128)(2,1)S(1)} %collective-permute-done.4.rest_4_) | copy-start | bytes 737284
  14.2 14.2 %collective-permute-start.12 = (bf16[30,32,128]{2,1,0:T(8,128)(2,1)S(1)}, bf16[30,32,128]{2,1,0:T(8,128)(2,1)S(1)}, u32[]{:S(2)}, u32[]{:S(2)}) collective-permute-start(bf16[30,32,128]{2,1,0:T(8,128)(2,1)S(1)} %collective-permute-done.4.rest_4_), channel_id=1, source_target_pairs={{0,1},{2,0},{4,2},{6,4},{7,6},{5,7},{3,5},{1,3},{8,9},{10,8},{12,1... | collective-permute-start | bytes 737288 | tf_op jit(solution)/shard_map/ppermute | solution.py:292
  14.7 13.8 %collective-permute-start.5 = (bf16[30,32,128]{2,1,0:T(8,128)(2,1)S(1)}, bf16[30,32,128]{2,1,0:T(8,128)(2,1)S(1)}, u32[]{:S(2)}, u32[]{:S(2)}) collective-permute-start(bf16[30,32,128]{2,1,0:T(8,128)(2,1)S(1)} %collective-permute-done.4.rest_4_), channel_id=1, source_target_pairs={{0,16},{8,24},{16,0},{24,8},{1,17},{9,25},{17,1},{25,9},{2,18},{10... | collective-permute-start | bytes 737288 | tf_op jit(solution)/shard_map/ppermute | solution.py:245
  28.5 6.6 %collective-permute-start.16 = (bf16[30,32,128]{2,1,0:T(8,128)(2,1)S(1)}, bf16[30,32,128]{2,1,0:T(8,128)(2,1)S(1)}, u32[]{:S(2)}, u32[]{:S(2)}) collective-permute-start(bf16[30,32,128]{2,1,0:T(8,128)(2,1)S(1)} %collective-permute-done.8.rest_8_), channel_id=1, source_target_pairs={{0,2},{2,4},{4,6},{6,7},{7,5},{5,3},{3,1},{1,0},{8,10},{10,12},{12... | collective-permute-start | bytes 737288 | tf_op jit(solution)/shard_map/ppermute | solution.py:292
  30.4 6.8 %collective-permute-start.20 = (bf16[30,32,128]{2,1,0:T(8,128)(2,1)S(1)}, bf16[30,32,128]{2,1,0:T(8,128)(2,1)S(1)}, u32[]{:S(2)}, u32[]{:S(2)}) collective-permute-start(bf16[30,32,128]{2,1,0:T(8,128)(2,1)S(1)} %collective-permute-done.12.rest_12_), channel_id=1, source_target_pairs={{0,1},{2,0},{4,2},{6,4},{7,6},{5,7},{3,5},{1,3},{8,9},{10,8},{12,1... | collective-permute-start | bytes 737288 | tf_op jit(solution)/shard_map/ppermute | solution.py:292
  30.6 8.1 %collective-permute-start.9 = (bf16[30,32,128]{2,1,0:T(8,128)(2,1)S(1)}, bf16[30,32,128]{2,1,0:T(8,128)(2,1)S(1)}, u32[]{:S(2)}, u32[]{:S(2)}) collective-permute-start(bf16[30,32,128]{2,1,0:T(8,128)(2,1)S(1)} %collective-permute-done.8.rest_8_), channel_id=1, source_target_pairs={{0,16},{8,24},{16,0},{24,8},{1,17},{9,25},{17,1},{25,9},{2,18},{10... | collective-permute-start | bytes 737288 | tf_op jit(solution)/shard_map/ppermute | solution.py:245
  32.3 9.0 %collective-permute-start.13 = (bf16[30,32,128]{2,1,0:T(8,128)(2,1)S(1)}, bf16[30,32,128]{2,1,0:T(8,128)(2,1)S(1)}, u32[]{:S(2)}, u32[]{:S(2)}) collective-permute-start(bf16[30,32,128]{2,1,0:T(8,128)(2,1)S(1)} %collective-permute-done.12.rest_12_), channel_id=1, source_target_pairs={{0,16},{8,24},{16,0},{24,8},{1,17},{9,25},{17,1},{25,9},{2,18},{10... | collective-permute-start | bytes 737288 | tf_op jit(solution)/shard_map/ppermute | solution.py:245
  35.1 6.2 %collective-permute-start.24 = (bf16[30,32,128]{2,1,0:T(8,128)(2,1)S(1)}, bf16[30,32,128]{2,1,0:T(8,128)(2,1)S(1)}, u32[]{:S(2)}, u32[]{:S(2)}) collective-permute-start(bf16[30,32,128]{2,1,0:T(8,128)(2,1)S(1)} %collective-permute-done.16.rest_16_), channel_id=1, source_target_pairs={{0,2},{2,4},{4,6},{6,7},{7,5},{5,3},{3,1},{1,0},{8,10},{10,12},{12... | collective-permute-start | bytes 737288 | tf_op jit(solution)/shard_map/ppermute | solution.py:292
  42.1 71.1 %all-to-all-start.1 = ((s16[8,496,384]{2,1,0:T(8,128)(2,1)}), s16[8,496,384]{2,1,0:T(8,128)(2,1)S(1)}, u32[]{:S(2)}, u32[]{:S(2)}) async-start(s16[8,496,384]{2,1,0:T(8,128)(2,1)} %shard_map.100), calls=%async_computation.1 | async-start | bytes 6094848 | tf_op jit(solution)/shard_map/all_to_all | solution.py:227
  48.4 1.6 collective-permute-start.2
  48.4 1.8 collective-permute-start.6
  48.9 3.2 %collective-permute-start.10 = (bf16[30,32,128]{2,1,0:T(8,128)(2,1)}, bf16[30,32,128]{2,1,0:T(8,128)(2,1)S(1)}, u32[]{:S(2)}, u32[]{:S(2)}) collective-permute-start(bf16[30,32,128]{2,1,0:T(8,128)(2,1)} %copy-done.19), channel_id=1, source_target_pairs={{0,8},{8,0},{16,24},{24,16},{1,9},{9,1},{17,25},{25,17},{2,10},{10... | collective-permute-start | bytes 737288 | tf_op jit(solution)/shard_map/ppermute | solution.py:245
  49.0 4.5 %collective-permute-start.14 = (bf16[30,32,128]{2,1,0:T(8,128)(2,1)}, bf16[30,32,128]{2,1,0:T(8,128)(2,1)}, u32[]{:S(2)}, u32[]{:S(2)}) collective-permute-start(bf16[30,32,128]{2,1,0:T(8,128)(2,1)} %copy-done.21), channel_id=1, source_target_pairs={{0,8},{8,0},{16,24},{24,16},{1,9},{9,1},{17,25},{25,17},{2,10},{10... | collective-permute-start | bytes 737288 | tf_op jit(solution)/shard_map/ppermute | solution.py:245
  49.4 4.1 %collective-permute-start.3 = (bf16[30,32,128]{2,1,0:T(8,128)(2,1)}, bf16[30,32,128]{2,1,0:T(8,128)(2,1)}, u32[]{:S(2)}, u32[]{:S(2)}) collective-permute-start(bf16[30,32,128]{2,1,0:T(8,128)(2,1)} %copy-done.20), channel_id=1, source_target_pairs={{0,8},{8,0},{16,24},{24,16},{1,9},{9,1},{17,25},{25,17},{2,10},{10... | collective-permute-start | bytes 737288 | tf_op jit(solution)/shard_map/ppermute | solution.py:245
  49.9 4.1 %collective-permute-start.7 = (bf16[30,32,128]{2,1,0:T(8,128)(2,1)}, bf16[30,32,128]{2,1,0:T(8,128)(2,1)S(1)}, u32[]{:S(2)}, u32[]{:S(2)}) collective-permute-start(bf16[30,32,128]{2,1,0:T(8,128)(2,1)} %copy-done.22), channel_id=1, source_target_pairs={{0,8},{8,0},{16,24},{24,16},{1,9},{9,1},{17,25},{25,17},{2,10},{10... | collective-permute-start | bytes 737288 | tf_op jit(solution)/shard_map/ppermute | solution.py:245
  50.6 9.0 %collective-permute-start.17 = (bf16[30,32,128]{2,1,0:T(8,128)(2,1)}, bf16[30,32,128]{2,1,0:T(8,128)(2,1)S(1)}, u32[]{:S(2)}, u32[]{:S(2)}) collective-permute-start(bf16[30,32,128]{2,1,0:T(8,128)(2,1)} %copy-done.23), channel_id=1, source_target_pairs={{0,16},{8,24},{16,0},{24,8},{1,17},{9,25},{17,1},{25,9},{2,18},{10... | collective-permute-start | bytes 737288 | tf_op jit(solution)/shard_map/ppermute | solution.py:245
  52.8 12.2 %collective-permute-start.21 = (bf16[30,32,128]{2,1,0:T(8,128)(2,1)}, bf16[30,32,128]{2,1,0:T(8,128)(2,1)}, u32[]{:S(2)}, u32[]{:S(2)}) collective-permute-start(bf16[30,32,128]{2,1,0:T(8,128)(2,1)} %copy-done.24), channel_id=1, source_target_pairs={{0,16},{8,24},{16,0},{24,8},{1,17},{9,25},{17,1},{25,9},{2,18},{10... | collective-permute-start | bytes 737288 | tf_op jit(solution)/shard_map/ppermute | solution.py:245
  53.5 11.5 %collective-permute-start.18 = (bf16[30,32,128]{2,1,0:T(8,128)(2,1)}, bf16[30,32,128]{2,1,0:T(8,128)(2,1)S(1)}, u32[]{:S(2)}, u32[]{:S(2)}) collective-permute-start(bf16[30,32,128]{2,1,0:T(8,128)(2,1)} %copy-done.23), channel_id=1, source_target_pairs={{0,8},{8,0},{16,24},{24,16},{1,9},{9,1},{17,25},{25,17},{2,10},{10... | collective-permute-start | bytes 737288 | tf_op jit(solution)/shard_map/ppermute | solution.py:245
  53.5 12.2 %collective-permute-start.22 = (bf16[30,32,128]{2,1,0:T(8,128)(2,1)}, bf16[30,32,128]{2,1,0:T(8,128)(2,1)S(1)}, u32[]{:S(2)}, u32[]{:S(2)}) collective-permute-start(bf16[30,32,128]{2,1,0:T(8,128)(2,1)} %copy-done.24), channel_id=1, source_target_pairs={{0,8},{8,0},{16,24},{24,16},{1,9},{9,1},{17,25},{25,17},{2,10},{10... | collective-permute-start | bytes 737288 | tf_op jit(solution)/shard_map/ppermute | solution.py:245
  54.0 12.9 %collective-permute-start.11 = (bf16[30,32,128]{2,1,0:T(8,128)(2,1)}, bf16[30,32,128]{2,1,0:T(8,128)(2,1)}, u32[]{:S(2)}, u32[]{:S(2)}) collective-permute-start(bf16[30,32,128]{2,1,0:T(8,128)(2,1)} %copy-done.25), channel_id=1, source_target_pairs={{0,8},{8,0},{16,24},{24,16},{1,9},{9,1},{17,25},{25,17},{2,10},{10... | collective-permute-start | bytes 737288 | tf_op jit(solution)/shard_map/ppermute | solution.py:245
  59.7 9.8 %collective-permute-start.25 = (bf16[30,32,128]{2,1,0:T(8,128)(2,1)}, bf16[30,32,128]{2,1,0:T(8,128)(2,1)}, u32[]{:S(2)}, u32[]{:S(2)}) collective-permute-start(bf16[30,32,128]{2,1,0:T(8,128)(2,1)} %copy-done.27), channel_id=1, source_target_pairs={{0,16},{8,24},{16,0},{24,8},{1,17},{9,25},{17,1},{25,9},{2,18},{10... | collective-permute-start | bytes 737288 | tf_op jit(solution)/shard_map/ppermute | solution.py:245
  65.0 7.4 %collective-permute-start.15 = (bf16[30,32,128]{2,1,0:T(8,128)(2,1)}, bf16[30,32,128]{2,1,0:T(8,128)(2,1)}, u32[]{:S(2)}, u32[]{:S(2)}) collective-permute-start(bf16[30,32,128]{2,1,0:T(8,128)(2,1)} %copy-done.26), channel_id=1, source_target_pairs={{0,8},{8,0},{16,24},{24,16},{1,9},{9,1},{17,25},{25,17},{2,10},{10... | collective-permute-start | bytes 737288 | tf_op jit(solution)/shard_map/ppermute | solution.py:245
  65.0 7.4 %collective-permute-start.26 = (bf16[30,32,128]{2,1,0:T(8,128)(2,1)}, bf16[30,32,128]{2,1,0:T(8,128)(2,1)}, u32[]{:S(2)}, u32[]{:S(2)}) collective-permute-start(bf16[30,32,128]{2,1,0:T(8,128)(2,1)} %copy-done.27), channel_id=1, source_target_pairs={{0,8},{8,0},{16,24},{24,16},{1,9},{9,1},{17,25},{25,17},{2,10},{10... | collective-permute-start | bytes 737288 | tf_op jit(solution)/shard_map/ppermute | solution.py:245
  66.4 6.0 %collective-permute-start.19 = (bf16[30,32,128]{2,1,0:T(8,128)(2,1)S(1)}, bf16[30,32,128]{2,1,0:T(8,128)(2,1)}, u32[]{:S(2)}, u32[]{:S(2)}) collective-permute-start(bf16[30,32,128]{2,1,0:T(8,128)(2,1)S(1)} %collective-permute-done.17.rest_17_), channel_id=1, source_target_pairs={{0,8},{8,0},{16,24},{24,16},{1,9},{9,1},{17,25},{25,17},{2,10},{10... | collective-permute-start | bytes 737288 | tf_op jit(solution)/shard_map/ppermute | solution.py:245
  66.9 5.5 %collective-permute-start.23 = (bf16[30,32,128]{2,1,0:T(8,128)(2,1)}, bf16[30,32,128]{2,1,0:T(8,128)(2,1)}, u32[]{:S(2)}, u32[]{:S(2)}) collective-permute-start(bf16[30,32,128]{2,1,0:T(8,128)(2,1)} %collective-permute-done.21.rest_21_), channel_id=1, source_target_pairs={{0,8},{8,0},{16,24},{24,16},{1,9},{9,1},{17,25},{25,17},{2,10},{10... | collective-permute-start | bytes 737288 | tf_op jit(solution)/shard_map/ppermute | solution.py:245
  69.5 3.0 collective-permute-start.27
  114.9 59.7 %all-to-all-start = ((s16[8,400,384]{2,1,0:T(8,128)(2,1)}), s16[8,400,384]{2,1,0:T(8,128)(2,1)S(1)}, u32[]{:S(2)}, u32[]{:S(2)}) async-start(s16[8,400,384]{2,1,0:T(8,128)(2,1)} %get-tuple-element.28), calls=%async_computation | async-start | bytes 4915200 | tf_op jit(solution)/shard_map/all_to_all | solution.py:227
  119.8 19.2 %collective-permute-start.28 = (s16[8,96,384]{2,1,0:T(8,128)(2,1)S(1)}, s16[8,96,384]{2,1,0:T(8,128)(2,1)}, u32[]{:S(2)}, u32[]{:S(2)}) collective-permute-start(s16[8,96,384]{2,1,0:T(8,128)(2,1)S(1)} %slice.12.rest_0_), channel_id=1, source_target_pairs={{0,16},{8,24},{16,0},{24,8},{1,17},{9,25},{17,1},{25,9},{2,18},{10... | collective-permute-start | bytes 1769480 | tf_op jit(solution)/shard_map/ppermute | solution.py:245
  139.0 35.5 %collective-permute-start.29 = (s16[8,96,384]{2,1,0:T(8,128)(2,1)S(1)}, s16[8,96,384]{2,1,0:T(8,128)(2,1)}, u32[]{:S(2)}, u32[]{:S(2)}) collective-permute-start(s16[8,96,384]{2,1,0:T(8,128)(2,1)S(1)} %slice.12.rest_0_), channel_id=1, source_target_pairs={{0,8},{8,0},{16,24},{24,16},{1,9},{9,1},{17,25},{25,17},{2,10},{10... | collective-permute-start | bytes 1769480 | tf_op jit(solution)/shard_map/ppermute | solution.py:245
  139.1 35.4 %collective-permute-start.30 = (s16[8,96,384]{2,1,0:T(8,128)(2,1)}, s16[8,96,384]{2,1,0:T(8,128)(2,1)}, u32[]{:S(2)}, u32[]{:S(2)}) collective-permute-start(s16[8,96,384]{2,1,0:T(8,128)(2,1)} %collective-permute-done.28.rest_1_), channel_id=1, source_target_pairs={{0,8},{8,0},{16,24},{24,16},{1,9},{9,1},{17,25},{25,17},{2,10},{10... | collective-permute-start | bytes 1769480 | tf_op jit(solution)/shard_map/ppermute | solution.py:245
  187.6 24.6 %all-to-all-start.2 = ((s16[8,400,128]{2,1,0:T(8,128)(2,1)}), s16[8,400,128]{2,1,0:T(8,128)(2,1)S(1)}, u32[]{:S(2)}, u32[]{:S(2)}) async-start(s16[8,400,128]{2,1,0:T(8,128)(2,1)} %shard_map.104), calls=%async_computation.2 | async-start | bytes 1638400 | tf_op jit(solution)/shard_map/all_to_all | solution.py:227
  212.2 24.6 %all-to-all-start.3 = ((s16[8,400,128]{2,1,0:T(8,128)(2,1)}), s16[8,400,128]{2,1,0:T(8,128)(2,1)S(1)}, u32[]{:S(2)}, u32[]{:S(2)}) async-start(s16[8,400,128]{2,1,0:T(8,128)(2,1)} %shard_map.106), calls=%async_computation.3 | async-start | bytes 1638400 | tf_op jit(solution)/shard_map/all_to_all | solution.py:227
  236.8 25.3 %all-to-all-start.4 = ((s16[8,400,128]{2,1,0:T(8,128)(2,1)}), s16[8,400,128]{2,1,0:T(8,128)(2,1)S(1)}, u32[]{:S(2)}, u32[]{:S(2)}) async-start(s16[8,400,128]{2,1,0:T(8,128)(2,1)} %shard_map.109), calls=%async_computation.4 | async-start | bytes 1638400 | tf_op jit(solution)/shard_map/all_to_all | solution.py:227
  240.4 21.2 %collective-permute-start.31 = (s16[8,400,128]{2,1,0:T(8,128)(2,1)S(1)}, s16[8,400,128]{2,1,0:T(8,128)(2,1)S(1)}, u32[]{:S(2)}, u32[]{:S(2)}) collective-permute-start(s16[8,400,128]{2,1,0:T(8,128)(2,1)S(1)} %copy-done.3), channel_id=1, source_target_pairs={{0,16},{8,24},{16,0},{24,8},{1,17},{9,25},{17,1},{25,9},{2,18},{10... | collective-permute-start | bytes 2457608 | tf_op jit(solution)/shard_map/ppermute | solution.py:245
  244.7 33.2 %collective-permute-start.34 = (s16[8,400,128]{2,1,0:T(8,128)(2,1)}, s16[8,400,128]{2,1,0:T(8,128)(2,1)S(1)}, u32[]{:S(2)}, u32[]{:S(2)}) collective-permute-start(s16[8,400,128]{2,1,0:T(8,128)(2,1)} %shard_map.107.refs_1_), channel_id=1, source_target_pairs={{0,16},{8,24},{16,0},{24,8},{1,17},{9,25},{17,1},{25,9},{2,18},{10... | collective-permute-start | bytes 2457608 | tf_op jit(solution)/shard_map/ppermute | solution.py:245
  261.6 18.3 %collective-permute-start.32 = (s16[8,400,128]{2,1,0:T(8,128)(2,1)S(1)}, s16[8,400,128]{2,1,0:T(8,128)(2,1)}, u32[]{:S(2)}, u32[]{:S(2)}) collective-permute-start(s16[8,400,128]{2,1,0:T(8,128)(2,1)S(1)} %copy-done.3), channel_id=1, source_target_pairs={{0,8},{8,0},{16,24},{24,16},{1,9},{9,1},{17,25},{25,17},{2,10},{10... | collective-permute-start | bytes 2457608 | tf_op jit(solution)/shard_map/ppermute | solution.py:245
  261.6 18.3 %collective-permute-start.33 = (s16[8,400,128]{2,1,0:T(8,128)(2,1)S(1)}, s16[8,400,128]{2,1,0:T(8,128)(2,1)}, u32[]{:S(2)}, u32[]{:S(2)}) collective-permute-start(s16[8,400,128]{2,1,0:T(8,128)(2,1)S(1)} %collective-permute-done.31.refs_1_), channel_id=1, source_target_pairs={{0,8},{8,0},{16,24},{24,16},{1,9},{9,1},{17,25},{25,17},{2,10},{10... | collective-permute-start | bytes 2457608 | tf_op jit(solution)/shard_map/ppermute | solution.py:245
  277.9 8.4 %collective-permute-start.35 = (s16[8,400,128]{2,1,0:T(8,128)(2,1)}, s16[8,400,128]{2,1,0:T(8,128)(2,1)S(1)}, u32[]{:S(2)}, u32[]{:S(2)}) collective-permute-start(s16[8,400,128]{2,1,0:T(8,128)(2,1)} %shard_map.107.refs_1_), channel_id=1, source_target_pairs={{0,8},{8,0},{16,24},{24,16},{1,9},{9,1},{17,25},{25,17},{2,10},{10... | collective-permute-start | bytes 2457608 | tf_op jit(solution)/shard_map/ppermute | solution.py:245
  277.9 8.4 %collective-permute-start.36 = (s16[8,400,128]{2,1,0:T(8,128)(2,1)S(1)}, s16[8,400,128]{2,1,0:T(8,128)(2,1)S(1)}, u32[]{:S(2)}, u32[]{:S(2)}) collective-permute-start(s16[8,400,128]{2,1,0:T(8,128)(2,1)S(1)} %collective-permute-done.34.refs_2_), channel_id=1, source_target_pairs={{0,8},{8,0},{16,24},{24,16},{1,9},{9,1},{17,25},{25,17},{2,10},{10... | collective-permute-start | bytes 2457608 | tf_op jit(solution)/shard_map/ppermute | solution.py:245
  278.4 20.4 %collective-permute-start.37 = (s16[8,400,128]{2,1,0:T(8,128)(2,1)}, s16[8,400,128]{2,1,0:T(8,128)(2,1)S(1)}, u32[]{:S(2)}, u32[]{:S(2)}) collective-permute-start(s16[8,400,128]{2,1,0:T(8,128)(2,1)} %shard_map.110.refs_1_), channel_id=1, source_target_pairs={{0,16},{8,24},{16,0},{24,8},{1,17},{9,25},{17,1},{25,9},{2,18},{10... | collective-permute-start | bytes 2457608 | tf_op jit(solution)/shard_map/ppermute | solution.py:245
  298.8 2.3 collective-permute-start.38
  298.8 3.5 %collective-permute-start.39 = (s16[8,400,128]{2,1,0:T(8,128)(2,1)S(1)}, s16[8,400,128]{2,1,0:T(8,128)(2,1)S(1)}, u32[]{:S(2)}, u32[]{:S(2)}) collective-permute-start(s16[8,400,128]{2,1,0:T(8,128)(2,1)S(1)} %collective-permute-done.37.refs_2_), channel_id=1, source_target_pairs={{0,8},{8,0},{16,24},{24,16},{1,9},{9,1},{17,25},{25,17},{2,10},{10... | collective-permute-start | bytes 2457608 | tf_op jit(solution)/shard_map/ppermute | solution.py:245
  (32 other events, 223.5 us)

commit v6 on v5

--- a/solution.py
+++ b/solution.py
@@ -70,18 +70,26 @@
     return total[:rows] + total[rows:]
 
 
-def pack_kernel(cols, place, v_ref, d_ref, out_ref, turned):
-    del cols
+def pack_kernel(here, v_ref, d_ref, out_ref, turned):
     put(out_ref, 0, v_ref[...].T)
     turned[...] = d_ref[...].T
     width, rows = turned.shape
     slab = out_ref.shape[1] - width - PAD
-    here = turned[pl.ds(pl.multiple_of(place[1, 0] * slab, slab), slab), :]
-    codes = jnp.floor(here * 32767.0 + 0.5)
+    mine = turned[pl.ds(pl.multiple_of(here[0, 0] * slab, slab), slab), :]
+    codes = jnp.floor(mine * 32767.0 + 0.5)
     out_ref[0, pl.ds(width + PAD, slab), :] = codes.astype(jnp.int32).astype(jnp.int16)
 
 
-def right_first_kernel(dims, cols, shift, place, v_ref, d_ref, own, *rest):
+def ring_at(spot, groups):
+    return jnp.where(spot * 2 < groups, 2 * spot, 2 * (groups - 1 - spot) + 1)
+
+
+def ring_spot(col, groups):
+    half = jnp.right_shift(col, 1)
+    return jnp.where(jnp.bitwise_and(col, 1) == 0, half, groups - 1 - half)
+
+
+def right_first_kernel(dims, groups, owners, masks, cols, shift, place, v_ref, d_ref, own, *rest):
     nblk, fill, blk, per = dims
     shards, (w_ref, u_ref, tiles_ref, halves, turned, tiles) = rest[:-6], rest[-6:]
     step = pl.program_id(0)
@@ -91,14 +99,21 @@
     def _():
         for b in range(nblk):
             split_into(halves, b, v_ref[:, b * blk : (b + 1) * blk])
-        tiles[pl.ds(pl.multiple_of(place[0, 0] * size, size), size), :] = own[...]
+        root, col = place[0, 0], place[0, 1]
+        tiles[pl.ds(pl.multiple_of(col * size, size), size), :] = own[...]
+        spot = ring_spot(col, groups)
+        bases = [
+            ring_at(lax.rem(spot + (owner + groups), groups), groups) * size
+            + jnp.bitwise_xor(root, mask) * shards[0].shape[1]
+            for owner in owners
+            for mask in masks
+        ]
 
         @pl.loop(0, size // blk)
         def _(b):
             for k, shard in enumerate(shards):
                 share = shard.shape[1]
-                base = place[0, 1 + k] * size + place[1, 1 + k] * share
-                at = pl.multiple_of(base + b * blk, share)
+                at = pl.multiple_of(bases[k] + b * blk, share)
                 tiles[pl.ds(at, share), :] = shard[b]
 
     here_tiles = tiles.at[pl.ds(pl.multiple_of(step * size, size), size), :]
@@ -147,7 +162,7 @@
         outs[t][...] = 0.5 * (moved + (d_ref[:, lanes] - shift[0, 0]) * here) - v_ref[:, lanes]
 
 
-def left_second_kernel(dims, chunk, cols, shift, far, tu_ref, tail_ref, y_ref, tiles, *rest):
+def left_second_kernel(dims, chunk, masks, cols, shift, place, tu_ref, tail_ref, y_ref, tiles, *rest):
     nblk, fill, blk, per = dims
     slabs, (_, out, halves, turned) = rest[:-4], rest[-4:]
     step = pl.program_id(0)
@@ -162,7 +177,7 @@
 
     for m, slab in enumerate(slabs):
         height = slab.shape[1]
-        at = pl.multiple_of(far[0, m] * height, height)
+        at = pl.multiple_of(jnp.bitwise_xor(place[0, 0], masks[m]) * height, height)
         turned[pl.ds(at, height), :] = slab[0].astype(jnp.int32).astype(jnp.float32)
     done = []
     for t in range(per):
@@ -255,16 +270,13 @@
         bit //= 2
     far = jnp.bitwise_xor(root, jnp.array(masks, jnp.int32))
     weights = rotation[root][far].reshape(1, -1)
-    far = far.reshape(1, -1)
+    place = jnp.stack([root, lax.axis_index("col")]).astype(jnp.int32).reshape(1, 2)
 
     ring = list(range(0, groups, 2)) + list(range(1, groups, 2))[::-1]
-    spot = jnp.array([ring.index(c) for c in range(groups)], jnp.int32)[lax.axis_index("col")]
     share = blk // roots
-    owners = [0]
+    owners = []
     for hop in range(1, groups // 2 + 1):
-        owners += [-hop] * roots + ([hop] * roots if 2 * hop < groups else [])
-    place = jnp.array(ring, jnp.int32)[(spot + jnp.array(owners, jnp.int32)) % groups]
-    place = jnp.stack([place, jnp.concatenate([far[0, :1]] + [far[0]] * (groups - 1))])
+        owners += [-hop, hop] if 2 * hop < groups else [-hop]
 
     slab = width // roots
     height = width + PAD + slab
@@ -273,13 +285,13 @@
         return call(
             pack_kernel,
             groups,
-            [smem(), smem(), piece, piece],
+            [smem(), piece, piece],
             pl.BlockSpec((1, height, rows), lambda q: (q, 0, 0)),
             jax.ShapeDtypeStruct((groups, height, rows), i16),
             [pltpu.VMEM((width, rows), f32)],
             0,
             size * 3,
-        )(block_cols, place, start, diagonal)
+        )(place, start, diagonal)
 
     own = jnp.swapaxes(string_blocks.reshape(-1, blk, blk), 1, 2)
     mine = lax.dynamic_slice_in_dim(own, root * share, share, 1)
@@ -295,13 +307,13 @@
             crossed.append(shards[1 - roots])
         if hop == 1:
             tv = pack(*lax.optimization_barrier((start, diagonal, forth, back))[:2])
-    tv = swap(lax.optimization_barrier((tv, forth, back, *crossed[2:4]))[0])
+    tv = swap(lax.optimization_barrier((tv, forth, back))[0])
     own = own.reshape(string_blocks.shape)
 
     once = pl.Buffered(1)
     shard_spec = pl.BlockSpec(mine.shape, lambda q: (0, 0, 0), pipeline_mode=once)
     w, tu, tiles = call(
-        functools.partial(right_first_kernel, dims),
+        functools.partial(right_first_kernel, dims, groups, owners, masks),
         groups,
         [smem(), smem(), smem(), whole, piece]
         + [pl.BlockSpec(string_blocks.shape, lambda q: (0, 0), pipeline_mode=once)]
@@ -352,7 +364,7 @@
     seconds = []
     for k in range(chunks):
         z = call(
-            functools.partial(left_second_kernel, dims, k),
+            functools.partial(left_second_kernel, dims, k, masks),
             groups,
             [
                 smem(),
@@ -368,9 +380,9 @@
             chunk_coded,
             jax.ShapeDtypeStruct((groups, rows + PAD, part), i16),
             [pltpu.VMEM((nblk, 2 * part, blk), jnp.bfloat16), pltpu.VMEM((width, rows), f32)],
-            work // chunks,
-            size * 4 // chunks,
-        )(block_cols, energy, far, tu, tu, y, tiles, *slabs, base[0] if k < 2 else seconds[k - 2])
+            work // chunks if k < 2 else 1,
+            size * 4 // chunks if k < 2 else 1,
+        )(block_cols, energy, place, tu, tu, y, tiles, *slabs, base[0] if k < 2 else seconds[k - 2])
         second = call(
             second_kernel,
             groups // many,
@@ -379,7 +391,7 @@
             jax.ShapeDtypeStruct((groups, rows + PAD, part), i16),
             [],
             0,
-            size * 2 // chunks,
+            1,
         )(weights, swap(z), base[k])
         seconds.append(second)
     out = []
@@ -395,7 +407,7 @@
                 jax.ShapeDtypeStruct((1, rows, strings), f32),
                 [],
                 0,
-                size * 3 // chunks,
+                1,
                 {1: 0} if out else {},
             )(weights, *out, *exchange(seconds[k], late))
         ]

time: 312 us -> 307 us (0.984)
  local copies, waits for them, and re-layouts: 20 us -> 15 us
  waiting for transfers between devices: 104 us -> 108 us
    all_to_all x5, waiting for transfers between devices: 45.3 us -> 34.3 us  [swap(): lax.all_to_all(pieces, 'col', split_axis=0, concat_axis=0, tiled=True)]
    ppermute x7, waiting for transfers between devices: 6.47 us -> 15.3 us  [blocked_shards(): moved = lax.ppermute(forth if way == 1 else back, 'col', pairs)]
    ppermute x33, waiting for transfers between devices: 52.5 us -> 58.9 us  [exchange(): have = have + [lax.ppermute(h, 'root', pairs) for h in have]]
    unnamed x72 -> x76, local copies, waits for them, and re-layouts: 11.1 us -> 8.85 us
  transfers between devices with their start and end apart: 45 -> 45, of which waited for: 18 -> 18; matrix products, arithmetic and copies ran while one was open for 4% -> 2% of each run, Pallas kernels for 37% -> 38%
where the time goes in v6:
time: 307 us; the launch traced here: 305 us
  Pallas kernels  133 us (43%)
  waiting for transfers between devices  108 us (35%)
  starting transfers between devices  47.2 us (15%)
  local copies, waits for them, and re-layouts  15 us (5%)
    ppermute x33, waiting for transfers between devices, exchange(): have = have + [lax.ppermute(h, 'root', pairs) for h in have]  58.9 us
    pallas_call x3, Pallas kernels, blocked_shards(): call(functools.partial(left_second_kernel, dims, k, masks), groups, [smem...  35 us
    all_to_all x5, waiting for transfers between devices, swap(): lax.all_to_all(pieces, 'col', split_axis=0, concat_axis=0, tiled=True)  34.3 us
    pallas_call x1, Pallas kernels, blocked_shards(): call(functools.partial(right_first_kernel, dims, groups, owners, masks),...  25.1 us
    all_to_all x5, starting transfers between devices, swap(): lax.all_to_all(pieces, 'col', split_axis=0, concat_axis=0, tiled=True)  20.3 us
    pallas_call x3, Pallas kernels, blocked_shards(): call(functools.partial(rotate_kernel, len(out)), groups, [smem()] + [pl.B...  19.1 us
    pallas_call x1, Pallas kernels, blocked_shards(): call(functools.partial(right_second_kernel, dims), groups, [smem(), smem(...  19.1 us
    ppermute x33, starting transfers between devices, exchange(): have = have + [lax.ppermute(h, 'root', pairs) for h in have]  18.2 us
  transfers between devices with their start and end apart: 45, of which 18 were waited for; matrix products, arithmetic and copies ran while one was open for 2% of the time, Pallas kernels for 38%

profile of v6, /device:TPU:0, one launch (start us, length us, event | category | flops | bytes accessed | tf_op | source)
XLA Modules:
  0.0 305.3 jit_solution(6077912691447884856)
XLA Ops:
  0.0 1.6 constant_dynamic-slice_fusion
  1.9 3.0 collective-permute-start.4
  5.1 5.9 %collective-permute-done.4.rest_4_ = bf16[30,32,128]{2,1,0:T(8,128)(2,1)S(1)} collective-permute-done((bf16[30,32,128]{2,1,0:T(8,128)(2,1)S(1)}, bf16[30,32,128]{2,1,0:T(8,128)(2,1)S(1)}, u32[]{:S(2)}, u32[]{:S(2)}) %collective-permute-start.4) | collective-permute-done | bytes 245792 | tf_op jit(solution)/shard_map/ppermute | solution.py:304
  11.0 1.7 collective-permute-start.12
  13.0 1.7 collective-permute-start.1
  15.7 8.8 %shard_map.73 = s16[8,496,384]{2,1,0:T(8,128)(2,1)} custom-call(s32[1,2]{1,0:T(1,128)} %add_bitcast_fusion.here.place, f32[384,3072]{1,0:T(8,128)} %bitcast.19, f32[384,3072]{1,0:T(8,128)} %d_ref.4), custom_call_target="tpu_custom_call" | custom-call | bytes 14155776 | tf_op jit(solution)/shard_map/pallas_call | solution.py:285
  24.8 1.5 collective-permute-start.16
  26.9 4.8 %collective-permute-done.16.rest_16_ = bf16[30,32,128]{2,1,0:T(8,128)(2,1)S(1)} collective-permute-done((bf16[30,32,128]{2,1,0:T(8,128)(2,1)S(1)}, bf16[30,32,128]{2,1,0:T(8,128)(2,1)S(1)}, u32[]{:S(2)}, u32[]{:S(2)}) %collective-permute-start.16) | collective-permute-done | bytes 245792 | tf_op jit(solution)/shard_map/ppermute | solution.py:304
  31.6 1.5 collective-permute-start.24
  33.2 4.7 %collective-permute-done.24.rest_24_ = bf16[30,32,128]{2,1,0:T(8,128)(2,1)S(1)} collective-permute-done((bf16[30,32,128]{2,1,0:T(8,128)(2,1)S(1)}, bf16[30,32,128]{2,1,0:T(8,128)(2,1)S(1)}, u32[]{:S(2)}, u32[]{:S(2)}) %collective-permute-start.24) | collective-permute-done | bytes 245792 | tf_op jit(solution)/shard_map/ppermute | solution.py:304
  38.5 5.8 %all-to-all-start.1 = ((s16[8,496,384]{2,1,0:T(8,128)(2,1)}), s16[8,496,384]{2,1,0:T(8,128)(2,1)S(1)}, u32[]{:S(2)}, u32[]{:S(2)}) async-start(s16[8,496,384]{2,1,0:T(8,128)(2,1)} %shard_map.73), calls=%async_computation.1 | async-start | bytes 6094848 | tf_op jit(solution)/shard_map/all_to_all | solution.py:242
  44.9 1.5 collective-permute-start.9
  48.3 5.6 %collective-permute-done.9.rest_9_ = bf16[30,32,128]{2,1,0:T(8,128)(2,1)S(1)} collective-permute-done((bf16[30,32,128]{2,1,0:T(8,128)(2,1)}, bf16[30,32,128]{2,1,0:T(8,128)(2,1)S(1)}, u32[]{:S(2)}, u32[]{:S(2)}) %collective-permute-start.9) | collective-permute-done | bytes 245792 | tf_op jit(solution)/shard_map/ppermute | solution.py:260
  53.9 4.5 %collective-permute-done.13.rest_13_ = bf16[30,32,128]{2,1,0:T(8,128)(2,1)} collective-permute-done((bf16[30,32,128]{2,1,0:T(8,128)(2,1)}, bf16[30,32,128]{2,1,0:T(8,128)(2,1)}, u32[]{:S(2)}, u32[]{:S(2)}) %collective-permute-start.13) | collective-permute-done | bytes 245792 | tf_op jit(solution)/shard_map/ppermute | solution.py:260
  58.4 1.5 collective-permute-start.17
  61.1 6.5 %collective-permute-done.17.rest_17_ = bf16[30,32,128]{2,1,0:T(8,128)(2,1)} collective-permute-done((bf16[30,32,128]{2,1,0:T(8,128)(2,1)}, bf16[30,32,128]{2,1,0:T(8,128)(2,1)}, u32[]{:S(2)}, u32[]{:S(2)}) %collective-permute-start.17) | collective-permute-done | bytes 245792 | tf_op jit(solution)/shard_map/ppermute | solution.py:260
  67.6 1.5 collective-permute-start.25
  69.1 3.8 %collective-permute-done.21.rest_21_ = bf16[30,32,128]{2,1,0:T(8,128)(2,1)} collective-permute-done((bf16[30,32,128]{2,1,0:T(8,128)(2,1)}, bf16[30,32,128]{2,1,0:T(8,128)(2,1)}, u32[]{:S(2)}, u32[]{:S(2)}) %collective-permute-start.21) | collective-permute-done | bytes 245792 | tf_op jit(solution)/shard_map/ppermute | solution.py:260
  74.0 2.4 collective-permute-done.25.rest_25_
  77.8 2.3 copy.16
  80.2 25.1 %shard_map.74 = (f32[384,3072]{1,0:T(8,128)}, s16[8,400,384]{2,1,0:T(8,128)(2,1)}, bf16[30720,128]{1,0:T(8,128)(2,1)}) custom-call(s32[24,10]{1,0:T(8,128)} %copy.21.cols, f32[1,1]{1,0:T(1,128)} %bitcast.14.shift, s32[1,2]{1,0:T(1,128)} %add_bitcast_fusion.here.place, f32[384,3072]{1,0:T(8,128)} %bitcast.20, f32[384,3072]{1,0:T(8,128)} %d_ref.4, ...), custom_call_target="tpu_custom_call" | custom-call | flops 6039797760 | bytes 28311552 | tf_op jit(solution)/shard_map/pallas_call | solution.py:315
  105.2 3.7 %all-to-all-done.1.tv_ref = s16[8,496,384]{2,1,0:T(8,128)(2,1)S(1)} async-done(((s16[8,496,384]{2,1,0:T(8,128)(2,1)}), s16[8,496,384]{2,1,0:T(8,128)(2,1)S(1)}, u32[]{:S(2)}, u32[]{:S(2)}) %all-to-all-start.1) | async-done | bytes 3047456 | tf_op jit(solution)/shard_map/all_to_all | solution.py:242
  108.9 1.7 copy-done.4
  110.6 3.8 %all-to-all-start = ((s16[8,400,384]{2,1,0:T(8,128)(2,1)}), s16[8,400,384]{2,1,0:T(8,128)(2,1)S(1)}, u32[]{:S(2)}, u32[]{:S(2)}) async-start(s16[8,400,384]{2,1,0:T(8,128)(2,1)} %get-tuple-element.28), calls=%async_computation | async-start | bytes 4915200 | tf_op jit(solution)/shard_map/all_to_all | solution.py:242
  115.5 1.6 collective-permute-start.28
  117.1 17.6 %shard_map.75.y_ref = f32[384,3072]{1,0:T(8,128)} custom-call(s32[24,10]{1,0:T(8,128)} %copy.21.cols, s16[8,496,384]{2,1,0:T(8,128)(2,1)} %copy-done.4, bf16[30720,128]{1,0:T(8,128)(2,1)} %get-tuple-element.30.tiles), custom_call_target="tpu_custom_call" | custom-call | flops 6039797760 | bytes 14155776 | tf_op jit(solution)/shard_map/pallas_call | solution.py:348
  135.3 19.1 %shard_map.76 = (f32[384,1024]{1,0:T(8,128)}, f32[384,1024]{1,0:T(8,128)}, f32[384,1024]{1,0:T(8,128)}) custom-call(s32[24,10]{1,0:T(8,128)} %copy.21.cols, f32[1,1]{1,0:T(1,128)} %bitcast.15.shift, f32[384,3072]{1,0:T(8,128)} %get-tuple-element.33.w_ref, f32[384,3072]{1,0:T(8,128)} %bitcast.21, f32[384,3072]{1,0:T(8,128)} %d_ref.4, ...), custom_call_target="tpu_custom_call" | custom-call | flops 6039797760 | bytes 23592960 | tf_op jit(solution)/shard_map/pallas_call | solution.py:337
  154.4 15.9 %all-to-all-done.tu_ref.tail_ref = s16[8,400,384]{2,1,0:T(8,128)(2,1)S(1)} async-done(((s16[8,400,384]{2,1,0:T(8,128)(2,1)}), s16[8,400,384]{2,1,0:T(8,128)(2,1)S(1)}, u32[]{:S(2)}, u32[]{:S(2)}) %all-to-all-start) | async-done | bytes 2457632 | tf_op jit(solution)/shard_map/all_to_all | solution.py:242
  171.7 11.6 %shard_map.77 = s16[8,400,128]{2,1,0:T(8,128)(2,1)} custom-call(s32[24,10]{1,0:T(8,128)} %copy.21.cols, f32[1,1]{1,0:T(1,128)} %bitcast.16.shift, s32[1,2]{1,0:T(1,128)} %add_bitcast_fusion.here.place, s16[8,400,384]{2,1,0:T(8,128)(2,1)} %copy-done.1, s16[8,400,384]{2,1,0:T(8,128)(2,1)} %copy-done.1, f32[384,3072]{1,0:T(8,128)} %shard_map.75.y_ref, ...), custom_call_target="tpu_custom_call" | custom-call | flops 2013265920 | bytes 6291456 | tf_op jit(solution)/shard_map/pallas_call | solution.py:366
  183.3 3.5 %all-to-all-start.2 = ((s16[8,400,128]{2,1,0:T(8,128)(2,1)}), s16[8,400,128]{2,1,0:T(8,128)(2,1)S(1)}, u32[]{:S(2)}, u32[]{:S(2)}) async-start(s16[8,400,128]{2,1,0:T(8,128)(2,1)} %shard_map.77), calls=%async_computation.2 | async-start | bytes 1638400 | tf_op jit(solution)/shard_map/all_to_all | solution.py:242
  186.9 11.6 %shard_map.79 = s16[8,400,128]{2,1,0:T(8,128)(2,1)} custom-call(s32[24,10]{1,0:T(8,128)} %copy.21.cols, f32[1,1]{1,0:T(1,128)} %bitcast.17.shift, s32[1,2]{1,0:T(1,128)} %add_bitcast_fusion.here.place, s16[8,400,384]{2,1,0:T(8,128)(2,1)} %copy-done.1, s16[8,400,384]{2,1,0:T(8,128)(2,1)} %copy-done.1, f32[384,3072]{1,0:T(8,128)} %shard_map.75.y_ref, ...), custom_call_target="tpu_custom_call" | custom-call | flops 2013265920 | bytes 6291456 | tf_op jit(solution)/shard_map/pallas_call | solution.py:366
  198.5 9.4 %all-to-all-done.2.z_ref = s16[8,400,128]{2,1,0:T(8,128)(2,1)S(1)} async-done(((s16[8,400,128]{2,1,0:T(8,128)(2,1)}), s16[8,400,128]{2,1,0:T(8,128)(2,1)S(1)}, u32[]{:S(2)}, u32[]{:S(2)}) %all-to-all-start.2) | async-done | bytes 819232 | tf_op jit(solution)/shard_map/all_to_all | solution.py:242
  207.9 3.6 %all-to-all-start.3 = ((s16[8,400,128]{2,1,0:T(8,128)(2,1)}), s16[8,400,128]{2,1,0:T(8,128)(2,1)S(1)}, u32[]{:S(2)}, u32[]{:S(2)}) async-start(s16[8,400,128]{2,1,0:T(8,128)(2,1)} %shard_map.79), calls=%async_computation.3 | async-start | bytes 1638400 | tf_op jit(solution)/shard_map/all_to_all | solution.py:242
  212.7 2.8 shard_map.78.refs_0_.rest_4_
  215.5 11.7 %shard_map.82 = s16[8,400,128]{2,1,0:T(8,128)(2,1)} custom-call(s32[24,10]{1,0:T(8,128)} %copy.21.cols, f32[1,1]{1,0:T(1,128)} %bitcast.18.shift, s32[1,2]{1,0:T(1,128)} %add_bitcast_fusion.here.place, s16[8,400,384]{2,1,0:T(8,128)(2,1)} %copy-done.1, s16[8,400,384]{2,1,0:T(8,128)(2,1)} %copy-done.1, f32[384,3072]{1,0:T(8,128)} %shard_map.75.y_ref, ...), custom_call_target="tpu_custom_call" | custom-call | flops 1 | bytes 1 | tf_op jit(solution)/shard_map/pallas_call | solution.py:366
  227.2 5.3 %all-to-all-done.3.z_ref = s16[8,400,128]{2,1,0:T(8,128)(2,1)S(1)} async-done(((s16[8,400,128]{2,1,0:T(8,128)(2,1)}), s16[8,400,128]{2,1,0:T(8,128)(2,1)S(1)}, u32[]{:S(2)}, u32[]{:S(2)}) %all-to-all-start.3) | async-done | bytes 819232 | tf_op jit(solution)/shard_map/all_to_all | solution.py:242
  232.5 3.6 %all-to-all-start.4 = ((s16[8,400,128]{2,1,0:T(8,128)(2,1)}), s16[8,400,128]{2,1,0:T(8,128)(2,1)S(1)}, u32[]{:S(2)}, u32[]{:S(2)}) async-start(s16[8,400,128]{2,1,0:T(8,128)(2,1)} %shard_map.82), calls=%async_computation.4 | async-start | bytes 1638400 | tf_op jit(solution)/shard_map/all_to_all | solution.py:242
  236.1 1.6 collective-permute-start.31
  237.7 2.8 shard_map.80.refs_1_
  241.0 16.4 %collective-permute-done.31.refs_1_ = s16[8,400,128]{2,1,0:T(8,128)(2,1)S(1)} collective-permute-done((s16[8,400,128]{2,1,0:T(8,128)(2,1)S(1)}, s16[8,400,128]{2,1,0:T(8,128)(2,1)S(1)}, u32[]{:S(2)}, u32[]{:S(2)}) %collective-permute-start.31) | collective-permute-done | bytes 819232 | tf_op jit(solution)/shard_map/ppermute | solution.py:260
  258.7 2.8 shard_map.83.refs_1_
  261.5 12.1 %collective-permute-done.34.refs_2_ = s16[8,400,128]{2,1,0:T(8,128)(2,1)S(1)} collective-permute-done((s16[8,400,128]{2,1,0:T(8,128)(2,1)}, s16[8,400,128]{2,1,0:T(8,128)(2,1)S(1)}, u32[]{:S(2)}, u32[]{:S(2)}) %collective-permute-start.34) | collective-permute-done | bytes 819232 | tf_op jit(solution)/shard_map/ppermute | solution.py:260
  274.1 1.5 collective-permute-start.37
  275.6 6.4 %shard_map.81.refs_0_ = f32[1,384,3072]{2,1,0:T(8,128)} custom-call(f32[1,4]{1,0:T(1,128)} %bitcast.30, s16[8,400,128]{2,1,0:T(8,128)(2,1)} %shard_map.78.refs_0_.rest_4_, s16[8,400,128]{2,1,0:T(8,128)(2,1)} %copy-done.15, s16[8,400,128]{2,1,0:T(8,128)(2,1)} %collective-permute-done.32.refs_2_, s16[8,400,128]{2,1,0:T(8,128)(2,1)} %collective-permute-done.33.refs_3_), custom_call_target="tpu_custom_call" | custom-call | bytes 1 | tf_op jit(solution)/shard_map/pallas_call | solution.py:402
  283.8 6.4 %shard_map.84.refs_0_ = f32[1,384,3072]{2,1,0:T(8,128)} custom-call(f32[1,4]{1,0:T(1,128)} %bitcast.31, f32[1,384,3072]{2,1,0:T(8,128)} %shard_map.81.refs_0_, s16[8,400,128]{2,1,0:T(8,128)(2,1)} %shard_map.80.refs_1_, s16[8,400,128]{2,1,0:T(8,128)(2,1)} %copy-done.9, s16[8,400,128]{2,1,0:T(8,128)(2,1)} %copy-done.11, ...), custom_call_target="tpu_custom_call", output_to_operand_aliasing={{}: (1, {})} | custom-call | bytes 1 | tf_op jit(solution)/shard_map/pallas_call | solution.py:402
  290.2 4.3 %collective-permute-done.37.refs_2_ = s16[8,400,128]{2,1,0:T(8,128)(2,1)S(1)} collective-permute-done((s16[8,400,128]{2,1,0:T(8,128)(2,1)}, s16[8,400,128]{2,1,0:T(8,128)(2,1)S(1)}, u32[]{:S(2)}, u32[]{:S(2)}) %collective-permute-start.37) | collective-permute-done | bytes 819232 | tf_op jit(solution)/shard_map/ppermute | solution.py:260
  295.0 1.8 collective-permute-done.38.refs_3_
  298.9 6.4 %shard_map.85 = f32[1,384,3072]{2,1,0:T(8,128)} custom-call(f32[1,4]{1,0:T(1,128)} %bitcast.32, f32[1,384,3072]{2,1,0:T(8,128)} %shard_map.84.refs_0_, s16[8,400,128]{2,1,0:T(8,128)(2,1)} %shard_map.83.refs_1_, s16[8,400,128]{2,1,0:T(8,128)(2,1)} %copy-done.10, s16[8,400,128]{2,1,0:T(8,128)(2,1)} %copy-done.13, ...), custom_call_target="tpu_custom_call", output_to_operand_aliasing={{}: (1, {})} | custom-call | bytes 1 | tf_op jit(solution)/shard_map/pallas_call | solution.py:402
  (139 shorter events, 20.2 us)
Async XLA Ops:
  0.0 211.5 %copy-start = (f32[4,4]{1,0:T(4,128)S(1)}, f32[4,4]{1,0:T(4,128)}, u32[]{:S(2)}) copy-start(f32[4,4]{1,0:T(4,128)} %param.10) | copy-start | bytes 196
  1.9 9.0 %collective-permute-start.4 = (bf16[30,32,128]{2,1,0:T(8,128)(2,1)S(1)}, bf16[30,32,128]{2,1,0:T(8,128)(2,1)S(1)}, u32[]{:S(2)}, u32[]{:S(2)}) collective-permute-start(bf16[30,32,128]{2,1,0:T(8,128)(2,1)S(1)} %bitcast.25), channel_id=1, source_target_pairs={{0,1},{2,0},{4,2},{6,4},{7,6},{5,7},{3,5},{1,3},{8,9},{10,8},{12,1... | collective-permute-start | bytes 737288 | tf_op jit(solution)/shard_map/ppermute | solution.py:304
  5.0 7.7 %collective-permute-start = (bf16[30,32,128]{2,1,0:T(8,128)(2,1)S(1)}, bf16[30,32,128]{2,1,0:T(8,128)(2,1)S(1)}, u32[]{:S(2)}, u32[]{:S(2)}) collective-permute-start(bf16[30,32,128]{2,1,0:T(8,128)(2,1)S(1)} %bitcast.26), channel_id=1, source_target_pairs={{0,2},{2,4},{4,6},{6,7},{7,5},{5,3},{3,1},{1,0},{8,10},{10,12},{12... | collective-permute-start | bytes 737288 | tf_op jit(solution)/shard_map/ppermute | solution.py:304
  11.0 33.4 %copy-start.17 = (bf16[30,32,128]{2,1,0:T(8,128)(2,1)}, bf16[30,32,128]{2,1,0:T(8,128)(2,1)S(1)}, u32[]{:S(2)}) copy-start(bf16[30,32,128]{2,1,0:T(8,128)(2,1)S(1)} %collective-permute-done.4.rest_4_) | copy-start | bytes 737284
  11.0 13.5 %collective-permute-start.12 = (bf16[30,32,128]{2,1,0:T(8,128)(2,1)S(1)}, bf16[30,32,128]{2,1,0:T(8,128)(2,1)S(1)}, u32[]{:S(2)}, u32[]{:S(2)}) collective-permute-start(bf16[30,32,128]{2,1,0:T(8,128)(2,1)S(1)} %collective-permute-done.4.rest_4_), channel_id=1, source_target_pairs={{0,1},{2,0},{4,2},{6,4},{7,6},{5,7},{3,5},{1,3},{8,9},{10,8},{12,1... | collective-permute-start | bytes 737288 | tf_op jit(solution)/shard_map/ppermute | solution.py:304
  12.7 11.8 %collective-permute-start.8 = (bf16[30,32,128]{2,1,0:T(8,128)(2,1)S(1)}, bf16[30,32,128]{2,1,0:T(8,128)(2,1)S(1)}, u32[]{:S(2)}, u32[]{:S(2)}) collective-permute-start(bf16[30,32,128]{2,1,0:T(8,128)(2,1)S(1)} %collective-permute-done.rest_0_), channel_id=1, source_target_pairs={{0,2},{2,4},{4,6},{6,7},{7,5},{5,3},{3,1},{1,0},{8,10},{10,12},{12... | collective-permute-start | bytes 737288 | tf_op jit(solution)/shard_map/ppermute | solution.py:304
  13.0 11.5 %collective-permute-start.1 = (bf16[30,32,128]{2,1,0:T(8,128)(2,1)S(1)}, bf16[30,32,128]{2,1,0:T(8,128)(2,1)S(1)}, u32[]{:S(2)}, u32[]{:S(2)}) collective-permute-start(bf16[30,32,128]{2,1,0:T(8,128)(2,1)S(1)} %collective-permute-done.rest_0_), channel_id=1, source_target_pairs={{0,16},{8,24},{16,0},{24,8},{1,17},{9,25},{17,1},{25,9},{2,18},{10... | collective-permute-start | bytes 737288 | tf_op jit(solution)/shard_map/ppermute | solution.py:260
  14.7 10.2 %collective-permute-start.5 = (bf16[30,32,128]{2,1,0:T(8,128)(2,1)S(1)}, bf16[30,32,128]{2,1,0:T(8,128)(2,1)S(1)}, u32[]{:S(2)}, u32[]{:S(2)}) collective-permute-start(bf16[30,32,128]{2,1,0:T(8,128)(2,1)S(1)} %collective-permute-done.4.rest_4_), channel_id=1, source_target_pairs={{0,16},{8,24},{16,0},{24,8},{1,17},{9,25},{17,1},{25,9},{2,18},{10... | collective-permute-start | bytes 737288 | tf_op jit(solution)/shard_map/ppermute | solution.py:260
  24.5 52.0 %copy-start.16 = (s32[24,10]{0,1:T(8,128)S(1)}, s32[24,10]{0,1:T(8,128)}, u32[]{:S(2)}) copy-start(s32[24,10]{0,1:T(8,128)} %param.12) | copy-start | bytes 2884
  24.8 6.8 %collective-permute-start.16 = (bf16[30,32,128]{2,1,0:T(8,128)(2,1)S(1)}, bf16[30,32,128]{2,1,0:T(8,128)(2,1)S(1)}, u32[]{:S(2)}, u32[]{:S(2)}) collective-permute-start(bf16[30,32,128]{2,1,0:T(8,128)(2,1)S(1)} %collective-permute-done.8.rest_8_), channel_id=1, source_target_pairs={{0,2},{2,4},{4,6},{6,7},{7,5},{5,3},{3,1},{1,0},{8,10},{10,12},{12... | collective-permute-start | bytes 737288 | tf_op jit(solution)/shard_map/ppermute | solution.py:304
  26.3 6.8 %collective-permute-start.20 = (bf16[30,32,128]{2,1,0:T(8,128)(2,1)S(1)}, bf16[30,32,128]{2,1,0:T(8,128)(2,1)S(1)}, u32[]{:S(2)}, u32[]{:S(2)}) collective-permute-start(bf16[30,32,128]{2,1,0:T(8,128)(2,1)S(1)} %collective-permute-done.12.rest_12_), channel_id=1, source_target_pairs={{0,1},{2,0},{4,2},{6,4},{7,6},{5,7},{3,5},{1,3},{8,9},{10,8},{12,1... | collective-permute-start | bytes 737288 | tf_op jit(solution)/shard_map/ppermute | solution.py:304
  31.6 6.2 %collective-permute-start.24 = (bf16[30,32,128]{2,1,0:T(8,128)(2,1)S(1)}, bf16[30,32,128]{2,1,0:T(8,128)(2,1)S(1)}, u32[]{:S(2)}, u32[]{:S(2)}) collective-permute-start(bf16[30,32,128]{2,1,0:T(8,128)(2,1)S(1)} %collective-permute-done.16.rest_16_), channel_id=1, source_target_pairs={{0,2},{2,4},{4,6},{6,7},{7,5},{5,3},{3,1},{1,0},{8,10},{10,12},{12... | collective-permute-start | bytes 737288 | tf_op jit(solution)/shard_map/ppermute | solution.py:304
  38.5 70.4 %all-to-all-start.1 = ((s16[8,496,384]{2,1,0:T(8,128)(2,1)}), s16[8,496,384]{2,1,0:T(8,128)(2,1)S(1)}, u32[]{:S(2)}, u32[]{:S(2)}) async-start(s16[8,496,384]{2,1,0:T(8,128)(2,1)} %shard_map.73), calls=%async_computation.1 | async-start | bytes 6094848 | tf_op jit(solution)/shard_map/all_to_all | solution.py:242
  44.3 2.6 collective-permute-start.2
  44.4 3.0 collective-permute-start.6
  44.9 9.0 %collective-permute-start.9 = (bf16[30,32,128]{2,1,0:T(8,128)(2,1)}, bf16[30,32,128]{2,1,0:T(8,128)(2,1)S(1)}, u32[]{:S(2)}, u32[]{:S(2)}) collective-permute-start(bf16[30,32,128]{2,1,0:T(8,128)(2,1)} %copy-done.20), channel_id=1, source_target_pairs={{0,16},{8,24},{16,0},{24,8},{1,17},{9,25},{17,1},{25,9},{2,18},{10... | collective-permute-start | bytes 737288 | tf_op jit(solution)/shard_map/ppermute | solution.py:260
  46.4 12.0 %collective-permute-start.13 = (bf16[30,32,128]{2,1,0:T(8,128)(2,1)}, bf16[30,32,128]{2,1,0:T(8,128)(2,1)}, u32[]{:S(2)}, u32[]{:S(2)}) collective-permute-start(bf16[30,32,128]{2,1,0:T(8,128)(2,1)} %copy-done.19), channel_id=1, source_target_pairs={{0,16},{8,24},{16,0},{24,8},{1,17},{9,25},{17,1},{25,9},{2,18},{10... | collective-permute-start | bytes 737288 | tf_op jit(solution)/shard_map/ppermute | solution.py:260
  46.9 13.0 %collective-permute-start.10 = (bf16[30,32,128]{2,1,0:T(8,128)(2,1)}, bf16[30,32,128]{2,1,0:T(8,128)(2,1)S(1)}, u32[]{:S(2)}, u32[]{:S(2)}) collective-permute-start(bf16[30,32,128]{2,1,0:T(8,128)(2,1)} %copy-done.20), channel_id=1, source_target_pairs={{0,8},{8,0},{16,24},{24,16},{1,9},{9,1},{17,25},{25,17},{2,10},{10... | collective-permute-start | bytes 737288 | tf_op jit(solution)/shard_map/ppermute | solution.py:260
  46.9 13.5 %collective-permute-start.14 = (bf16[30,32,128]{2,1,0:T(8,128)(2,1)}, bf16[30,32,128]{2,1,0:T(8,128)(2,1)S(1)}, u32[]{:S(2)}, u32[]{:S(2)}) collective-permute-start(bf16[30,32,128]{2,1,0:T(8,128)(2,1)} %copy-done.19), channel_id=1, source_target_pairs={{0,8},{8,0},{16,24},{24,16},{1,9},{9,1},{17,25},{25,17},{2,10},{10... | collective-permute-start | bytes 737288 | tf_op jit(solution)/shard_map/ppermute | solution.py:260
  47.6 12.8 %collective-permute-start.3 = (bf16[30,32,128]{2,1,0:T(8,128)(2,1)}, bf16[30,32,128]{2,1,0:T(8,128)(2,1)S(1)}, u32[]{:S(2)}, u32[]{:S(2)}) collective-permute-start(bf16[30,32,128]{2,1,0:T(8,128)(2,1)} %copy-done.21), channel_id=1, source_target_pairs={{0,8},{8,0},{16,24},{24,16},{1,9},{9,1},{17,25},{25,17},{2,10},{10... | collective-permute-start | bytes 737288 | tf_op jit(solution)/shard_map/ppermute | solution.py:260
  53.9 7.1 %collective-permute-start.7 = (bf16[30,32,128]{2,1,0:T(8,128)(2,1)}, bf16[30,32,128]{2,1,0:T(8,128)(2,1)S(1)}, u32[]{:S(2)}, u32[]{:S(2)}) collective-permute-start(bf16[30,32,128]{2,1,0:T(8,128)(2,1)} %copy-done.22), channel_id=1, source_target_pairs={{0,8},{8,0},{16,24},{24,16},{1,9},{9,1},{17,25},{25,17},{2,10},{10... | collective-permute-start | bytes 737288 | tf_op jit(solution)/shard_map/ppermute | solution.py:260
  58.4 9.2 %collective-permute-start.17 = (bf16[30,32,128]{2,1,0:T(8,128)(2,1)}, bf16[30,32,128]{2,1,0:T(8,128)(2,1)}, u32[]{:S(2)}, u32[]{:S(2)}) collective-permute-start(bf16[30,32,128]{2,1,0:T(8,128)(2,1)} %copy-done.23), channel_id=1, source_target_pairs={{0,16},{8,24},{16,0},{24,8},{1,17},{9,25},{17,1},{25,9},{2,18},{10... | collective-permute-start | bytes 737288 | tf_op jit(solution)/shard_map/ppermute | solution.py:260
  59.9 13.0 %collective-permute-start.21 = (bf16[30,32,128]{2,1,0:T(8,128)(2,1)}, bf16[30,32,128]{2,1,0:T(8,128)(2,1)}, u32[]{:S(2)}, u32[]{:S(2)}) collective-permute-start(bf16[30,32,128]{2,1,0:T(8,128)(2,1)} %copy-done.24), channel_id=1, source_target_pairs={{0,16},{8,24},{16,0},{24,8},{1,17},{9,25},{17,1},{25,9},{2,18},{10... | collective-permute-start | bytes 737288 | tf_op jit(solution)/shard_map/ppermute | solution.py:260
  60.5 12.4 %collective-permute-start.18 = (bf16[30,32,128]{2,1,0:T(8,128)(2,1)}, bf16[30,32,128]{2,1,0:T(8,128)(2,1)S(1)}, u32[]{:S(2)}, u32[]{:S(2)}) collective-permute-start(bf16[30,32,128]{2,1,0:T(8,128)(2,1)} %copy-done.23), channel_id=1, source_target_pairs={{0,8},{8,0},{16,24},{24,16},{1,9},{9,1},{17,25},{25,17},{2,10},{10... | collective-permute-start | bytes 737288 | tf_op jit(solution)/shard_map/ppermute | solution.py:260
  60.5 12.9 %collective-permute-start.22 = (bf16[30,32,128]{2,1,0:T(8,128)(2,1)}, bf16[30,32,128]{2,1,0:T(8,128)(2,1)S(1)}, u32[]{:S(2)}, u32[]{:S(2)}) collective-permute-start(bf16[30,32,128]{2,1,0:T(8,128)(2,1)} %copy-done.24), channel_id=1, source_target_pairs={{0,8},{8,0},{16,24},{24,16},{1,9},{9,1},{17,25},{25,17},{2,10},{10... | collective-permute-start | bytes 737288 | tf_op jit(solution)/shard_map/ppermute | solution.py:260
  61.0 12.5 %collective-permute-start.11 = (bf16[30,32,128]{2,1,0:T(8,128)(2,1)S(1)}, bf16[30,32,128]{2,1,0:T(8,128)(2,1)S(1)}, u32[]{:S(2)}, u32[]{:S(2)}) collective-permute-start(bf16[30,32,128]{2,1,0:T(8,128)(2,1)S(1)} %collective-permute-done.9.rest_9_), channel_id=1, source_target_pairs={{0,8},{8,0},{16,24},{24,16},{1,9},{9,1},{17,25},{25,17},{2,10},{10... | collective-permute-start | bytes 737288 | tf_op jit(solution)/shard_map/ppermute | solution.py:260
  67.6 8.7 %collective-permute-start.25 = (bf16[30,32,128]{2,1,0:T(8,128)(2,1)}, bf16[30,32,128]{2,1,0:T(8,128)(2,1)}, u32[]{:S(2)}, u32[]{:S(2)}) collective-permute-start(bf16[30,32,128]{2,1,0:T(8,128)(2,1)} %copy-done.25), channel_id=1, source_target_pairs={{0,16},{8,24},{16,0},{24,8},{1,17},{9,25},{17,1},{25,9},{2,18},{10... | collective-permute-start | bytes 737288 | tf_op jit(solution)/shard_map/ppermute | solution.py:260
  72.9 7.2 %collective-permute-start.15 = (bf16[30,32,128]{2,1,0:T(8,128)(2,1)}, bf16[30,32,128]{2,1,0:T(8,128)(2,1)}, u32[]{:S(2)}, u32[]{:S(2)}) collective-permute-start(bf16[30,32,128]{2,1,0:T(8,128)(2,1)} %collective-permute-done.13.rest_13_), channel_id=1, source_target_pairs={{0,8},{8,0},{16,24},{24,16},{1,9},{9,1},{17,25},{25,17},{2,10},{10... | collective-permute-start | bytes 737288 | tf_op jit(solution)/shard_map/ppermute | solution.py:260
  72.9 7.2 %collective-permute-start.26 = (bf16[30,32,128]{2,1,0:T(8,128)(2,1)}, bf16[30,32,128]{2,1,0:T(8,128)(2,1)}, u32[]{:S(2)}, u32[]{:S(2)}) collective-permute-start(bf16[30,32,128]{2,1,0:T(8,128)(2,1)} %copy-done.25), channel_id=1, source_target_pairs={{0,8},{8,0},{16,24},{24,16},{1,9},{9,1},{17,25},{25,17},{2,10},{10... | collective-permute-start | bytes 737288 | tf_op jit(solution)/shard_map/ppermute | solution.py:260
  73.4 6.7 %collective-permute-start.19 = (bf16[30,32,128]{2,1,0:T(8,128)(2,1)}, bf16[30,32,128]{2,1,0:T(8,128)(2,1)}, u32[]{:S(2)}, u32[]{:S(2)}) collective-permute-start(bf16[30,32,128]{2,1,0:T(8,128)(2,1)} %collective-permute-done.17.rest_17_), channel_id=1, source_target_pairs={{0,8},{8,0},{16,24},{24,16},{1,9},{9,1},{17,25},{25,17},{2,10},{10... | collective-permute-start | bytes 737288 | tf_op jit(solution)/shard_map/ppermute | solution.py:260
  73.5 6.6 %collective-permute-start.23 = (bf16[30,32,128]{2,1,0:T(8,128)(2,1)}, bf16[30,32,128]{2,1,0:T(8,128)(2,1)}, u32[]{:S(2)}, u32[]{:S(2)}) collective-permute-start(bf16[30,32,128]{2,1,0:T(8,128)(2,1)} %collective-permute-done.21.rest_21_), channel_id=1, source_target_pairs={{0,8},{8,0},{16,24},{24,16},{1,9},{9,1},{17,25},{25,17},{2,10},{10... | collective-permute-start | bytes 737288 | tf_op jit(solution)/shard_map/ppermute | solution.py:260
  76.4 3.7 %collective-permute-start.27 = (bf16[30,32,128]{2,1,0:T(8,128)(2,1)}, bf16[30,32,128]{2,1,0:T(8,128)(2,1)}, u32[]{:S(2)}, u32[]{:S(2)}) collective-permute-start(bf16[30,32,128]{2,1,0:T(8,128)(2,1)} %collective-permute-done.25.rest_25_), channel_id=1, source_target_pairs={{0,8},{8,0},{16,24},{24,16},{1,9},{9,1},{17,25},{25,17},{2,10},{10... | collective-permute-start | bytes 737288 | tf_op jit(solution)/shard_map/ppermute | solution.py:260
  110.6 59.7 %all-to-all-start = ((s16[8,400,384]{2,1,0:T(8,128)(2,1)}), s16[8,400,384]{2,1,0:T(8,128)(2,1)S(1)}, u32[]{:S(2)}, u32[]{:S(2)}) async-start(s16[8,400,384]{2,1,0:T(8,128)(2,1)} %get-tuple-element.28), calls=%async_computation | async-start | bytes 4915200 | tf_op jit(solution)/shard_map/all_to_all | solution.py:242
  115.5 19.2 %collective-permute-start.28 = (s16[8,96,384]{2,1,0:T(8,128)(2,1)S(1)}, s16[8,96,384]{2,1,0:T(8,128)(2,1)}, u32[]{:S(2)}, u32[]{:S(2)}) collective-permute-start(s16[8,96,384]{2,1,0:T(8,128)(2,1)S(1)} %slice.6.rest_0_), channel_id=1, source_target_pairs={{0,16},{8,24},{16,0},{24,8},{1,17},{9,25},{17,1},{25,9},{2,18},{10... | collective-permute-start | bytes 1769480 | tf_op jit(solution)/shard_map/ppermute | solution.py:260
  134.7 35.5 %collective-permute-start.29 = (s16[8,96,384]{2,1,0:T(8,128)(2,1)S(1)}, s16[8,96,384]{2,1,0:T(8,128)(2,1)}, u32[]{:S(2)}, u32[]{:S(2)}) collective-permute-start(s16[8,96,384]{2,1,0:T(8,128)(2,1)S(1)} %slice.6.rest_0_), channel_id=1, source_target_pairs={{0,8},{8,0},{16,24},{24,16},{1,9},{9,1},{17,25},{25,17},{2,10},{10... | collective-permute-start | bytes 1769480 | tf_op jit(solution)/shard_map/ppermute | solution.py:260
  134.8 35.5 %collective-permute-start.30 = (s16[8,96,384]{2,1,0:T(8,128)(2,1)}, s16[8,96,384]{2,1,0:T(8,128)(2,1)}, u32[]{:S(2)}, u32[]{:S(2)}) collective-permute-start(s16[8,96,384]{2,1,0:T(8,128)(2,1)} %collective-permute-done.28.rest_1_), channel_id=1, source_target_pairs={{0,8},{8,0},{16,24},{24,16},{1,9},{9,1},{17,25},{25,17},{2,10},{10... | collective-permute-start | bytes 1769480 | tf_op jit(solution)/shard_map/ppermute | solution.py:260
  183.3 24.6 %all-to-all-start.2 = ((s16[8,400,128]{2,1,0:T(8,128)(2,1)}), s16[8,400,128]{2,1,0:T(8,128)(2,1)S(1)}, u32[]{:S(2)}, u32[]{:S(2)}) async-start(s16[8,400,128]{2,1,0:T(8,128)(2,1)} %shard_map.77), calls=%async_computation.2 | async-start | bytes 1638400 | tf_op jit(solution)/shard_map/all_to_all | solution.py:242
  207.9 24.6 %all-to-all-start.3 = ((s16[8,400,128]{2,1,0:T(8,128)(2,1)}), s16[8,400,128]{2,1,0:T(8,128)(2,1)S(1)}, u32[]{:S(2)}, u32[]{:S(2)}) async-start(s16[8,400,128]{2,1,0:T(8,128)(2,1)} %shard_map.79), calls=%async_computation.3 | async-start | bytes 1638400 | tf_op jit(solution)/shard_map/all_to_all | solution.py:242
  232.5 25.3 %all-to-all-start.4 = ((s16[8,400,128]{2,1,0:T(8,128)(2,1)}), s16[8,400,128]{2,1,0:T(8,128)(2,1)S(1)}, u32[]{:S(2)}, u32[]{:S(2)}) async-start(s16[8,400,128]{2,1,0:T(8,128)(2,1)} %shard_map.82), calls=%async_computation.4 | async-start | bytes 1638400 | tf_op jit(solution)/shard_map/all_to_all | solution.py:242
  236.1 21.2 %collective-permute-start.31 = (s16[8,400,128]{2,1,0:T(8,128)(2,1)S(1)}, s16[8,400,128]{2,1,0:T(8,128)(2,1)S(1)}, u32[]{:S(2)}, u32[]{:S(2)}) collective-permute-start(s16[8,400,128]{2,1,0:T(8,128)(2,1)S(1)} %copy-done.3), channel_id=1, source_target_pairs={{0,16},{8,24},{16,0},{24,8},{1,17},{9,25},{17,1},{25,9},{2,18},{10... | collective-permute-start | bytes 2457608 | tf_op jit(solution)/shard_map/ppermute | solution.py:260
  240.4 33.2 %collective-permute-start.34 = (s16[8,400,128]{2,1,0:T(8,128)(2,1)}, s16[8,400,128]{2,1,0:T(8,128)(2,1)S(1)}, u32[]{:S(2)}, u32[]{:S(2)}) collective-permute-start(s16[8,400,128]{2,1,0:T(8,128)(2,1)} %shard_map.80.refs_1_), channel_id=1, source_target_pairs={{0,16},{8,24},{16,0},{24,8},{1,17},{9,25},{17,1},{25,9},{2,18},{10... | collective-permute-start | bytes 2457608 | tf_op jit(solution)/shard_map/ppermute | solution.py:260
  257.3 18.3 %collective-permute-start.32 = (s16[8,400,128]{2,1,0:T(8,128)(2,1)S(1)}, s16[8,400,128]{2,1,0:T(8,128)(2,1)}, u32[]{:S(2)}, u32[]{:S(2)}) collective-permute-start(s16[8,400,128]{2,1,0:T(8,128)(2,1)S(1)} %copy-done.3), channel_id=1, source_target_pairs={{0,8},{8,0},{16,24},{24,16},{1,9},{9,1},{17,25},{25,17},{2,10},{10... | collective-permute-start | bytes 2457608 | tf_op jit(solution)/shard_map/ppermute | solution.py:260
  257.3 18.3 %collective-permute-start.33 = (s16[8,400,128]{2,1,0:T(8,128)(2,1)S(1)}, s16[8,400,128]{2,1,0:T(8,128)(2,1)}, u32[]{:S(2)}, u32[]{:S(2)}) collective-permute-start(s16[8,400,128]{2,1,0:T(8,128)(2,1)S(1)} %collective-permute-done.31.refs_1_), channel_id=1, source_target_pairs={{0,8},{8,0},{16,24},{24,16},{1,9},{9,1},{17,25},{25,17},{2,10},{10... | collective-permute-start | bytes 2457608 | tf_op jit(solution)/shard_map/ppermute | solution.py:260
  273.6 8.4 %collective-permute-start.35 = (s16[8,400,128]{2,1,0:T(8,128)(2,1)}, s16[8,400,128]{2,1,0:T(8,128)(2,1)S(1)}, u32[]{:S(2)}, u32[]{:S(2)}) collective-permute-start(s16[8,400,128]{2,1,0:T(8,128)(2,1)} %shard_map.80.refs_1_), channel_id=1, source_target_pairs={{0,8},{8,0},{16,24},{24,16},{1,9},{9,1},{17,25},{25,17},{2,10},{10... | collective-permute-start | bytes 2457608 | tf_op jit(solution)/shard_map/ppermute | solution.py:260
  273.6 8.4 %collective-permute-start.36 = (s16[8,400,128]{2,1,0:T(8,128)(2,1)S(1)}, s16[8,400,128]{2,1,0:T(8,128)(2,1)S(1)}, u32[]{:S(2)}, u32[]{:S(2)}) collective-permute-start(s16[8,400,128]{2,1,0:T(8,128)(2,1)S(1)} %collective-permute-done.34.refs_2_), channel_id=1, source_target_pairs={{0,8},{8,0},{16,24},{24,16},{1,9},{9,1},{17,25},{25,17},{2,10},{10... | collective-permute-start | bytes 2457608 | tf_op jit(solution)/shard_map/ppermute | solution.py:260
  274.1 20.4 %collective-permute-start.37 = (s16[8,400,128]{2,1,0:T(8,128)(2,1)}, s16[8,400,128]{2,1,0:T(8,128)(2,1)S(1)}, u32[]{:S(2)}, u32[]{:S(2)}) collective-permute-start(s16[8,400,128]{2,1,0:T(8,128)(2,1)} %shard_map.83.refs_1_), channel_id=1, source_target_pairs={{0,16},{8,24},{16,0},{24,8},{1,17},{9,25},{17,1},{25,9},{2,18},{10... | collective-permute-start | bytes 2457608 | tf_op jit(solution)/shard_map/ppermute | solution.py:260
  294.5 2.3 collective-permute-start.38
  294.5 3.5 %collective-permute-start.39 = (s16[8,400,128]{2,1,0:T(8,128)(2,1)S(1)}, s16[8,400,128]{2,1,0:T(8,128)(2,1)S(1)}, u32[]{:S(2)}, u32[]{:S(2)}) collective-permute-start(s16[8,400,128]{2,1,0:T(8,128)(2,1)S(1)} %collective-permute-done.37.refs_2_), channel_id=1, source_target_pairs={{0,8},{8,0},{16,24},{24,16},{1,9},{9,1},{17,25},{25,17},{2,10},{10... | collective-permute-start | bytes 2457608 | tf_op jit(solution)/shard_map/ppermute | solution.py:260
  (34 other events, 305.0 us)

commit v7 on v6

--- a/solution.py
+++ b/solution.py
@@ -70,14 +70,16 @@
     return total[:rows] + total[rows:]
 
 
-def pack_kernel(here, v_ref, d_ref, out_ref, turned):
-    put(out_ref, 0, v_ref[...].T)
-    turned[...] = d_ref[...].T
-    width, rows = turned.shape
+def pack_kernel(here, v_ref, d_ref, out_ref):
+    many, rows = out_ref.shape[0], out_ref.shape[2]
+    width = v_ref.shape[1] // many
     slab = out_ref.shape[1] - width - PAD
-    mine = turned[pl.ds(pl.multiple_of(here[0, 0] * slab, slab), slab), :]
-    codes = jnp.floor(mine * 32767.0 + 0.5)
-    out_ref[0, pl.ds(width + PAD, slab), :] = codes.astype(jnp.int32).astype(jnp.int16)
+    at = pl.multiple_of(here[0, 0] * slab, slab)
+    for n in range(many):
+        put(out_ref, n, v_ref[:, n * width : (n + 1) * width].T)
+        mine = d_ref[pl.ds(at, slab), n * width : (n + 1) * width]
+        codes = jnp.floor(mine * 32767.0 + 0.5)
+        out_ref[n, pl.ds(width + PAD, slab), :] = codes.astype(jnp.int32).astype(jnp.int16)
 
 
 def ring_at(spot, groups):
@@ -162,7 +164,7 @@
         outs[t][...] = 0.5 * (moved + (d_ref[:, lanes] - shift[0, 0]) * here) - v_ref[:, lanes]
 
 
-def left_second_kernel(dims, chunk, masks, cols, shift, place, tu_ref, tail_ref, y_ref, tiles, *rest):
+def left_second_kernel(dims, masks, cols, shift, place, tu_ref, tail_ref, y_ref, tiles, *rest):
     nblk, fill, blk, per = dims
     slabs, (_, out, halves, turned) = rest[:-4], rest[-4:]
     step = pl.program_id(0)
@@ -183,7 +185,7 @@
     for t in range(per):
         block = step * per + t
         here = y_ref[:, pl.ds(pl.multiple_of(block * blk, blk), blk)]
-        diagonal = turned[chunk * part : (chunk + 1) * part, t * blk : (t + 1) * blk]
+        diagonal = turned[t * blk : (t + 1) * blk, :].T
         moved = apply_row(halves, tiles, t, cols, block, fill, blk)
         done.append((0.5 * (moved + (diagonal * (1.0 / 32767.0) - shift[0, 0]) * here)).T)
     put(out, 0, jnp.concatenate(done, axis=0))
@@ -253,14 +255,15 @@
     work = 2 * 2 * rows * strings * fill * blk
     size = 4 * rows * strings
 
-    def exchange(value, late=None):
-        have, bit = [value], roots // 2
+    def cross(have, bit):
+        pairs = [(r, r ^ bit) for r in range(roots)]
+        return have + [lax.ppermute(h, "root", pairs) for h in have]
+
+    def exchange(have, bit=roots // 2, late=None):
+        if late is not None:
+            have = list(lax.optimization_barrier((*have, late)))[:-1]
         while bit:
-            pairs = [(r, r ^ bit) for r in range(roots)]
-            have = have + [lax.ppermute(h, "root", pairs) for h in have]
-            if late is not None:
-                have = list(lax.optimization_barrier(tuple(have) + (late,)))[:-1]
-                late = None
+            have = cross(have, bit)
             bit //= 2
         return have
 
@@ -278,17 +281,19 @@
     for hop in range(1, groups // 2 + 1):
         owners += [-hop, hop] if 2 * hop < groups else [-hop]
 
-    slab = width // roots
+    slab = rows // roots
     height = width + PAD + slab
 
     def pack(start, diagonal):
+        pair = 2 if groups % 2 == 0 else 1
+        pieces = pl.BlockSpec((rows, pair * width), lambda q: (0, q))
         return call(
             pack_kernel,
-            groups,
-            [smem(), piece, piece],
-            pl.BlockSpec((1, height, rows), lambda q: (q, 0, 0)),
+            groups // pair,
+            [smem(), pieces, pieces],
+            pl.BlockSpec((pair, height, rows), lambda q: (q, 0, 0)),
             jax.ShapeDtypeStruct((groups, height, rows), i16),
-            [pltpu.VMEM((width, rows), f32)],
+            [],
             0,
             size * 3,
         )(place, start, diagonal)
@@ -303,7 +308,7 @@
             pairs = [(ring[s], ring[(s + way) % groups]) for s in range(groups)]
             moved = lax.ppermute(forth if way == 1 else back, "col", pairs)
             forth, back = (moved, back) if way == 1 else (forth, moved)
-            shards += exchange(moved)
+            shards += exchange([moved])
             crossed.append(shards[1 - roots])
         if hop == 1:
             tv = pack(*lax.optimization_barrier((start, diagonal, forth, back))[:2])
@@ -356,15 +361,16 @@
         size * 3,
     )(block_cols, tv, tiles)
 
-    slabs = exchange(tv[:, width + PAD :], y)
+    half = roots // 2
+    slabs = exchange(cross([tv[:, width + PAD :]], half), half // 2, y)
     part = width // chunks
     chunk_coded = pl.BlockSpec((1, rows + PAD, part), lambda q: (q, 0, 0))
     many = 4 if groups % 4 == 0 else 1
     many_coded = pl.BlockSpec((many, rows + PAD, part), lambda q: (q, 0, 0))
-    seconds = []
+    seconds, crossings = [], []
     for k in range(chunks):
         z = call(
-            functools.partial(left_second_kernel, dims, k, masks),
+            functools.partial(left_second_kernel, dims, masks),
             groups,
             [
                 smem(),
@@ -375,14 +381,16 @@
                 pl.BlockSpec((part, strings), lambda q, k=k: (k, 0), pipeline_mode=once),
                 tile_spec,
             ]
-            + [pl.BlockSpec((1, slab, rows), lambda q: (q, 0, 0))] * roots
+            + [pl.BlockSpec((1, slab, part), lambda q, k=k: (q, 0, k))] * roots
             + [pl.BlockSpec(memory_space=pl.ANY)],
             chunk_coded,
             jax.ShapeDtypeStruct((groups, rows + PAD, part), i16),
-            [pltpu.VMEM((nblk, 2 * part, blk), jnp.bfloat16), pltpu.VMEM((width, rows), f32)],
-            work // chunks if k < 2 else 1,
-            size * 4 // chunks if k < 2 else 1,
+            [pltpu.VMEM((nblk, 2 * part, blk), jnp.bfloat16), pltpu.VMEM((rows, part), f32)],
+            work // chunks,
+            size * 4 // chunks,
         )(block_cols, energy, place, tu, tu, y, tiles, *slabs, base[0] if k < 2 else seconds[k - 2])
+        if k > 1:
+            z = lax.optimization_barrier((z, *crossings[k - 2]))[0]
         second = call(
             second_kernel,
             groups // many,
@@ -394,6 +402,7 @@
             1,
         )(weights, swap(z), base[k])
         seconds.append(second)
+        crossings.append(cross([second], half))
     out = []
     for k in range(chunks):
         late = seconds[k + 1] if k < chunks - 1 else out[0] if out else None
@@ -409,7 +418,7 @@
                 0,
                 1,
                 {1: 0} if out else {},
-            )(weights, *out, *exchange(seconds[k], late))
+            )(weights, *out, *exchange(crossings[k], half // 2, late))
         ]
     return out[0]
 
@@ -456,7 +465,7 @@
         blk = strings // block_cols.shape[0]
         width = strings // groups
         regular = blk % LANES == 0 and width % blk == 0 and rows == width
-        regular = regular and roots & (roots - 1) == 0 and width % (16 * roots) == 0
+        regular = regular and roots > 1 and roots & (roots - 1) == 0 and width % (16 * roots) == 0
         regular = regular and groups % 2 == 0 and blk % (16 * roots) == 0
         args = (coeffs, diagonal, shift, rotation, string_blocks, block_cols)
         if regular:

time: 307 us -> 298 us (0.971)
  waiting for transfers between devices: 108 us -> 98.5 us
  starting transfers between devices: 47.2 us -> 50.7 us
    ppermute x33, waiting for transfers between devices: 58.9 us -> 39.6 us  [cross(): return have + [lax.ppermute(h, 'root', pairs) for h in have]]
    all_to_all x5, waiting for transfers between devices: 34.3 us -> 43.6 us  [swap(): lax.all_to_all(pieces, 'col', split_axis=0, concat_axis=0, tiled=True)]
  transfers between devices with their start and end apart: 45 -> 45, of which waited for: 18 -> 17; matrix products, arithmetic and copies ran while one was open for 2% -> 2% of each run, Pallas kernels for 38% -> 38%
where the time goes in v7:
time: 298 us; the launch traced here: 296 us
  Pallas kernels  130 us (44%)
  waiting for transfers between devices  98.5 us (33%)
  starting transfers between devices  50.7 us (17%)
  local copies, waits for them, and re-layouts  15 us (5%)
    all_to_all x5, waiting for transfers between devices, swap(): lax.all_to_all(pieces, 'col', split_axis=0, concat_axis=0, tiled=True)  43.6 us
    ppermute x33, waiting for transfers between devices, cross(): return have + [lax.ppermute(h, 'root', pairs) for h in have]  39.6 us
    pallas_call x3, Pallas kernels, blocked_shards(): call(functools.partial(left_second_kernel, dims, masks), groups, [smem(),...  34.4 us
    pallas_call x1, Pallas kernels, blocked_shards(): call(functools.partial(right_first_kernel, dims, groups, owners, masks),...  25.1 us
    all_to_all x5, starting transfers between devices, swap(): lax.all_to_all(pieces, 'col', split_axis=0, concat_axis=0, tiled=True)  22.6 us
    ppermute x33, starting transfers between devices, cross(): return have + [lax.ppermute(h, 'root', pairs) for h in have]  19.2 us
    pallas_call x3, Pallas kernels, blocked_shards(): call(functools.partial(rotate_kernel, len(out)), groups, [smem()] + [pl.B...  19.1 us
    pallas_call x1, Pallas kernels, blocked_shards(): call(functools.partial(right_second_kernel, dims), groups, [smem(), smem(...  19.1 us
  transfers between devices with their start and end apart: 45, of which 17 were waited for; matrix products, arithmetic and copies ran while one was open for 2% of the time, Pallas kernels for 38%

profile of v7, /device:TPU:0, one launch (start us, length us, event | category | flops | bytes accessed | tf_op | source)
XLA Modules:
  0.0 296.3 jit_solution(7878860739516451134)
XLA Ops:
  0.0 1.6 constant_dynamic-slice_fusion
  1.9 3.0 %collective-permute-start.4 = (bf16[30,32,128]{2,1,0:T(8,128)(2,1)S(1)}, bf16[30,32,128]{2,1,0:T(8,128)(2,1)S(1)}, u32[]{:S(2)}, u32[]{:S(2)}) collective-permute-start(bf16[30,32,128]{2,1,0:T(8,128)(2,1)S(1)} %bitcast.25), channel_id=1, source_target_pairs={{0,1},{2,0},{4,2},{6,4},{7,6},{5,7},{3,5},{1,3},{8,9},{10,8},{12,1... | collective-permute-start | bytes 737288 | tf_op jit(solution)/shard_map/ppermute | solution.py:309
  5.1 5.9 %collective-permute-done.4.rest_4_ = bf16[30,32,128]{2,1,0:T(8,128)(2,1)S(1)} collective-permute-done((bf16[30,32,128]{2,1,0:T(8,128)(2,1)S(1)}, bf16[30,32,128]{2,1,0:T(8,128)(2,1)S(1)}, u32[]{:S(2)}, u32[]{:S(2)}) %collective-permute-start.4) | collective-permute-done | bytes 245792 | tf_op jit(solution)/shard_map/ppermute | solution.py:309
  11.0 1.7 collective-permute-start.12
  13.0 1.7 collective-permute-start.1
  15.7 6.7 %shard_map.73 = s16[8,496,384]{2,1,0:T(8,128)(2,1)} custom-call(s32[1,2]{1,0:T(1,128)} %add_bitcast_fusion.here.place, f32[384,3072]{1,0:T(8,128)} %bitcast.19, f32[384,3072]{1,0:T(8,128)} %d_ref.4), custom_call_target="tpu_custom_call" | custom-call | bytes 14155776 | tf_op jit(solution)/shard_map/pallas_call | solution.py:290
  22.5 2.4 collective-permute-done.5.rest_5_
  26.9 4.9 %collective-permute-done.16.rest_16_ = bf16[30,32,128]{2,1,0:T(8,128)(2,1)S(1)} collective-permute-done((bf16[30,32,128]{2,1,0:T(8,128)(2,1)S(1)}, bf16[30,32,128]{2,1,0:T(8,128)(2,1)S(1)}, u32[]{:S(2)}, u32[]{:S(2)}) %collective-permute-start.16) | collective-permute-done | bytes 245792 | tf_op jit(solution)/shard_map/ppermute | solution.py:309
  31.7 1.7 collective-permute-start.24
  33.5 4.4 %collective-permute-done.24.rest_24_ = bf16[30,32,128]{2,1,0:T(8,128)(2,1)S(1)} collective-permute-done((bf16[30,32,128]{2,1,0:T(8,128)(2,1)S(1)}, bf16[30,32,128]{2,1,0:T(8,128)(2,1)S(1)}, u32[]{:S(2)}, u32[]{:S(2)}) %collective-permute-start.24) | collective-permute-done | bytes 245792 | tf_op jit(solution)/shard_map/ppermute | solution.py:309
  38.6 6.0 %all-to-all-start.1 = ((s16[8,496,384]{2,1,0:T(8,128)(2,1)}), s16[8,496,384]{2,1,0:T(8,128)(2,1)S(1)}, u32[]{:S(2)}, u32[]{:S(2)}) async-start(s16[8,496,384]{2,1,0:T(8,128)(2,1)} %shard_map.73), calls=%async_computation.1 | async-start | bytes 6094848 | tf_op jit(solution)/shard_map/all_to_all | solution.py:244
  45.2 1.5 collective-permute-start.9
  48.6 5.6 %collective-permute-done.9.rest_9_ = bf16[30,32,128]{2,1,0:T(8,128)(2,1)S(1)} collective-permute-done((bf16[30,32,128]{2,1,0:T(8,128)(2,1)}, bf16[30,32,128]{2,1,0:T(8,128)(2,1)S(1)}, u32[]{:S(2)}, u32[]{:S(2)}) %collective-permute-start.9) | collective-permute-done | bytes 245792 | tf_op jit(solution)/shard_map/ppermute | solution.py:260
  54.2 4.5 %collective-permute-done.13.rest_13_ = bf16[30,32,128]{2,1,0:T(8,128)(2,1)} collective-permute-done((bf16[30,32,128]{2,1,0:T(8,128)(2,1)}, bf16[30,32,128]{2,1,0:T(8,128)(2,1)}, u32[]{:S(2)}, u32[]{:S(2)}) %collective-permute-start.13) | collective-permute-done | bytes 245792 | tf_op jit(solution)/shard_map/ppermute | solution.py:260
  58.7 1.5 collective-permute-start.17
  61.5 6.5 %collective-permute-done.17.rest_17_ = bf16[30,32,128]{2,1,0:T(8,128)(2,1)} collective-permute-done((bf16[30,32,128]{2,1,0:T(8,128)(2,1)}, bf16[30,32,128]{2,1,0:T(8,128)(2,1)}, u32[]{:S(2)}, u32[]{:S(2)}) %collective-permute-start.17) | collective-permute-done | bytes 245792 | tf_op jit(solution)/shard_map/ppermute | solution.py:260
  67.9 1.5 collective-permute-start.25
  69.4 3.8 %collective-permute-done.21.rest_21_ = bf16[30,32,128]{2,1,0:T(8,128)(2,1)} collective-permute-done((bf16[30,32,128]{2,1,0:T(8,128)(2,1)}, bf16[30,32,128]{2,1,0:T(8,128)(2,1)}, u32[]{:S(2)}, u32[]{:S(2)}) %collective-permute-start.21) | collective-permute-done | bytes 245792 | tf_op jit(solution)/shard_map/ppermute | solution.py:260
  74.3 2.4 collective-permute-done.25.rest_25_
  78.1 2.3 copy.16
  80.5 25.1 %shard_map.74 = (f32[384,3072]{1,0:T(8,128)}, s16[8,400,384]{2,1,0:T(8,128)(2,1)}, bf16[30720,128]{1,0:T(8,128)(2,1)}) custom-call(s32[24,10]{1,0:T(8,128)} %copy.21.cols, f32[1,1]{1,0:T(1,128)} %bitcast.14.shift, s32[1,2]{1,0:T(1,128)} %add_bitcast_fusion.here.place, f32[384,3072]{1,0:T(8,128)} %bitcast.20, f32[384,3072]{1,0:T(8,128)} %d_ref.4, ...), custom_call_target="tpu_custom_call" | custom-call | flops 6039797760 | bytes 28311552 | tf_op jit(solution)/shard_map/pallas_call | solution.py:320
  105.5 3.3 %all-to-all-done.1.tv_ref = s16[8,496,384]{2,1,0:T(8,128)(2,1)S(1)} async-done(((s16[8,496,384]{2,1,0:T(8,128)(2,1)}), s16[8,496,384]{2,1,0:T(8,128)(2,1)S(1)}, u32[]{:S(2)}, u32[]{:S(2)}) %all-to-all-start.1) | async-done | bytes 3047456 | tf_op jit(solution)/shard_map/all_to_all | solution.py:244
  108.9 1.6 copy-done.4
  110.5 3.8 %all-to-all-start = ((s16[8,400,384]{2,1,0:T(8,128)(2,1)}), s16[8,400,384]{2,1,0:T(8,128)(2,1)S(1)}, u32[]{:S(2)}, u32[]{:S(2)}) async-start(s16[8,400,384]{2,1,0:T(8,128)(2,1)} %get-tuple-element.29), calls=%async_computation | async-start | bytes 4915200 | tf_op jit(solution)/shard_map/all_to_all | solution.py:244
  115.5 1.6 collective-permute-start.28
  117.0 17.6 %shard_map.75.y_ref = f32[384,3072]{1,0:T(8,128)} custom-call(s32[24,10]{1,0:T(8,128)} %copy.21.cols, s16[8,496,384]{2,1,0:T(8,128)(2,1)} %copy-done.4, bf16[30720,128]{1,0:T(8,128)(2,1)} %get-tuple-element.31.tiles), custom_call_target="tpu_custom_call" | custom-call | flops 6039797760 | bytes 14155776 | tf_op jit(solution)/shard_map/pallas_call | solution.py:353
  135.2 19.1 %shard_map.76 = (f32[384,1024]{1,0:T(8,128)}, f32[384,1024]{1,0:T(8,128)}, f32[384,1024]{1,0:T(8,128)}) custom-call(s32[24,10]{1,0:T(8,128)} %copy.21.cols, f32[1,1]{1,0:T(1,128)} %bitcast.15.shift, f32[384,3072]{1,0:T(8,128)} %get-tuple-element.34.w_ref, f32[384,3072]{1,0:T(8,128)} %bitcast.21, f32[384,3072]{1,0:T(8,128)} %d_ref.4, ...), custom_call_target="tpu_custom_call" | custom-call | flops 6039797760 | bytes 23592960 | tf_op jit(solution)/shard_map/pallas_call | solution.py:342
  154.3 15.9 %all-to-all-done.tu_ref.tail_ref = s16[8,400,384]{2,1,0:T(8,128)(2,1)S(1)} async-done(((s16[8,400,384]{2,1,0:T(8,128)(2,1)}), s16[8,400,384]{2,1,0:T(8,128)(2,1)S(1)}, u32[]{:S(2)}, u32[]{:S(2)}) %all-to-all-start) | async-done | bytes 2457632 | tf_op jit(solution)/shard_map/all_to_all | solution.py:244
  171.6 11.5 %shard_map.77 = s16[8,400,128]{2,1,0:T(8,128)(2,1)} custom-call(s32[24,10]{1,0:T(8,128)} %copy.21.cols, f32[1,1]{1,0:T(1,128)} %bitcast.16.shift, s32[1,2]{1,0:T(1,128)} %add_bitcast_fusion.here.place, s16[8,400,384]{2,1,0:T(8,128)(2,1)} %copy-done.1, s16[8,400,384]{2,1,0:T(8,128)(2,1)} %copy-done.1, f32[384,3072]{1,0:T(8,128)} %shard_map.75.y_ref, ...), custom_call_target="tpu_custom_call" | custom-call | flops 2013265920 | bytes 6291456 | tf_op jit(solution)/shard_map/pallas_call | solution.py:372
  183.1 3.5 %all-to-all-start.2 = ((s16[8,400,128]{2,1,0:T(8,128)(2,1)}), s16[8,400,128]{2,1,0:T(8,128)(2,1)S(1)}, u32[]{:S(2)}, u32[]{:S(2)}) async-start(s16[8,400,128]{2,1,0:T(8,128)(2,1)} %shard_map.77), calls=%async_computation.2 | async-start | bytes 1638400 | tf_op jit(solution)/shard_map/all_to_all | solution.py:244
  186.6 11.5 %shard_map.79 = s16[8,400,128]{2,1,0:T(8,128)(2,1)} custom-call(s32[24,10]{1,0:T(8,128)} %copy.21.cols, f32[1,1]{1,0:T(1,128)} %bitcast.17.shift, s32[1,2]{1,0:T(1,128)} %add_bitcast_fusion.here.place, s16[8,400,384]{2,1,0:T(8,128)(2,1)} %copy-done.1, s16[8,400,384]{2,1,0:T(8,128)(2,1)} %copy-done.1, f32[384,3072]{1,0:T(8,128)} %shard_map.75.y_ref, ...), custom_call_target="tpu_custom_call" | custom-call | flops 2013265920 | bytes 6291456 | tf_op jit(solution)/shard_map/pallas_call | solution.py:372
  198.1 9.6 %all-to-all-done.2.z_ref = s16[8,400,128]{2,1,0:T(8,128)(2,1)S(1)} async-done(((s16[8,400,128]{2,1,0:T(8,128)(2,1)}), s16[8,400,128]{2,1,0:T(8,128)(2,1)S(1)}, u32[]{:S(2)}, u32[]{:S(2)}) %all-to-all-start.2) | async-done | bytes 819232 | tf_op jit(solution)/shard_map/all_to_all | solution.py:244
  207.7 3.6 %all-to-all-start.3 = ((s16[8,400,128]{2,1,0:T(8,128)(2,1)}), s16[8,400,128]{2,1,0:T(8,128)(2,1)S(1)}, u32[]{:S(2)}, u32[]{:S(2)}) async-start(s16[8,400,128]{2,1,0:T(8,128)(2,1)} %shard_map.79), calls=%async_computation.3 | async-start | bytes 1638400 | tf_op jit(solution)/shard_map/all_to_all | solution.py:244
  212.5 2.8 shard_map.78.refs_0_.rest_4_
  215.3 1.5 collective-permute-start.31
  216.8 11.5 %shard_map.82 = s16[8,400,128]{2,1,0:T(8,128)(2,1)} custom-call(s32[24,10]{1,0:T(8,128)} %copy.21.cols, f32[1,1]{1,0:T(1,128)} %bitcast.18.shift, s32[1,2]{1,0:T(1,128)} %add_bitcast_fusion.here.place, s16[8,400,384]{2,1,0:T(8,128)(2,1)} %copy-done.1, s16[8,400,384]{2,1,0:T(8,128)(2,1)} %copy-done.1, f32[384,3072]{1,0:T(8,128)} %shard_map.75.y_ref, ...), custom_call_target="tpu_custom_call" | custom-call | flops 2013265920 | bytes 6291456 | tf_op jit(solution)/shard_map/pallas_call | solution.py:372
  228.2 7.1 %collective-permute-done.31.refs_1_ = s16[8,400,128]{2,1,0:T(8,128)(2,1)S(1)} collective-permute-done((s16[8,400,128]{2,1,0:T(8,128)(2,1)}, s16[8,400,128]{2,1,0:T(8,128)(2,1)S(1)}, u32[]{:S(2)}, u32[]{:S(2)}) %collective-permute-start.31) | collective-permute-done | bytes 819232 | tf_op jit(solution)/shard_map/ppermute | solution.py:260
  235.4 5.7 %all-to-all-start.4 = ((s16[8,400,128]{2,1,0:T(8,128)(2,1)}), s16[8,400,128]{2,1,0:T(8,128)(2,1)S(1)}, u32[]{:S(2)}, u32[]{:S(2)}) async-start(s16[8,400,128]{2,1,0:T(8,128)(2,1)} %shard_map.82), calls=%async_computation.4 | async-start | bytes 1638400 | tf_op jit(solution)/shard_map/all_to_all | solution.py:244
  241.1 2.8 shard_map.80.refs_1_
  243.8 1.5 collective-permute-start.34
  245.9 14.9 %all-to-all-done.4.z_ref = s16[8,400,128]{2,1,0:T(8,128)(2,1)S(1)} async-done(((s16[8,400,128]{2,1,0:T(8,128)(2,1)}), s16[8,400,128]{2,1,0:T(8,128)(2,1)S(1)}, u32[]{:S(2)}, u32[]{:S(2)}) %all-to-all-start.4) | async-done | bytes 819232 | tf_op jit(solution)/shard_map/all_to_all | solution.py:244
  261.6 2.8 shard_map.83.refs_1_
  265.0 1.5 collective-permute-start.37
  266.5 6.4 %shard_map.81.refs_0_ = f32[1,384,3072]{2,1,0:T(8,128)} custom-call(f32[1,4]{1,0:T(1,128)} %bitcast.30, s16[8,400,128]{2,1,0:T(8,128)(2,1)} %shard_map.78.refs_0_.rest_4_, s16[8,400,128]{2,1,0:T(8,128)(2,1)} %copy-done.15, s16[8,400,128]{2,1,0:T(8,128)(2,1)} %collective-permute-done.32.refs_2_, s16[8,400,128]{2,1,0:T(8,128)(2,1)} %collective-permute-done.33.refs_3_), custom_call_target="tpu_custom_call" | custom-call | bytes 1 | tf_op jit(solution)/shard_map/pallas_call | solution.py:411
  274.7 6.4 %shard_map.84.refs_0_ = f32[1,384,3072]{2,1,0:T(8,128)} custom-call(f32[1,4]{1,0:T(1,128)} %bitcast.31, f32[1,384,3072]{2,1,0:T(8,128)} %shard_map.81.refs_0_, s16[8,400,128]{2,1,0:T(8,128)(2,1)} %shard_map.80.refs_1_, s16[8,400,128]{2,1,0:T(8,128)(2,1)} %copy-done.9, s16[8,400,128]{2,1,0:T(8,128)(2,1)} %copy-done.11, ...), custom_call_target="tpu_custom_call", output_to_operand_aliasing={{}: (1, {})} | custom-call | bytes 1 | tf_op jit(solution)/shard_map/pallas_call | solution.py:411
  281.1 4.4 %collective-permute-done.37.refs_2_ = s16[8,400,128]{2,1,0:T(8,128)(2,1)S(1)} collective-permute-done((s16[8,400,128]{2,1,0:T(8,128)(2,1)}, s16[8,400,128]{2,1,0:T(8,128)(2,1)S(1)}, u32[]{:S(2)}, u32[]{:S(2)}) %collective-permute-start.37) | collective-permute-done | bytes 819232 | tf_op jit(solution)/shard_map/ppermute | solution.py:260
  286.0 1.8 collective-permute-done.38.refs_3_
  289.9 6.4 %shard_map.85 = f32[1,384,3072]{2,1,0:T(8,128)} custom-call(f32[1,4]{1,0:T(1,128)} %bitcast.32, f32[1,384,3072]{2,1,0:T(8,128)} %shard_map.84.refs_0_, s16[8,400,128]{2,1,0:T(8,128)(2,1)} %shard_map.83.refs_1_, s16[8,400,128]{2,1,0:T(8,128)(2,1)} %copy-done.10, s16[8,400,128]{2,1,0:T(8,128)(2,1)} %copy-done.13, ...), custom_call_target="tpu_custom_call", output_to_operand_aliasing={{}: (1, {})} | custom-call | bytes 1 | tf_op jit(solution)/shard_map/pallas_call | solution.py:411
  (139 shorter events, 20.8 us)
Async XLA Ops:
  0.0 211.2 %copy-start = (f32[4,4]{1,0:T(4,128)S(1)}, f32[4,4]{1,0:T(4,128)}, u32[]{:S(2)}) copy-start(f32[4,4]{1,0:T(4,128)} %param.10) | copy-start | bytes 196
  1.9 9.0 %collective-permute-start.4 = (bf16[30,32,128]{2,1,0:T(8,128)(2,1)S(1)}, bf16[30,32,128]{2,1,0:T(8,128)(2,1)S(1)}, u32[]{:S(2)}, u32[]{:S(2)}) collective-permute-start(bf16[30,32,128]{2,1,0:T(8,128)(2,1)S(1)} %bitcast.25), channel_id=1, source_target_pairs={{0,1},{2,0},{4,2},{6,4},{7,6},{5,7},{3,5},{1,3},{8,9},{10,8},{12,1... | collective-permute-start | bytes 737288 | tf_op jit(solution)/shard_map/ppermute | solution.py:309
  5.0 7.7 %collective-permute-start = (bf16[30,32,128]{2,1,0:T(8,128)(2,1)S(1)}, bf16[30,32,128]{2,1,0:T(8,128)(2,1)S(1)}, u32[]{:S(2)}, u32[]{:S(2)}) collective-permute-start(bf16[30,32,128]{2,1,0:T(8,128)(2,1)S(1)} %bitcast.26), channel_id=1, source_target_pairs={{0,2},{2,4},{4,6},{6,7},{7,5},{5,3},{3,1},{1,0},{8,10},{10,12},{12... | collective-permute-start | bytes 737288 | tf_op jit(solution)/shard_map/ppermute | solution.py:309
  11.0 33.8 %copy-start.17 = (bf16[30,32,128]{2,1,0:T(8,128)(2,1)}, bf16[30,32,128]{2,1,0:T(8,128)(2,1)S(1)}, u32[]{:S(2)}) copy-start(bf16[30,32,128]{2,1,0:T(8,128)(2,1)S(1)} %collective-permute-done.4.rest_4_) | copy-start | bytes 737284
  11.0 11.5 %collective-permute-start.12 = (bf16[30,32,128]{2,1,0:T(8,128)(2,1)S(1)}, bf16[30,32,128]{2,1,0:T(8,128)(2,1)S(1)}, u32[]{:S(2)}, u32[]{:S(2)}) collective-permute-start(bf16[30,32,128]{2,1,0:T(8,128)(2,1)S(1)} %collective-permute-done.4.rest_4_), channel_id=1, source_target_pairs={{0,1},{2,0},{4,2},{6,4},{7,6},{5,7},{3,5},{1,3},{8,9},{10,8},{12,1... | collective-permute-start | bytes 737288 | tf_op jit(solution)/shard_map/ppermute | solution.py:309
  12.7 9.8 %collective-permute-start.8 = (bf16[30,32,128]{2,1,0:T(8,128)(2,1)S(1)}, bf16[30,32,128]{2,1,0:T(8,128)(2,1)S(1)}, u32[]{:S(2)}, u32[]{:S(2)}) collective-permute-start(bf16[30,32,128]{2,1,0:T(8,128)(2,1)S(1)} %collective-permute-done.rest_0_), channel_id=1, source_target_pairs={{0,2},{2,4},{4,6},{6,7},{7,5},{5,3},{3,1},{1,0},{8,10},{10,12},{12... | collective-permute-start | bytes 737288 | tf_op jit(solution)/shard_map/ppermute | solution.py:309
  13.0 9.5 %collective-permute-start.1 = (bf16[30,32,128]{2,1,0:T(8,128)(2,1)S(1)}, bf16[30,32,128]{2,1,0:T(8,128)(2,1)S(1)}, u32[]{:S(2)}, u32[]{:S(2)}) collective-permute-start(bf16[30,32,128]{2,1,0:T(8,128)(2,1)S(1)} %collective-permute-done.rest_0_), channel_id=1, source_target_pairs={{0,16},{8,24},{16,0},{24,8},{1,17},{9,25},{17,1},{25,9},{2,18},{10... | collective-permute-start | bytes 737288 | tf_op jit(solution)/shard_map/ppermute | solution.py:260
  14.7 10.2 %collective-permute-start.5 = (bf16[30,32,128]{2,1,0:T(8,128)(2,1)S(1)}, bf16[30,32,128]{2,1,0:T(8,128)(2,1)S(1)}, u32[]{:S(2)}, u32[]{:S(2)}) collective-permute-start(bf16[30,32,128]{2,1,0:T(8,128)(2,1)S(1)} %collective-permute-done.4.rest_4_), channel_id=1, source_target_pairs={{0,16},{8,24},{16,0},{24,8},{1,17},{9,25},{17,1},{25,9},{2,18},{10... | collective-permute-start | bytes 737288 | tf_op jit(solution)/shard_map/ppermute | solution.py:260
  22.4 54.4 %copy-start.16 = (s32[24,10]{0,1:T(8,128)S(1)}, s32[24,10]{0,1:T(8,128)}, u32[]{:S(2)}) copy-start(s32[24,10]{0,1:T(8,128)} %param.12) | copy-start | bytes 2884
  24.8 6.9 %collective-permute-start.16 = (bf16[30,32,128]{2,1,0:T(8,128)(2,1)S(1)}, bf16[30,32,128]{2,1,0:T(8,128)(2,1)S(1)}, u32[]{:S(2)}, u32[]{:S(2)}) collective-permute-start(bf16[30,32,128]{2,1,0:T(8,128)(2,1)S(1)} %collective-permute-done.8.rest_8_), channel_id=1, source_target_pairs={{0,2},{2,4},{4,6},{6,7},{7,5},{5,3},{3,1},{1,0},{8,10},{10,12},{12... | collective-permute-start | bytes 737288 | tf_op jit(solution)/shard_map/ppermute | solution.py:309
  26.3 7.2 %collective-permute-start.20 = (bf16[30,32,128]{2,1,0:T(8,128)(2,1)S(1)}, bf16[30,32,128]{2,1,0:T(8,128)(2,1)S(1)}, u32[]{:S(2)}, u32[]{:S(2)}) collective-permute-start(bf16[30,32,128]{2,1,0:T(8,128)(2,1)S(1)} %collective-permute-done.12.rest_12_), channel_id=1, source_target_pairs={{0,1},{2,0},{4,2},{6,4},{7,6},{5,7},{3,5},{1,3},{8,9},{10,8},{12,1... | collective-permute-start | bytes 737288 | tf_op jit(solution)/shard_map/ppermute | solution.py:309
  31.7 6.2 %collective-permute-start.24 = (bf16[30,32,128]{2,1,0:T(8,128)(2,1)S(1)}, bf16[30,32,128]{2,1,0:T(8,128)(2,1)S(1)}, u32[]{:S(2)}, u32[]{:S(2)}) collective-permute-start(bf16[30,32,128]{2,1,0:T(8,128)(2,1)S(1)} %collective-permute-done.16.rest_16_), channel_id=1, source_target_pairs={{0,2},{2,4},{4,6},{6,7},{7,5},{5,3},{3,1},{1,0},{8,10},{10,12},{12... | collective-permute-start | bytes 737288 | tf_op jit(solution)/shard_map/ppermute | solution.py:309
  38.6 70.2 %all-to-all-start.1 = ((s16[8,496,384]{2,1,0:T(8,128)(2,1)}), s16[8,496,384]{2,1,0:T(8,128)(2,1)S(1)}, u32[]{:S(2)}, u32[]{:S(2)}) async-start(s16[8,496,384]{2,1,0:T(8,128)(2,1)} %shard_map.73), calls=%async_computation.1 | async-start | bytes 6094848 | tf_op jit(solution)/shard_map/all_to_all | solution.py:244
  44.6 2.6 collective-permute-start.2
  44.7 3.0 %collective-permute-start.6 = (bf16[30,32,128]{2,1,0:T(8,128)(2,1)S(1)}, bf16[30,32,128]{2,1,0:T(8,128)(2,1)S(1)}, u32[]{:S(2)}, u32[]{:S(2)}) collective-permute-start(bf16[30,32,128]{2,1,0:T(8,128)(2,1)S(1)} %collective-permute-done.4.rest_4_), channel_id=1, source_target_pairs={{0,8},{8,0},{16,24},{24,16},{1,9},{9,1},{17,25},{25,17},{2,10},{10... | collective-permute-start | bytes 737288 | tf_op jit(solution)/shard_map/ppermute | solution.py:260
  45.2 9.0 %collective-permute-start.9 = (bf16[30,32,128]{2,1,0:T(8,128)(2,1)}, bf16[30,32,128]{2,1,0:T(8,128)(2,1)S(1)}, u32[]{:S(2)}, u32[]{:S(2)}) collective-permute-start(bf16[30,32,128]{2,1,0:T(8,128)(2,1)} %copy-done.20), channel_id=1, source_target_pairs={{0,16},{8,24},{16,0},{24,8},{1,17},{9,25},{17,1},{25,9},{2,18},{10... | collective-permute-start | bytes 737288 | tf_op jit(solution)/shard_map/ppermute | solution.py:260
  46.7 12.0 %collective-permute-start.13 = (bf16[30,32,128]{2,1,0:T(8,128)(2,1)}, bf16[30,32,128]{2,1,0:T(8,128)(2,1)}, u32[]{:S(2)}, u32[]{:S(2)}) collective-permute-start(bf16[30,32,128]{2,1,0:T(8,128)(2,1)} %copy-done.19), channel_id=1, source_target_pairs={{0,16},{8,24},{16,0},{24,8},{1,17},{9,25},{17,1},{25,9},{2,18},{10... | collective-permute-start | bytes 737288 | tf_op jit(solution)/shard_map/ppermute | solution.py:260
  47.2 13.0 %collective-permute-start.10 = (bf16[30,32,128]{2,1,0:T(8,128)(2,1)}, bf16[30,32,128]{2,1,0:T(8,128)(2,1)S(1)}, u32[]{:S(2)}, u32[]{:S(2)}) collective-permute-start(bf16[30,32,128]{2,1,0:T(8,128)(2,1)} %copy-done.20), channel_id=1, source_target_pairs={{0,8},{8,0},{16,24},{24,16},{1,9},{9,1},{17,25},{25,17},{2,10},{10... | collective-permute-start | bytes 737288 | tf_op jit(solution)/shard_map/ppermute | solution.py:260
  47.2 13.5 %collective-permute-start.14 = (bf16[30,32,128]{2,1,0:T(8,128)(2,1)}, bf16[30,32,128]{2,1,0:T(8,128)(2,1)S(1)}, u32[]{:S(2)}, u32[]{:S(2)}) collective-permute-start(bf16[30,32,128]{2,1,0:T(8,128)(2,1)} %copy-done.19), channel_id=1, source_target_pairs={{0,8},{8,0},{16,24},{24,16},{1,9},{9,1},{17,25},{25,17},{2,10},{10... | collective-permute-start | bytes 737288 | tf_op jit(solution)/shard_map/ppermute | solution.py:260
  47.9 12.8 %collective-permute-start.3 = (bf16[30,32,128]{2,1,0:T(8,128)(2,1)}, bf16[30,32,128]{2,1,0:T(8,128)(2,1)S(1)}, u32[]{:S(2)}, u32[]{:S(2)}) collective-permute-start(bf16[30,32,128]{2,1,0:T(8,128)(2,1)} %copy-done.21), channel_id=1, source_target_pairs={{0,8},{8,0},{16,24},{24,16},{1,9},{9,1},{17,25},{25,17},{2,10},{10... | collective-permute-start | bytes 737288 | tf_op jit(solution)/shard_map/ppermute | solution.py:260
  54.2 7.1 %collective-permute-start.7 = (bf16[30,32,128]{2,1,0:T(8,128)(2,1)}, bf16[30,32,128]{2,1,0:T(8,128)(2,1)S(1)}, u32[]{:S(2)}, u32[]{:S(2)}) collective-permute-start(bf16[30,32,128]{2,1,0:T(8,128)(2,1)} %copy-done.22), channel_id=1, source_target_pairs={{0,8},{8,0},{16,24},{24,16},{1,9},{9,1},{17,25},{25,17},{2,10},{10... | collective-permute-start | bytes 737288 | tf_op jit(solution)/shard_map/ppermute | solution.py:260
  58.7 9.2 %collective-permute-start.17 = (bf16[30,32,128]{2,1,0:T(8,128)(2,1)}, bf16[30,32,128]{2,1,0:T(8,128)(2,1)}, u32[]{:S(2)}, u32[]{:S(2)}) collective-permute-start(bf16[30,32,128]{2,1,0:T(8,128)(2,1)} %copy-done.23), channel_id=1, source_target_pairs={{0,16},{8,24},{16,0},{24,8},{1,17},{9,25},{17,1},{25,9},{2,18},{10... | collective-permute-start | bytes 737288 | tf_op jit(solution)/shard_map/ppermute | solution.py:260
  60.2 13.0 %collective-permute-start.21 = (bf16[30,32,128]{2,1,0:T(8,128)(2,1)}, bf16[30,32,128]{2,1,0:T(8,128)(2,1)}, u32[]{:S(2)}, u32[]{:S(2)}) collective-permute-start(bf16[30,32,128]{2,1,0:T(8,128)(2,1)} %copy-done.24), channel_id=1, source_target_pairs={{0,16},{8,24},{16,0},{24,8},{1,17},{9,25},{17,1},{25,9},{2,18},{10... | collective-permute-start | bytes 737288 | tf_op jit(solution)/shard_map/ppermute | solution.py:260
  60.8 12.4 %collective-permute-start.18 = (bf16[30,32,128]{2,1,0:T(8,128)(2,1)}, bf16[30,32,128]{2,1,0:T(8,128)(2,1)S(1)}, u32[]{:S(2)}, u32[]{:S(2)}) collective-permute-start(bf16[30,32,128]{2,1,0:T(8,128)(2,1)} %copy-done.23), channel_id=1, source_target_pairs={{0,8},{8,0},{16,24},{24,16},{1,9},{9,1},{17,25},{25,17},{2,10},{10... | collective-permute-start | bytes 737288 | tf_op jit(solution)/shard_map/ppermute | solution.py:260
  60.8 12.9 %collective-permute-start.22 = (bf16[30,32,128]{2,1,0:T(8,128)(2,1)}, bf16[30,32,128]{2,1,0:T(8,128)(2,1)S(1)}, u32[]{:S(2)}, u32[]{:S(2)}) collective-permute-start(bf16[30,32,128]{2,1,0:T(8,128)(2,1)} %copy-done.24), channel_id=1, source_target_pairs={{0,8},{8,0},{16,24},{24,16},{1,9},{9,1},{17,25},{25,17},{2,10},{10... | collective-permute-start | bytes 737288 | tf_op jit(solution)/shard_map/ppermute | solution.py:260
  61.3 12.5 %collective-permute-start.11 = (bf16[30,32,128]{2,1,0:T(8,128)(2,1)S(1)}, bf16[30,32,128]{2,1,0:T(8,128)(2,1)S(1)}, u32[]{:S(2)}, u32[]{:S(2)}) collective-permute-start(bf16[30,32,128]{2,1,0:T(8,128)(2,1)S(1)} %collective-permute-done.9.rest_9_), channel_id=1, source_target_pairs={{0,8},{8,0},{16,24},{24,16},{1,9},{9,1},{17,25},{25,17},{2,10},{10... | collective-permute-start | bytes 737288 | tf_op jit(solution)/shard_map/ppermute | solution.py:260
  67.9 8.7 %collective-permute-start.25 = (bf16[30,32,128]{2,1,0:T(8,128)(2,1)}, bf16[30,32,128]{2,1,0:T(8,128)(2,1)}, u32[]{:S(2)}, u32[]{:S(2)}) collective-permute-start(bf16[30,32,128]{2,1,0:T(8,128)(2,1)} %copy-done.25), channel_id=1, source_target_pairs={{0,16},{8,24},{16,0},{24,8},{1,17},{9,25},{17,1},{25,9},{2,18},{10... | collective-permute-start | bytes 737288 | tf_op jit(solution)/shard_map/ppermute | solution.py:260
  73.2 7.2 %collective-permute-start.15 = (bf16[30,32,128]{2,1,0:T(8,128)(2,1)}, bf16[30,32,128]{2,1,0:T(8,128)(2,1)}, u32[]{:S(2)}, u32[]{:S(2)}) collective-permute-start(bf16[30,32,128]{2,1,0:T(8,128)(2,1)} %collective-permute-done.13.rest_13_), channel_id=1, source_target_pairs={{0,8},{8,0},{16,24},{24,16},{1,9},{9,1},{17,25},{25,17},{2,10},{10... | collective-permute-start | bytes 737288 | tf_op jit(solution)/shard_map/ppermute | solution.py:260
  73.2 7.2 %collective-permute-start.26 = (bf16[30,32,128]{2,1,0:T(8,128)(2,1)}, bf16[30,32,128]{2,1,0:T(8,128)(2,1)}, u32[]{:S(2)}, u32[]{:S(2)}) collective-permute-start(bf16[30,32,128]{2,1,0:T(8,128)(2,1)} %copy-done.25), channel_id=1, source_target_pairs={{0,8},{8,0},{16,24},{24,16},{1,9},{9,1},{17,25},{25,17},{2,10},{10... | collective-permute-start | bytes 737288 | tf_op jit(solution)/shard_map/ppermute | solution.py:260
  73.7 6.7 %collective-permute-start.19 = (bf16[30,32,128]{2,1,0:T(8,128)(2,1)}, bf16[30,32,128]{2,1,0:T(8,128)(2,1)}, u32[]{:S(2)}, u32[]{:S(2)}) collective-permute-start(bf16[30,32,128]{2,1,0:T(8,128)(2,1)} %collective-permute-done.17.rest_17_), channel_id=1, source_target_pairs={{0,8},{8,0},{16,24},{24,16},{1,9},{9,1},{17,25},{25,17},{2,10},{10... | collective-permute-start | bytes 737288 | tf_op jit(solution)/shard_map/ppermute | solution.py:260
  73.8 6.6 %collective-permute-start.23 = (bf16[30,32,128]{2,1,0:T(8,128)(2,1)}, bf16[30,32,128]{2,1,0:T(8,128)(2,1)}, u32[]{:S(2)}, u32[]{:S(2)}) collective-permute-start(bf16[30,32,128]{2,1,0:T(8,128)(2,1)} %collective-permute-done.21.rest_21_), channel_id=1, source_target_pairs={{0,8},{8,0},{16,24},{24,16},{1,9},{9,1},{17,25},{25,17},{2,10},{10... | collective-permute-start | bytes 737288 | tf_op jit(solution)/shard_map/ppermute | solution.py:260
  76.7 3.7 %collective-permute-start.27 = (bf16[30,32,128]{2,1,0:T(8,128)(2,1)}, bf16[30,32,128]{2,1,0:T(8,128)(2,1)}, u32[]{:S(2)}, u32[]{:S(2)}) collective-permute-start(bf16[30,32,128]{2,1,0:T(8,128)(2,1)} %collective-permute-done.25.rest_25_), channel_id=1, source_target_pairs={{0,8},{8,0},{16,24},{24,16},{1,9},{9,1},{17,25},{25,17},{2,10},{10... | collective-permute-start | bytes 737288 | tf_op jit(solution)/shard_map/ppermute | solution.py:260
  110.5 59.7 %all-to-all-start = ((s16[8,400,384]{2,1,0:T(8,128)(2,1)}), s16[8,400,384]{2,1,0:T(8,128)(2,1)S(1)}, u32[]{:S(2)}, u32[]{:S(2)}) async-start(s16[8,400,384]{2,1,0:T(8,128)(2,1)} %get-tuple-element.29), calls=%async_computation | async-start | bytes 4915200 | tf_op jit(solution)/shard_map/all_to_all | solution.py:244
  115.5 19.2 %collective-permute-start.28 = (s16[8,96,384]{2,1,0:T(8,128)(2,1)S(1)}, s16[8,96,384]{2,1,0:T(8,128)(2,1)}, u32[]{:S(2)}, u32[]{:S(2)}) collective-permute-start(s16[8,96,384]{2,1,0:T(8,128)(2,1)S(1)} %slice.6.rest_0_), channel_id=1, source_target_pairs={{0,16},{8,24},{16,0},{24,8},{1,17},{9,25},{17,1},{25,9},{2,18},{10... | collective-permute-start | bytes 1769480 | tf_op jit(solution)/shard_map/ppermute | solution.py:260
  134.6 35.5 %collective-permute-start.29 = (s16[8,96,384]{2,1,0:T(8,128)(2,1)S(1)}, s16[8,96,384]{2,1,0:T(8,128)(2,1)}, u32[]{:S(2)}, u32[]{:S(2)}) collective-permute-start(s16[8,96,384]{2,1,0:T(8,128)(2,1)S(1)} %slice.6.rest_0_), channel_id=1, source_target_pairs={{0,8},{8,0},{16,24},{24,16},{1,9},{9,1},{17,25},{25,17},{2,10},{10... | collective-permute-start | bytes 1769480 | tf_op jit(solution)/shard_map/ppermute | solution.py:260
  134.7 35.5 %collective-permute-start.30 = (s16[8,96,384]{2,1,0:T(8,128)(2,1)}, s16[8,96,384]{2,1,0:T(8,128)(2,1)}, u32[]{:S(2)}, u32[]{:S(2)}) collective-permute-start(s16[8,96,384]{2,1,0:T(8,128)(2,1)} %collective-permute-done.28.rest_1_), channel_id=1, source_target_pairs={{0,8},{8,0},{16,24},{24,16},{1,9},{9,1},{17,25},{25,17},{2,10},{10... | collective-permute-start | bytes 1769480 | tf_op jit(solution)/shard_map/ppermute | solution.py:260
  183.1 24.6 %all-to-all-start.2 = ((s16[8,400,128]{2,1,0:T(8,128)(2,1)}), s16[8,400,128]{2,1,0:T(8,128)(2,1)S(1)}, u32[]{:S(2)}, u32[]{:S(2)}) async-start(s16[8,400,128]{2,1,0:T(8,128)(2,1)} %shard_map.77), calls=%async_computation.2 | async-start | bytes 1638400 | tf_op jit(solution)/shard_map/all_to_all | solution.py:244
  207.7 27.7 %all-to-all-start.3 = ((s16[8,400,128]{2,1,0:T(8,128)(2,1)}), s16[8,400,128]{2,1,0:T(8,128)(2,1)S(1)}, u32[]{:S(2)}, u32[]{:S(2)}) async-start(s16[8,400,128]{2,1,0:T(8,128)(2,1)} %shard_map.79), calls=%async_computation.3 | async-start | bytes 1638400 | tf_op jit(solution)/shard_map/all_to_all | solution.py:244
  215.3 20.1 %collective-permute-start.31 = (s16[8,400,128]{2,1,0:T(8,128)(2,1)}, s16[8,400,128]{2,1,0:T(8,128)(2,1)S(1)}, u32[]{:S(2)}, u32[]{:S(2)}) collective-permute-start(s16[8,400,128]{2,1,0:T(8,128)(2,1)} %shard_map.78.refs_0_.rest_4_), channel_id=1, source_target_pairs={{0,16},{8,24},{16,0},{24,8},{1,17},{9,25},{17,1},{25,9},{2,18},{10... | collective-permute-start | bytes 2457608 | tf_op jit(solution)/shard_map/ppermute | solution.py:260
  235.4 25.4 %all-to-all-start.4 = ((s16[8,400,128]{2,1,0:T(8,128)(2,1)}), s16[8,400,128]{2,1,0:T(8,128)(2,1)S(1)}, u32[]{:S(2)}, u32[]{:S(2)}) async-start(s16[8,400,128]{2,1,0:T(8,128)(2,1)} %shard_map.82), calls=%async_computation.4 | async-start | bytes 1638400 | tf_op jit(solution)/shard_map/all_to_all | solution.py:244
  243.8 20.6 %collective-permute-start.34 = (s16[8,400,128]{2,1,0:T(8,128)(2,1)}, s16[8,400,128]{2,1,0:T(8,128)(2,1)S(1)}, u32[]{:S(2)}, u32[]{:S(2)}) collective-permute-start(s16[8,400,128]{2,1,0:T(8,128)(2,1)} %shard_map.80.refs_1_), channel_id=1, source_target_pairs={{0,16},{8,24},{16,0},{24,8},{1,17},{9,25},{17,1},{25,9},{2,18},{10... | collective-permute-start | bytes 2457608 | tf_op jit(solution)/shard_map/ppermute | solution.py:260
  245.4 21.2 %collective-permute-start.32 = (s16[8,400,128]{2,1,0:T(8,128)(2,1)S(1)}, s16[8,400,128]{2,1,0:T(8,128)(2,1)}, u32[]{:S(2)}, u32[]{:S(2)}) collective-permute-start(s16[8,400,128]{2,1,0:T(8,128)(2,1)S(1)} %copy-done.3), channel_id=1, source_target_pairs={{0,8},{8,0},{16,24},{24,16},{1,9},{9,1},{17,25},{25,17},{2,10},{10... | collective-permute-start | bytes 2457608 | tf_op jit(solution)/shard_map/ppermute | solution.py:260
  245.4 21.2 %collective-permute-start.33 = (s16[8,400,128]{2,1,0:T(8,128)(2,1)S(1)}, s16[8,400,128]{2,1,0:T(8,128)(2,1)}, u32[]{:S(2)}, u32[]{:S(2)}) collective-permute-start(s16[8,400,128]{2,1,0:T(8,128)(2,1)S(1)} %collective-permute-done.31.refs_1_), channel_id=1, source_target_pairs={{0,8},{8,0},{16,24},{24,16},{1,9},{9,1},{17,25},{25,17},{2,10},{10... | collective-permute-start | bytes 2457608 | tf_op jit(solution)/shard_map/ppermute | solution.py:260
  264.4 8.5 %collective-permute-start.35 = (s16[8,400,128]{2,1,0:T(8,128)(2,1)}, s16[8,400,128]{2,1,0:T(8,128)(2,1)S(1)}, u32[]{:S(2)}, u32[]{:S(2)}) collective-permute-start(s16[8,400,128]{2,1,0:T(8,128)(2,1)} %shard_map.80.refs_1_), channel_id=1, source_target_pairs={{0,8},{8,0},{16,24},{24,16},{1,9},{9,1},{17,25},{25,17},{2,10},{10... | collective-permute-start | bytes 2457608 | tf_op jit(solution)/shard_map/ppermute | solution.py:260
  264.5 8.4 %collective-permute-start.36 = (s16[8,400,128]{2,1,0:T(8,128)(2,1)S(1)}, s16[8,400,128]{2,1,0:T(8,128)(2,1)S(1)}, u32[]{:S(2)}, u32[]{:S(2)}) collective-permute-start(s16[8,400,128]{2,1,0:T(8,128)(2,1)S(1)} %collective-permute-done.34.refs_2_), channel_id=1, source_target_pairs={{0,8},{8,0},{16,24},{24,16},{1,9},{9,1},{17,25},{25,17},{2,10},{10... | collective-permute-start | bytes 2457608 | tf_op jit(solution)/shard_map/ppermute | solution.py:260
  265.0 20.4 %collective-permute-start.37 = (s16[8,400,128]{2,1,0:T(8,128)(2,1)}, s16[8,400,128]{2,1,0:T(8,128)(2,1)S(1)}, u32[]{:S(2)}, u32[]{:S(2)}) collective-permute-start(s16[8,400,128]{2,1,0:T(8,128)(2,1)} %shard_map.83.refs_1_), channel_id=1, source_target_pairs={{0,16},{8,24},{16,0},{24,8},{1,17},{9,25},{17,1},{25,9},{2,18},{10... | collective-permute-start | bytes 2457608 | tf_op jit(solution)/shard_map/ppermute | solution.py:260
  285.5 2.3 collective-permute-start.38
  285.5 3.5 %collective-permute-start.39 = (s16[8,400,128]{2,1,0:T(8,128)(2,1)S(1)}, s16[8,400,128]{2,1,0:T(8,128)(2,1)S(1)}, u32[]{:S(2)}, u32[]{:S(2)}) collective-permute-start(s16[8,400,128]{2,1,0:T(8,128)(2,1)S(1)} %collective-permute-done.37.refs_2_), channel_id=1, source_target_pairs={{0,8},{8,0},{16,24},{24,16},{1,9},{9,1},{17,25},{25,17},{2,10},{10... | collective-permute-start | bytes 2457608 | tf_op jit(solution)/shard_map/ppermute | solution.py:260
  (34 other events, 321.7 us)

commit v8 on v7

--- a/solution.py
+++ b/solution.py
@@ -164,15 +164,16 @@
         outs[t][...] = 0.5 * (moved + (d_ref[:, lanes] - shift[0, 0]) * here) - v_ref[:, lanes]
 
 
-def left_second_kernel(dims, masks, cols, shift, place, tu_ref, tail_ref, y_ref, tiles, *rest):
+def left_second_kernel(dims, masks, place, cols, shift, tu_ref, tail_ref, y_ref, tiles, *rest):
     nblk, fill, blk, per = dims
-    slabs, (_, out, halves, turned) = rest[:-4], rest[-4:]
+    groups = nblk // per
+    slabs, outs, (halves, turned) = rest[: len(masks)], rest[len(masks) + 1 : -2], rest[-2:]
     step = pl.program_id(0)
-    part = y_ref.shape[0]
+    to = jnp.bitwise_xor(place[0, 1], step)
 
     @pl.when(step == 0)
     def _():
-        for p in range(nblk // per):
+        for p in range(groups):
             value = decode(tu_ref[p], tail_ref[p]) + y_ref[:, p * per * blk : (p + 1) * per * blk]
             for t in range(per):
                 split_into(halves, p * per + t, value[:, t * blk : (t + 1) * blk])
@@ -183,22 +184,34 @@
         turned[pl.ds(at, height), :] = slab[0].astype(jnp.int32).astype(jnp.float32)
     done = []
     for t in range(per):
-        block = step * per + t
+        block = to * per + t
         here = y_ref[:, pl.ds(pl.multiple_of(block * blk, blk), blk)]
         diagonal = turned[t * blk : (t + 1) * blk, :].T
         moved = apply_row(halves, tiles, t, cols, block, fill, blk)
         done.append((0.5 * (moved + (diagonal * (1.0 / 32767.0) - shift[0, 0]) * here)).T)
-    put(out, 0, jnp.concatenate(done, axis=0))
-
-
-def second_kernel(weights, z_ref, p_ref, out_ref):
-    del weights
-    part = z_ref.shape[2]
-    for n in range(z_ref.shape[0]):
-        put(out_ref, n, take(z_ref, n) + p_ref[:, n * part : (n + 1) * part])
-
-
-def rotate_kernel(aliased, weights, *refs):
+    codes, tail = encode(jnp.concatenate(done, axis=0))
+    for m, out in enumerate(outs):
+
+        @pl.when(step == m)
+        def _(out=out):
+            out[pl.ds(0, codes.shape[0]), :] = codes
+            out[pl.ds(codes.shape[0], PAD), :] = tail
+
+
+def second_kernel(place, weights, p_ref, after, *refs):
+    del weights, after
+    pieces, out_ref = refs[:-1], refs[-1]
+    part = out_ref.shape[2]
+    height = out_ref.shape[1] - PAD
+    for n, piece in enumerate(pieces):
+        m = len(pieces) - 1 - n
+        at = pl.multiple_of(jnp.bitwise_xor(place[0, 1], m) * part, part)
+        value = decode(piece[pl.ds(0, height), :], piece[pl.ds(height, PAD), :])
+        put(out_ref, m, value + p_ref[:, pl.ds(at, part)])
+
+
+def rotate_kernel(aliased, place, weights, *refs):
+    del place
     ins, out_ref = refs[aliased:-1], refs[-1]
     total = weights[0, 0] * take(ins[0], 0)
     for m in range(1, len(ins)):
@@ -210,14 +223,17 @@
     return pl.BlockSpec(memory_space=pltpu.SMEM)
 
 
-def call(kernel, grid, in_specs, out_specs, out_shape, scratch, flops, moved, aliases={}):
+def call(kernel, grid, in_specs, out_specs, out_shape, scratch, flops, moved, aliases={}, ahead=0):
     return pl.pallas_call(
         kernel,
-        grid=(grid,),
-        in_specs=in_specs,
-        out_specs=out_specs,
+        grid_spec=pltpu.PrefetchScalarGridSpec(
+            num_scalar_prefetch=ahead,
+            grid=(grid,),
+            in_specs=in_specs,
+            out_specs=out_specs,
+            scratch_shapes=scratch,
+        ),
         out_shape=out_shape,
-        scratch_shapes=scratch,
         input_output_aliases=aliases,
         compiler_params=pltpu.CompilerParams(
             dimension_semantics=("arbitrary",), vmem_limit_bytes=LIMIT
@@ -364,61 +380,83 @@
     half = roots // 2
     slabs = exchange(cross([tv[:, width + PAD :]], half), half // 2, y)
     part = width // chunks
-    chunk_coded = pl.BlockSpec((1, rows + PAD, part), lambda q: (q, 0, 0))
-    many = 4 if groups % 4 == 0 else 1
-    many_coded = pl.BlockSpec((many, rows + PAD, part), lambda q: (q, 0, 0))
-    seconds, crossings = [], []
-    for k in range(chunks):
-        z = call(
+    half = roots // 2
+    slabs = exchange(cross([tv[:, width + PAD :]], half), half // 2, y)
+
+    def aim(q, place):
+        return jnp.bitwise_xor(place[0, 1], q)
+
+    def all_of(*shape):
+        return pl.BlockSpec(shape, lambda q, s: (0,) * len(shape), pipeline_mode=once)
+
+    coded_piece = jax.ShapeDtypeStruct((rows + PAD, part), i16)
+    def left_second(k, after):
+        return call(
             functools.partial(left_second_kernel, dims, masks),
             groups,
             [
                 smem(),
                 smem(),
-                smem(),
-                pl.BlockSpec((groups, part, rows), lambda q, k=k: (0, k, 0), pipeline_mode=once),
-                pl.BlockSpec((groups, PAD, rows), lambda q: (0, width // PAD, 0), pipeline_mode=once),
-                pl.BlockSpec((part, strings), lambda q, k=k: (k, 0), pipeline_mode=once),
-                tile_spec,
+                pl.BlockSpec((groups, part, rows), lambda q, s: (0, k, 0), pipeline_mode=once),
+                pl.BlockSpec((groups, PAD, rows), lambda q, s: (0, width // PAD, 0), pipeline_mode=once),
+                pl.BlockSpec((part, strings), lambda q, s: (k, 0), pipeline_mode=once),
+                pl.BlockSpec((per * fill * blk, blk), lambda q, s: (aim(q, s), 0)),
             ]
-            + [pl.BlockSpec((1, slab, part), lambda q, k=k: (q, 0, k))] * roots
+            + [pl.BlockSpec((1, slab, part), lambda q, s: (aim(q, s), 0, k))] * roots
             + [pl.BlockSpec(memory_space=pl.ANY)],
-            chunk_coded,
-            jax.ShapeDtypeStruct((groups, rows + PAD, part), i16),
+            [pl.BlockSpec((rows + PAD, part), lambda q, s: (0, 0))] * groups,
+            [coded_piece] * groups,
             [pltpu.VMEM((nblk, 2 * part, blk), jnp.bfloat16), pltpu.VMEM((rows, part), f32)],
             work // chunks,
             size * 4 // chunks,
-        )(block_cols, energy, place, tu, tu, y, tiles, *slabs, base[0] if k < 2 else seconds[k - 2])
+            {},
+            1,
+        )(place, block_cols, energy, tu, tu, y, tiles, *slabs, after)
+
+    seconds, crossings = [], []
+    made = [left_second(0, base[0])]
+    for k in range(chunks):
+        pieces = list(made[k])
         if k > 1:
-            z = lax.optimization_barrier((z, *crossings[k - 2]))[0]
+            pieces[1] = lax.optimization_barrier((pieces[1], *crossings[k - 2]))[0]
+        for m in range(groups - 1, 0, -1):
+            pieces[m] = lax.ppermute(pieces[m], "col", [(c, c ^ m) for c in range(groups)])
+        if k + 1 < chunks:
+            made.append(left_second(k + 1, seconds[k - 1] if k else base[0]))
         second = call(
             second_kernel,
-            groups // many,
-            [smem(), many_coded, pl.BlockSpec((rows, many * part), lambda q: (0, q))],
-            many_coded,
+            1,
+            [smem(), all_of(rows, groups * part), pl.BlockSpec(memory_space=pl.ANY)]
+            + [all_of(rows + PAD, part)] * groups,
+            pl.BlockSpec((groups, rows + PAD, part), lambda q, s: (0, 0, 0)),
             jax.ShapeDtypeStruct((groups, rows + PAD, part), i16),
             [],
             0,
             1,
-        )(weights, swap(z), base[k])
+            {},
+            1,
+        )(place, weights, base[k], made[-1][0], *pieces[::-1])
         seconds.append(second)
         crossings.append(cross([second], half))
     out = []
     for k in range(chunks):
         late = seconds[k + 1] if k < chunks - 1 else out[0] if out else None
-        slot = pl.BlockSpec((1, rows, part), lambda q, k=k: (0, 0, q * chunks + k))
+        slot = pl.BlockSpec((1, rows, part), lambda q, s, k=k: (0, 0, aim(q, s) * chunks + k))
         out = [
             call(
                 functools.partial(rotate_kernel, len(out)),
                 groups,
-                [smem()] + [pl.BlockSpec(memory_space=pl.ANY)] * len(out) + [chunk_coded] * roots,
+                [smem()]
+                + [pl.BlockSpec(memory_space=pl.ANY)] * len(out)
+                + [pl.BlockSpec((1, rows + PAD, part), lambda q, s: (q, 0, 0))] * roots,
                 slot,
                 jax.ShapeDtypeStruct((1, rows, strings), f32),
                 [],
                 0,
                 1,
-                {1: 0} if out else {},
-            )(weights, *out, *exchange(crossings[k], half // 2, late))
+                {2: 0} if out else {},
+                1,
+            )(place, weights, *out, *exchange(crossings[k], half // 2, late))
         ]
     return out[0]
 
@@ -466,7 +504,7 @@
         width = strings // groups
         regular = blk % LANES == 0 and width % blk == 0 and rows == width
         regular = regular and roots > 1 and roots & (roots - 1) == 0 and width % (16 * roots) == 0
-        regular = regular and groups % 2 == 0 and blk % (16 * roots) == 0
+        regular = regular and groups > 1 and groups & (groups - 1) == 0 and blk % (16 * roots) == 0
         args = (coeffs, diagonal, shift, rotation, string_blocks, block_cols)
         if regular:
             return blocked_shards((roots, groups), *args)

time: 298 us -> 306 us (1.027)
  waiting for transfers between devices: 98.5 us -> 68 us
  starting transfers between devices: 50.7 us -> 74.2 us
  Pallas kernels: 130 us -> 140 us
  local copies, waits for them, and re-layouts: 15 us -> 20.1 us
    ppermute x0 -> x21, starting transfers between devices: none -> 38.2 us  [blocked_shards(): lax.ppermute(pieces[m], 'col', [(c, c ^ m) for c in range(groups)])]
    all_to_all x5 -> x2, waiting for transfers between devices: 43.6 us -> 18.8 us  [swap(): lax.all_to_all(pieces, 'col', split_axis=0, concat_axis=0, tiled=True)]
    all_to_all x5 -> x2, starting transfers between devices: 22.6 us -> 9.72 us  [swap(): lax.all_to_all(pieces, 'col', split_axis=0, concat_axis=0, tiled=True)]
    ppermute x33, waiting for transfers between devices: 39.6 us -> 28.1 us  [cross(): return have + [lax.ppermute(h, 'root', pairs) for h in have]]
    pallas_call x6, Pallas kernels: 42.8 us -> 50 us  [the longest x3 38.2 us: left_second(): call(functools.partial(left_second_kernel, dims, masks), groups, [smem(),...]
    ppermute x0 -> x21, waiting for transfers between devices: none -> 6.76 us  [blocked_shards(): lax.ppermute(pieces[m], 'col', [(c, c ^ m) for c in range(groups)])]
    unnamed x76 -> x120, local copies, waits for them, and re-layouts: 8.82 us -> 13.9 us
  transfers between devices with their start and end apart: 45 -> 63, of which waited for: 17 -> 19; matrix products, arithmetic and copies ran while one was open for 2% -> 2% of each run, Pallas kernels for 38% -> 40%
where the time goes in v8:
time: 306 us; the launch traced here: 304 us
  Pallas kernels  140 us (46%)
  starting transfers between devices  74.2 us (24%)
  waiting for transfers between devices  68 us (22%)
  local copies, waits for them, and re-layouts  20.1 us (7%)
    pallas_call x3, Pallas kernels, left_second(): call(functools.partial(left_second_kernel, dims, masks), groups, [smem(),...  38.2 us
    ppermute x21, starting transfers between devices, blocked_shards(): lax.ppermute(pieces[m], 'col', [(c, c ^ m) for c in range(groups)])  38.2 us
    ppermute x33, waiting for transfers between devices, cross(): return have + [lax.ppermute(h, 'root', pairs) for h in have]  28.1 us
    pallas_call x1, Pallas kernels, blocked_shards(): call(functools.partial(right_first_kernel, dims, groups, owners, masks),...  25.1 us
    pallas_call x3, Pallas kernels, blocked_shards(): call(functools.partial(rotate_kernel, len(out)), groups, [smem()] + [pl.B...  21.1 us
    pallas_call x1, Pallas kernels, blocked_shards(): call(functools.partial(right_second_kernel, dims), groups, [smem(), smem(...  19.1 us
    all_to_all x2, waiting for transfers between devices, swap(): lax.all_to_all(pieces, 'col', split_axis=0, concat_axis=0, tiled=True)  18.8 us
    pallas_call x1, Pallas kernels, blocked_shards(): call(functools.partial(left_first_kernel, dims), groups, [smem(), all_cod...  17.7 us
  transfers between devices with their start and end apart: 63, of which 19 were waited for; matrix products, arithmetic and copies ran while one was open for 2% of the time, Pallas kernels for 40%

profile of v8, /device:TPU:0, one launch (start us, length us, event | category | flops | bytes accessed | tf_op | source)
XLA Modules:
  0.0 303.8 jit_solution(6390067924075811242)
XLA Ops:
  0.0 1.6 constant_dynamic-slice_fusion
  1.9 3.1 %collective-permute-start = (bf16[30,32,128]{2,1,0:T(8,128)(2,1)S(1)}, bf16[30,32,128]{2,1,0:T(8,128)(2,1)S(1)}, u32[]{:S(2)}, u32[]{:S(2)}) collective-permute-start(bf16[30,32,128]{2,1,0:T(8,128)(2,1)S(1)} %bitcast.25), channel_id=1, source_target_pairs={{0,2},{2,4},{4,6},{6,7},{7,5},{5,3},{3,1},{1,0},{8,10},{10,12},{12... | collective-permute-start | bytes 737288 | tf_op jit(solution)/shard_map/ppermute | solution.py:325
  5.0 5.9 %collective-permute-done.rest_0_ = bf16[30,32,128]{2,1,0:T(8,128)(2,1)S(1)} collective-permute-done((bf16[30,32,128]{2,1,0:T(8,128)(2,1)S(1)}, bf16[30,32,128]{2,1,0:T(8,128)(2,1)S(1)}, u32[]{:S(2)}, u32[]{:S(2)}) %collective-permute-start) | collective-permute-done | bytes 245792 | tf_op jit(solution)/shard_map/ppermute | solution.py:325
  10.9 1.7 collective-permute-start.1
  16.6 6.8 %shard_map.73 = s16[8,496,384]{2,1,0:T(8,128)(2,1)} custom-call(s32[1,2]{1,0:T(1,128)} %add_bitcast_fusion.here.place, f32[384,3072]{1,0:T(8,128)} %bitcast.19, f32[384,3072]{1,0:T(8,128)} %d_ref.4), custom_call_target="tpu_custom_call" | custom-call | bytes 14155776 | tf_op jit(solution)/shard_map/pallas_call | solution.py:306
  23.4 1.6 collective-permute-start.16
  25.5 4.4 %collective-permute-done.16.rest_16_ = bf16[30,32,128]{2,1,0:T(8,128)(2,1)S(1)} collective-permute-done((bf16[30,32,128]{2,1,0:T(8,128)(2,1)S(1)}, bf16[30,32,128]{2,1,0:T(8,128)(2,1)S(1)}, u32[]{:S(2)}, u32[]{:S(2)}) %collective-permute-start.16) | collective-permute-done | bytes 245792 | tf_op jit(solution)/shard_map/ppermute | solution.py:325
  29.9 2.0 collective-permute-start.24
  31.9 4.2 %collective-permute-done.24.rest_24_ = bf16[30,32,128]{2,1,0:T(8,128)(2,1)S(1)} collective-permute-done((bf16[30,32,128]{2,1,0:T(8,128)(2,1)S(1)}, bf16[30,32,128]{2,1,0:T(8,128)(2,1)S(1)}, u32[]{:S(2)}, u32[]{:S(2)}) %collective-permute-start.24) | collective-permute-done | bytes 245792 | tf_op jit(solution)/shard_map/ppermute | solution.py:325
  36.7 5.9 %all-to-all-start.1 = ((s16[8,496,384]{2,1,0:T(8,128)(2,1)}), s16[8,496,384]{2,1,0:T(8,128)(2,1)S(1)}, u32[]{:S(2)}, u32[]{:S(2)}) async-start(s16[8,496,384]{2,1,0:T(8,128)(2,1)} %shard_map.73), calls=%async_computation.1 | async-start | bytes 6094848 | tf_op jit(solution)/shard_map/all_to_all | solution.py:260
  47.4 4.9 %collective-permute-done.9.rest_9_ = bf16[30,32,128]{2,1,0:T(8,128)(2,1)S(1)} collective-permute-done((bf16[30,32,128]{2,1,0:T(8,128)(2,1)}, bf16[30,32,128]{2,1,0:T(8,128)(2,1)S(1)}, u32[]{:S(2)}, u32[]{:S(2)}) %collective-permute-start.9) | collective-permute-done | bytes 245792 | tf_op jit(solution)/shard_map/ppermute | solution.py:276
  53.0 4.1 %collective-permute-done.13.rest_13_ = bf16[30,32,128]{2,1,0:T(8,128)(2,1)S(1)} collective-permute-done((bf16[30,32,128]{2,1,0:T(8,128)(2,1)}, bf16[30,32,128]{2,1,0:T(8,128)(2,1)S(1)}, u32[]{:S(2)}, u32[]{:S(2)}) %collective-permute-start.13) | collective-permute-done | bytes 245792 | tf_op jit(solution)/shard_map/ppermute | solution.py:276
  61.1 5.2 %collective-permute-done.17.rest_17_ = bf16[30,32,128]{2,1,0:T(8,128)(2,1)} collective-permute-done((bf16[30,32,128]{2,1,0:T(8,128)(2,1)}, bf16[30,32,128]{2,1,0:T(8,128)(2,1)}, u32[]{:S(2)}, u32[]{:S(2)}) %collective-permute-start.17) | collective-permute-done | bytes 245792 | tf_op jit(solution)/shard_map/ppermute | solution.py:276
  66.8 4.7 %collective-permute-done.21.rest_21_ = bf16[30,32,128]{2,1,0:T(8,128)(2,1)} collective-permute-done((bf16[30,32,128]{2,1,0:T(8,128)(2,1)}, bf16[30,32,128]{2,1,0:T(8,128)(2,1)}, u32[]{:S(2)}, u32[]{:S(2)}) %collective-permute-start.21) | collective-permute-done | bytes 245792 | tf_op jit(solution)/shard_map/ppermute | solution.py:276
  71.5 4.8 %collective-permute-done.25.rest_25_ = bf16[30,32,128]{2,1,0:T(8,128)(2,1)} collective-permute-done((bf16[30,32,128]{2,1,0:T(8,128)(2,1)}, bf16[30,32,128]{2,1,0:T(8,128)(2,1)}, u32[]{:S(2)}, u32[]{:S(2)}) %collective-permute-start.25) | collective-permute-done | bytes 245792 | tf_op jit(solution)/shard_map/ppermute | solution.py:276
  77.7 2.3 copy.16
  80.0 25.1 %shard_map.74 = (f32[384,3072]{1,0:T(8,128)}, s16[8,400,384]{2,1,0:T(8,128)(2,1)}, bf16[30720,128]{1,0:T(8,128)(2,1)}) custom-call(s32[24,10]{1,0:T(8,128)} %copy.19.cols, f32[1,1]{1,0:T(1,128)} %bitcast.14.shift, s32[1,2]{1,0:T(1,128)} %add_bitcast_fusion.here.place, f32[384,3072]{1,0:T(8,128)} %bitcast.20, f32[384,3072]{1,0:T(8,128)} %d_ref.4, ...), custom_call_target="tpu_custom_call" | custom-call | flops 6039797760 | bytes 28311552 | tf_op jit(solution)/shard_map/pallas_call | solution.py:336
  105.2 2.3 all-to-all-done.1.tv_ref
  107.5 1.6 copy-done.4
  109.1 3.8 %all-to-all-start = ((s16[8,400,384]{2,1,0:T(8,128)(2,1)}), s16[8,400,384]{2,1,0:T(8,128)(2,1)S(1)}, u32[]{:S(2)}, u32[]{:S(2)}) async-start(s16[8,400,384]{2,1,0:T(8,128)(2,1)} %get-tuple-element.56), calls=%async_computation | async-start | bytes 4915200 | tf_op jit(solution)/shard_map/all_to_all | solution.py:260
  115.6 17.7 %shard_map.76.y_ref = f32[384,3072]{1,0:T(8,128)} custom-call(s32[24,10]{1,0:T(8,128)} %copy.19.cols, s16[8,496,384]{2,1,0:T(8,128)(2,1)} %copy-done.4, bf16[30720,128]{1,0:T(8,128)(2,1)} %get-tuple-element.54.tiles), custom_call_target="tpu_custom_call" | custom-call | flops 6039797760 | bytes 14155776 | tf_op jit(solution)/shard_map/pallas_call | solution.py:369
  133.9 19.1 %shard_map.75 = (f32[384,1024]{1,0:T(8,128)}, f32[384,1024]{1,0:T(8,128)}, f32[384,1024]{1,0:T(8,128)}) custom-call(s32[24,10]{1,0:T(8,128)} %copy.19.cols, f32[1,1]{1,0:T(1,128)} %bitcast.15.shift, f32[384,3072]{1,0:T(8,128)} %get-tuple-element.53.w_ref, f32[384,3072]{1,0:T(8,128)} %bitcast.21, f32[384,3072]{1,0:T(8,128)} %d_ref.4, ...), custom_call_target="tpu_custom_call" | custom-call | flops 6039797760 | bytes 23592960 | tf_op jit(solution)/shard_map/pallas_call | solution.py:358
  153.0 16.4 %all-to-all-done.tu_ref.tail_ref = s16[8,400,384]{2,1,0:T(8,128)(2,1)S(1)} async-done(((s16[8,400,384]{2,1,0:T(8,128)(2,1)}), s16[8,400,384]{2,1,0:T(8,128)(2,1)S(1)}, u32[]{:S(2)}, u32[]{:S(2)}) %all-to-all-start) | async-done | bytes 2457632 | tf_op jit(solution)/shard_map/all_to_all | solution.py:260
  170.8 12.6 %shard_map.78 = (s16[400,128]{1,0:T(8,128)(2,1)}, s16[400,128]{1,0:T(8,128)(2,1)}, s16[400,128]{1,0:T(8,128)(2,1)}, s16[400,128]{1,0:T(8,128)(2,1)}, s16[400,128...) custom-call(s32[1,2]{1,0:T(1,128)} %add_bitcast_fusion.here.place, ...), custom_call_target="tpu_custom_call" | custom-call | flops 2013265920 | bytes 6291456 | tf_op jit(solution)/shard_map/pallas_call | solution.py:394
  183.5 2.4 collective-permute-start.31
  185.9 2.4 collective-permute-start.32
  188.2 3.0 collective-permute-start.34
  191.2 12.8 %shard_map.77 = (s16[400,128]{1,0:T(8,128)(2,1)}, s16[400,128]{1,0:T(8,128)(2,1)}, s16[400,128]{1,0:T(8,128)(2,1)}, s16[400,128]{1,0:T(8,128)(2,1)}, s16[400,128...) custom-call(s32[1,2]{1,0:T(1,128)} %add_bitcast_fusion.here.place, ...), custom_call_target="tpu_custom_call" | custom-call | flops 2013265920 | bytes 6291456 | tf_op jit(solution)/shard_map/pallas_call | solution.py:394
  204.0 3.0 collective-permute-start.36
  207.6 2.3 collective-permute-start.39
  210.0 2.3 collective-permute-start.40
  213.5 2.9 collective-permute-start.42
  217.1 4.0 %shard_map.79.rest_4_.refs_0_ = s16[8,400,128]{2,1,0:T(8,128)(2,1)} custom-call(s32[1,2]{1,0:T(1,128)} %add_bitcast_fusion.here.place, f32[1,4]{1,0:T(1,128)} %bitcast.27, f32[384,1024]{1,0:T(8,128)} %get-tuple-element.55.rest_4_.p_ref, s16[400,128]{1,0:T(8,128)(2,1)} %get-tuple-element.60.after.refs_7_, s16[400,128]{1,0:T(8,128)(2,1)} %copy-done.18, ...), custom_call_target="tpu_custom_call" | custom-call | bytes 1 | tf_op jit(solution)/shard_map/pallas_call | solution.py:426
  221.0 2.4 collective-permute-start.44
  224.0 1.7 collective-permute-done.41.refs_2_
  227.2 12.8 %shard_map.80 = (s16[400,128]{1,0:T(8,128)(2,1)}, s16[400,128]{1,0:T(8,128)(2,1)}, s16[400,128]{1,0:T(8,128)(2,1)}, s16[400,128]{1,0:T(8,128)(2,1)}, s16[400,128...) custom-call(s32[1,2]{1,0:T(1,128)} %add_bitcast_fusion.here.place, ...), custom_call_target="tpu_custom_call" | custom-call | flops 2013265920 | bytes 6291456 | tf_op jit(solution)/shard_map/pallas_call | solution.py:394
  240.8 3.9 %shard_map.81.refs_1_ = s16[8,400,128]{2,1,0:T(8,128)(2,1)} custom-call(s32[1,2]{1,0:T(1,128)} %add_bitcast_fusion.here.place, f32[1,4]{1,0:T(1,128)} %bitcast.28, f32[384,1024]{1,0:T(8,128)} %get-tuple-element.69.p_ref, s16[400,128]{1,0:T(8,128)(2,1)} %get-tuple-element.70.after.refs_7_, s16[400,128]{1,0:T(8,128)(2,1)} %copy-done.15, ...), custom_call_target="tpu_custom_call" | custom-call | bytes 1 | tf_op jit(solution)/shard_map/pallas_call | solution.py:426
  245.2 2.5 collective-permute-start.49
  247.7 1.9 collective-permute-start.50
  249.6 3.3 %collective-permute-start.52 = (s16[400,128]{1,0:T(8,128)(2,1)}, s16[400,128]{1,0:T(8,128)(2,1)S(1)}, u32[]{:S(2)}, u32[]{:S(2)}) collective-permute-start(s16[400,128]{1,0:T(8,128)(2,1)} %get-tuple-element.84), channel_id=1, source_target_pairs={{0,4},{1,5},{2,6},{3,7},{4,0},{5,1},{6,2},{7,3},{8,12},{9,13},{10,... | collective-permute-start | bytes 307208 | tf_op jit(solution)/shard_map/ppermute | solution.py:423
  253.9 4.2 %collective-permute-start.53 = (s16[400,128]{1,0:T(8,128)(2,1)}, s16[400,128]{1,0:T(8,128)(2,1)S(1)}, u32[]{:S(2)}, u32[]{:S(2)}) collective-permute-start(s16[400,128]{1,0:T(8,128)(2,1)} %get-tuple-element.85), channel_id=1, source_target_pairs={{0,3},{1,2},{2,1},{3,0},{4,7},{5,6},{6,5},{7,4},{8,11},{9,10},{10,... | collective-permute-start | bytes 307208 | tf_op jit(solution)/shard_map/ppermute | solution.py:423
  258.1 3.0 collective-permute-start.54
  263.9 2.9 collective-permute-done.55.refs_6_
  267.4 3.9 %shard_map.83.refs_1_ = s16[8,400,128]{2,1,0:T(8,128)(2,1)} custom-call(s32[1,2]{1,0:T(1,128)} %add_bitcast_fusion.here.place, f32[1,4]{1,0:T(1,128)} %bitcast.29, f32[384,1024]{1,0:T(8,128)} %get-tuple-element.80.p_ref, s16[400,128]{1,0:T(8,128)(2,1)} %get-tuple-element.70.after.refs_7_, s16[400,128]{1,0:T(8,128)(2,1)} %copy-done.25, ...), custom_call_target="tpu_custom_call" | custom-call | bytes 1 | tf_op jit(solution)/shard_map/pallas_call | solution.py:426
  275.2 7.0 %shard_map.82.refs_0_ = f32[1,384,3072]{2,1,0:T(8,128)} custom-call(s32[1,2]{1,0:T(1,128)} %add_bitcast_fusion.here.place, f32[1,4]{1,0:T(1,128)} %bitcast.30, s16[8,400,128]{2,1,0:T(8,128)(2,1)} %shard_map.79.rest_4_.refs_0_, s16[8,400,128]{2,1,0:T(8,128)(2,1)} %copy-done.6, s16[8,400,128]{2,1,0:T(8,128)(2,1)} %copy-done.8, s16[8,400,128]{2,1,0:T(8,128)(2,1)} %copy-done.9), custom_call_target="tpu_custom_call" | custom-call | bytes 1 | tf_op jit(solution)/shard_map/pallas_call | solution.py:446
  284.1 7.0 %shard_map.84.refs_0_ = f32[1,384,3072]{2,1,0:T(8,128)} custom-call(s32[1,2]{1,0:T(1,128)} %add_bitcast_fusion.here.place, f32[1,4]{1,0:T(1,128)} %bitcast.31, f32[1,384,3072]{2,1,0:T(8,128)} %shard_map.82.refs_0_, s16[8,400,128]{2,1,0:T(8,128)(2,1)} %shard_map.81.refs_1_, s16[8,400,128]{2,1,0:T(8,128)(2,1)} %copy-done.7, ...), custom_call_target="tpu_custom_call", output_to_operand_aliasing={{}: (2, {})} | custom-call | bytes 1 | tf_op jit(solution)/shard_map/pallas_call | solution.py:446
  292.9 1.8 collective-permute-done.59.refs_3_
  296.8 7.0 %shard_map.85 = f32[1,384,3072]{2,1,0:T(8,128)} custom-call(s32[1,2]{1,0:T(1,128)} %add_bitcast_fusion.here.place, f32[1,4]{1,0:T(1,128)} %bitcast.32, f32[1,384,3072]{2,1,0:T(8,128)} %shard_map.84.refs_0_, s16[8,400,128]{2,1,0:T(8,128)(2,1)} %shard_map.83.refs_1_, s16[8,400,128]{2,1,0:T(8,128)(2,1)} %copy-done.10, ...), custom_call_target="tpu_custom_call", output_to_operand_aliasing={{}: (2, {})} | custom-call | bytes 1 | tf_op jit(solution)/shard_map/pallas_call | solution.py:446
  (219 shorter events, 40.5 us)
Async XLA Ops:
  1.9 9.0 %collective-permute-start = (bf16[30,32,128]{2,1,0:T(8,128)(2,1)S(1)}, bf16[30,32,128]{2,1,0:T(8,128)(2,1)S(1)}, u32[]{:S(2)}, u32[]{:S(2)}) collective-permute-start(bf16[30,32,128]{2,1,0:T(8,128)(2,1)S(1)} %bitcast.25), channel_id=1, source_target_pairs={{0,2},{2,4},{4,6},{6,7},{7,5},{5,3},{3,1},{1,0},{8,10},{10,12},{12... | collective-permute-start | bytes 737288 | tf_op jit(solution)/shard_map/ppermute | solution.py:325
  10.9 12.4 %collective-permute-start.1 = (bf16[30,32,128]{2,1,0:T(8,128)(2,1)S(1)}, bf16[30,32,128]{2,1,0:T(8,128)(2,1)S(1)}, u32[]{:S(2)}, u32[]{:S(2)}) collective-permute-start(bf16[30,32,128]{2,1,0:T(8,128)(2,1)S(1)} %collective-permute-done.rest_0_), channel_id=1, source_target_pairs={{0,16},{8,24},{16,0},{24,8},{1,17},{9,25},{17,1},{25,9},{2,18},{10... | collective-permute-start | bytes 737288 | tf_op jit(solution)/shard_map/ppermute | solution.py:276
  12.6 10.7 %collective-permute-start.5 = (bf16[30,32,128]{2,1,0:T(8,128)(2,1)S(1)}, bf16[30,32,128]{2,1,0:T(8,128)(2,1)S(1)}, u32[]{:S(2)}, u32[]{:S(2)}) collective-permute-start(bf16[30,32,128]{2,1,0:T(8,128)(2,1)S(1)} %collective-permute-done.4.rest_4_), channel_id=1, source_target_pairs={{0,16},{8,24},{16,0},{24,8},{1,17},{9,25},{17,1},{25,9},{2,18},{10... | collective-permute-start | bytes 737288 | tf_op jit(solution)/shard_map/ppermute | solution.py:276
  13.9 9.5 %collective-permute-start.8 = (bf16[30,32,128]{2,1,0:T(8,128)(2,1)S(1)}, bf16[30,32,128]{2,1,0:T(8,128)(2,1)S(1)}, u32[]{:S(2)}, u32[]{:S(2)}) collective-permute-start(bf16[30,32,128]{2,1,0:T(8,128)(2,1)S(1)} %collective-permute-done.rest_0_), channel_id=1, source_target_pairs={{0,2},{2,4},{4,6},{6,7},{7,5},{5,3},{3,1},{1,0},{8,10},{10,12},{12... | collective-permute-start | bytes 737288 | tf_op jit(solution)/shard_map/ppermute | solution.py:325
  15.5 7.9 %collective-permute-start.12 = (bf16[30,32,128]{2,1,0:T(8,128)(2,1)S(1)}, bf16[30,32,128]{2,1,0:T(8,128)(2,1)S(1)}, u32[]{:S(2)}, u32[]{:S(2)}) collective-permute-start(bf16[30,32,128]{2,1,0:T(8,128)(2,1)S(1)} %collective-permute-done.4.rest_4_), channel_id=1, source_target_pairs={{0,1},{2,0},{4,2},{6,4},{7,6},{5,7},{3,5},{1,3},{8,9},{10,8},{12,1... | collective-permute-start | bytes 737288 | tf_op jit(solution)/shard_map/ppermute | solution.py:325
  36.7 70.7 %all-to-all-start.1 = ((s16[8,496,384]{2,1,0:T(8,128)(2,1)}), s16[8,496,384]{2,1,0:T(8,128)(2,1)S(1)}, u32[]{:S(2)}, u32[]{:S(2)}) async-start(s16[8,496,384]{2,1,0:T(8,128)(2,1)} %shard_map.73), calls=%async_computation.1 | async-start | bytes 6094848 | tf_op jit(solution)/shard_map/all_to_all | solution.py:260
  43.3 9.0 %collective-permute-start.9 = (bf16[30,32,128]{2,1,0:T(8,128)(2,1)}, bf16[30,32,128]{2,1,0:T(8,128)(2,1)S(1)}, u32[]{:S(2)}, u32[]{:S(2)}) collective-permute-start(bf16[30,32,128]{2,1,0:T(8,128)(2,1)} %copy-done.41), channel_id=1, source_target_pairs={{0,16},{8,24},{16,0},{24,8},{1,17},{9,25},{17,1},{25,9},{2,18},{10... | collective-permute-start | bytes 737288 | tf_op jit(solution)/shard_map/ppermute | solution.py:276
  44.8 12.3 %collective-permute-start.13 = (bf16[30,32,128]{2,1,0:T(8,128)(2,1)}, bf16[30,32,128]{2,1,0:T(8,128)(2,1)S(1)}, u32[]{:S(2)}, u32[]{:S(2)}) collective-permute-start(bf16[30,32,128]{2,1,0:T(8,128)(2,1)} %copy-done.42), channel_id=1, source_target_pairs={{0,16},{8,24},{16,0},{24,8},{1,17},{9,25},{17,1},{25,9},{2,18},{10... | collective-permute-start | bytes 737288 | tf_op jit(solution)/shard_map/ppermute | solution.py:276
  45.4 11.8 %collective-permute-start.7 = (bf16[30,32,128]{2,1,0:T(8,128)(2,1)}, bf16[30,32,128]{2,1,0:T(8,128)(2,1)S(1)}, u32[]{:S(2)}, u32[]{:S(2)}) collective-permute-start(bf16[30,32,128]{2,1,0:T(8,128)(2,1)} %copy-done.40), channel_id=1, source_target_pairs={{0,8},{8,0},{16,24},{24,16},{1,9},{9,1},{17,25},{25,17},{2,10},{10... | collective-permute-start | bytes 737288 | tf_op jit(solution)/shard_map/ppermute | solution.py:276
  46.1 12.6 %collective-permute-start.10 = (bf16[30,32,128]{2,1,0:T(8,128)(2,1)}, bf16[30,32,128]{2,1,0:T(8,128)(2,1)S(1)}, u32[]{:S(2)}, u32[]{:S(2)}) collective-permute-start(bf16[30,32,128]{2,1,0:T(8,128)(2,1)} %copy-done.41), channel_id=1, source_target_pairs={{0,8},{8,0},{16,24},{24,16},{1,9},{9,1},{17,25},{25,17},{2,10},{10... | collective-permute-start | bytes 737288 | tf_op jit(solution)/shard_map/ppermute | solution.py:276
  47.4 11.4 %collective-permute-start.14 = (bf16[30,32,128]{2,1,0:T(8,128)(2,1)}, bf16[30,32,128]{2,1,0:T(8,128)(2,1)S(1)}, u32[]{:S(2)}, u32[]{:S(2)}) collective-permute-start(bf16[30,32,128]{2,1,0:T(8,128)(2,1)} %copy-done.42), channel_id=1, source_target_pairs={{0,8},{8,0},{16,24},{24,16},{1,9},{9,1},{17,25},{25,17},{2,10},{10... | collective-permute-start | bytes 737288 | tf_op jit(solution)/shard_map/ppermute | solution.py:276
  57.1 9.1 %collective-permute-start.17 = (bf16[30,32,128]{2,1,0:T(8,128)(2,1)}, bf16[30,32,128]{2,1,0:T(8,128)(2,1)}, u32[]{:S(2)}, u32[]{:S(2)}) collective-permute-start(bf16[30,32,128]{2,1,0:T(8,128)(2,1)} %copy-done.43), channel_id=1, source_target_pairs={{0,16},{8,24},{16,0},{24,8},{1,17},{9,25},{17,1},{25,9},{2,18},{10... | collective-permute-start | bytes 737288 | tf_op jit(solution)/shard_map/ppermute | solution.py:276
  58.9 12.7 %collective-permute-start.21 = (bf16[30,32,128]{2,1,0:T(8,128)(2,1)}, bf16[30,32,128]{2,1,0:T(8,128)(2,1)}, u32[]{:S(2)}, u32[]{:S(2)}) collective-permute-start(bf16[30,32,128]{2,1,0:T(8,128)(2,1)} %copy-done.44), channel_id=1, source_target_pairs={{0,16},{8,24},{16,0},{24,8},{1,17},{9,25},{17,1},{25,9},{2,18},{10... | collective-permute-start | bytes 737288 | tf_op jit(solution)/shard_map/ppermute | solution.py:276
  59.4 16.9 %collective-permute-start.25 = (bf16[30,32,128]{2,1,0:T(8,128)(2,1)}, bf16[30,32,128]{2,1,0:T(8,128)(2,1)}, u32[]{:S(2)}, u32[]{:S(2)}) collective-permute-start(bf16[30,32,128]{2,1,0:T(8,128)(2,1)} %copy-done.45), channel_id=1, source_target_pairs={{0,16},{8,24},{16,0},{24,8},{1,17},{9,25},{17,1},{25,9},{2,18},{10... | collective-permute-start | bytes 737288 | tf_op jit(solution)/shard_map/ppermute | solution.py:276
  61.0 19.0 %collective-permute-start.22 = (bf16[30,32,128]{2,1,0:T(8,128)(2,1)}, bf16[30,32,128]{2,1,0:T(8,128)(2,1)}, u32[]{:S(2)}, u32[]{:S(2)}) collective-permute-start(bf16[30,32,128]{2,1,0:T(8,128)(2,1)} %copy-done.44), channel_id=1, source_target_pairs={{0,8},{8,0},{16,24},{24,16},{1,9},{9,1},{17,25},{25,17},{2,10},{10... | collective-permute-start | bytes 737288 | tf_op jit(solution)/shard_map/ppermute | solution.py:276
  66.3 13.7 %collective-permute-start.26 = (bf16[30,32,128]{2,1,0:T(8,128)(2,1)}, bf16[30,32,128]{2,1,0:T(8,128)(2,1)}, u32[]{:S(2)}, u32[]{:S(2)}) collective-permute-start(bf16[30,32,128]{2,1,0:T(8,128)(2,1)} %copy-done.45), channel_id=1, source_target_pairs={{0,8},{8,0},{16,24},{24,16},{1,9},{9,1},{17,25},{25,17},{2,10},{10... | collective-permute-start | bytes 737288 | tf_op jit(solution)/shard_map/ppermute | solution.py:276
  66.3 13.7 %collective-permute-start.19 = (bf16[30,32,128]{2,1,0:T(8,128)(2,1)}, bf16[30,32,128]{2,1,0:T(8,128)(2,1)}, u32[]{:S(2)}, u32[]{:S(2)}) collective-permute-start(bf16[30,32,128]{2,1,0:T(8,128)(2,1)} %collective-permute-done.17.rest_17_), channel_id=1, source_target_pairs={{0,8},{8,0},{16,24},{24,16},{1,9},{9,1},{17,25},{25,17},{2,10},{10... | collective-permute-start | bytes 737288 | tf_op jit(solution)/shard_map/ppermute | solution.py:276
  71.5 8.4 %collective-permute-start.23 = (bf16[30,32,128]{2,1,0:T(8,128)(2,1)}, bf16[30,32,128]{2,1,0:T(8,128)(2,1)}, u32[]{:S(2)}, u32[]{:S(2)}) collective-permute-start(bf16[30,32,128]{2,1,0:T(8,128)(2,1)} %collective-permute-done.21.rest_21_), channel_id=1, source_target_pairs={{0,8},{8,0},{16,24},{24,16},{1,9},{9,1},{17,25},{25,17},{2,10},{10... | collective-permute-start | bytes 737288 | tf_op jit(solution)/shard_map/ppermute | solution.py:276
  109.1 60.3 %all-to-all-start = ((s16[8,400,384]{2,1,0:T(8,128)(2,1)}), s16[8,400,384]{2,1,0:T(8,128)(2,1)S(1)}, u32[]{:S(2)}, u32[]{:S(2)}) async-start(s16[8,400,384]{2,1,0:T(8,128)(2,1)} %get-tuple-element.56), calls=%async_computation | async-start | bytes 4915200 | tf_op jit(solution)/shard_map/all_to_all | solution.py:260
  114.1 19.2 %collective-permute-start.28 = (s16[8,96,384]{2,1,0:T(8,128)(2,1)S(1)}, s16[8,96,384]{2,1,0:T(8,128)(2,1)}, u32[]{:S(2)}, u32[]{:S(2)}) collective-permute-start(s16[8,96,384]{2,1,0:T(8,128)(2,1)S(1)} %slice.6.rest_0_), channel_id=1, source_target_pairs={{0,16},{8,24},{16,0},{24,8},{1,17},{9,25},{17,1},{25,9},{2,18},{10... | collective-permute-start | bytes 1769480 | tf_op jit(solution)/shard_map/ppermute | solution.py:276
  133.3 36.1 %collective-permute-start.29 = (s16[8,96,384]{2,1,0:T(8,128)(2,1)S(1)}, s16[8,96,384]{2,1,0:T(8,128)(2,1)}, u32[]{:S(2)}, u32[]{:S(2)}) collective-permute-start(s16[8,96,384]{2,1,0:T(8,128)(2,1)S(1)} %slice.6.rest_0_), channel_id=1, source_target_pairs={{0,8},{8,0},{16,24},{24,16},{1,9},{9,1},{17,25},{25,17},{2,10},{10... | collective-permute-start | bytes 1769480 | tf_op jit(solution)/shard_map/ppermute | solution.py:276
  133.4 36.0 %collective-permute-start.30 = (s16[8,96,384]{2,1,0:T(8,128)(2,1)}, s16[8,96,384]{2,1,0:T(8,128)(2,1)}, u32[]{:S(2)}, u32[]{:S(2)}) collective-permute-start(s16[8,96,384]{2,1,0:T(8,128)(2,1)} %collective-permute-done.28.rest_1_), channel_id=1, source_target_pairs={{0,8},{8,0},{16,24},{24,16},{1,9},{9,1},{17,25},{25,17},{2,10},{10... | collective-permute-start | bytes 1769480 | tf_op jit(solution)/shard_map/ppermute | solution.py:276
  183.5 20.5 %collective-permute-start.31 = (s16[400,128]{1,0:T(8,128)(2,1)}, s16[400,128]{1,0:T(8,128)(2,1)S(1)}, u32[]{:S(2)}, u32[]{:S(2)}) collective-permute-start(s16[400,128]{1,0:T(8,128)(2,1)} %get-tuple-element.61), channel_id=1, source_target_pairs={{0,7},{1,6},{2,5},{3,4},{4,3},{5,2},{6,1},{7,0},{8,15},{9,14},{10,... | collective-permute-start | bytes 307208 | tf_op jit(solution)/shard_map/ppermute | solution.py:423
  185.9 21.1 %collective-permute-start.32 = (s16[400,128]{1,0:T(8,128)(2,1)}, s16[400,128]{1,0:T(8,128)(2,1)S(1)}, u32[]{:S(2)}, u32[]{:S(2)}) collective-permute-start(s16[400,128]{1,0:T(8,128)(2,1)} %get-tuple-element.62), channel_id=1, source_target_pairs={{0,6},{1,7},{2,4},{3,5},{4,2},{5,3},{6,0},{7,1},{8,14},{9,15},{10,... | collective-permute-start | bytes 307208 | tf_op jit(solution)/shard_map/ppermute | solution.py:423
  188.2 19.4 %collective-permute-start.33 = (s16[400,128]{1,0:T(8,128)(2,1)}, s16[400,128]{1,0:T(8,128)(2,1)S(1)}, u32[]{:S(2)}, u32[]{:S(2)}) collective-permute-start(s16[400,128]{1,0:T(8,128)(2,1)} %get-tuple-element.63), channel_id=1, source_target_pairs={{0,5},{1,4},{2,7},{3,6},{4,1},{5,0},{6,3},{7,2},{8,13},{9,12},{10,... | collective-permute-start | bytes 307208 | tf_op jit(solution)/shard_map/ppermute | solution.py:423
  188.2 21.7 %collective-permute-start.34 = (s16[400,128]{1,0:T(8,128)(2,1)}, s16[400,128]{1,0:T(8,128)(2,1)S(1)}, u32[]{:S(2)}, u32[]{:S(2)}) collective-permute-start(s16[400,128]{1,0:T(8,128)(2,1)} %get-tuple-element.64), channel_id=1, source_target_pairs={{0,4},{1,5},{2,6},{3,7},{4,0},{5,1},{6,2},{7,3},{8,12},{9,13},{10,... | collective-permute-start | bytes 307208 | tf_op jit(solution)/shard_map/ppermute | solution.py:423
  191.2 21.1 %collective-permute-start.35 = (s16[400,128]{1,0:T(8,128)(2,1)}, s16[400,128]{1,0:T(8,128)(2,1)S(1)}, u32[]{:S(2)}, u32[]{:S(2)}) collective-permute-start(s16[400,128]{1,0:T(8,128)(2,1)} %get-tuple-element.65), channel_id=1, source_target_pairs={{0,3},{1,2},{2,1},{3,0},{4,7},{5,6},{6,5},{7,4},{8,11},{9,10},{10,... | collective-permute-start | bytes 307208 | tf_op jit(solution)/shard_map/ppermute | solution.py:423
  204.0 9.5 %collective-permute-start.36 = (s16[400,128]{1,0:T(8,128)(2,1)S(1)}, s16[400,128]{1,0:T(8,128)(2,1)S(1)}, u32[]{:S(2)}, u32[]{:S(2)}) collective-permute-start(s16[400,128]{1,0:T(8,128)(2,1)S(1)} %copy-done.57), channel_id=1, source_target_pairs={{0,2},{1,3},{2,0},{3,1},{4,6},{5,7},{6,4},{7,5},{8,10},{9,11},{10,... | collective-permute-start | bytes 307208 | tf_op jit(solution)/shard_map/ppermute | solution.py:423
  206.9 9.5 %collective-permute-start.37 = (s16[400,128]{1,0:T(8,128)(2,1)S(1)}, s16[400,128]{1,0:T(8,128)(2,1)S(1)}, u32[]{:S(2)}, u32[]{:S(2)}) collective-permute-start(s16[400,128]{1,0:T(8,128)(2,1)S(1)} %copy-done.56), channel_id=1, source_target_pairs={{0,1},{1,0},{2,3},{3,2},{4,5},{5,4},{6,7},{7,6},{8,9},{9,8},{10,11... | collective-permute-start | bytes 307208 | tf_op jit(solution)/shard_map/ppermute | solution.py:423
  207.6 13.4 %collective-permute-start.39 = (s16[400,128]{1,0:T(8,128)(2,1)}, s16[400,128]{1,0:T(8,128)(2,1)S(1)}, u32[]{:S(2)}, u32[]{:S(2)}) collective-permute-start(s16[400,128]{1,0:T(8,128)(2,1)} %get-tuple-element.71), channel_id=1, source_target_pairs={{0,7},{1,6},{2,5},{3,4},{4,3},{5,2},{6,1},{7,0},{8,15},{9,14},{10,... | collective-permute-start | bytes 307208 | tf_op jit(solution)/shard_map/ppermute | solution.py:423
  210.0 13.5 %collective-permute-start.40 = (s16[400,128]{1,0:T(8,128)(2,1)}, s16[400,128]{1,0:T(8,128)(2,1)S(1)}, u32[]{:S(2)}, u32[]{:S(2)}) collective-permute-start(s16[400,128]{1,0:T(8,128)(2,1)} %get-tuple-element.72), channel_id=1, source_target_pairs={{0,6},{1,7},{2,4},{3,5},{4,2},{5,3},{6,0},{7,1},{8,14},{9,15},{10,... | collective-permute-start | bytes 307208 | tf_op jit(solution)/shard_map/ppermute | solution.py:423
  212.3 13.4 %collective-permute-start.41 = (s16[400,128]{1,0:T(8,128)(2,1)}, s16[400,128]{1,0:T(8,128)(2,1)S(1)}, u32[]{:S(2)}, u32[]{:S(2)}) collective-permute-start(s16[400,128]{1,0:T(8,128)(2,1)} %get-tuple-element.73), channel_id=1, source_target_pairs={{0,5},{1,4},{2,7},{3,6},{4,1},{5,0},{6,3},{7,2},{8,13},{9,12},{10,... | collective-permute-start | bytes 307208 | tf_op jit(solution)/shard_map/ppermute | solution.py:423
  213.5 26.5 %collective-permute-start.42 = (s16[400,128]{1,0:T(8,128)(2,1)}, s16[400,128]{1,0:T(8,128)(2,1)S(1)}, u32[]{:S(2)}, u32[]{:S(2)}) collective-permute-start(s16[400,128]{1,0:T(8,128)(2,1)} %get-tuple-element.74), channel_id=1, source_target_pairs={{0,4},{1,5},{2,6},{3,7},{4,0},{5,1},{6,2},{7,3},{8,12},{9,13},{10,... | collective-permute-start | bytes 307208 | tf_op jit(solution)/shard_map/ppermute | solution.py:423
  216.4 23.6 %collective-permute-start.43 = (s16[400,128]{1,0:T(8,128)(2,1)}, s16[400,128]{1,0:T(8,128)(2,1)S(1)}, u32[]{:S(2)}, u32[]{:S(2)}) collective-permute-start(s16[400,128]{1,0:T(8,128)(2,1)} %get-tuple-element.75), channel_id=1, source_target_pairs={{0,3},{1,2},{2,1},{3,0},{4,7},{5,6},{6,5},{7,4},{8,11},{9,10},{10,... | collective-permute-start | bytes 307208 | tf_op jit(solution)/shard_map/ppermute | solution.py:423
  221.0 19.0 %collective-permute-start.44 = (s16[400,128]{1,0:T(8,128)(2,1)}, s16[400,128]{1,0:T(8,128)(2,1)S(1)}, u32[]{:S(2)}, u32[]{:S(2)}) collective-permute-start(s16[400,128]{1,0:T(8,128)(2,1)} %get-tuple-element.76), channel_id=1, source_target_pairs={{0,2},{1,3},{2,0},{3,1},{4,6},{5,7},{6,4},{7,5},{8,10},{9,11},{10,... | collective-permute-start | bytes 307208 | tf_op jit(solution)/shard_map/ppermute | solution.py:423
  223.4 16.7 %collective-permute-start.45 = (s16[400,128]{1,0:T(8,128)(2,1)}, s16[400,128]{1,0:T(8,128)(2,1)S(1)}, u32[]{:S(2)}, u32[]{:S(2)}) collective-permute-start(s16[400,128]{1,0:T(8,128)(2,1)} %get-tuple-element.77), channel_id=1, source_target_pairs={{0,1},{1,0},{2,3},{3,2},{4,5},{5,4},{6,7},{7,6},{8,9},{9,8},{10,11... | collective-permute-start | bytes 307208 | tf_op jit(solution)/shard_map/ppermute | solution.py:423
  225.7 23.9 %collective-permute-start.38 = (s16[8,400,128]{2,1,0:T(8,128)(2,1)}, s16[8,400,128]{2,1,0:T(8,128)(2,1)S(1)}, u32[]{:S(2)}, u32[]{:S(2)}) collective-permute-start(s16[8,400,128]{2,1,0:T(8,128)(2,1)} %shard_map.79.rest_4_.refs_0_), channel_id=1, source_target_pairs={{0,16},{8,24},{16,0},{24,8},{1,17},{9,25},{17,1},{25,9},{2,18},{10... | collective-permute-start | bytes 2457608 | tf_op jit(solution)/shard_map/ppermute | solution.py:276
  244.7 26.7 %collective-permute-start.48 = (s16[8,400,128]{2,1,0:T(8,128)(2,1)}, s16[8,400,128]{2,1,0:T(8,128)(2,1)S(1)}, u32[]{:S(2)}, u32[]{:S(2)}) collective-permute-start(s16[8,400,128]{2,1,0:T(8,128)(2,1)} %shard_map.81.refs_1_), channel_id=1, source_target_pairs={{0,16},{8,24},{16,0},{24,8},{1,17},{9,25},{17,1},{25,9},{2,18},{10... | collective-permute-start | bytes 2457608 | tf_op jit(solution)/shard_map/ppermute | solution.py:276
  245.2 8.7 %collective-permute-start.49 = (s16[400,128]{1,0:T(8,128)(2,1)}, s16[400,128]{1,0:T(8,128)(2,1)S(1)}, u32[]{:S(2)}, u32[]{:S(2)}) collective-permute-start(s16[400,128]{1,0:T(8,128)(2,1)} %get-tuple-element.81), channel_id=1, source_target_pairs={{0,7},{1,6},{2,5},{3,4},{4,3},{5,2},{6,1},{7,0},{8,15},{9,14},{10,... | collective-permute-start | bytes 307208 | tf_op jit(solution)/shard_map/ppermute | solution.py:423
  247.7 10.4 %collective-permute-start.50 = (s16[400,128]{1,0:T(8,128)(2,1)}, s16[400,128]{1,0:T(8,128)(2,1)S(1)}, u32[]{:S(2)}, u32[]{:S(2)}) collective-permute-start(s16[400,128]{1,0:T(8,128)(2,1)} %get-tuple-element.82), channel_id=1, source_target_pairs={{0,6},{1,7},{2,4},{3,5},{4,2},{5,3},{6,0},{7,1},{8,14},{9,15},{10,... | collective-permute-start | bytes 307208 | tf_op jit(solution)/shard_map/ppermute | solution.py:423
  249.6 12.4 %collective-permute-start.51 = (s16[400,128]{1,0:T(8,128)(2,1)}, s16[400,128]{1,0:T(8,128)(2,1)S(1)}, u32[]{:S(2)}, u32[]{:S(2)}) collective-permute-start(s16[400,128]{1,0:T(8,128)(2,1)} %get-tuple-element.83), channel_id=1, source_target_pairs={{0,5},{1,4},{2,7},{3,6},{4,1},{5,0},{6,3},{7,2},{8,13},{9,12},{10,... | collective-permute-start | bytes 307208 | tf_op jit(solution)/shard_map/ppermute | solution.py:423
  249.6 13.7 %collective-permute-start.52 = (s16[400,128]{1,0:T(8,128)(2,1)}, s16[400,128]{1,0:T(8,128)(2,1)S(1)}, u32[]{:S(2)}, u32[]{:S(2)}) collective-permute-start(s16[400,128]{1,0:T(8,128)(2,1)} %get-tuple-element.84), channel_id=1, source_target_pairs={{0,4},{1,5},{2,6},{3,7},{4,0},{5,1},{6,2},{7,3},{8,12},{9,13},{10,... | collective-permute-start | bytes 307208 | tf_op jit(solution)/shard_map/ppermute | solution.py:423
  253.9 9.7 %collective-permute-start.53 = (s16[400,128]{1,0:T(8,128)(2,1)}, s16[400,128]{1,0:T(8,128)(2,1)S(1)}, u32[]{:S(2)}, u32[]{:S(2)}) collective-permute-start(s16[400,128]{1,0:T(8,128)(2,1)} %get-tuple-element.85), channel_id=1, source_target_pairs={{0,3},{1,2},{2,1},{3,0},{4,7},{5,6},{6,5},{7,4},{8,11},{9,10},{10,... | collective-permute-start | bytes 307208 | tf_op jit(solution)/shard_map/ppermute | solution.py:423
  263.3 10.1 %collective-permute-start.46 = (s16[8,400,128]{2,1,0:T(8,128)(2,1)S(1)}, s16[8,400,128]{2,1,0:T(8,128)(2,1)S(1)}, u32[]{:S(2)}, u32[]{:S(2)}) collective-permute-start(s16[8,400,128]{2,1,0:T(8,128)(2,1)S(1)} %copy-done.3), channel_id=1, source_target_pairs={{0,8},{8,0},{16,24},{24,16},{1,9},{9,1},{17,25},{25,17},{2,10},{10... | collective-permute-start | bytes 2457608 | tf_op jit(solution)/shard_map/ppermute | solution.py:276
  263.6 9.8 %collective-permute-start.47 = (s16[8,400,128]{2,1,0:T(8,128)(2,1)S(1)}, s16[8,400,128]{2,1,0:T(8,128)(2,1)S(1)}, u32[]{:S(2)}, u32[]{:S(2)}) collective-permute-start(s16[8,400,128]{2,1,0:T(8,128)(2,1)S(1)} %collective-permute-done.38.refs_1_), channel_id=1, source_target_pairs={{0,8},{8,0},{16,24},{24,16},{1,9},{9,1},{17,25},{25,17},{2,10},{10... | collective-permute-start | bytes 2457608 | tf_op jit(solution)/shard_map/ppermute | solution.py:276
  271.4 10.9 %collective-permute-start.56 = (s16[8,400,128]{2,1,0:T(8,128)(2,1)}, s16[8,400,128]{2,1,0:T(8,128)(2,1)S(1)}, u32[]{:S(2)}, u32[]{:S(2)}) collective-permute-start(s16[8,400,128]{2,1,0:T(8,128)(2,1)} %shard_map.81.refs_1_), channel_id=1, source_target_pairs={{0,8},{8,0},{16,24},{24,16},{1,9},{9,1},{17,25},{25,17},{2,10},{10... | collective-permute-start | bytes 2457608 | tf_op jit(solution)/shard_map/ppermute | solution.py:276
  271.4 10.8 %collective-permute-start.57 = (s16[8,400,128]{2,1,0:T(8,128)(2,1)S(1)}, s16[8,400,128]{2,1,0:T(8,128)(2,1)S(1)}, u32[]{:S(2)}, u32[]{:S(2)}) collective-permute-start(s16[8,400,128]{2,1,0:T(8,128)(2,1)S(1)} %collective-permute-done.48.refs_2_), channel_id=1, source_target_pairs={{0,8},{8,0},{16,24},{24,16},{1,9},{9,1},{17,25},{25,17},{2,10},{10... | collective-permute-start | bytes 2457608 | tf_op jit(solution)/shard_map/ppermute | solution.py:276
  271.9 20.4 %collective-permute-start.58 = (s16[8,400,128]{2,1,0:T(8,128)(2,1)}, s16[8,400,128]{2,1,0:T(8,128)(2,1)S(1)}, u32[]{:S(2)}, u32[]{:S(2)}) collective-permute-start(s16[8,400,128]{2,1,0:T(8,128)(2,1)} %shard_map.83.refs_1_), channel_id=1, source_target_pairs={{0,16},{8,24},{16,0},{24,8},{1,17},{9,25},{17,1},{25,9},{2,18},{10... | collective-permute-start | bytes 2457608 | tf_op jit(solution)/shard_map/ppermute | solution.py:276
  (74 other events, 807.7 us)

commit v9 on v7

--- a/solution.py
+++ b/solution.py
@@ -93,7 +93,7 @@
 
 def right_first_kernel(dims, groups, owners, masks, cols, shift, place, v_ref, d_ref, own, *rest):
     nblk, fill, blk, per = dims
-    shards, (w_ref, u_ref, tiles_ref, halves, turned, tiles) = rest[:-6], rest[-6:]
+    shards, (w_ref, u_ref, more_ref, tiles_ref, halves, turned, tiles) = rest[:-7], rest[-7:]
     step = pl.program_id(0)
     size = own.shape[0]
 
@@ -128,7 +128,9 @@
         whole = moved + (d_ref[:, lanes] - shift[0, 0]) * here
         w_ref[:, lanes] = whole
         turned[lanes, :] = (moved + whole).T
-    put(u_ref, 0, turned[...])
+    first = u_ref.shape[1] - PAD
+    put(u_ref, 0, turned[:first])
+    put(more_ref, 0, turned[first:])
 
 
 def left_first_kernel(dims, cols, tv_ref, tiles, y_ref, halves):
@@ -146,8 +148,9 @@
         y_ref[:, t * blk : (t + 1) * blk] = apply_row(halves, tiles, t, cols, step * per + t, fill, blk)
 
 
-def right_second_kernel(dims, cols, shift, w_ref, v_ref, d_ref, tiles, *rest):
+def right_second_kernel(dims, cols, shift, w_ref, v_ref, d_ref, tiles, after, *rest):
     nblk, fill, blk, per = dims
+    del after
     outs, halves = rest[:-1], rest[-1]
     step = pl.program_id(0)
 
@@ -317,16 +320,20 @@
 
     once = pl.Buffered(1)
     shard_spec = pl.BlockSpec(mine.shape, lambda q: (0, 0, 0), pipeline_mode=once)
-    w, tu, tiles = call(
+    part = width // chunks
+    w, tu, more, tiles = call(
         functools.partial(right_first_kernel, dims, groups, owners, masks),
         groups,
         [smem(), smem(), smem(), whole, piece]
         + [pl.BlockSpec(string_blocks.shape, lambda q: (0, 0), pipeline_mode=once)]
         + [shard_spec] * len(shards),
-        [piece, coded, tile_spec],
+        [piece]
+        + [pl.BlockSpec((1, n + PAD, rows), lambda q: (q, 0, 0)) for n in (part, width - part)]
+        + [tile_spec],
         [
             row_shape,
-            codes_shape,
+            jax.ShapeDtypeStruct((groups, part + PAD, rows), i16),
+            jax.ShapeDtypeStruct((groups, width - part + PAD, rows), i16),
             jax.ShapeDtypeStruct((nblk * fill * blk, blk), string_blocks.dtype),
         ],
         [
@@ -338,17 +345,18 @@
         size * 6,
     )(block_cols, energy, place, start, diagonal, own, *shards)
     tu = swap(tu)
+    more = swap(lax.optimization_barrier((more, tu))[0])
 
     base = call(
         functools.partial(right_second_kernel, dims),
         groups,
-        [smem(), smem(), whole, piece, piece, tile_spec],
+        [smem(), smem(), whole, piece, piece, tile_spec, pl.BlockSpec(memory_space=pl.ANY)],
         [pl.BlockSpec((rows, blk), lambda q: (0, q))] * chunks,
         [jax.ShapeDtypeStruct((rows, groups * blk), f32)] * chunks,
         [row_halves],
         work,
         size * 5,
-    )(block_cols, energy, w, start, diagonal, tiles)
+    )(block_cols, energy, w, start, diagonal, tiles, tu)
 
     y = call(
         functools.partial(left_first_kernel, dims),
@@ -363,12 +371,12 @@
 
     half = roots // 2
     slabs = exchange(cross([tv[:, width + PAD :]], half), half // 2, y)
-    part = width // chunks
     chunk_coded = pl.BlockSpec((1, rows + PAD, part), lambda q: (q, 0, 0))
     many = 4 if groups % 4 == 0 else 1
     many_coded = pl.BlockSpec((many, rows + PAD, part), lambda q: (q, 0, 0))
     seconds, crossings = [], []
     for k in range(chunks):
+        source, at, n = (more, k - 1, width - part) if k else (tu, 0, part)
         z = call(
             functools.partial(left_second_kernel, dims, masks),
             groups,
@@ -376,8 +384,8 @@
                 smem(),
                 smem(),
                 smem(),
-                pl.BlockSpec((groups, part, rows), lambda q, k=k: (0, k, 0), pipeline_mode=once),
-                pl.BlockSpec((groups, PAD, rows), lambda q: (0, width // PAD, 0), pipeline_mode=once),
+                pl.BlockSpec((groups, part, rows), lambda q, at=at: (0, at, 0), pipeline_mode=once),
+                pl.BlockSpec((groups, PAD, rows), lambda q, n=n: (0, n // PAD, 0), pipeline_mode=once),
                 pl.BlockSpec((part, strings), lambda q, k=k: (k, 0), pipeline_mode=once),
                 tile_spec,
             ]
@@ -388,7 +396,7 @@
             [pltpu.VMEM((nblk, 2 * part, blk), jnp.bfloat16), pltpu.VMEM((rows, part), f32)],
             work // chunks,
             size * 4 // chunks,
-        )(block_cols, energy, place, tu, tu, y, tiles, *slabs, base[0] if k < 2 else seconds[k - 2])
+        )(block_cols, energy, place, source, source, y, tiles, *slabs, base[0] if k < 2 else seconds[k - 2])
         if k > 1:
             z = lax.optimization_barrier((z, *crossings[k - 2]))[0]
         second = call(
@@ -464,7 +472,7 @@
         rows, strings = coeffs.shape[1:]
         blk = strings // block_cols.shape[0]
         width = strings // groups
-        regular = blk % LANES == 0 and width % blk == 0 and rows == width
+        regular = blk % LANES == 0 and width % blk == 0 and rows == width > blk
         regular = regular and roots > 1 and roots & (roots - 1) == 0 and width % (16 * roots) == 0
         regular = regular and groups % 2 == 0 and blk % (16 * roots) == 0
         args = (coeffs, diagonal, shift, rotation, string_blocks, block_cols)

time: 298 us -> 362 us (1.21)
  waiting for transfers between devices: 98.5 us -> 165 us
  local copies, waits for them, and re-layouts: 15 us -> 11 us
    all_to_all x5 -> x6, waiting for transfers between devices: 43.6 us -> 117 us  [swap(): lax.all_to_all(pieces, 'col', split_axis=0, concat_axis=0, tiled=True)]
    ppermute x33, waiting for transfers between devices: 39.6 us -> 31 us  [cross(): return have + [lax.ppermute(h, 'root', pairs) for h in have]]
    all_to_all x5 -> x6, starting transfers between devices: 22.6 us -> 28.2 us  [swap(): lax.all_to_all(pieces, 'col', split_axis=0, concat_axis=0, tiled=True)]
    ppermute x33, starting transfers between devices: 19.2 us -> 14.7 us  [cross(): return have + [lax.ppermute(h, 'root', pairs) for h in have]]
    unnamed x76 -> x86, local copies, waits for them, and re-layouts: 8.82 us -> 5.75 us
  transfers between devices with their start and end apart: 45 -> 46, of which waited for: 17 -> 18; matrix products, arithmetic and copies ran while one was open for 2% -> 1% of each run, Pallas kernels for 38% -> 28%
where the time goes in v9:
time: 362 us; the launch traced here: 360 us
  waiting for transfers between devices  165 us (46%)
  Pallas kernels  130 us (36%)
  starting transfers between devices  51.5 us (14%)
  local copies, waits for them, and re-layouts  11 us (3%)
    all_to_all x6, waiting for transfers between devices, swap(): lax.all_to_all(pieces, 'col', split_axis=0, concat_axis=0, tiled=True)  117 us
    pallas_call x3, Pallas kernels, blocked_shards(): call(functools.partial(left_second_kernel, dims, masks), groups, [smem(),...  34.4 us
    ppermute x33, waiting for transfers between devices, cross(): return have + [lax.ppermute(h, 'root', pairs) for h in have]  31 us
    all_to_all x6, starting transfers between devices, swap(): lax.all_to_all(pieces, 'col', split_axis=0, concat_axis=0, tiled=True)  28.2 us
    pallas_call x1, Pallas kernels, blocked_shards(): call(functools.partial(right_first_kernel, dims, groups, owners, masks),...  24.7 us
    pallas_call x1, Pallas kernels, blocked_shards(): call(functools.partial(right_second_kernel, dims), groups, [smem(), smem(...  19.1 us
    pallas_call x3, Pallas kernels, blocked_shards(): call(functools.partial(rotate_kernel, len(out)), groups, [smem()] + [pl.B...  19.1 us
    pallas_call x1, Pallas kernels, blocked_shards(): call(functools.partial(left_first_kernel, dims), groups, [smem(), all_cod...  17.6 us
  transfers between devices with their start and end apart: 46, of which 18 were waited for; matrix products, arithmetic and copies ran while one was open for 1% of the time, Pallas kernels for 28%

profile of v9, /device:TPU:0, one launch (start us, length us, event | category | flops | bytes accessed | tf_op | source)
XLA Modules:
  0.0 359.7 jit_solution(15739004427654372905)
XLA Ops:
  0.0 1.6 constant_dynamic-slice_fusion
  1.9 3.0 collective-permute-start.4
  5.1 5.9 %collective-permute-done.4.rest_4_ = bf16[30,32,128]{2,1,0:T(8,128)(2,1)S(1)} collective-permute-done((bf16[30,32,128]{2,1,0:T(8,128)(2,1)S(1)}, bf16[30,32,128]{2,1,0:T(8,128)(2,1)S(1)}, u32[]{:S(2)}, u32[]{:S(2)}) %collective-permute-start.4) | collective-permute-done | bytes 245792 | tf_op jit(solution)/shard_map/ppermute | solution.py:312
  11.0 1.7 collective-permute-start.12
  13.0 1.7 collective-permute-start.1
  15.0 3.1 collective-permute-done.12.rest_12_
  18.8 6.8 %shard_map.73 = s16[8,496,384]{2,1,0:T(8,128)(2,1)} custom-call(s32[1,2]{1,0:T(1,128)} %add_bitcast_fusion.here.place, f32[384,3072]{1,0:T(8,128)} %bitcast.19, f32[384,3072]{1,0:T(8,128)} %d_ref.4), custom_call_target="tpu_custom_call" | custom-call | bytes 14155776 | tf_op jit(solution)/shard_map/pallas_call | solution.py:293
  25.7 1.5 collective-permute-start.16
  27.8 1.3 collective-permute-start.9
  29.8 4.3 %collective-permute-done.16.rest_16_ = bf16[30,32,128]{2,1,0:T(8,128)(2,1)S(1)} collective-permute-done((bf16[30,32,128]{2,1,0:T(8,128)(2,1)S(1)}, bf16[30,32,128]{2,1,0:T(8,128)(2,1)S(1)}, u32[]{:S(2)}, u32[]{:S(2)}) %collective-permute-start.16) | collective-permute-done | bytes 245792 | tf_op jit(solution)/shard_map/ppermute | solution.py:312
  35.2 1.4 collective-permute-done.9.rest_9_
  36.6 4.2 %collective-permute-done.13.rest_13_ = bf16[30,32,128]{2,1,0:T(8,128)(2,1)S(1)} collective-permute-done((bf16[30,32,128]{2,1,0:T(8,128)(2,1)S(1)}, bf16[30,32,128]{2,1,0:T(8,128)(2,1)S(1)}, u32[]{:S(2)}, u32[]{:S(2)}) %collective-permute-start.13) | collective-permute-done | bytes 245792 | tf_op jit(solution)/shard_map/ppermute | solution.py:263
  40.8 1.4 collective-permute-start.24
  42.2 1.5 collective-permute-start.17
  44.8 3.0 collective-permute-done.24.rest_24_
  47.8 3.4 collective-permute-done.17.rest_17_
  51.2 1.5 collective-permute-start.25
  52.7 3.7 %collective-permute-done.21.rest_21_ = bf16[30,32,128]{2,1,0:T(8,128)(2,1)S(1)} collective-permute-done((bf16[30,32,128]{2,1,0:T(8,128)(2,1)S(1)}, bf16[30,32,128]{2,1,0:T(8,128)(2,1)S(1)}, u32[]{:S(2)}, u32[]{:S(2)}) %collective-permute-start.21) | collective-permute-done | bytes 245792 | tf_op jit(solution)/shard_map/ppermute | solution.py:263
  57.6 1.9 collective-permute-done.25.rest_25_
  61.0 1.4 copy.16
  62.4 24.7 %shard_map.74 = (f32[384,3072]{1,0:T(8,128)}, s16[8,144,384]{2,1,0:T(8,128)(2,1)}, s16[8,272,384]{2,1,0:T(8,128)(2,1)}, bf16[30720,128]{1,0:T(8,128)(2,1)}) custom-call(s32[24,10]{1,0:T(8,128)} %copy.21.cols, f32[1,1]{1,0:T(1,128)} %bitcast.14.shift, s32[1,2]{1,0:T(1,128)} %add_bitcast_fusion.here.place, f32[384,3072]{1,0:T(8,128)} %bitcast.20, ...), custom_call_target="tpu_custom_call" | custom-call | flops 6039797760 | bytes 28311552 | tf_op jit(solution)/shard_map/pallas_call | solution.py:324
  87.2 4.8 %all-to-all-start = ((s16[8,144,384]{2,1,0:T(8,128)(2,1)}), s16[8,144,384]{2,1,0:T(8,128)(2,1)S(1)}, u32[]{:S(2)}, u32[]{:S(2)}) async-start(s16[8,144,384]{2,1,0:T(8,128)(2,1)} %get-tuple-element.31), calls=%async_computation | async-start | bytes 1769472 | tf_op jit(solution)/shard_map/all_to_all | solution.py:247
  92.0 22.9 %all-to-all-done.after.tu_ref.tail_ref = s16[8,144,384]{2,1,0:T(8,128)(2,1)S(1)} async-done(((s16[8,144,384]{2,1,0:T(8,128)(2,1)}), s16[8,144,384]{2,1,0:T(8,128)(2,1)S(1)}, u32[]{:S(2)}, u32[]{:S(2)}) %all-to-all-start) | async-done | bytes 884768 | tf_op jit(solution)/shard_map/all_to_all | solution.py:247
  114.9 4.4 %all-to-all-start.1 = ((s16[8,496,384]{2,1,0:T(8,128)(2,1)}), s16[8,496,384]{2,1,0:T(8,128)(2,1)}, u32[]{:S(2)}, u32[]{:S(2)}) async-start(s16[8,496,384]{2,1,0:T(8,128)(2,1)} %shard_map.73), calls=%async_computation.1 | async-start | bytes 6094848 | tf_op jit(solution)/shard_map/all_to_all | solution.py:247
  119.3 68.4 %all-to-all-done.1.tv_ref = s16[8,496,384]{2,1,0:T(8,128)(2,1)} async-done(((s16[8,496,384]{2,1,0:T(8,128)(2,1)}), s16[8,496,384]{2,1,0:T(8,128)(2,1)}, u32[]{:S(2)}, u32[]{:S(2)}) %all-to-all-start.1) | async-done | bytes 3047456 | tf_op jit(solution)/shard_map/all_to_all | solution.py:247
  187.8 3.8 %all-to-all-start.3 = ((s16[8,272,384]{2,1,0:T(8,128)(2,1)}), s16[8,272,384]{2,1,0:T(8,128)(2,1)S(1)}, u32[]{:S(2)}, u32[]{:S(2)}) async-start(s16[8,272,384]{2,1,0:T(8,128)(2,1)} %get-tuple-element.39), calls=%async_computation.3 | async-start | bytes 3342336 | tf_op jit(solution)/shard_map/all_to_all | solution.py:247
  192.7 1.6 collective-permute-start.28
  194.2 17.6 %shard_map.75.y_ref = f32[384,3072]{1,0:T(8,128)} custom-call(s32[24,10]{1,0:T(8,128)} %copy.21.cols, s16[8,496,384]{2,1,0:T(8,128)(2,1)} %all-to-all-done.1.tv_ref, bf16[30720,128]{1,0:T(8,128)(2,1)} %get-tuple-element.33.tiles), custom_call_target="tpu_custom_call" | custom-call | flops 6039797760 | bytes 14155776 | tf_op jit(solution)/shard_map/pallas_call | solution.py:361
  212.4 19.1 %shard_map.76 = (f32[384,1024]{1,0:T(8,128)}, f32[384,1024]{1,0:T(8,128)}, f32[384,1024]{1,0:T(8,128)}) custom-call(s32[24,10]{1,0:T(8,128)} %copy.21.cols, f32[1,1]{1,0:T(1,128)} %bitcast.15.shift, f32[384,3072]{1,0:T(8,128)} %get-tuple-element.36.w_ref, f32[384,3072]{1,0:T(8,128)} %bitcast.21, f32[384,3072]{1,0:T(8,128)} %d_ref.4, ...), custom_call_target="tpu_custom_call" | custom-call | flops 6039797760 | bytes 23592960 | tf_op jit(solution)/shard_map/pallas_call | solution.py:350
  232.6 11.5 %shard_map.77 = s16[8,400,128]{2,1,0:T(8,128)(2,1)} custom-call(s32[24,10]{1,0:T(8,128)} %copy.21.cols, f32[1,1]{1,0:T(1,128)} %bitcast.16.shift, s32[1,2]{1,0:T(1,128)} %add_bitcast_fusion.here.place, s16[8,144,384]{2,1,0:T(8,128)(2,1)} %copy-done.2, s16[8,144,384]{2,1,0:T(8,128)(2,1)} %copy-done.2, f32[384,3072]{1,0:T(8,128)} %shard_map.75.y_ref, ...), custom_call_target="tpu_custom_call" | custom-call | flops 2013265920 | bytes 6291456 | tf_op jit(solution)/shard_map/pallas_call | solution.py:380
  244.1 5.9 %all-to-all-start.2 = ((s16[8,400,128]{2,1,0:T(8,128)(2,1)}), s16[8,400,128]{2,1,0:T(8,128)(2,1)S(1)}, u32[]{:S(2)}, u32[]{:S(2)}) async-start(s16[8,400,128]{2,1,0:T(8,128)(2,1)} %shard_map.77), calls=%async_computation.2 | async-start | bytes 1638400 | tf_op jit(solution)/shard_map/all_to_all | solution.py:247
  250.0 11.5 %shard_map.79 = s16[8,400,128]{2,1,0:T(8,128)(2,1)} custom-call(s32[24,10]{1,0:T(8,128)} %copy.21.cols, f32[1,1]{1,0:T(1,128)} %bitcast.17.shift, s32[1,2]{1,0:T(1,128)} %add_bitcast_fusion.here.place, s16[8,272,384]{2,1,0:T(8,128)(2,1)} %copy-done.1, s16[8,272,384]{2,1,0:T(8,128)(2,1)} %copy-done.1, f32[384,3072]{1,0:T(8,128)} %shard_map.75.y_ref, ...), custom_call_target="tpu_custom_call" | custom-call | flops 2013265920 | bytes 6291456 | tf_op jit(solution)/shard_map/pallas_call | solution.py:380
  261.4 9.6 %all-to-all-done.2.z_ref = s16[8,400,128]{2,1,0:T(8,128)(2,1)S(1)} async-done(((s16[8,400,128]{2,1,0:T(8,128)(2,1)}), s16[8,400,128]{2,1,0:T(8,128)(2,1)S(1)}, u32[]{:S(2)}, u32[]{:S(2)}) %all-to-all-start.2) | async-done | bytes 819232 | tf_op jit(solution)/shard_map/all_to_all | solution.py:247
  271.0 3.6 all-to-all-start.4
  274.7 1.2 gather_fusion
  275.9 2.8 shard_map.78.refs_0_.rest_4_
  279.2 11.5 %shard_map.82 = s16[8,400,128]{2,1,0:T(8,128)(2,1)} custom-call(s32[24,10]{1,0:T(8,128)} %copy.21.cols, f32[1,1]{1,0:T(1,128)} %bitcast.18.shift, s32[1,2]{1,0:T(1,128)} %add_bitcast_fusion.here.place, s16[8,272,384]{2,1,0:T(8,128)(2,1)} %copy-done.1, s16[8,272,384]{2,1,0:T(8,128)(2,1)} %copy-done.1, f32[384,3072]{1,0:T(8,128)} %shard_map.75.y_ref, ...), custom_call_target="tpu_custom_call" | custom-call | flops 2013265920 | bytes 6291456 | tf_op jit(solution)/shard_map/pallas_call | solution.py:380
  290.7 8.1 %collective-permute-done.31.refs_1_ = s16[8,400,128]{2,1,0:T(8,128)(2,1)S(1)} collective-permute-done((s16[8,400,128]{2,1,0:T(8,128)(2,1)}, s16[8,400,128]{2,1,0:T(8,128)(2,1)S(1)}, u32[]{:S(2)}, u32[]{:S(2)}) %collective-permute-start.31) | collective-permute-done | bytes 819232 | tf_op jit(solution)/shard_map/ppermute | solution.py:263
  298.8 5.7 %all-to-all-start.5 = ((s16[8,400,128]{2,1,0:T(8,128)(2,1)}), s16[8,400,128]{2,1,0:T(8,128)(2,1)S(1)}, u32[]{:S(2)}, u32[]{:S(2)}) async-start(s16[8,400,128]{2,1,0:T(8,128)(2,1)} %shard_map.82), calls=%async_computation.5 | async-start | bytes 1638400 | tf_op jit(solution)/shard_map/all_to_all | solution.py:247
  304.5 2.8 shard_map.80.refs_1_
  308.3 15.9 %all-to-all-done.5.z_ref = s16[8,400,128]{2,1,0:T(8,128)(2,1)S(1)} async-done(((s16[8,400,128]{2,1,0:T(8,128)(2,1)}), s16[8,400,128]{2,1,0:T(8,128)(2,1)S(1)}, u32[]{:S(2)}, u32[]{:S(2)}) %all-to-all-start.5) | async-done | bytes 819232 | tf_op jit(solution)/shard_map/all_to_all | solution.py:247
  325.1 2.8 shard_map.83.refs_1_
  329.0 6.4 %shard_map.81.refs_0_ = f32[1,384,3072]{2,1,0:T(8,128)} custom-call(f32[1,4]{1,0:T(1,128)} %bitcast.30, s16[8,400,128]{2,1,0:T(8,128)(2,1)} %shard_map.78.refs_0_.rest_4_, s16[8,400,128]{2,1,0:T(8,128)(2,1)} %copy-done.19, s16[8,400,128]{2,1,0:T(8,128)(2,1)} %collective-permute-done.32.refs_2_, s16[8,400,128]{2,1,0:T(8,128)(2,1)} %collective-permute-done.33.refs_3_), custom_call_target="tpu_custom_call" | custom-call | bytes 1 | tf_op jit(solution)/shard_map/pallas_call | solution.py:419
  337.2 6.4 %shard_map.84.refs_0_ = f32[1,384,3072]{2,1,0:T(8,128)} custom-call(f32[1,4]{1,0:T(1,128)} %bitcast.31, f32[1,384,3072]{2,1,0:T(8,128)} %shard_map.81.refs_0_, s16[8,400,128]{2,1,0:T(8,128)(2,1)} %shard_map.80.refs_1_, s16[8,400,128]{2,1,0:T(8,128)(2,1)} %copy-done.13, s16[8,400,128]{2,1,0:T(8,128)(2,1)} %copy-done.15, ...), custom_call_target="tpu_custom_call", output_to_operand_aliasing={{}: (1, {})} | custom-call | bytes 1 | tf_op jit(solution)/shard_map/pallas_call | solution.py:419
  343.5 5.4 %collective-permute-done.37.refs_2_ = s16[8,400,128]{2,1,0:T(8,128)(2,1)S(1)} collective-permute-done((s16[8,400,128]{2,1,0:T(8,128)(2,1)}, s16[8,400,128]{2,1,0:T(8,128)(2,1)S(1)}, u32[]{:S(2)}, u32[]{:S(2)}) %collective-permute-start.37) | collective-permute-done | bytes 819232 | tf_op jit(solution)/shard_map/ppermute | solution.py:263
  349.4 1.8 collective-permute-done.38.refs_3_
  351.2 1.2 collective-permute-done.39.refs_4_
  353.3 6.4 %shard_map.85 = f32[1,384,3072]{2,1,0:T(8,128)} custom-call(f32[1,4]{1,0:T(1,128)} %bitcast.32, f32[1,384,3072]{2,1,0:T(8,128)} %shard_map.84.refs_0_, s16[8,400,128]{2,1,0:T(8,128)(2,1)} %shard_map.83.refs_1_, s16[8,400,128]{2,1,0:T(8,128)(2,1)} %copy-done.14, s16[8,400,128]{2,1,0:T(8,128)(2,1)} %copy-done.17, ...), custom_call_target="tpu_custom_call", output_to_operand_aliasing={{}: (1, {})} | custom-call | bytes 1 | tf_op jit(solution)/shard_map/pallas_call | solution.py:419
  (151 shorter events, 17.0 us)
Async XLA Ops:
  0.0 274.6 %copy-start = (f32[4,4]{1,0:T(4,128)S(1)}, f32[4,4]{1,0:T(4,128)}, u32[]{:S(2)}) copy-start(f32[4,4]{1,0:T(4,128)} %param.10) | copy-start | bytes 196
  1.9 9.0 %collective-permute-start.4 = (bf16[30,32,128]{2,1,0:T(8,128)(2,1)S(1)}, bf16[30,32,128]{2,1,0:T(8,128)(2,1)S(1)}, u32[]{:S(2)}, u32[]{:S(2)}) collective-permute-start(bf16[30,32,128]{2,1,0:T(8,128)(2,1)S(1)} %bitcast.25), channel_id=1, source_target_pairs={{0,1},{2,0},{4,2},{6,4},{7,6},{5,7},{3,5},{1,3},{8,9},{10,8},{12,1... | collective-permute-start | bytes 737288 | tf_op jit(solution)/shard_map/ppermute | solution.py:312
  5.0 7.7 %collective-permute-start = (bf16[30,32,128]{2,1,0:T(8,128)(2,1)S(1)}, bf16[30,32,128]{2,1,0:T(8,128)(2,1)S(1)}, u32[]{:S(2)}, u32[]{:S(2)}) collective-permute-start(bf16[30,32,128]{2,1,0:T(8,128)(2,1)S(1)} %bitcast.26), channel_id=1, source_target_pairs={{0,2},{2,4},{4,6},{6,7},{7,5},{5,3},{3,1},{1,0},{8,10},{10,12},{12... | collective-permute-start | bytes 737288 | tf_op jit(solution)/shard_map/ppermute | solution.py:312
  11.0 7.1 %collective-permute-start.12 = (bf16[30,32,128]{2,1,0:T(8,128)(2,1)S(1)}, bf16[30,32,128]{2,1,0:T(8,128)(2,1)S(1)}, u32[]{:S(2)}, u32[]{:S(2)}) collective-permute-start(bf16[30,32,128]{2,1,0:T(8,128)(2,1)S(1)} %collective-permute-done.4.rest_4_), channel_id=1, source_target_pairs={{0,1},{2,0},{4,2},{6,4},{7,6},{5,7},{3,5},{1,3},{8,9},{10,8},{12,1... | collective-permute-start | bytes 737288 | tf_op jit(solution)/shard_map/ppermute | solution.py:312
  12.7 13.0 %collective-permute-start.8 = (bf16[30,32,128]{2,1,0:T(8,128)(2,1)S(1)}, bf16[30,32,128]{2,1,0:T(8,128)(2,1)S(1)}, u32[]{:S(2)}, u32[]{:S(2)}) collective-permute-start(bf16[30,32,128]{2,1,0:T(8,128)(2,1)S(1)} %collective-permute-done.rest_0_), channel_id=1, source_target_pairs={{0,2},{2,4},{4,6},{6,7},{7,5},{5,3},{3,1},{1,0},{8,10},{10,12},{12... | collective-permute-start | bytes 737288 | tf_op jit(solution)/shard_map/ppermute | solution.py:312
  13.0 12.7 %collective-permute-start.1 = (bf16[30,32,128]{2,1,0:T(8,128)(2,1)S(1)}, bf16[30,32,128]{2,1,0:T(8,128)(2,1)S(1)}, u32[]{:S(2)}, u32[]{:S(2)}) collective-permute-start(bf16[30,32,128]{2,1,0:T(8,128)(2,1)S(1)} %collective-permute-done.rest_0_), channel_id=1, source_target_pairs={{0,16},{8,24},{16,0},{24,8},{1,17},{9,25},{17,1},{25,9},{2,18},{10... | collective-permute-start | bytes 737288 | tf_op jit(solution)/shard_map/ppermute | solution.py:263
  14.7 11.0 %collective-permute-start.5 = (bf16[30,32,128]{2,1,0:T(8,128)(2,1)S(1)}, bf16[30,32,128]{2,1,0:T(8,128)(2,1)S(1)}, u32[]{:S(2)}, u32[]{:S(2)}) collective-permute-start(bf16[30,32,128]{2,1,0:T(8,128)(2,1)S(1)} %collective-permute-done.4.rest_4_), channel_id=1, source_target_pairs={{0,16},{8,24},{16,0},{24,8},{1,17},{9,25},{17,1},{25,9},{2,18},{10... | collective-permute-start | bytes 737288 | tf_op jit(solution)/shard_map/ppermute | solution.py:263
  15.0 14.1 %collective-permute-start.2 = (bf16[30,32,128]{2,1,0:T(8,128)(2,1)S(1)}, bf16[30,32,128]{2,1,0:T(8,128)(2,1)S(1)}, u32[]{:S(2)}, u32[]{:S(2)}) collective-permute-start(bf16[30,32,128]{2,1,0:T(8,128)(2,1)S(1)} %collective-permute-done.rest_0_), channel_id=1, source_target_pairs={{0,8},{8,0},{16,24},{24,16},{1,9},{9,1},{17,25},{25,17},{2,10},{10... | collective-permute-start | bytes 737288 | tf_op jit(solution)/shard_map/ppermute | solution.py:263
  18.1 11.7 %collective-permute-start.6 = (bf16[30,32,128]{2,1,0:T(8,128)(2,1)S(1)}, bf16[30,32,128]{2,1,0:T(8,128)(2,1)S(1)}, u32[]{:S(2)}, u32[]{:S(2)}) collective-permute-start(bf16[30,32,128]{2,1,0:T(8,128)(2,1)S(1)} %collective-permute-done.4.rest_4_), channel_id=1, source_target_pairs={{0,8},{8,0},{16,24},{24,16},{1,9},{9,1},{17,25},{25,17},{2,10},{10... | collective-permute-start | bytes 737288 | tf_op jit(solution)/shard_map/ppermute | solution.py:263
  25.7 8.4 %collective-permute-start.16 = (bf16[30,32,128]{2,1,0:T(8,128)(2,1)S(1)}, bf16[30,32,128]{2,1,0:T(8,128)(2,1)S(1)}, u32[]{:S(2)}, u32[]{:S(2)}) collective-permute-start(bf16[30,32,128]{2,1,0:T(8,128)(2,1)S(1)} %collective-permute-done.8.rest_8_), channel_id=1, source_target_pairs={{0,2},{2,4},{4,6},{6,7},{7,5},{5,3},{3,1},{1,0},{8,10},{10,12},{12... | collective-permute-start | bytes 737288 | tf_op jit(solution)/shard_map/ppermute | solution.py:312
  27.2 8.1 %collective-permute-start.20 = (bf16[30,32,128]{2,1,0:T(8,128)(2,1)S(1)}, bf16[30,32,128]{2,1,0:T(8,128)(2,1)S(1)}, u32[]{:S(2)}, u32[]{:S(2)}) collective-permute-start(bf16[30,32,128]{2,1,0:T(8,128)(2,1)S(1)} %collective-permute-done.12.rest_12_), channel_id=1, source_target_pairs={{0,1},{2,0},{4,2},{6,4},{7,6},{5,7},{3,5},{1,3},{8,9},{10,8},{12,1... | collective-permute-start | bytes 737288 | tf_op jit(solution)/shard_map/ppermute | solution.py:312
  27.8 8.8 %collective-permute-start.9 = (bf16[30,32,128]{2,1,0:T(8,128)(2,1)S(1)}, bf16[30,32,128]{2,1,0:T(8,128)(2,1)S(1)}, u32[]{:S(2)}, u32[]{:S(2)}) collective-permute-start(bf16[30,32,128]{2,1,0:T(8,128)(2,1)S(1)} %collective-permute-done.8.rest_8_), channel_id=1, source_target_pairs={{0,16},{8,24},{16,0},{24,8},{1,17},{9,25},{17,1},{25,9},{2,18},{10... | collective-permute-start | bytes 737288 | tf_op jit(solution)/shard_map/ppermute | solution.py:263
  29.1 11.7 %collective-permute-start.13 = (bf16[30,32,128]{2,1,0:T(8,128)(2,1)S(1)}, bf16[30,32,128]{2,1,0:T(8,128)(2,1)S(1)}, u32[]{:S(2)}, u32[]{:S(2)}) collective-permute-start(bf16[30,32,128]{2,1,0:T(8,128)(2,1)S(1)} %collective-permute-done.12.rest_12_), channel_id=1, source_target_pairs={{0,16},{8,24},{16,0},{24,8},{1,17},{9,25},{17,1},{25,9},{2,18},{10... | collective-permute-start | bytes 737288 | tf_op jit(solution)/shard_map/ppermute | solution.py:263
  29.8 12.4 %collective-permute-start.10 = (bf16[30,32,128]{2,1,0:T(8,128)(2,1)S(1)}, bf16[30,32,128]{2,1,0:T(8,128)(2,1)S(1)}, u32[]{:S(2)}, u32[]{:S(2)}) collective-permute-start(bf16[30,32,128]{2,1,0:T(8,128)(2,1)S(1)} %collective-permute-done.8.rest_8_), channel_id=1, source_target_pairs={{0,8},{8,0},{16,24},{24,16},{1,9},{9,1},{17,25},{25,17},{2,10},{10... | collective-permute-start | bytes 737288 | tf_op jit(solution)/shard_map/ppermute | solution.py:263
  34.1 9.7 %collective-permute-start.14 = (bf16[30,32,128]{2,1,0:T(8,128)(2,1)S(1)}, bf16[30,32,128]{2,1,0:T(8,128)(2,1)S(1)}, u32[]{:S(2)}, u32[]{:S(2)}) collective-permute-start(bf16[30,32,128]{2,1,0:T(8,128)(2,1)S(1)} %collective-permute-done.12.rest_12_), channel_id=1, source_target_pairs={{0,8},{8,0},{16,24},{24,16},{1,9},{9,1},{17,25},{25,17},{2,10},{10... | collective-permute-start | bytes 737288 | tf_op jit(solution)/shard_map/ppermute | solution.py:263
  35.2 9.1 %collective-permute-start.3 = (bf16[30,32,128]{2,1,0:T(8,128)(2,1)S(1)}, bf16[30,32,128]{2,1,0:T(8,128)(2,1)S(1)}, u32[]{:S(2)}, u32[]{:S(2)}) collective-permute-start(bf16[30,32,128]{2,1,0:T(8,128)(2,1)S(1)} %collective-permute-done.1.rest_1_), channel_id=1, source_target_pairs={{0,8},{8,0},{16,24},{24,16},{1,9},{9,1},{17,25},{25,17},{2,10},{10... | collective-permute-start | bytes 737288 | tf_op jit(solution)/shard_map/ppermute | solution.py:263
  36.6 7.7 %collective-permute-start.7 = (bf16[30,32,128]{2,1,0:T(8,128)(2,1)S(1)}, bf16[30,32,128]{2,1,0:T(8,128)(2,1)S(1)}, u32[]{:S(2)}, u32[]{:S(2)}) collective-permute-start(bf16[30,32,128]{2,1,0:T(8,128)(2,1)S(1)} %collective-permute-done.5.rest_5_), channel_id=1, source_target_pairs={{0,8},{8,0},{16,24},{24,16},{1,9},{9,1},{17,25},{25,17},{2,10},{10... | collective-permute-start | bytes 737288 | tf_op jit(solution)/shard_map/ppermute | solution.py:263
  40.8 7.0 %collective-permute-start.24 = (bf16[30,32,128]{2,1,0:T(8,128)(2,1)S(1)}, bf16[30,32,128]{2,1,0:T(8,128)(2,1)}, u32[]{:S(2)}, u32[]{:S(2)}) collective-permute-start(bf16[30,32,128]{2,1,0:T(8,128)(2,1)S(1)} %collective-permute-done.16.rest_16_), channel_id=1, source_target_pairs={{0,2},{2,4},{4,6},{6,7},{7,5},{5,3},{3,1},{1,0},{8,10},{10,12},{12... | collective-permute-start | bytes 737288 | tf_op jit(solution)/shard_map/ppermute | solution.py:312
  42.2 9.0 %collective-permute-start.17 = (bf16[30,32,128]{2,1,0:T(8,128)(2,1)S(1)}, bf16[30,32,128]{2,1,0:T(8,128)(2,1)}, u32[]{:S(2)}, u32[]{:S(2)}) collective-permute-start(bf16[30,32,128]{2,1,0:T(8,128)(2,1)S(1)} %collective-permute-done.16.rest_16_), channel_id=1, source_target_pairs={{0,16},{8,24},{16,0},{24,8},{1,17},{9,25},{17,1},{25,9},{2,18},{10... | collective-permute-start | bytes 737288 | tf_op jit(solution)/shard_map/ppermute | solution.py:263
  43.7 12.7 %collective-permute-start.21 = (bf16[30,32,128]{2,1,0:T(8,128)(2,1)S(1)}, bf16[30,32,128]{2,1,0:T(8,128)(2,1)S(1)}, u32[]{:S(2)}, u32[]{:S(2)}) collective-permute-start(bf16[30,32,128]{2,1,0:T(8,128)(2,1)S(1)} %collective-permute-done.20.rest_20_), channel_id=1, source_target_pairs={{0,16},{8,24},{16,0},{24,8},{1,17},{9,25},{17,1},{25,9},{2,18},{10... | collective-permute-start | bytes 737288 | tf_op jit(solution)/shard_map/ppermute | solution.py:263
  44.3 12.1 %collective-permute-start.18 = (bf16[30,32,128]{2,1,0:T(8,128)(2,1)S(1)}, bf16[30,32,128]{2,1,0:T(8,128)(2,1)S(1)}, u32[]{:S(2)}, u32[]{:S(2)}) collective-permute-start(bf16[30,32,128]{2,1,0:T(8,128)(2,1)S(1)} %collective-permute-done.16.rest_16_), channel_id=1, source_target_pairs={{0,8},{8,0},{16,24},{24,16},{1,9},{9,1},{17,25},{25,17},{2,10},{10... | collective-permute-start | bytes 737288 | tf_op jit(solution)/shard_map/ppermute | solution.py:263
  44.3 12.7 %collective-permute-start.22 = (bf16[30,32,128]{2,1,0:T(8,128)(2,1)S(1)}, bf16[30,32,128]{2,1,0:T(8,128)(2,1)S(1)}, u32[]{:S(2)}, u32[]{:S(2)}) collective-permute-start(bf16[30,32,128]{2,1,0:T(8,128)(2,1)S(1)} %collective-permute-done.20.rest_20_), channel_id=1, source_target_pairs={{0,8},{8,0},{16,24},{24,16},{1,9},{9,1},{17,25},{25,17},{2,10},{10... | collective-permute-start | bytes 737288 | tf_op jit(solution)/shard_map/ppermute | solution.py:263
  47.8 9.3 %collective-permute-start.11 = (bf16[30,32,128]{2,1,0:T(8,128)(2,1)S(1)}, bf16[30,32,128]{2,1,0:T(8,128)(2,1)S(1)}, u32[]{:S(2)}, u32[]{:S(2)}) collective-permute-start(bf16[30,32,128]{2,1,0:T(8,128)(2,1)S(1)} %collective-permute-done.9.rest_9_), channel_id=1, source_target_pairs={{0,8},{8,0},{16,24},{24,16},{1,9},{9,1},{17,25},{25,17},{2,10},{10... | collective-permute-start | bytes 737288 | tf_op jit(solution)/shard_map/ppermute | solution.py:263
  51.2 8.3 %collective-permute-start.25 = (bf16[30,32,128]{2,1,0:T(8,128)(2,1)}, bf16[30,32,128]{2,1,0:T(8,128)(2,1)}, u32[]{:S(2)}, u32[]{:S(2)}) collective-permute-start(bf16[30,32,128]{2,1,0:T(8,128)(2,1)} %collective-permute-done.24.rest_24_), channel_id=1, source_target_pairs={{0,16},{8,24},{16,0},{24,8},{1,17},{9,25},{17,1},{25,9},{2,18},{10... | collective-permute-start | bytes 737288 | tf_op jit(solution)/shard_map/ppermute | solution.py:263
  56.4 5.9 %collective-permute-start.15 = (bf16[30,32,128]{2,1,0:T(8,128)(2,1)S(1)}, bf16[30,32,128]{2,1,0:T(8,128)(2,1)}, u32[]{:S(2)}, u32[]{:S(2)}) collective-permute-start(bf16[30,32,128]{2,1,0:T(8,128)(2,1)S(1)} %collective-permute-done.13.rest_13_), channel_id=1, source_target_pairs={{0,8},{8,0},{16,24},{24,16},{1,9},{9,1},{17,25},{25,17},{2,10},{10... | collective-permute-start | bytes 737288 | tf_op jit(solution)/shard_map/ppermute | solution.py:263
  56.4 5.9 %collective-permute-start.26 = (bf16[30,32,128]{2,1,0:T(8,128)(2,1)}, bf16[30,32,128]{2,1,0:T(8,128)(2,1)}, u32[]{:S(2)}, u32[]{:S(2)}) collective-permute-start(bf16[30,32,128]{2,1,0:T(8,128)(2,1)} %collective-permute-done.24.rest_24_), channel_id=1, source_target_pairs={{0,8},{8,0},{16,24},{24,16},{1,9},{9,1},{17,25},{25,17},{2,10},{10... | collective-permute-start | bytes 737288 | tf_op jit(solution)/shard_map/ppermute | solution.py:263
  57.0 5.3 %collective-permute-start.19 = (bf16[30,32,128]{2,1,0:T(8,128)(2,1)}, bf16[30,32,128]{2,1,0:T(8,128)(2,1)}, u32[]{:S(2)}, u32[]{:S(2)}) collective-permute-start(bf16[30,32,128]{2,1,0:T(8,128)(2,1)} %collective-permute-done.17.rest_17_), channel_id=1, source_target_pairs={{0,8},{8,0},{16,24},{24,16},{1,9},{9,1},{17,25},{25,17},{2,10},{10... | collective-permute-start | bytes 737288 | tf_op jit(solution)/shard_map/ppermute | solution.py:263
  57.1 5.2 %collective-permute-start.23 = (bf16[30,32,128]{2,1,0:T(8,128)(2,1)S(1)}, bf16[30,32,128]{2,1,0:T(8,128)(2,1)}, u32[]{:S(2)}, u32[]{:S(2)}) collective-permute-start(bf16[30,32,128]{2,1,0:T(8,128)(2,1)S(1)} %collective-permute-done.21.rest_21_), channel_id=1, source_target_pairs={{0,8},{8,0},{16,24},{24,16},{1,9},{9,1},{17,25},{25,17},{2,10},{10... | collective-permute-start | bytes 737288 | tf_op jit(solution)/shard_map/ppermute | solution.py:263
  59.5 2.8 collective-permute-start.27
  87.2 27.7 %all-to-all-start = ((s16[8,144,384]{2,1,0:T(8,128)(2,1)}), s16[8,144,384]{2,1,0:T(8,128)(2,1)S(1)}, u32[]{:S(2)}, u32[]{:S(2)}) async-start(s16[8,144,384]{2,1,0:T(8,128)(2,1)} %get-tuple-element.31), calls=%async_computation | async-start | bytes 1769472 | tf_op jit(solution)/shard_map/all_to_all | solution.py:247
  114.9 72.9 %copy-start.2 = (s16[8,144,384]{2,1,0:T(8,128)(2,1)}, s16[8,144,384]{2,1,0:T(8,128)(2,1)S(1)}, u32[]{:S(2)}) copy-start(s16[8,144,384]{2,1,0:T(8,128)(2,1)S(1)} %all-to-all-done.after.tu_ref.tail_ref) | copy-start | bytes 2654212
  114.9 72.9 %all-to-all-start.1 = ((s16[8,496,384]{2,1,0:T(8,128)(2,1)}), s16[8,496,384]{2,1,0:T(8,128)(2,1)}, u32[]{:S(2)}, u32[]{:S(2)}) async-start(s16[8,496,384]{2,1,0:T(8,128)(2,1)} %shard_map.73), calls=%async_computation.1 | async-start | bytes 6094848 | tf_op jit(solution)/shard_map/all_to_all | solution.py:247
  187.8 56.3 %all-to-all-start.3 = ((s16[8,272,384]{2,1,0:T(8,128)(2,1)}), s16[8,272,384]{2,1,0:T(8,128)(2,1)S(1)}, u32[]{:S(2)}, u32[]{:S(2)}) async-start(s16[8,272,384]{2,1,0:T(8,128)(2,1)} %get-tuple-element.39), calls=%async_computation.3 | async-start | bytes 3342336 | tf_op jit(solution)/shard_map/all_to_all | solution.py:247
  192.7 19.2 %collective-permute-start.28 = (s16[8,96,384]{2,1,0:T(8,128)(2,1)S(1)}, s16[8,96,384]{2,1,0:T(8,128)(2,1)S(1)}, u32[]{:S(2)}, u32[]{:S(2)}) collective-permute-start(s16[8,96,384]{2,1,0:T(8,128)(2,1)S(1)} %slice.6.rest_0_), channel_id=1, source_target_pairs={{0,16},{8,24},{16,0},{24,8},{1,17},{9,25},{17,1},{25,9},{2,18},{10... | collective-permute-start | bytes 1769480 | tf_op jit(solution)/shard_map/ppermute | solution.py:263
  211.9 19.7 %collective-permute-start.29 = (s16[8,96,384]{2,1,0:T(8,128)(2,1)S(1)}, s16[8,96,384]{2,1,0:T(8,128)(2,1)S(1)}, u32[]{:S(2)}, u32[]{:S(2)}) collective-permute-start(s16[8,96,384]{2,1,0:T(8,128)(2,1)S(1)} %slice.6.rest_0_), channel_id=1, source_target_pairs={{0,8},{8,0},{16,24},{24,16},{1,9},{9,1},{17,25},{25,17},{2,10},{10... | collective-permute-start | bytes 1769480 | tf_op jit(solution)/shard_map/ppermute | solution.py:263
  211.9 19.6 %collective-permute-start.30 = (s16[8,96,384]{2,1,0:T(8,128)(2,1)S(1)}, s16[8,96,384]{2,1,0:T(8,128)(2,1)S(1)}, u32[]{:S(2)}, u32[]{:S(2)}) collective-permute-start(s16[8,96,384]{2,1,0:T(8,128)(2,1)S(1)} %collective-permute-done.28.rest_1_), channel_id=1, source_target_pairs={{0,8},{8,0},{16,24},{24,16},{1,9},{9,1},{17,25},{25,17},{2,10},{10... | collective-permute-start | bytes 1769480 | tf_op jit(solution)/shard_map/ppermute | solution.py:263
  244.1 26.9 %all-to-all-start.2 = ((s16[8,400,128]{2,1,0:T(8,128)(2,1)}), s16[8,400,128]{2,1,0:T(8,128)(2,1)S(1)}, u32[]{:S(2)}, u32[]{:S(2)}) async-start(s16[8,400,128]{2,1,0:T(8,128)(2,1)} %shard_map.77), calls=%async_computation.2 | async-start | bytes 1638400 | tf_op jit(solution)/shard_map/all_to_all | solution.py:247
  271.0 27.7 %all-to-all-start.4 = ((s16[8,400,128]{2,1,0:T(8,128)(2,1)}), s16[8,400,128]{2,1,0:T(8,128)(2,1)S(1)}, u32[]{:S(2)}, u32[]{:S(2)}) async-start(s16[8,400,128]{2,1,0:T(8,128)(2,1)} %shard_map.79), calls=%async_computation.4 | async-start | bytes 1638400 | tf_op jit(solution)/shard_map/all_to_all | solution.py:247
  278.7 20.1 %collective-permute-start.31 = (s16[8,400,128]{2,1,0:T(8,128)(2,1)}, s16[8,400,128]{2,1,0:T(8,128)(2,1)S(1)}, u32[]{:S(2)}, u32[]{:S(2)}) collective-permute-start(s16[8,400,128]{2,1,0:T(8,128)(2,1)} %shard_map.78.refs_0_.rest_4_), channel_id=1, source_target_pairs={{0,16},{8,24},{16,0},{24,8},{1,17},{9,25},{17,1},{25,9},{2,18},{10... | collective-permute-start | bytes 2457608 | tf_op jit(solution)/shard_map/ppermute | solution.py:263
  298.8 25.4 %all-to-all-start.5 = ((s16[8,400,128]{2,1,0:T(8,128)(2,1)}), s16[8,400,128]{2,1,0:T(8,128)(2,1)S(1)}, u32[]{:S(2)}, u32[]{:S(2)}) async-start(s16[8,400,128]{2,1,0:T(8,128)(2,1)} %shard_map.82), calls=%async_computation.5 | async-start | bytes 1638400 | tf_op jit(solution)/shard_map/all_to_all | solution.py:247
  307.3 20.6 %collective-permute-start.34 = (s16[8,400,128]{2,1,0:T(8,128)(2,1)}, s16[8,400,128]{2,1,0:T(8,128)(2,1)S(1)}, u32[]{:S(2)}, u32[]{:S(2)}) collective-permute-start(s16[8,400,128]{2,1,0:T(8,128)(2,1)} %shard_map.80.refs_1_), channel_id=1, source_target_pairs={{0,16},{8,24},{16,0},{24,8},{1,17},{9,25},{17,1},{25,9},{2,18},{10... | collective-permute-start | bytes 2457608 | tf_op jit(solution)/shard_map/ppermute | solution.py:263
  307.8 21.2 %collective-permute-start.32 = (s16[8,400,128]{2,1,0:T(8,128)(2,1)S(1)}, s16[8,400,128]{2,1,0:T(8,128)(2,1)}, u32[]{:S(2)}, u32[]{:S(2)}) collective-permute-start(s16[8,400,128]{2,1,0:T(8,128)(2,1)S(1)} %copy-done.4), channel_id=1, source_target_pairs={{0,8},{8,0},{16,24},{24,16},{1,9},{9,1},{17,25},{25,17},{2,10},{10... | collective-permute-start | bytes 2457608 | tf_op jit(solution)/shard_map/ppermute | solution.py:263
  307.8 21.2 %collective-permute-start.33 = (s16[8,400,128]{2,1,0:T(8,128)(2,1)S(1)}, s16[8,400,128]{2,1,0:T(8,128)(2,1)}, u32[]{:S(2)}, u32[]{:S(2)}) collective-permute-start(s16[8,400,128]{2,1,0:T(8,128)(2,1)S(1)} %collective-permute-done.31.refs_1_), channel_id=1, source_target_pairs={{0,8},{8,0},{16,24},{24,16},{1,9},{9,1},{17,25},{25,17},{2,10},{10... | collective-permute-start | bytes 2457608 | tf_op jit(solution)/shard_map/ppermute | solution.py:263
  327.9 7.5 %collective-permute-start.35 = (s16[8,400,128]{2,1,0:T(8,128)(2,1)}, s16[8,400,128]{2,1,0:T(8,128)(2,1)S(1)}, u32[]{:S(2)}, u32[]{:S(2)}) collective-permute-start(s16[8,400,128]{2,1,0:T(8,128)(2,1)} %shard_map.80.refs_1_), channel_id=1, source_target_pairs={{0,8},{8,0},{16,24},{24,16},{1,9},{9,1},{17,25},{25,17},{2,10},{10... | collective-permute-start | bytes 2457608 | tf_op jit(solution)/shard_map/ppermute | solution.py:263
  328.0 7.4 %collective-permute-start.36 = (s16[8,400,128]{2,1,0:T(8,128)(2,1)S(1)}, s16[8,400,128]{2,1,0:T(8,128)(2,1)S(1)}, u32[]{:S(2)}, u32[]{:S(2)}) collective-permute-start(s16[8,400,128]{2,1,0:T(8,128)(2,1)S(1)} %collective-permute-done.34.refs_2_), channel_id=1, source_target_pairs={{0,8},{8,0},{16,24},{24,16},{1,9},{9,1},{17,25},{25,17},{2,10},{10... | collective-permute-start | bytes 2457608 | tf_op jit(solution)/shard_map/ppermute | solution.py:263
  328.5 20.4 %collective-permute-start.37 = (s16[8,400,128]{2,1,0:T(8,128)(2,1)}, s16[8,400,128]{2,1,0:T(8,128)(2,1)S(1)}, u32[]{:S(2)}, u32[]{:S(2)}) collective-permute-start(s16[8,400,128]{2,1,0:T(8,128)(2,1)} %shard_map.83.refs_1_), channel_id=1, source_target_pairs={{0,16},{8,24},{16,0},{24,8},{1,17},{9,25},{17,1},{25,9},{2,18},{10... | collective-permute-start | bytes 2457608 | tf_op jit(solution)/shard_map/ppermute | solution.py:263
  348.9 2.3 collective-permute-start.38
  348.9 3.5 collective-permute-start.39
  (40 other events, 628.9 us)

commit v10 on v9

--- a/solution.py
+++ b/solution.py
@@ -264,7 +264,7 @@
 
     def exchange(have, bit=roots // 2, late=None):
         if late is not None:
-            have = list(lax.optimization_barrier((*have, late)))[:-1]
+            have = have[:1] + list(lax.optimization_barrier((*have[1:], late)))[:-1]
         while bit:
             have = cross(have, bit)
             bit //= 2
@@ -344,8 +344,19 @@
         work,
         size * 6,
     )(block_cols, energy, place, start, diagonal, own, *shards)
-    tu = swap(tu)
-    more = swap(lax.optimization_barrier((more, tu))[0])
+    tu = swap(lax.optimization_barrier((tu, tv))[0])
+
+    y = call(
+        functools.partial(left_first_kernel, dims),
+        groups,
+        [smem(), all_coded, tile_spec],
+        pl.BlockSpec((width, width), lambda q: (0, q)),
+        jax.ShapeDtypeStruct((width, strings), f32),
+        [col_halves],
+        work,
+        size * 3,
+    )(block_cols, tv, tiles)
+    more = swap(lax.optimization_barrier((more, tu, y))[0])
 
     base = call(
         functools.partial(right_second_kernel, dims),
@@ -357,17 +368,6 @@
         work,
         size * 5,
     )(block_cols, energy, w, start, diagonal, tiles, tu)
-
-    y = call(
-        functools.partial(left_first_kernel, dims),
-        groups,
-        [smem(), all_coded, tile_spec],
-        pl.BlockSpec((width, width), lambda q: (0, q)),
-        jax.ShapeDtypeStruct((width, strings), f32),
-        [col_halves],
-        work,
-        size * 3,
-    )(block_cols, tv, tiles)
 
     half = roots // 2
     slabs = exchange(cross([tv[:, width + PAD :]], half), half // 2, y)

time: 362 us -> 303 us (0.84)
  waiting for transfers between devices: 165 us -> 98.1 us
  local copies, waits for them, and re-layouts: 11 us -> 16.9 us
    all_to_all x6, waiting for transfers between devices: 117 us -> 32.4 us  [swap(): lax.all_to_all(pieces, 'col', split_axis=0, concat_axis=0, tiled=True)]
    ppermute x33, waiting for transfers between devices: 31 us -> 51.2 us  [cross(): return have + [lax.ppermute(h, 'root', pairs) for h in have]]
    unnamed x86 -> x80, local copies, waits for them, and re-layouts: 5.75 us -> 10.8 us
  transfers between devices with their start and end apart: 46 -> 46, of which waited for: 18 -> 16; matrix products, arithmetic and copies ran while one was open for 1% -> 2% of each run, Pallas kernels for 28% -> 41%
where the time goes in v10:
time: 303 us; the launch traced here: 301 us
  Pallas kernels  130 us (43%)
  waiting for transfers between devices  98.1 us (32%)
  starting transfers between devices  54.5 us (18%)
  local copies, waits for them, and re-layouts  16.9 us (6%)
    ppermute x33, waiting for transfers between devices, cross(): return have + [lax.ppermute(h, 'root', pairs) for h in have]  51.2 us
    pallas_call x3, Pallas kernels, blocked_shards(): call(functools.partial(left_second_kernel, dims, masks), groups, [smem(),...  34.4 us
    all_to_all x6, waiting for transfers between devices, swap(): lax.all_to_all(pieces, 'col', split_axis=0, concat_axis=0, tiled=True)  32.4 us
    all_to_all x6, starting transfers between devices, swap(): lax.all_to_all(pieces, 'col', split_axis=0, concat_axis=0, tiled=True)  28.4 us
    pallas_call x1, Pallas kernels, blocked_shards(): call(functools.partial(right_first_kernel, dims, groups, owners, masks),...  24.7 us
    pallas_call x1, Pallas kernels, blocked_shards(): call(functools.partial(right_second_kernel, dims), groups, [smem(), smem(...  19.3 us
    pallas_call x3, Pallas kernels, blocked_shards(): call(functools.partial(rotate_kernel, len(out)), groups, [smem()] + [pl.B...  19.1 us
    pallas_call x1, Pallas kernels, blocked_shards(): call(functools.partial(left_first_kernel, dims), groups, [smem(), all_cod...  17.6 us
  transfers between devices with their start and end apart: 46, of which 16 were waited for; matrix products, arithmetic and copies ran while one was open for 2% of the time, Pallas kernels for 41%

profile of v10, /device:TPU:0, one launch (start us, length us, event | category | flops | bytes accessed | tf_op | source)
XLA Modules:
  0.0 301.3 jit_solution(16727066214258224575)
XLA Ops:
  0.0 1.6 constant_dynamic-slice_fusion
  1.9 3.1 %collective-permute-start = (bf16[30,32,128]{2,1,0:T(8,128)(2,1)S(1)}, bf16[30,32,128]{2,1,0:T(8,128)(2,1)S(1)}, u32[]{:S(2)}, u32[]{:S(2)}) collective-permute-start(bf16[30,32,128]{2,1,0:T(8,128)(2,1)S(1)} %bitcast.25), channel_id=1, source_target_pairs={{0,2},{2,4},{4,6},{6,7},{7,5},{5,3},{3,1},{1,0},{8,10},{10,12},{12... | collective-permute-start | bytes 737288 | tf_op jit(solution)/shard_map/ppermute | solution.py:312
  5.0 5.9 %collective-permute-done.rest_0_ = bf16[30,32,128]{2,1,0:T(8,128)(2,1)S(1)} collective-permute-done((bf16[30,32,128]{2,1,0:T(8,128)(2,1)S(1)}, bf16[30,32,128]{2,1,0:T(8,128)(2,1)S(1)}, u32[]{:S(2)}, u32[]{:S(2)}) %collective-permute-start) | collective-permute-done | bytes 245792 | tf_op jit(solution)/shard_map/ppermute | solution.py:312
  10.9 1.7 collective-permute-start.1
  13.9 1.6 collective-permute-start.8
  16.6 6.7 %shard_map.73 = s16[8,496,384]{2,1,0:T(8,128)(2,1)} custom-call(s32[1,2]{1,0:T(1,128)} %add_bitcast_fusion.here.place, f32[384,3072]{1,0:T(8,128)} %bitcast.19, f32[384,3072]{1,0:T(8,128)} %d_ref.4), custom_call_target="tpu_custom_call" | custom-call | bytes 14155776 | tf_op jit(solution)/shard_map/pallas_call | solution.py:293
  23.4 1.6 collective-permute-start.16
  25.5 4.3 %collective-permute-done.16.rest_16_ = bf16[30,32,128]{2,1,0:T(8,128)(2,1)S(1)} collective-permute-done((bf16[30,32,128]{2,1,0:T(8,128)(2,1)S(1)}, bf16[30,32,128]{2,1,0:T(8,128)(2,1)S(1)}, u32[]{:S(2)}, u32[]{:S(2)}) %collective-permute-start.16) | collective-permute-done | bytes 245792 | tf_op jit(solution)/shard_map/ppermute | solution.py:312
  29.8 2.0 collective-permute-start.24
  31.8 4.2 %collective-permute-done.24.rest_24_ = bf16[30,32,128]{2,1,0:T(8,128)(2,1)S(1)} collective-permute-done((bf16[30,32,128]{2,1,0:T(8,128)(2,1)S(1)}, bf16[30,32,128]{2,1,0:T(8,128)(2,1)S(1)}, u32[]{:S(2)}, u32[]{:S(2)}) %collective-permute-start.24) | collective-permute-done | bytes 245792 | tf_op jit(solution)/shard_map/ppermute | solution.py:312
  36.7 6.0 %all-to-all-start = ((s16[8,496,384]{2,1,0:T(8,128)(2,1)}), s16[8,496,384]{2,1,0:T(8,128)(2,1)S(1)}, u32[]{:S(2)}, u32[]{:S(2)}) async-start(s16[8,496,384]{2,1,0:T(8,128)(2,1)} %shard_map.73), calls=%async_computation | async-start | bytes 6094848 | tf_op jit(solution)/shard_map/all_to_all | solution.py:247
  47.5 4.8 %collective-permute-done.9.rest_9_ = bf16[30,32,128]{2,1,0:T(8,128)(2,1)S(1)} collective-permute-done((bf16[30,32,128]{2,1,0:T(8,128)(2,1)}, bf16[30,32,128]{2,1,0:T(8,128)(2,1)S(1)}, u32[]{:S(2)}, u32[]{:S(2)}) %collective-permute-start.9) | collective-permute-done | bytes 245792 | tf_op jit(solution)/shard_map/ppermute | solution.py:263
  53.0 4.1 %collective-permute-done.13.rest_13_ = bf16[30,32,128]{2,1,0:T(8,128)(2,1)S(1)} collective-permute-done((bf16[30,32,128]{2,1,0:T(8,128)(2,1)}, bf16[30,32,128]{2,1,0:T(8,128)(2,1)S(1)}, u32[]{:S(2)}, u32[]{:S(2)}) %collective-permute-start.13) | collective-permute-done | bytes 245792 | tf_op jit(solution)/shard_map/ppermute | solution.py:263
  57.1 1.6 collective-permute-start.17
  59.4 1.6 collective-permute-start.25
  61.0 5.2 %collective-permute-done.17.rest_17_ = bf16[30,32,128]{2,1,0:T(8,128)(2,1)} collective-permute-done((bf16[30,32,128]{2,1,0:T(8,128)(2,1)}, bf16[30,32,128]{2,1,0:T(8,128)(2,1)}, u32[]{:S(2)}, u32[]{:S(2)}) %collective-permute-start.17) | collective-permute-done | bytes 245792 | tf_op jit(solution)/shard_map/ppermute | solution.py:263
  66.8 4.7 %collective-permute-done.21.rest_21_ = bf16[30,32,128]{2,1,0:T(8,128)(2,1)} collective-permute-done((bf16[30,32,128]{2,1,0:T(8,128)(2,1)}, bf16[30,32,128]{2,1,0:T(8,128)(2,1)}, u32[]{:S(2)}, u32[]{:S(2)}) %collective-permute-start.21) | collective-permute-done | bytes 245792 | tf_op jit(solution)/shard_map/ppermute | solution.py:263
  71.5 4.8 %collective-permute-done.25.rest_25_ = bf16[30,32,128]{2,1,0:T(8,128)(2,1)} collective-permute-done((bf16[30,32,128]{2,1,0:T(8,128)(2,1)}, bf16[30,32,128]{2,1,0:T(8,128)(2,1)}, u32[]{:S(2)}, u32[]{:S(2)}) %collective-permute-start.25) | collective-permute-done | bytes 245792 | tf_op jit(solution)/shard_map/ppermute | solution.py:263
  77.7 2.2 copy.16
  80.0 24.7 %shard_map.74 = (f32[384,3072]{1,0:T(8,128)}, s16[8,144,384]{2,1,0:T(8,128)(2,1)}, s16[8,272,384]{2,1,0:T(8,128)(2,1)}, bf16[30720,128]{1,0:T(8,128)(2,1)}) custom-call(s32[24,10]{1,0:T(8,128)} %copy.21.cols, f32[1,1]{1,0:T(1,128)} %bitcast.14.shift, s32[1,2]{1,0:T(1,128)} %add_bitcast_fusion.here.place, f32[384,3072]{1,0:T(8,128)} %bitcast.20, ...), custom_call_target="tpu_custom_call" | custom-call | flops 6039797760 | bytes 28311552 | tf_op jit(solution)/shard_map/pallas_call | solution.py:324
  104.6 2.8 all-to-all-done.tv_ref
  107.5 1.6 copy-done.8
  109.1 3.5 %all-to-all-start.1 = ((s16[8,144,384]{2,1,0:T(8,128)(2,1)}), s16[8,144,384]{2,1,0:T(8,128)(2,1)S(1)}, u32[]{:S(2)}, u32[]{:S(2)}) async-start(s16[8,144,384]{2,1,0:T(8,128)(2,1)} %get-tuple-element.30), calls=%async_computation.1 | async-start | bytes 1769472 | tf_op jit(solution)/shard_map/all_to_all | solution.py:247
  112.6 17.6 %shard_map.75.y_ref = f32[384,3072]{1,0:T(8,128)} custom-call(s32[24,10]{1,0:T(8,128)} %copy.21.cols, s16[8,496,384]{2,1,0:T(8,128)(2,1)} %copy-done.8, bf16[30720,128]{1,0:T(8,128)(2,1)} %get-tuple-element.31.tiles), custom_call_target="tpu_custom_call" | custom-call | flops 6039797760 | bytes 14155776 | tf_op jit(solution)/shard_map/pallas_call | solution.py:349
  130.2 4.9 %all-to-all-done.1.after.tu_ref.tail_ref = s16[8,144,384]{2,1,0:T(8,128)(2,1)S(1)} async-done(((s16[8,144,384]{2,1,0:T(8,128)(2,1)}), s16[8,144,384]{2,1,0:T(8,128)(2,1)S(1)}, u32[]{:S(2)}, u32[]{:S(2)}) %all-to-all-start.1) | async-done | bytes 884768 | tf_op jit(solution)/shard_map/all_to_all | solution.py:247
  135.1 3.8 %all-to-all-start.3 = ((s16[8,272,384]{2,1,0:T(8,128)(2,1)}), s16[8,272,384]{2,1,0:T(8,128)(2,1)S(1)}, u32[]{:S(2)}, u32[]{:S(2)}) async-start(s16[8,272,384]{2,1,0:T(8,128)(2,1)} %get-tuple-element.36), calls=%async_computation.3 | async-start | bytes 3342336 | tf_op jit(solution)/shard_map/all_to_all | solution.py:247
  140.0 1.6 collective-permute-start.28
  141.6 13.3 %collective-permute-done.28.rest_1_ = s16[8,96,384]{2,1,0:T(8,128)(2,1)S(1)} collective-permute-done((s16[8,96,384]{2,1,0:T(8,128)(2,1)S(1)}, s16[8,96,384]{2,1,0:T(8,128)(2,1)S(1)}, u32[]{:S(2)}, u32[]{:S(2)}) %collective-permute-start.28) | collective-permute-done | bytes 589856 | tf_op jit(solution)/shard_map/ppermute | solution.py:263
  154.9 19.3 %shard_map.76 = (f32[384,1024]{1,0:T(8,128)}, f32[384,1024]{1,0:T(8,128)}, f32[384,1024]{1,0:T(8,128)}) custom-call(s32[24,10]{1,0:T(8,128)} %copy.21.cols, f32[1,1]{1,0:T(1,128)} %bitcast.15.shift, f32[384,3072]{1,0:T(8,128)} %get-tuple-element.33.w_ref, f32[384,3072]{1,0:T(8,128)} %bitcast.21, f32[384,3072]{1,0:T(8,128)} %d_ref.4, ...), custom_call_target="tpu_custom_call" | custom-call | flops 6039797760 | bytes 23592960 | tf_op jit(solution)/shard_map/pallas_call | solution.py:361
  175.3 11.5 %shard_map.77 = s16[8,400,128]{2,1,0:T(8,128)(2,1)} custom-call(s32[24,10]{1,0:T(8,128)} %copy.21.cols, f32[1,1]{1,0:T(1,128)} %bitcast.16.shift, s32[1,2]{1,0:T(1,128)} %add_bitcast_fusion.here.place, s16[8,144,384]{2,1,0:T(8,128)(2,1)} %copy-done.2, s16[8,144,384]{2,1,0:T(8,128)(2,1)} %copy-done.2, f32[384,3072]{1,0:T(8,128)} %shard_map.75.y_ref, ...), custom_call_target="tpu_custom_call" | custom-call | flops 2013265920 | bytes 6291456 | tf_op jit(solution)/shard_map/pallas_call | solution.py:380
  186.8 5.7 %all-to-all-start.2 = ((s16[8,400,128]{2,1,0:T(8,128)(2,1)}), s16[8,400,128]{2,1,0:T(8,128)(2,1)S(1)}, u32[]{:S(2)}, u32[]{:S(2)}) async-start(s16[8,400,128]{2,1,0:T(8,128)(2,1)} %shard_map.77), calls=%async_computation.2 | async-start | bytes 1638400 | tf_op jit(solution)/shard_map/all_to_all | solution.py:247
  192.5 11.5 %shard_map.79 = s16[8,400,128]{2,1,0:T(8,128)(2,1)} custom-call(s32[24,10]{1,0:T(8,128)} %copy.21.cols, f32[1,1]{1,0:T(1,128)} %bitcast.17.shift, s32[1,2]{1,0:T(1,128)} %add_bitcast_fusion.here.place, s16[8,272,384]{2,1,0:T(8,128)(2,1)} %copy-done.1, s16[8,272,384]{2,1,0:T(8,128)(2,1)} %copy-done.1, f32[384,3072]{1,0:T(8,128)} %shard_map.75.y_ref, ...), custom_call_target="tpu_custom_call" | custom-call | flops 2013265920 | bytes 6291456 | tf_op jit(solution)/shard_map/pallas_call | solution.py:380
  204.0 9.8 %all-to-all-done.2.z_ref = s16[8,400,128]{2,1,0:T(8,128)(2,1)S(1)} async-done(((s16[8,400,128]{2,1,0:T(8,128)(2,1)}), s16[8,400,128]{2,1,0:T(8,128)(2,1)S(1)}, u32[]{:S(2)}, u32[]{:S(2)}) %all-to-all-start.2) | async-done | bytes 819232 | tf_op jit(solution)/shard_map/all_to_all | solution.py:247
  213.9 3.6 %all-to-all-start.4 = ((s16[8,400,128]{2,1,0:T(8,128)(2,1)}), s16[8,400,128]{2,1,0:T(8,128)(2,1)S(1)}, u32[]{:S(2)}, u32[]{:S(2)}) async-start(s16[8,400,128]{2,1,0:T(8,128)(2,1)} %shard_map.79), calls=%async_computation.4 | async-start | bytes 1638400 | tf_op jit(solution)/shard_map/all_to_all | solution.py:247
  218.7 2.8 shard_map.78.refs_0_.rest_4_
  221.5 1.5 collective-permute-start.31
  223.0 11.5 %shard_map.82 = s16[8,400,128]{2,1,0:T(8,128)(2,1)} custom-call(s32[24,10]{1,0:T(8,128)} %copy.21.cols, f32[1,1]{1,0:T(1,128)} %bitcast.18.shift, s32[1,2]{1,0:T(1,128)} %add_bitcast_fusion.here.place, s16[8,272,384]{2,1,0:T(8,128)(2,1)} %copy-done.1, s16[8,272,384]{2,1,0:T(8,128)(2,1)} %copy-done.1, f32[384,3072]{1,0:T(8,128)} %shard_map.75.y_ref, ...), custom_call_target="tpu_custom_call" | custom-call | flops 2013265920 | bytes 6291456 | tf_op jit(solution)/shard_map/pallas_call | solution.py:380
  234.4 7.2 %collective-permute-done.31.refs_1_ = s16[8,400,128]{2,1,0:T(8,128)(2,1)} collective-permute-done((s16[8,400,128]{2,1,0:T(8,128)(2,1)}, s16[8,400,128]{2,1,0:T(8,128)(2,1)}, u32[]{:S(2)}, u32[]{:S(2)}) %collective-permute-start.31) | collective-permute-done | bytes 819232 | tf_op jit(solution)/shard_map/ppermute | solution.py:263
  241.7 5.7 %all-to-all-start.5 = ((s16[8,400,128]{2,1,0:T(8,128)(2,1)}), s16[8,400,128]{2,1,0:T(8,128)(2,1)S(1)}, u32[]{:S(2)}, u32[]{:S(2)}) async-start(s16[8,400,128]{2,1,0:T(8,128)(2,1)} %shard_map.82), calls=%async_computation.5 | async-start | bytes 1638400 | tf_op jit(solution)/shard_map/all_to_all | solution.py:247
  247.4 2.8 shard_map.80.refs_1_
  252.2 14.9 %all-to-all-done.5.z_ref = s16[8,400,128]{2,1,0:T(8,128)(2,1)S(1)} async-done(((s16[8,400,128]{2,1,0:T(8,128)(2,1)}), s16[8,400,128]{2,1,0:T(8,128)(2,1)S(1)}, u32[]{:S(2)}, u32[]{:S(2)}) %all-to-all-start.5) | async-done | bytes 819232 | tf_op jit(solution)/shard_map/all_to_all | solution.py:247
  268.0 2.8 shard_map.83.refs_1_
  270.8 1.6 collective-permute-start.37
  272.6 6.4 %shard_map.81.refs_0_ = f32[1,384,3072]{2,1,0:T(8,128)} custom-call(f32[1,4]{1,0:T(1,128)} %bitcast.30, s16[8,400,128]{2,1,0:T(8,128)(2,1)} %shard_map.78.refs_0_.rest_4_, s16[8,400,128]{2,1,0:T(8,128)(2,1)} %collective-permute-done.31.refs_1_, s16[8,400,128]{2,1,0:T(8,128)(2,1)} %collective-permute-done.32.refs_2_, ...), custom_call_target="tpu_custom_call" | custom-call | bytes 1 | tf_op jit(solution)/shard_map/pallas_call | solution.py:419
  280.8 6.4 %shard_map.84.refs_0_ = f32[1,384,3072]{2,1,0:T(8,128)} custom-call(f32[1,4]{1,0:T(1,128)} %bitcast.31, f32[1,384,3072]{2,1,0:T(8,128)} %shard_map.81.refs_0_, s16[8,400,128]{2,1,0:T(8,128)(2,1)} %shard_map.80.refs_1_, s16[8,400,128]{2,1,0:T(8,128)(2,1)} %copy-done.12, s16[8,400,128]{2,1,0:T(8,128)(2,1)} %copy-done.13, ...), custom_call_target="tpu_custom_call", output_to_operand_aliasing={{}: (1, {})} | custom-call | bytes 1 | tf_op jit(solution)/shard_map/pallas_call | solution.py:419
  287.1 4.6 %collective-permute-done.37.refs_2_ = s16[8,400,128]{2,1,0:T(8,128)(2,1)S(1)} collective-permute-done((s16[8,400,128]{2,1,0:T(8,128)(2,1)}, s16[8,400,128]{2,1,0:T(8,128)(2,1)S(1)}, u32[]{:S(2)}, u32[]{:S(2)}) %collective-permute-start.37) | collective-permute-done | bytes 819232 | tf_op jit(solution)/shard_map/ppermute | solution.py:263
  291.7 2.3 collective-permute-done.39.refs_4_
  295.0 6.4 %shard_map.85 = f32[1,384,3072]{2,1,0:T(8,128)} custom-call(f32[1,4]{1,0:T(1,128)} %bitcast.32, f32[1,384,3072]{2,1,0:T(8,128)} %shard_map.84.refs_0_, s16[8,400,128]{2,1,0:T(8,128)(2,1)} %shard_map.83.refs_1_, s16[8,400,128]{2,1,0:T(8,128)(2,1)} %copy-done.14, s16[8,400,128]{2,1,0:T(8,128)(2,1)} %copy-done.15, ...), custom_call_target="tpu_custom_call", output_to_operand_aliasing={{}: (1, {})} | custom-call | bytes 1 | tf_op jit(solution)/shard_map/pallas_call | solution.py:419
  (145 shorter events, 20.6 us)
Async XLA Ops:
  0.0 217.5 %copy-start = (f32[4,4]{1,0:T(4,128)S(1)}, f32[4,4]{1,0:T(4,128)}, u32[]{:S(2)}) copy-start(f32[4,4]{1,0:T(4,128)} %param.10) | copy-start | bytes 196
  1.9 9.0 %collective-permute-start = (bf16[30,32,128]{2,1,0:T(8,128)(2,1)S(1)}, bf16[30,32,128]{2,1,0:T(8,128)(2,1)S(1)}, u32[]{:S(2)}, u32[]{:S(2)}) collective-permute-start(bf16[30,32,128]{2,1,0:T(8,128)(2,1)S(1)} %bitcast.25), channel_id=1, source_target_pairs={{0,2},{2,4},{4,6},{6,7},{7,5},{5,3},{3,1},{1,0},{8,10},{10,12},{12... | collective-permute-start | bytes 737288 | tf_op jit(solution)/shard_map/ppermute | solution.py:312
  5.0 7.6 %collective-permute-start.4 = (bf16[30,32,128]{2,1,0:T(8,128)(2,1)S(1)}, bf16[30,32,128]{2,1,0:T(8,128)(2,1)S(1)}, u32[]{:S(2)}, u32[]{:S(2)}) collective-permute-start(bf16[30,32,128]{2,1,0:T(8,128)(2,1)S(1)} %bitcast.26), channel_id=1, source_target_pairs={{0,1},{2,0},{4,2},{6,4},{7,6},{5,7},{3,5},{1,3},{8,9},{10,8},{12,1... | collective-permute-start | bytes 737288 | tf_op jit(solution)/shard_map/ppermute | solution.py:312
  10.9 12.4 %collective-permute-start.1 = (bf16[30,32,128]{2,1,0:T(8,128)(2,1)S(1)}, bf16[30,32,128]{2,1,0:T(8,128)(2,1)S(1)}, u32[]{:S(2)}, u32[]{:S(2)}) collective-permute-start(bf16[30,32,128]{2,1,0:T(8,128)(2,1)S(1)} %collective-permute-done.rest_0_), channel_id=1, source_target_pairs={{0,16},{8,24},{16,0},{24,8},{1,17},{9,25},{17,1},{25,9},{2,18},{10... | collective-permute-start | bytes 737288 | tf_op jit(solution)/shard_map/ppermute | solution.py:263
  12.6 10.7 %collective-permute-start.5 = (bf16[30,32,128]{2,1,0:T(8,128)(2,1)S(1)}, bf16[30,32,128]{2,1,0:T(8,128)(2,1)S(1)}, u32[]{:S(2)}, u32[]{:S(2)}) collective-permute-start(bf16[30,32,128]{2,1,0:T(8,128)(2,1)S(1)} %collective-permute-done.4.rest_4_), channel_id=1, source_target_pairs={{0,16},{8,24},{16,0},{24,8},{1,17},{9,25},{17,1},{25,9},{2,18},{10... | collective-permute-start | bytes 737288 | tf_op jit(solution)/shard_map/ppermute | solution.py:263
  13.9 9.4 %collective-permute-start.8 = (bf16[30,32,128]{2,1,0:T(8,128)(2,1)S(1)}, bf16[30,32,128]{2,1,0:T(8,128)(2,1)S(1)}, u32[]{:S(2)}, u32[]{:S(2)}) collective-permute-start(bf16[30,32,128]{2,1,0:T(8,128)(2,1)S(1)} %collective-permute-done.rest_0_), channel_id=1, source_target_pairs={{0,2},{2,4},{4,6},{6,7},{7,5},{5,3},{3,1},{1,0},{8,10},{10,12},{12... | collective-permute-start | bytes 737288 | tf_op jit(solution)/shard_map/ppermute | solution.py:312
  15.5 7.9 %collective-permute-start.12 = (bf16[30,32,128]{2,1,0:T(8,128)(2,1)S(1)}, bf16[30,32,128]{2,1,0:T(8,128)(2,1)S(1)}, u32[]{:S(2)}, u32[]{:S(2)}) collective-permute-start(bf16[30,32,128]{2,1,0:T(8,128)(2,1)S(1)} %collective-permute-done.4.rest_4_), channel_id=1, source_target_pairs={{0,1},{2,0},{4,2},{6,4},{7,6},{5,7},{3,5},{1,3},{8,9},{10,8},{12,1... | collective-permute-start | bytes 737288 | tf_op jit(solution)/shard_map/ppermute | solution.py:312
  23.3 53.0 %copy-start.18 = (s32[24,10]{0,1:T(8,128)S(1)}, s32[24,10]{0,1:T(8,128)}, u32[]{:S(2)}) copy-start(s32[24,10]{0,1:T(8,128)} %param.12) | copy-start | bytes 2884
  23.4 6.4 %collective-permute-start.16 = (bf16[30,32,128]{2,1,0:T(8,128)(2,1)S(1)}, bf16[30,32,128]{2,1,0:T(8,128)(2,1)S(1)}, u32[]{:S(2)}, u32[]{:S(2)}) collective-permute-start(bf16[30,32,128]{2,1,0:T(8,128)(2,1)S(1)} %collective-permute-done.8.rest_8_), channel_id=1, source_target_pairs={{0,2},{2,4},{4,6},{6,7},{7,5},{5,3},{3,1},{1,0},{8,10},{10,12},{12... | collective-permute-start | bytes 737288 | tf_op jit(solution)/shard_map/ppermute | solution.py:312
  25.0 6.8 %collective-permute-start.20 = (bf16[30,32,128]{2,1,0:T(8,128)(2,1)S(1)}, bf16[30,32,128]{2,1,0:T(8,128)(2,1)S(1)}, u32[]{:S(2)}, u32[]{:S(2)}) collective-permute-start(bf16[30,32,128]{2,1,0:T(8,128)(2,1)S(1)} %collective-permute-done.12.rest_12_), channel_id=1, source_target_pairs={{0,1},{2,0},{4,2},{6,4},{7,6},{5,7},{3,5},{1,3},{8,9},{10,8},{12,1... | collective-permute-start | bytes 737288 | tf_op jit(solution)/shard_map/ppermute | solution.py:312
  29.8 6.2 %collective-permute-start.24 = (bf16[30,32,128]{2,1,0:T(8,128)(2,1)S(1)}, bf16[30,32,128]{2,1,0:T(8,128)(2,1)S(1)}, u32[]{:S(2)}, u32[]{:S(2)}) collective-permute-start(bf16[30,32,128]{2,1,0:T(8,128)(2,1)S(1)} %collective-permute-done.16.rest_16_), channel_id=1, source_target_pairs={{0,2},{2,4},{4,6},{6,7},{7,5},{5,3},{3,1},{1,0},{8,10},{10,12},{12... | collective-permute-start | bytes 737288 | tf_op jit(solution)/shard_map/ppermute | solution.py:312
  36.7 70.8 %all-to-all-start = ((s16[8,496,384]{2,1,0:T(8,128)(2,1)}), s16[8,496,384]{2,1,0:T(8,128)(2,1)S(1)}, u32[]{:S(2)}, u32[]{:S(2)}) async-start(s16[8,496,384]{2,1,0:T(8,128)(2,1)} %shard_map.73), calls=%async_computation | async-start | bytes 6094848 | tf_op jit(solution)/shard_map/all_to_all | solution.py:247
  42.7 2.7 collective-permute-start.2
  42.7 2.6 collective-permute-start.6
  43.2 3.5 %collective-permute-start.3 = (bf16[30,32,128]{2,1,0:T(8,128)(2,1)}, bf16[30,32,128]{2,1,0:T(8,128)(2,1)S(1)}, u32[]{:S(2)}, u32[]{:S(2)}) collective-permute-start(bf16[30,32,128]{2,1,0:T(8,128)(2,1)} %copy-done.21), channel_id=1, source_target_pairs={{0,8},{8,0},{16,24},{24,16},{1,9},{9,1},{17,25},{25,17},{2,10},{10... | collective-permute-start | bytes 737288 | tf_op jit(solution)/shard_map/ppermute | solution.py:263
  43.3 9.0 %collective-permute-start.9 = (bf16[30,32,128]{2,1,0:T(8,128)(2,1)}, bf16[30,32,128]{2,1,0:T(8,128)(2,1)S(1)}, u32[]{:S(2)}, u32[]{:S(2)}) collective-permute-start(bf16[30,32,128]{2,1,0:T(8,128)(2,1)} %copy-done.23), channel_id=1, source_target_pairs={{0,16},{8,24},{16,0},{24,8},{1,17},{9,25},{17,1},{25,9},{2,18},{10... | collective-permute-start | bytes 737288 | tf_op jit(solution)/shard_map/ppermute | solution.py:263
  44.8 12.3 %collective-permute-start.13 = (bf16[30,32,128]{2,1,0:T(8,128)(2,1)}, bf16[30,32,128]{2,1,0:T(8,128)(2,1)S(1)}, u32[]{:S(2)}, u32[]{:S(2)}) collective-permute-start(bf16[30,32,128]{2,1,0:T(8,128)(2,1)} %copy-done.24), channel_id=1, source_target_pairs={{0,16},{8,24},{16,0},{24,8},{1,17},{9,25},{17,1},{25,9},{2,18},{10... | collective-permute-start | bytes 737288 | tf_op jit(solution)/shard_map/ppermute | solution.py:263
  45.4 11.8 %collective-permute-start.7 = (bf16[30,32,128]{2,1,0:T(8,128)(2,1)}, bf16[30,32,128]{2,1,0:T(8,128)(2,1)S(1)}, u32[]{:S(2)}, u32[]{:S(2)}) collective-permute-start(bf16[30,32,128]{2,1,0:T(8,128)(2,1)} %copy-done.22), channel_id=1, source_target_pairs={{0,8},{8,0},{16,24},{24,16},{1,9},{9,1},{17,25},{25,17},{2,10},{10... | collective-permute-start | bytes 737288 | tf_op jit(solution)/shard_map/ppermute | solution.py:263
  46.1 12.6 %collective-permute-start.10 = (bf16[30,32,128]{2,1,0:T(8,128)(2,1)}, bf16[30,32,128]{2,1,0:T(8,128)(2,1)S(1)}, u32[]{:S(2)}, u32[]{:S(2)}) collective-permute-start(bf16[30,32,128]{2,1,0:T(8,128)(2,1)} %copy-done.23), channel_id=1, source_target_pairs={{0,8},{8,0},{16,24},{24,16},{1,9},{9,1},{17,25},{25,17},{2,10},{10... | collective-permute-start | bytes 737288 | tf_op jit(solution)/shard_map/ppermute | solution.py:263
  47.5 11.4 %collective-permute-start.14 = (bf16[30,32,128]{2,1,0:T(8,128)(2,1)}, bf16[30,32,128]{2,1,0:T(8,128)(2,1)S(1)}, u32[]{:S(2)}, u32[]{:S(2)}) collective-permute-start(bf16[30,32,128]{2,1,0:T(8,128)(2,1)} %copy-done.24), channel_id=1, source_target_pairs={{0,8},{8,0},{16,24},{24,16},{1,9},{9,1},{17,25},{25,17},{2,10},{10... | collective-permute-start | bytes 737288 | tf_op jit(solution)/shard_map/ppermute | solution.py:263
  53.0 6.4 %collective-permute-start.11 = (bf16[30,32,128]{2,1,0:T(8,128)(2,1)S(1)}, bf16[30,32,128]{2,1,0:T(8,128)(2,1)S(1)}, u32[]{:S(2)}, u32[]{:S(2)}) collective-permute-start(bf16[30,32,128]{2,1,0:T(8,128)(2,1)S(1)} %collective-permute-done.9.rest_9_), channel_id=1, source_target_pairs={{0,8},{8,0},{16,24},{24,16},{1,9},{9,1},{17,25},{25,17},{2,10},{10... | collective-permute-start | bytes 737288 | tf_op jit(solution)/shard_map/ppermute | solution.py:263
  57.1 3.9 %collective-permute-start.15 = (bf16[30,32,128]{2,1,0:T(8,128)(2,1)S(1)}, bf16[30,32,128]{2,1,0:T(8,128)(2,1)S(1)}, u32[]{:S(2)}, u32[]{:S(2)}) collective-permute-start(bf16[30,32,128]{2,1,0:T(8,128)(2,1)S(1)} %collective-permute-done.13.rest_13_), channel_id=1, source_target_pairs={{0,8},{8,0},{16,24},{24,16},{1,9},{9,1},{17,25},{25,17},{2,10},{10... | collective-permute-start | bytes 737288 | tf_op jit(solution)/shard_map/ppermute | solution.py:263
  57.1 9.1 %collective-permute-start.17 = (bf16[30,32,128]{2,1,0:T(8,128)(2,1)}, bf16[30,32,128]{2,1,0:T(8,128)(2,1)}, u32[]{:S(2)}, u32[]{:S(2)}) collective-permute-start(bf16[30,32,128]{2,1,0:T(8,128)(2,1)} %copy-done.25), channel_id=1, source_target_pairs={{0,16},{8,24},{16,0},{24,8},{1,17},{9,25},{17,1},{25,9},{2,18},{10... | collective-permute-start | bytes 737288 | tf_op jit(solution)/shard_map/ppermute | solution.py:263
  58.7 7.6 %collective-permute-start.18 = (bf16[30,32,128]{2,1,0:T(8,128)(2,1)}, bf16[30,32,128]{2,1,0:T(8,128)(2,1)}, u32[]{:S(2)}, u32[]{:S(2)}) collective-permute-start(bf16[30,32,128]{2,1,0:T(8,128)(2,1)} %copy-done.25), channel_id=1, source_target_pairs={{0,8},{8,0},{16,24},{24,16},{1,9},{9,1},{17,25},{25,17},{2,10},{10... | collective-permute-start | bytes 737288 | tf_op jit(solution)/shard_map/ppermute | solution.py:263
  58.9 12.7 %collective-permute-start.21 = (bf16[30,32,128]{2,1,0:T(8,128)(2,1)}, bf16[30,32,128]{2,1,0:T(8,128)(2,1)}, u32[]{:S(2)}, u32[]{:S(2)}) collective-permute-start(bf16[30,32,128]{2,1,0:T(8,128)(2,1)} %copy-done.26), channel_id=1, source_target_pairs={{0,16},{8,24},{16,0},{24,8},{1,17},{9,25},{17,1},{25,9},{2,18},{10... | collective-permute-start | bytes 737288 | tf_op jit(solution)/shard_map/ppermute | solution.py:263
  59.4 16.9 %collective-permute-start.25 = (bf16[30,32,128]{2,1,0:T(8,128)(2,1)}, bf16[30,32,128]{2,1,0:T(8,128)(2,1)}, u32[]{:S(2)}, u32[]{:S(2)}) collective-permute-start(bf16[30,32,128]{2,1,0:T(8,128)(2,1)} %copy-done.27), channel_id=1, source_target_pairs={{0,16},{8,24},{16,0},{24,8},{1,17},{9,25},{17,1},{25,9},{2,18},{10... | collective-permute-start | bytes 737288 | tf_op jit(solution)/shard_map/ppermute | solution.py:263
  61.0 19.0 %collective-permute-start.22 = (bf16[30,32,128]{2,1,0:T(8,128)(2,1)}, bf16[30,32,128]{2,1,0:T(8,128)(2,1)}, u32[]{:S(2)}, u32[]{:S(2)}) collective-permute-start(bf16[30,32,128]{2,1,0:T(8,128)(2,1)} %copy-done.26), channel_id=1, source_target_pairs={{0,8},{8,0},{16,24},{24,16},{1,9},{9,1},{17,25},{25,17},{2,10},{10... | collective-permute-start | bytes 737288 | tf_op jit(solution)/shard_map/ppermute | solution.py:263
  66.3 13.7 %collective-permute-start.26 = (bf16[30,32,128]{2,1,0:T(8,128)(2,1)}, bf16[30,32,128]{2,1,0:T(8,128)(2,1)}, u32[]{:S(2)}, u32[]{:S(2)}) collective-permute-start(bf16[30,32,128]{2,1,0:T(8,128)(2,1)} %copy-done.27), channel_id=1, source_target_pairs={{0,8},{8,0},{16,24},{24,16},{1,9},{9,1},{17,25},{25,17},{2,10},{10... | collective-permute-start | bytes 737288 | tf_op jit(solution)/shard_map/ppermute | solution.py:263
  66.3 13.7 %collective-permute-start.19 = (bf16[30,32,128]{2,1,0:T(8,128)(2,1)}, bf16[30,32,128]{2,1,0:T(8,128)(2,1)}, u32[]{:S(2)}, u32[]{:S(2)}) collective-permute-start(bf16[30,32,128]{2,1,0:T(8,128)(2,1)} %collective-permute-done.17.rest_17_), channel_id=1, source_target_pairs={{0,8},{8,0},{16,24},{24,16},{1,9},{9,1},{17,25},{25,17},{2,10},{10... | collective-permute-start | bytes 737288 | tf_op jit(solution)/shard_map/ppermute | solution.py:263
  71.5 8.4 %collective-permute-start.23 = (bf16[30,32,128]{2,1,0:T(8,128)(2,1)}, bf16[30,32,128]{2,1,0:T(8,128)(2,1)}, u32[]{:S(2)}, u32[]{:S(2)}) collective-permute-start(bf16[30,32,128]{2,1,0:T(8,128)(2,1)} %collective-permute-done.21.rest_21_), channel_id=1, source_target_pairs={{0,8},{8,0},{16,24},{24,16},{1,9},{9,1},{17,25},{25,17},{2,10},{10... | collective-permute-start | bytes 737288 | tf_op jit(solution)/shard_map/ppermute | solution.py:263
  76.3 3.6 %collective-permute-start.27 = (bf16[30,32,128]{2,1,0:T(8,128)(2,1)}, bf16[30,32,128]{2,1,0:T(8,128)(2,1)}, u32[]{:S(2)}, u32[]{:S(2)}) collective-permute-start(bf16[30,32,128]{2,1,0:T(8,128)(2,1)} %collective-permute-done.25.rest_25_), channel_id=1, source_target_pairs={{0,8},{8,0},{16,24},{24,16},{1,9},{9,1},{17,25},{25,17},{2,10},{10... | collective-permute-start | bytes 737288 | tf_op jit(solution)/shard_map/ppermute | solution.py:263
  109.1 26.1 %all-to-all-start.1 = ((s16[8,144,384]{2,1,0:T(8,128)(2,1)}), s16[8,144,384]{2,1,0:T(8,128)(2,1)S(1)}, u32[]{:S(2)}, u32[]{:S(2)}) async-start(s16[8,144,384]{2,1,0:T(8,128)(2,1)} %get-tuple-element.30), calls=%async_computation.1 | async-start | bytes 1769472 | tf_op jit(solution)/shard_map/all_to_all | solution.py:247
  135.1 51.7 %all-to-all-start.3 = ((s16[8,272,384]{2,1,0:T(8,128)(2,1)}), s16[8,272,384]{2,1,0:T(8,128)(2,1)S(1)}, u32[]{:S(2)}, u32[]{:S(2)}) async-start(s16[8,272,384]{2,1,0:T(8,128)(2,1)} %get-tuple-element.36), calls=%async_computation.3 | async-start | bytes 3342336 | tf_op jit(solution)/shard_map/all_to_all | solution.py:247
  140.0 14.9 %collective-permute-start.28 = (s16[8,96,384]{2,1,0:T(8,128)(2,1)S(1)}, s16[8,96,384]{2,1,0:T(8,128)(2,1)S(1)}, u32[]{:S(2)}, u32[]{:S(2)}) collective-permute-start(s16[8,96,384]{2,1,0:T(8,128)(2,1)S(1)} %slice.6.rest_0_), channel_id=1, source_target_pairs={{0,16},{8,24},{16,0},{24,8},{1,17},{9,25},{17,1},{25,9},{2,18},{10... | collective-permute-start | bytes 1769480 | tf_op jit(solution)/shard_map/ppermute | solution.py:263
  141.6 32.6 %collective-permute-start.29 = (s16[8,96,384]{2,1,0:T(8,128)(2,1)S(1)}, s16[8,96,384]{2,1,0:T(8,128)(2,1)S(1)}, u32[]{:S(2)}, u32[]{:S(2)}) collective-permute-start(s16[8,96,384]{2,1,0:T(8,128)(2,1)S(1)} %slice.6.rest_0_), channel_id=1, source_target_pairs={{0,8},{8,0},{16,24},{24,16},{1,9},{9,1},{17,25},{25,17},{2,10},{10... | collective-permute-start | bytes 1769480 | tf_op jit(solution)/shard_map/ppermute | solution.py:263
  154.9 19.3 %collective-permute-start.30 = (s16[8,96,384]{2,1,0:T(8,128)(2,1)S(1)}, s16[8,96,384]{2,1,0:T(8,128)(2,1)S(1)}, u32[]{:S(2)}, u32[]{:S(2)}) collective-permute-start(s16[8,96,384]{2,1,0:T(8,128)(2,1)S(1)} %collective-permute-done.28.rest_1_), channel_id=1, source_target_pairs={{0,8},{8,0},{16,24},{24,16},{1,9},{9,1},{17,25},{25,17},{2,10},{10... | collective-permute-start | bytes 1769480 | tf_op jit(solution)/shard_map/ppermute | solution.py:263
  186.8 27.1 %all-to-all-start.2 = ((s16[8,400,128]{2,1,0:T(8,128)(2,1)}), s16[8,400,128]{2,1,0:T(8,128)(2,1)S(1)}, u32[]{:S(2)}, u32[]{:S(2)}) async-start(s16[8,400,128]{2,1,0:T(8,128)(2,1)} %shard_map.77), calls=%async_computation.2 | async-start | bytes 1638400 | tf_op jit(solution)/shard_map/all_to_all | solution.py:247
  213.9 27.8 %all-to-all-start.4 = ((s16[8,400,128]{2,1,0:T(8,128)(2,1)}), s16[8,400,128]{2,1,0:T(8,128)(2,1)S(1)}, u32[]{:S(2)}, u32[]{:S(2)}) async-start(s16[8,400,128]{2,1,0:T(8,128)(2,1)} %shard_map.79), calls=%async_computation.4 | async-start | bytes 1638400 | tf_op jit(solution)/shard_map/all_to_all | solution.py:247
  221.5 20.2 %collective-permute-start.31 = (s16[8,400,128]{2,1,0:T(8,128)(2,1)}, s16[8,400,128]{2,1,0:T(8,128)(2,1)}, u32[]{:S(2)}, u32[]{:S(2)}) collective-permute-start(s16[8,400,128]{2,1,0:T(8,128)(2,1)} %shard_map.78.refs_0_.rest_4_), channel_id=1, source_target_pairs={{0,16},{8,24},{16,0},{24,8},{1,17},{9,25},{17,1},{25,9},{2,18},{10... | collective-permute-start | bytes 2457608 | tf_op jit(solution)/shard_map/ppermute | solution.py:263
  241.7 25.4 %all-to-all-start.5 = ((s16[8,400,128]{2,1,0:T(8,128)(2,1)}), s16[8,400,128]{2,1,0:T(8,128)(2,1)S(1)}, u32[]{:S(2)}, u32[]{:S(2)}) async-start(s16[8,400,128]{2,1,0:T(8,128)(2,1)} %shard_map.82), calls=%async_computation.5 | async-start | bytes 1638400 | tf_op jit(solution)/shard_map/all_to_all | solution.py:247
  250.2 20.6 %collective-permute-start.34 = (s16[8,400,128]{2,1,0:T(8,128)(2,1)}, s16[8,400,128]{2,1,0:T(8,128)(2,1)S(1)}, u32[]{:S(2)}, u32[]{:S(2)}) collective-permute-start(s16[8,400,128]{2,1,0:T(8,128)(2,1)} %shard_map.80.refs_1_), channel_id=1, source_target_pairs={{0,16},{8,24},{16,0},{24,8},{1,17},{9,25},{17,1},{25,9},{2,18},{10... | collective-permute-start | bytes 2457608 | tf_op jit(solution)/shard_map/ppermute | solution.py:263
  251.7 20.7 %collective-permute-start.32 = (s16[8,400,128]{2,1,0:T(8,128)(2,1)S(1)}, s16[8,400,128]{2,1,0:T(8,128)(2,1)}, u32[]{:S(2)}, u32[]{:S(2)}) collective-permute-start(s16[8,400,128]{2,1,0:T(8,128)(2,1)S(1)} %copy-done.4), channel_id=1, source_target_pairs={{0,8},{8,0},{16,24},{24,16},{1,9},{9,1},{17,25},{25,17},{2,10},{10... | collective-permute-start | bytes 2457608 | tf_op jit(solution)/shard_map/ppermute | solution.py:263
  251.7 27.3 %collective-permute-start.35 = (s16[8,400,128]{2,1,0:T(8,128)(2,1)}, s16[8,400,128]{2,1,0:T(8,128)(2,1)S(1)}, u32[]{:S(2)}, u32[]{:S(2)}) collective-permute-start(s16[8,400,128]{2,1,0:T(8,128)(2,1)} %shard_map.80.refs_1_), channel_id=1, source_target_pairs={{0,8},{8,0},{16,24},{24,16},{1,9},{9,1},{17,25},{25,17},{2,10},{10... | collective-permute-start | bytes 2457608 | tf_op jit(solution)/shard_map/ppermute | solution.py:263
  252.2 20.4 %collective-permute-start.33 = (s16[8,400,128]{2,1,0:T(8,128)(2,1)}, s16[8,400,128]{2,1,0:T(8,128)(2,1)}, u32[]{:S(2)}, u32[]{:S(2)}) collective-permute-start(s16[8,400,128]{2,1,0:T(8,128)(2,1)} %collective-permute-done.31.refs_1_), channel_id=1, source_target_pairs={{0,8},{8,0},{16,24},{24,16},{1,9},{9,1},{17,25},{25,17},{2,10},{10... | collective-permute-start | bytes 2457608 | tf_op jit(solution)/shard_map/ppermute | solution.py:263
  270.8 8.2 %collective-permute-start.36 = (s16[8,400,128]{2,1,0:T(8,128)(2,1)S(1)}, s16[8,400,128]{2,1,0:T(8,128)(2,1)S(1)}, u32[]{:S(2)}, u32[]{:S(2)}) collective-permute-start(s16[8,400,128]{2,1,0:T(8,128)(2,1)S(1)} %collective-permute-done.34.refs_2_), channel_id=1, source_target_pairs={{0,8},{8,0},{16,24},{24,16},{1,9},{9,1},{17,25},{25,17},{2,10},{10... | collective-permute-start | bytes 2457608 | tf_op jit(solution)/shard_map/ppermute | solution.py:263
  270.8 20.9 %collective-permute-start.37 = (s16[8,400,128]{2,1,0:T(8,128)(2,1)}, s16[8,400,128]{2,1,0:T(8,128)(2,1)S(1)}, u32[]{:S(2)}, u32[]{:S(2)}) collective-permute-start(s16[8,400,128]{2,1,0:T(8,128)(2,1)} %shard_map.83.refs_1_), channel_id=1, source_target_pairs={{0,16},{8,24},{16,0},{24,8},{1,17},{9,25},{17,1},{25,9},{2,18},{10... | collective-permute-start | bytes 2457608 | tf_op jit(solution)/shard_map/ppermute | solution.py:263
  272.4 19.3 %collective-permute-start.38 = (s16[8,400,128]{2,1,0:T(8,128)(2,1)}, s16[8,400,128]{2,1,0:T(8,128)(2,1)S(1)}, u32[]{:S(2)}, u32[]{:S(2)}) collective-permute-start(s16[8,400,128]{2,1,0:T(8,128)(2,1)} %shard_map.83.refs_1_), channel_id=1, source_target_pairs={{0,8},{8,0},{16,24},{24,16},{1,9},{9,1},{17,25},{25,17},{2,10},{10... | collective-permute-start | bytes 2457608 | tf_op jit(solution)/shard_map/ppermute | solution.py:263
  291.7 2.3 collective-permute-start.39
  (37 other events, 333.7 us)

commit v11 on v10

--- a/solution.py
+++ b/solution.py
@@ -370,7 +370,7 @@
     )(block_cols, energy, w, start, diagonal, tiles, tu)
 
     half = roots // 2
-    slabs = exchange(cross([tv[:, width + PAD :]], half), half // 2, y)
+    slabs = exchange(cross([tv[:, width + PAD :]], half), half // 2, base[0])
     chunk_coded = pl.BlockSpec((1, rows + PAD, part), lambda q: (q, 0, 0))
     many = 4 if groups % 4 == 0 else 1
     many_coded = pl.BlockSpec((many, rows + PAD, part), lambda q: (q, 0, 0))

time: 303 us -> 292 us (0.964)
  waiting for transfers between devices: 98.1 us -> 89 us
    ppermute x33, waiting for transfers between devices: 51.2 us -> 39.6 us  [cross(): return have + [lax.ppermute(h, 'root', pairs) for h in have]]
  transfers between devices with their start and end apart: 46 -> 46, of which waited for: 16 -> 17; matrix products, arithmetic and copies ran while one was open for 2% -> 2% of each run, Pallas kernels for 41% -> 43%
where the time goes in v11:
time: 292 us; the launch traced here: 290 us
  Pallas kernels  130 us (45%)
  waiting for transfers between devices  89 us (30%)
  starting transfers between devices  52.9 us (18%)
  local copies, waits for them, and re-layouts  16.7 us (6%)
    ppermute x33, waiting for transfers between devices, cross(): return have + [lax.ppermute(h, 'root', pairs) for h in have]  39.6 us
    all_to_all x6, waiting for transfers between devices, swap(): lax.all_to_all(pieces, 'col', split_axis=0, concat_axis=0, tiled=True)  35 us
    pallas_call x3, Pallas kernels, blocked_shards(): call(functools.partial(left_second_kernel, dims, masks), groups, [smem(),...  34.4 us
    all_to_all x6, starting transfers between devices, swap(): lax.all_to_all(pieces, 'col', split_axis=0, concat_axis=0, tiled=True)  26.2 us
    pallas_call x1, Pallas kernels, blocked_shards(): call(functools.partial(right_first_kernel, dims, groups, owners, masks),...  24.7 us
    pallas_call x1, Pallas kernels, blocked_shards(): call(functools.partial(right_second_kernel, dims), groups, [smem(), smem(...  19.1 us
    pallas_call x3, Pallas kernels, blocked_shards(): call(functools.partial(rotate_kernel, len(out)), groups, [smem()] + [pl.B...  19.1 us
    pallas_call x1, Pallas kernels, blocked_shards(): call(functools.partial(left_first_kernel, dims), groups, [smem(), all_cod...  17.6 us
  transfers between devices with their start and end apart: 46, of which 17 were waited for; matrix products, arithmetic and copies ran while one was open for 2% of the time, Pallas kernels for 43%

profile of v11, /device:TPU:0, one launch (start us, length us, event | category | flops | bytes accessed | tf_op | source)
XLA Modules:
  0.0 290.1 jit_solution(15664436231884454835)
XLA Ops:
  0.0 1.6 constant_dynamic-slice_fusion
  1.9 3.1 %collective-permute-start = (bf16[30,32,128]{2,1,0:T(8,128)(2,1)S(1)}, bf16[30,32,128]{2,1,0:T(8,128)(2,1)S(1)}, u32[]{:S(2)}, u32[]{:S(2)}) collective-permute-start(bf16[30,32,128]{2,1,0:T(8,128)(2,1)S(1)} %bitcast.25), channel_id=1, source_target_pairs={{0,2},{2,4},{4,6},{6,7},{7,5},{5,3},{3,1},{1,0},{8,10},{10,12},{12... | collective-permute-start | bytes 737288 | tf_op jit(solution)/shard_map/ppermute | solution.py:312
  5.0 5.9 %collective-permute-done.rest_0_ = bf16[30,32,128]{2,1,0:T(8,128)(2,1)S(1)} collective-permute-done((bf16[30,32,128]{2,1,0:T(8,128)(2,1)S(1)}, bf16[30,32,128]{2,1,0:T(8,128)(2,1)S(1)}, u32[]{:S(2)}, u32[]{:S(2)}) %collective-permute-start) | collective-permute-done | bytes 245792 | tf_op jit(solution)/shard_map/ppermute | solution.py:312
  10.9 1.7 collective-permute-start.1
  13.9 1.6 collective-permute-start.8
  16.6 6.7 %shard_map.73 = s16[8,496,384]{2,1,0:T(8,128)(2,1)} custom-call(s32[1,2]{1,0:T(1,128)} %add_bitcast_fusion.here.place, f32[384,3072]{1,0:T(8,128)} %bitcast.19, f32[384,3072]{1,0:T(8,128)} %d_ref.4), custom_call_target="tpu_custom_call" | custom-call | bytes 14155776 | tf_op jit(solution)/shard_map/pallas_call | solution.py:293
  23.4 1.6 collective-permute-start.16
  25.5 4.3 %collective-permute-done.16.rest_16_ = bf16[30,32,128]{2,1,0:T(8,128)(2,1)S(1)} collective-permute-done((bf16[30,32,128]{2,1,0:T(8,128)(2,1)S(1)}, bf16[30,32,128]{2,1,0:T(8,128)(2,1)S(1)}, u32[]{:S(2)}, u32[]{:S(2)}) %collective-permute-start.16) | collective-permute-done | bytes 245792 | tf_op jit(solution)/shard_map/ppermute | solution.py:312
  29.8 2.0 collective-permute-start.24
  31.8 4.2 %collective-permute-done.24.rest_24_ = bf16[30,32,128]{2,1,0:T(8,128)(2,1)S(1)} collective-permute-done((bf16[30,32,128]{2,1,0:T(8,128)(2,1)S(1)}, bf16[30,32,128]{2,1,0:T(8,128)(2,1)S(1)}, u32[]{:S(2)}, u32[]{:S(2)}) %collective-permute-start.24) | collective-permute-done | bytes 245792 | tf_op jit(solution)/shard_map/ppermute | solution.py:312
  36.7 6.0 %all-to-all-start = ((s16[8,496,384]{2,1,0:T(8,128)(2,1)}), s16[8,496,384]{2,1,0:T(8,128)(2,1)S(1)}, u32[]{:S(2)}, u32[]{:S(2)}) async-start(s16[8,496,384]{2,1,0:T(8,128)(2,1)} %shard_map.73), calls=%async_computation | async-start | bytes 6094848 | tf_op jit(solution)/shard_map/all_to_all | solution.py:247
  47.5 4.8 %collective-permute-done.9.rest_9_ = bf16[30,32,128]{2,1,0:T(8,128)(2,1)S(1)} collective-permute-done((bf16[30,32,128]{2,1,0:T(8,128)(2,1)}, bf16[30,32,128]{2,1,0:T(8,128)(2,1)S(1)}, u32[]{:S(2)}, u32[]{:S(2)}) %collective-permute-start.9) | collective-permute-done | bytes 245792 | tf_op jit(solution)/shard_map/ppermute | solution.py:263
  53.0 4.1 %collective-permute-done.13.rest_13_ = bf16[30,32,128]{2,1,0:T(8,128)(2,1)S(1)} collective-permute-done((bf16[30,32,128]{2,1,0:T(8,128)(2,1)}, bf16[30,32,128]{2,1,0:T(8,128)(2,1)S(1)}, u32[]{:S(2)}, u32[]{:S(2)}) %collective-permute-start.13) | collective-permute-done | bytes 245792 | tf_op jit(solution)/shard_map/ppermute | solution.py:263
  57.1 1.6 collective-permute-start.17
  59.4 1.6 collective-permute-start.25
  61.0 5.2 %collective-permute-done.17.rest_17_ = bf16[30,32,128]{2,1,0:T(8,128)(2,1)} collective-permute-done((bf16[30,32,128]{2,1,0:T(8,128)(2,1)}, bf16[30,32,128]{2,1,0:T(8,128)(2,1)}, u32[]{:S(2)}, u32[]{:S(2)}) %collective-permute-start.17) | collective-permute-done | bytes 245792 | tf_op jit(solution)/shard_map/ppermute | solution.py:263
  66.8 4.7 %collective-permute-done.21.rest_21_ = bf16[30,32,128]{2,1,0:T(8,128)(2,1)} collective-permute-done((bf16[30,32,128]{2,1,0:T(8,128)(2,1)}, bf16[30,32,128]{2,1,0:T(8,128)(2,1)}, u32[]{:S(2)}, u32[]{:S(2)}) %collective-permute-start.21) | collective-permute-done | bytes 245792 | tf_op jit(solution)/shard_map/ppermute | solution.py:263
  71.5 4.8 %collective-permute-done.25.rest_25_ = bf16[30,32,128]{2,1,0:T(8,128)(2,1)} collective-permute-done((bf16[30,32,128]{2,1,0:T(8,128)(2,1)}, bf16[30,32,128]{2,1,0:T(8,128)(2,1)}, u32[]{:S(2)}, u32[]{:S(2)}) %collective-permute-start.25) | collective-permute-done | bytes 245792 | tf_op jit(solution)/shard_map/ppermute | solution.py:263
  77.7 2.2 copy.16
  80.0 24.7 %shard_map.74 = (f32[384,3072]{1,0:T(8,128)}, s16[8,144,384]{2,1,0:T(8,128)(2,1)}, s16[8,272,384]{2,1,0:T(8,128)(2,1)}, bf16[30720,128]{1,0:T(8,128)(2,1)}) custom-call(s32[24,10]{1,0:T(8,128)} %copy.21.cols, f32[1,1]{1,0:T(1,128)} %bitcast.14.shift, s32[1,2]{1,0:T(1,128)} %add_bitcast_fusion.here.place, f32[384,3072]{1,0:T(8,128)} %bitcast.20, ...), custom_call_target="tpu_custom_call" | custom-call | flops 6039797760 | bytes 28311552 | tf_op jit(solution)/shard_map/pallas_call | solution.py:324
  104.6 2.8 all-to-all-done.tv_ref
  107.5 1.6 copy-done.8
  109.1 3.5 %all-to-all-start.1 = ((s16[8,144,384]{2,1,0:T(8,128)(2,1)}), s16[8,144,384]{2,1,0:T(8,128)(2,1)S(1)}, u32[]{:S(2)}, u32[]{:S(2)}) async-start(s16[8,144,384]{2,1,0:T(8,128)(2,1)} %get-tuple-element.30), calls=%async_computation.1 | async-start | bytes 1769472 | tf_op jit(solution)/shard_map/all_to_all | solution.py:247
  112.7 17.6 %shard_map.75.y_ref = f32[384,3072]{1,0:T(8,128)} custom-call(s32[24,10]{1,0:T(8,128)} %copy.21.cols, s16[8,496,384]{2,1,0:T(8,128)(2,1)} %copy-done.8, bf16[30720,128]{1,0:T(8,128)(2,1)} %get-tuple-element.31.tiles), custom_call_target="tpu_custom_call" | custom-call | flops 6039797760 | bytes 14155776 | tf_op jit(solution)/shard_map/pallas_call | solution.py:349
  130.3 4.9 %all-to-all-done.1.after.tu_ref.tail_ref = s16[8,144,384]{2,1,0:T(8,128)(2,1)S(1)} async-done(((s16[8,144,384]{2,1,0:T(8,128)(2,1)}), s16[8,144,384]{2,1,0:T(8,128)(2,1)S(1)}, u32[]{:S(2)}, u32[]{:S(2)}) %all-to-all-start.1) | async-done | bytes 884768 | tf_op jit(solution)/shard_map/all_to_all | solution.py:247
  135.2 3.8 %all-to-all-start.3 = ((s16[8,272,384]{2,1,0:T(8,128)(2,1)}), s16[8,272,384]{2,1,0:T(8,128)(2,1)S(1)}, u32[]{:S(2)}, u32[]{:S(2)}) async-start(s16[8,272,384]{2,1,0:T(8,128)(2,1)} %get-tuple-element.36), calls=%async_computation.3 | async-start | bytes 3342336 | tf_op jit(solution)/shard_map/all_to_all | solution.py:247
  140.1 1.6 collective-permute-start.28
  141.6 19.1 %shard_map.76 = (f32[384,1024]{1,0:T(8,128)}, f32[384,1024]{1,0:T(8,128)}, f32[384,1024]{1,0:T(8,128)}) custom-call(s32[24,10]{1,0:T(8,128)} %copy.21.cols, f32[1,1]{1,0:T(1,128)} %bitcast.15.shift, f32[384,3072]{1,0:T(8,128)} %get-tuple-element.32.w_ref, f32[384,3072]{1,0:T(8,128)} %bitcast.21, f32[384,3072]{1,0:T(8,128)} %d_ref.4, ...), custom_call_target="tpu_custom_call" | custom-call | flops 6039797760 | bytes 23592960 | tf_op jit(solution)/shard_map/pallas_call | solution.py:361
  161.3 1.6 collective-permute-done.30.rest_3_
  163.8 11.5 %shard_map.77 = s16[8,400,128]{2,1,0:T(8,128)(2,1)} custom-call(s32[24,10]{1,0:T(8,128)} %copy.21.cols, f32[1,1]{1,0:T(1,128)} %bitcast.16.shift, s32[1,2]{1,0:T(1,128)} %add_bitcast_fusion.here.place, s16[8,144,384]{2,1,0:T(8,128)(2,1)} %copy-done.2, s16[8,144,384]{2,1,0:T(8,128)(2,1)} %copy-done.2, f32[384,3072]{1,0:T(8,128)} %shard_map.75.y_ref, ...), custom_call_target="tpu_custom_call" | custom-call | flops 2013265920 | bytes 6291456 | tf_op jit(solution)/shard_map/pallas_call | solution.py:380
  175.3 2.9 all-to-all-done.3.tu_ref.tail_ref
  178.1 3.6 %all-to-all-start.2 = ((s16[8,400,128]{2,1,0:T(8,128)(2,1)}), s16[8,400,128]{2,1,0:T(8,128)(2,1)S(1)}, u32[]{:S(2)}, u32[]{:S(2)}) async-start(s16[8,400,128]{2,1,0:T(8,128)(2,1)} %shard_map.77), calls=%async_computation.2 | async-start | bytes 1638400 | tf_op jit(solution)/shard_map/all_to_all | solution.py:247
  181.7 11.5 %shard_map.79 = s16[8,400,128]{2,1,0:T(8,128)(2,1)} custom-call(s32[24,10]{1,0:T(8,128)} %copy.21.cols, f32[1,1]{1,0:T(1,128)} %bitcast.17.shift, s32[1,2]{1,0:T(1,128)} %add_bitcast_fusion.here.place, s16[8,272,384]{2,1,0:T(8,128)(2,1)} %copy-done.1, s16[8,272,384]{2,1,0:T(8,128)(2,1)} %copy-done.1, f32[384,3072]{1,0:T(8,128)} %shard_map.75.y_ref, ...), custom_call_target="tpu_custom_call" | custom-call | flops 2013265920 | bytes 6291456 | tf_op jit(solution)/shard_map/pallas_call | solution.py:380
  193.2 9.6 %all-to-all-done.2.z_ref = s16[8,400,128]{2,1,0:T(8,128)(2,1)S(1)} async-done(((s16[8,400,128]{2,1,0:T(8,128)(2,1)}), s16[8,400,128]{2,1,0:T(8,128)(2,1)S(1)}, u32[]{:S(2)}, u32[]{:S(2)}) %all-to-all-start.2) | async-done | bytes 819232 | tf_op jit(solution)/shard_map/all_to_all | solution.py:247
  202.8 3.6 %all-to-all-start.4 = ((s16[8,400,128]{2,1,0:T(8,128)(2,1)}), s16[8,400,128]{2,1,0:T(8,128)(2,1)S(1)}, u32[]{:S(2)}, u32[]{:S(2)}) async-start(s16[8,400,128]{2,1,0:T(8,128)(2,1)} %shard_map.79), calls=%async_computation.4 | async-start | bytes 1638400 | tf_op jit(solution)/shard_map/all_to_all | solution.py:247
  207.6 2.8 shard_map.78.refs_0_.rest_4_
  211.8 11.5 %shard_map.82 = s16[8,400,128]{2,1,0:T(8,128)(2,1)} custom-call(s32[24,10]{1,0:T(8,128)} %copy.21.cols, f32[1,1]{1,0:T(1,128)} %bitcast.18.shift, s32[1,2]{1,0:T(1,128)} %add_bitcast_fusion.here.place, s16[8,272,384]{2,1,0:T(8,128)(2,1)} %copy-done.1, s16[8,272,384]{2,1,0:T(8,128)(2,1)} %copy-done.1, f32[384,3072]{1,0:T(8,128)} %shard_map.75.y_ref, ...), custom_call_target="tpu_custom_call" | custom-call | flops 2013265920 | bytes 6291456 | tf_op jit(solution)/shard_map/pallas_call | solution.py:380
  223.3 7.2 %collective-permute-done.31.refs_1_ = s16[8,400,128]{2,1,0:T(8,128)(2,1)} collective-permute-done((s16[8,400,128]{2,1,0:T(8,128)(2,1)}, s16[8,400,128]{2,1,0:T(8,128)(2,1)}, u32[]{:S(2)}, u32[]{:S(2)}) %collective-permute-start.31) | collective-permute-done | bytes 819232 | tf_op jit(solution)/shard_map/ppermute | solution.py:263
  230.5 5.7 %all-to-all-start.5 = ((s16[8,400,128]{2,1,0:T(8,128)(2,1)}), s16[8,400,128]{2,1,0:T(8,128)(2,1)S(1)}, u32[]{:S(2)}, u32[]{:S(2)}) async-start(s16[8,400,128]{2,1,0:T(8,128)(2,1)} %shard_map.82), calls=%async_computation.5 | async-start | bytes 1638400 | tf_op jit(solution)/shard_map/all_to_all | solution.py:247
  236.3 2.8 shard_map.80.refs_1_
  241.0 14.9 %all-to-all-done.5.z_ref = s16[8,400,128]{2,1,0:T(8,128)(2,1)S(1)} async-done(((s16[8,400,128]{2,1,0:T(8,128)(2,1)}), s16[8,400,128]{2,1,0:T(8,128)(2,1)S(1)}, u32[]{:S(2)}, u32[]{:S(2)}) %all-to-all-start.5) | async-done | bytes 819232 | tf_op jit(solution)/shard_map/all_to_all | solution.py:247
  256.8 2.8 shard_map.83.refs_1_
  259.7 1.6 collective-permute-start.37
  261.4 6.4 %shard_map.81.refs_0_ = f32[1,384,3072]{2,1,0:T(8,128)} custom-call(f32[1,4]{1,0:T(1,128)} %bitcast.30, s16[8,400,128]{2,1,0:T(8,128)(2,1)} %shard_map.78.refs_0_.rest_4_, s16[8,400,128]{2,1,0:T(8,128)(2,1)} %collective-permute-done.31.refs_1_, s16[8,400,128]{2,1,0:T(8,128)(2,1)} %collective-permute-done.32.refs_2_, ...), custom_call_target="tpu_custom_call" | custom-call | bytes 1 | tf_op jit(solution)/shard_map/pallas_call | solution.py:419
  269.6 6.4 %shard_map.84.refs_0_ = f32[1,384,3072]{2,1,0:T(8,128)} custom-call(f32[1,4]{1,0:T(1,128)} %bitcast.31, f32[1,384,3072]{2,1,0:T(8,128)} %shard_map.81.refs_0_, s16[8,400,128]{2,1,0:T(8,128)(2,1)} %shard_map.80.refs_1_, s16[8,400,128]{2,1,0:T(8,128)(2,1)} %copy-done.12, s16[8,400,128]{2,1,0:T(8,128)(2,1)} %copy-done.13, ...), custom_call_target="tpu_custom_call", output_to_operand_aliasing={{}: (1, {})} | custom-call | bytes 1 | tf_op jit(solution)/shard_map/pallas_call | solution.py:419
  275.9 4.6 %collective-permute-done.37.refs_2_ = s16[8,400,128]{2,1,0:T(8,128)(2,1)S(1)} collective-permute-done((s16[8,400,128]{2,1,0:T(8,128)(2,1)}, s16[8,400,128]{2,1,0:T(8,128)(2,1)S(1)}, u32[]{:S(2)}, u32[]{:S(2)}) %collective-permute-start.37) | collective-permute-done | bytes 819232 | tf_op jit(solution)/shard_map/ppermute | solution.py:263
  280.6 2.3 collective-permute-done.39.refs_4_
  283.8 6.4 %shard_map.85 = f32[1,384,3072]{2,1,0:T(8,128)} custom-call(f32[1,4]{1,0:T(1,128)} %bitcast.32, f32[1,384,3072]{2,1,0:T(8,128)} %shard_map.84.refs_0_, s16[8,400,128]{2,1,0:T(8,128)(2,1)} %shard_map.83.refs_1_, s16[8,400,128]{2,1,0:T(8,128)(2,1)} %copy-done.14, s16[8,400,128]{2,1,0:T(8,128)(2,1)} %copy-done.15, ...), custom_call_target="tpu_custom_call", output_to_operand_aliasing={{}: (1, {})} | custom-call | bytes 1 | tf_op jit(solution)/shard_map/pallas_call | solution.py:419
  (145 shorter events, 22.4 us)
Async XLA Ops:
  0.0 206.4 %copy-start = (f32[4,4]{1,0:T(4,128)S(1)}, f32[4,4]{1,0:T(4,128)}, u32[]{:S(2)}) copy-start(f32[4,4]{1,0:T(4,128)} %param.10) | copy-start | bytes 196
  1.9 9.0 %collective-permute-start = (bf16[30,32,128]{2,1,0:T(8,128)(2,1)S(1)}, bf16[30,32,128]{2,1,0:T(8,128)(2,1)S(1)}, u32[]{:S(2)}, u32[]{:S(2)}) collective-permute-start(bf16[30,32,128]{2,1,0:T(8,128)(2,1)S(1)} %bitcast.25), channel_id=1, source_target_pairs={{0,2},{2,4},{4,6},{6,7},{7,5},{5,3},{3,1},{1,0},{8,10},{10,12},{12... | collective-permute-start | bytes 737288 | tf_op jit(solution)/shard_map/ppermute | solution.py:312
  5.0 7.6 %collective-permute-start.4 = (bf16[30,32,128]{2,1,0:T(8,128)(2,1)S(1)}, bf16[30,32,128]{2,1,0:T(8,128)(2,1)S(1)}, u32[]{:S(2)}, u32[]{:S(2)}) collective-permute-start(bf16[30,32,128]{2,1,0:T(8,128)(2,1)S(1)} %bitcast.26), channel_id=1, source_target_pairs={{0,1},{2,0},{4,2},{6,4},{7,6},{5,7},{3,5},{1,3},{8,9},{10,8},{12,1... | collective-permute-start | bytes 737288 | tf_op jit(solution)/shard_map/ppermute | solution.py:312
  10.9 12.4 %collective-permute-start.1 = (bf16[30,32,128]{2,1,0:T(8,128)(2,1)S(1)}, bf16[30,32,128]{2,1,0:T(8,128)(2,1)S(1)}, u32[]{:S(2)}, u32[]{:S(2)}) collective-permute-start(bf16[30,32,128]{2,1,0:T(8,128)(2,1)S(1)} %collective-permute-done.rest_0_), channel_id=1, source_target_pairs={{0,16},{8,24},{16,0},{24,8},{1,17},{9,25},{17,1},{25,9},{2,18},{10... | collective-permute-start | bytes 737288 | tf_op jit(solution)/shard_map/ppermute | solution.py:263
  12.6 10.7 %collective-permute-start.5 = (bf16[30,32,128]{2,1,0:T(8,128)(2,1)S(1)}, bf16[30,32,128]{2,1,0:T(8,128)(2,1)S(1)}, u32[]{:S(2)}, u32[]{:S(2)}) collective-permute-start(bf16[30,32,128]{2,1,0:T(8,128)(2,1)S(1)} %collective-permute-done.4.rest_4_), channel_id=1, source_target_pairs={{0,16},{8,24},{16,0},{24,8},{1,17},{9,25},{17,1},{25,9},{2,18},{10... | collective-permute-start | bytes 737288 | tf_op jit(solution)/shard_map/ppermute | solution.py:263
  13.9 9.4 %collective-permute-start.8 = (bf16[30,32,128]{2,1,0:T(8,128)(2,1)S(1)}, bf16[30,32,128]{2,1,0:T(8,128)(2,1)S(1)}, u32[]{:S(2)}, u32[]{:S(2)}) collective-permute-start(bf16[30,32,128]{2,1,0:T(8,128)(2,1)S(1)} %collective-permute-done.rest_0_), channel_id=1, source_target_pairs={{0,2},{2,4},{4,6},{6,7},{7,5},{5,3},{3,1},{1,0},{8,10},{10,12},{12... | collective-permute-start | bytes 737288 | tf_op jit(solution)/shard_map/ppermute | solution.py:312
  15.5 7.9 %collective-permute-start.12 = (bf16[30,32,128]{2,1,0:T(8,128)(2,1)S(1)}, bf16[30,32,128]{2,1,0:T(8,128)(2,1)S(1)}, u32[]{:S(2)}, u32[]{:S(2)}) collective-permute-start(bf16[30,32,128]{2,1,0:T(8,128)(2,1)S(1)} %collective-permute-done.4.rest_4_), channel_id=1, source_target_pairs={{0,1},{2,0},{4,2},{6,4},{7,6},{5,7},{3,5},{1,3},{8,9},{10,8},{12,1... | collective-permute-start | bytes 737288 | tf_op jit(solution)/shard_map/ppermute | solution.py:312
  23.3 53.0 %copy-start.18 = (s32[24,10]{0,1:T(8,128)S(1)}, s32[24,10]{0,1:T(8,128)}, u32[]{:S(2)}) copy-start(s32[24,10]{0,1:T(8,128)} %param.12) | copy-start | bytes 2884
  23.4 6.4 %collective-permute-start.16 = (bf16[30,32,128]{2,1,0:T(8,128)(2,1)S(1)}, bf16[30,32,128]{2,1,0:T(8,128)(2,1)S(1)}, u32[]{:S(2)}, u32[]{:S(2)}) collective-permute-start(bf16[30,32,128]{2,1,0:T(8,128)(2,1)S(1)} %collective-permute-done.8.rest_8_), channel_id=1, source_target_pairs={{0,2},{2,4},{4,6},{6,7},{7,5},{5,3},{3,1},{1,0},{8,10},{10,12},{12... | collective-permute-start | bytes 737288 | tf_op jit(solution)/shard_map/ppermute | solution.py:312
  25.0 6.8 %collective-permute-start.20 = (bf16[30,32,128]{2,1,0:T(8,128)(2,1)S(1)}, bf16[30,32,128]{2,1,0:T(8,128)(2,1)S(1)}, u32[]{:S(2)}, u32[]{:S(2)}) collective-permute-start(bf16[30,32,128]{2,1,0:T(8,128)(2,1)S(1)} %collective-permute-done.12.rest_12_), channel_id=1, source_target_pairs={{0,1},{2,0},{4,2},{6,4},{7,6},{5,7},{3,5},{1,3},{8,9},{10,8},{12,1... | collective-permute-start | bytes 737288 | tf_op jit(solution)/shard_map/ppermute | solution.py:312
  29.8 6.2 %collective-permute-start.24 = (bf16[30,32,128]{2,1,0:T(8,128)(2,1)S(1)}, bf16[30,32,128]{2,1,0:T(8,128)(2,1)S(1)}, u32[]{:S(2)}, u32[]{:S(2)}) collective-permute-start(bf16[30,32,128]{2,1,0:T(8,128)(2,1)S(1)} %collective-permute-done.16.rest_16_), channel_id=1, source_target_pairs={{0,2},{2,4},{4,6},{6,7},{7,5},{5,3},{3,1},{1,0},{8,10},{10,12},{12... | collective-permute-start | bytes 737288 | tf_op jit(solution)/shard_map/ppermute | solution.py:312
  36.7 70.8 %all-to-all-start = ((s16[8,496,384]{2,1,0:T(8,128)(2,1)}), s16[8,496,384]{2,1,0:T(8,128)(2,1)S(1)}, u32[]{:S(2)}, u32[]{:S(2)}) async-start(s16[8,496,384]{2,1,0:T(8,128)(2,1)} %shard_map.73), calls=%async_computation | async-start | bytes 6094848 | tf_op jit(solution)/shard_map/all_to_all | solution.py:247
  42.7 2.7 collective-permute-start.2
  42.7 2.6 collective-permute-start.6
  43.2 3.5 %collective-permute-start.3 = (bf16[30,32,128]{2,1,0:T(8,128)(2,1)}, bf16[30,32,128]{2,1,0:T(8,128)(2,1)S(1)}, u32[]{:S(2)}, u32[]{:S(2)}) collective-permute-start(bf16[30,32,128]{2,1,0:T(8,128)(2,1)} %copy-done.21), channel_id=1, source_target_pairs={{0,8},{8,0},{16,24},{24,16},{1,9},{9,1},{17,25},{25,17},{2,10},{10... | collective-permute-start | bytes 737288 | tf_op jit(solution)/shard_map/ppermute | solution.py:263
  43.3 9.0 %collective-permute-start.9 = (bf16[30,32,128]{2,1,0:T(8,128)(2,1)}, bf16[30,32,128]{2,1,0:T(8,128)(2,1)S(1)}, u32[]{:S(2)}, u32[]{:S(2)}) collective-permute-start(bf16[30,32,128]{2,1,0:T(8,128)(2,1)} %copy-done.23), channel_id=1, source_target_pairs={{0,16},{8,24},{16,0},{24,8},{1,17},{9,25},{17,1},{25,9},{2,18},{10... | collective-permute-start | bytes 737288 | tf_op jit(solution)/shard_map/ppermute | solution.py:263
  44.8 12.3 %collective-permute-start.13 = (bf16[30,32,128]{2,1,0:T(8,128)(2,1)}, bf16[30,32,128]{2,1,0:T(8,128)(2,1)S(1)}, u32[]{:S(2)}, u32[]{:S(2)}) collective-permute-start(bf16[30,32,128]{2,1,0:T(8,128)(2,1)} %copy-done.24), channel_id=1, source_target_pairs={{0,16},{8,24},{16,0},{24,8},{1,17},{9,25},{17,1},{25,9},{2,18},{10... | collective-permute-start | bytes 737288 | tf_op jit(solution)/shard_map/ppermute | solution.py:263
  45.4 11.8 %collective-permute-start.7 = (bf16[30,32,128]{2,1,0:T(8,128)(2,1)}, bf16[30,32,128]{2,1,0:T(8,128)(2,1)S(1)}, u32[]{:S(2)}, u32[]{:S(2)}) collective-permute-start(bf16[30,32,128]{2,1,0:T(8,128)(2,1)} %copy-done.22), channel_id=1, source_target_pairs={{0,8},{8,0},{16,24},{24,16},{1,9},{9,1},{17,25},{25,17},{2,10},{10... | collective-permute-start | bytes 737288 | tf_op jit(solution)/shard_map/ppermute | solution.py:263
  46.1 12.6 %collective-permute-start.10 = (bf16[30,32,128]{2,1,0:T(8,128)(2,1)}, bf16[30,32,128]{2,1,0:T(8,128)(2,1)S(1)}, u32[]{:S(2)}, u32[]{:S(2)}) collective-permute-start(bf16[30,32,128]{2,1,0:T(8,128)(2,1)} %copy-done.23), channel_id=1, source_target_pairs={{0,8},{8,0},{16,24},{24,16},{1,9},{9,1},{17,25},{25,17},{2,10},{10... | collective-permute-start | bytes 737288 | tf_op jit(solution)/shard_map/ppermute | solution.py:263
  47.5 11.4 %collective-permute-start.14 = (bf16[30,32,128]{2,1,0:T(8,128)(2,1)}, bf16[30,32,128]{2,1,0:T(8,128)(2,1)S(1)}, u32[]{:S(2)}, u32[]{:S(2)}) collective-permute-start(bf16[30,32,128]{2,1,0:T(8,128)(2,1)} %copy-done.24), channel_id=1, source_target_pairs={{0,8},{8,0},{16,24},{24,16},{1,9},{9,1},{17,25},{25,17},{2,10},{10... | collective-permute-start | bytes 737288 | tf_op jit(solution)/shard_map/ppermute | solution.py:263
  53.0 6.4 %collective-permute-start.11 = (bf16[30,32,128]{2,1,0:T(8,128)(2,1)S(1)}, bf16[30,32,128]{2,1,0:T(8,128)(2,1)S(1)}, u32[]{:S(2)}, u32[]{:S(2)}) collective-permute-start(bf16[30,32,128]{2,1,0:T(8,128)(2,1)S(1)} %collective-permute-done.9.rest_9_), channel_id=1, source_target_pairs={{0,8},{8,0},{16,24},{24,16},{1,9},{9,1},{17,25},{25,17},{2,10},{10... | collective-permute-start | bytes 737288 | tf_op jit(solution)/shard_map/ppermute | solution.py:263
  57.1 3.9 %collective-permute-start.15 = (bf16[30,32,128]{2,1,0:T(8,128)(2,1)S(1)}, bf16[30,32,128]{2,1,0:T(8,128)(2,1)S(1)}, u32[]{:S(2)}, u32[]{:S(2)}) collective-permute-start(bf16[30,32,128]{2,1,0:T(8,128)(2,1)S(1)} %collective-permute-done.13.rest_13_), channel_id=1, source_target_pairs={{0,8},{8,0},{16,24},{24,16},{1,9},{9,1},{17,25},{25,17},{2,10},{10... | collective-permute-start | bytes 737288 | tf_op jit(solution)/shard_map/ppermute | solution.py:263
  57.1 9.1 %collective-permute-start.17 = (bf16[30,32,128]{2,1,0:T(8,128)(2,1)}, bf16[30,32,128]{2,1,0:T(8,128)(2,1)}, u32[]{:S(2)}, u32[]{:S(2)}) collective-permute-start(bf16[30,32,128]{2,1,0:T(8,128)(2,1)} %copy-done.25), channel_id=1, source_target_pairs={{0,16},{8,24},{16,0},{24,8},{1,17},{9,25},{17,1},{25,9},{2,18},{10... | collective-permute-start | bytes 737288 | tf_op jit(solution)/shard_map/ppermute | solution.py:263
  58.7 7.6 %collective-permute-start.18 = (bf16[30,32,128]{2,1,0:T(8,128)(2,1)}, bf16[30,32,128]{2,1,0:T(8,128)(2,1)}, u32[]{:S(2)}, u32[]{:S(2)}) collective-permute-start(bf16[30,32,128]{2,1,0:T(8,128)(2,1)} %copy-done.25), channel_id=1, source_target_pairs={{0,8},{8,0},{16,24},{24,16},{1,9},{9,1},{17,25},{25,17},{2,10},{10... | collective-permute-start | bytes 737288 | tf_op jit(solution)/shard_map/ppermute | solution.py:263
  58.9 12.7 %collective-permute-start.21 = (bf16[30,32,128]{2,1,0:T(8,128)(2,1)}, bf16[30,32,128]{2,1,0:T(8,128)(2,1)}, u32[]{:S(2)}, u32[]{:S(2)}) collective-permute-start(bf16[30,32,128]{2,1,0:T(8,128)(2,1)} %copy-done.26), channel_id=1, source_target_pairs={{0,16},{8,24},{16,0},{24,8},{1,17},{9,25},{17,1},{25,9},{2,18},{10... | collective-permute-start | bytes 737288 | tf_op jit(solution)/shard_map/ppermute | solution.py:263
  59.4 16.9 %collective-permute-start.25 = (bf16[30,32,128]{2,1,0:T(8,128)(2,1)}, bf16[30,32,128]{2,1,0:T(8,128)(2,1)}, u32[]{:S(2)}, u32[]{:S(2)}) collective-permute-start(bf16[30,32,128]{2,1,0:T(8,128)(2,1)} %copy-done.27), channel_id=1, source_target_pairs={{0,16},{8,24},{16,0},{24,8},{1,17},{9,25},{17,1},{25,9},{2,18},{10... | collective-permute-start | bytes 737288 | tf_op jit(solution)/shard_map/ppermute | solution.py:263
  61.0 19.0 %collective-permute-start.22 = (bf16[30,32,128]{2,1,0:T(8,128)(2,1)}, bf16[30,32,128]{2,1,0:T(8,128)(2,1)}, u32[]{:S(2)}, u32[]{:S(2)}) collective-permute-start(bf16[30,32,128]{2,1,0:T(8,128)(2,1)} %copy-done.26), channel_id=1, source_target_pairs={{0,8},{8,0},{16,24},{24,16},{1,9},{9,1},{17,25},{25,17},{2,10},{10... | collective-permute-start | bytes 737288 | tf_op jit(solution)/shard_map/ppermute | solution.py:263
  66.3 13.7 %collective-permute-start.26 = (bf16[30,32,128]{2,1,0:T(8,128)(2,1)}, bf16[30,32,128]{2,1,0:T(8,128)(2,1)}, u32[]{:S(2)}, u32[]{:S(2)}) collective-permute-start(bf16[30,32,128]{2,1,0:T(8,128)(2,1)} %copy-done.27), channel_id=1, source_target_pairs={{0,8},{8,0},{16,24},{24,16},{1,9},{9,1},{17,25},{25,17},{2,10},{10... | collective-permute-start | bytes 737288 | tf_op jit(solution)/shard_map/ppermute | solution.py:263
  66.3 13.7 %collective-permute-start.19 = (bf16[30,32,128]{2,1,0:T(8,128)(2,1)}, bf16[30,32,128]{2,1,0:T(8,128)(2,1)}, u32[]{:S(2)}, u32[]{:S(2)}) collective-permute-start(bf16[30,32,128]{2,1,0:T(8,128)(2,1)} %collective-permute-done.17.rest_17_), channel_id=1, source_target_pairs={{0,8},{8,0},{16,24},{24,16},{1,9},{9,1},{17,25},{25,17},{2,10},{10... | collective-permute-start | bytes 737288 | tf_op jit(solution)/shard_map/ppermute | solution.py:263
  71.5 8.4 %collective-permute-start.23 = (bf16[30,32,128]{2,1,0:T(8,128)(2,1)}, bf16[30,32,128]{2,1,0:T(8,128)(2,1)}, u32[]{:S(2)}, u32[]{:S(2)}) collective-permute-start(bf16[30,32,128]{2,1,0:T(8,128)(2,1)} %collective-permute-done.21.rest_21_), channel_id=1, source_target_pairs={{0,8},{8,0},{16,24},{24,16},{1,9},{9,1},{17,25},{25,17},{2,10},{10... | collective-permute-start | bytes 737288 | tf_op jit(solution)/shard_map/ppermute | solution.py:263
  76.3 3.6 %collective-permute-start.27 = (bf16[30,32,128]{2,1,0:T(8,128)(2,1)}, bf16[30,32,128]{2,1,0:T(8,128)(2,1)}, u32[]{:S(2)}, u32[]{:S(2)}) collective-permute-start(bf16[30,32,128]{2,1,0:T(8,128)(2,1)} %collective-permute-done.25.rest_25_), channel_id=1, source_target_pairs={{0,8},{8,0},{16,24},{24,16},{1,9},{9,1},{17,25},{25,17},{2,10},{10... | collective-permute-start | bytes 737288 | tf_op jit(solution)/shard_map/ppermute | solution.py:263
  109.1 26.1 %all-to-all-start.1 = ((s16[8,144,384]{2,1,0:T(8,128)(2,1)}), s16[8,144,384]{2,1,0:T(8,128)(2,1)S(1)}, u32[]{:S(2)}, u32[]{:S(2)}) async-start(s16[8,144,384]{2,1,0:T(8,128)(2,1)} %get-tuple-element.30), calls=%async_computation.1 | async-start | bytes 1769472 | tf_op jit(solution)/shard_map/all_to_all | solution.py:247
  135.2 43.0 %all-to-all-start.3 = ((s16[8,272,384]{2,1,0:T(8,128)(2,1)}), s16[8,272,384]{2,1,0:T(8,128)(2,1)S(1)}, u32[]{:S(2)}, u32[]{:S(2)}) async-start(s16[8,272,384]{2,1,0:T(8,128)(2,1)} %get-tuple-element.36), calls=%async_computation.3 | async-start | bytes 3342336 | tf_op jit(solution)/shard_map/all_to_all | solution.py:247
  140.1 20.7 %collective-permute-start.28 = (s16[8,96,384]{2,1,0:T(8,128)(2,1)S(1)}, s16[8,96,384]{2,1,0:T(8,128)(2,1)S(1)}, u32[]{:S(2)}, u32[]{:S(2)}) collective-permute-start(s16[8,96,384]{2,1,0:T(8,128)(2,1)S(1)} %slice.6.rest_0_), channel_id=1, source_target_pairs={{0,16},{8,24},{16,0},{24,8},{1,17},{9,25},{17,1},{25,9},{2,18},{10... | collective-permute-start | bytes 1769480 | tf_op jit(solution)/shard_map/ppermute | solution.py:263
  141.6 19.7 %collective-permute-start.29 = (s16[8,96,384]{2,1,0:T(8,128)(2,1)S(1)}, s16[8,96,384]{2,1,0:T(8,128)(2,1)S(1)}, u32[]{:S(2)}, u32[]{:S(2)}) collective-permute-start(s16[8,96,384]{2,1,0:T(8,128)(2,1)S(1)} %slice.6.rest_0_), channel_id=1, source_target_pairs={{0,8},{8,0},{16,24},{24,16},{1,9},{9,1},{17,25},{25,17},{2,10},{10... | collective-permute-start | bytes 1769480 | tf_op jit(solution)/shard_map/ppermute | solution.py:263
  160.8 2.2 collective-permute-start.30
  178.1 24.7 %all-to-all-start.2 = ((s16[8,400,128]{2,1,0:T(8,128)(2,1)}), s16[8,400,128]{2,1,0:T(8,128)(2,1)S(1)}, u32[]{:S(2)}, u32[]{:S(2)}) async-start(s16[8,400,128]{2,1,0:T(8,128)(2,1)} %shard_map.77), calls=%async_computation.2 | async-start | bytes 1638400 | tf_op jit(solution)/shard_map/all_to_all | solution.py:247
  202.8 27.7 %all-to-all-start.4 = ((s16[8,400,128]{2,1,0:T(8,128)(2,1)}), s16[8,400,128]{2,1,0:T(8,128)(2,1)S(1)}, u32[]{:S(2)}, u32[]{:S(2)}) async-start(s16[8,400,128]{2,1,0:T(8,128)(2,1)} %shard_map.79), calls=%async_computation.4 | async-start | bytes 1638400 | tf_op jit(solution)/shard_map/all_to_all | solution.py:247
  210.3 20.2 %collective-permute-start.31 = (s16[8,400,128]{2,1,0:T(8,128)(2,1)}, s16[8,400,128]{2,1,0:T(8,128)(2,1)}, u32[]{:S(2)}, u32[]{:S(2)}) collective-permute-start(s16[8,400,128]{2,1,0:T(8,128)(2,1)} %shard_map.78.refs_0_.rest_4_), channel_id=1, source_target_pairs={{0,16},{8,24},{16,0},{24,8},{1,17},{9,25},{17,1},{25,9},{2,18},{10... | collective-permute-start | bytes 2457608 | tf_op jit(solution)/shard_map/ppermute | solution.py:263
  230.5 25.4 %all-to-all-start.5 = ((s16[8,400,128]{2,1,0:T(8,128)(2,1)}), s16[8,400,128]{2,1,0:T(8,128)(2,1)S(1)}, u32[]{:S(2)}, u32[]{:S(2)}) async-start(s16[8,400,128]{2,1,0:T(8,128)(2,1)} %shard_map.82), calls=%async_computation.5 | async-start | bytes 1638400 | tf_op jit(solution)/shard_map/all_to_all | solution.py:247
  239.0 20.6 %collective-permute-start.34 = (s16[8,400,128]{2,1,0:T(8,128)(2,1)}, s16[8,400,128]{2,1,0:T(8,128)(2,1)S(1)}, u32[]{:S(2)}, u32[]{:S(2)}) collective-permute-start(s16[8,400,128]{2,1,0:T(8,128)(2,1)} %shard_map.80.refs_1_), channel_id=1, source_target_pairs={{0,16},{8,24},{16,0},{24,8},{1,17},{9,25},{17,1},{25,9},{2,18},{10... | collective-permute-start | bytes 2457608 | tf_op jit(solution)/shard_map/ppermute | solution.py:263
  240.5 20.7 %collective-permute-start.32 = (s16[8,400,128]{2,1,0:T(8,128)(2,1)S(1)}, s16[8,400,128]{2,1,0:T(8,128)(2,1)}, u32[]{:S(2)}, u32[]{:S(2)}) collective-permute-start(s16[8,400,128]{2,1,0:T(8,128)(2,1)S(1)} %copy-done.4), channel_id=1, source_target_pairs={{0,8},{8,0},{16,24},{24,16},{1,9},{9,1},{17,25},{25,17},{2,10},{10... | collective-permute-start | bytes 2457608 | tf_op jit(solution)/shard_map/ppermute | solution.py:263
  240.5 27.3 %collective-permute-start.35 = (s16[8,400,128]{2,1,0:T(8,128)(2,1)}, s16[8,400,128]{2,1,0:T(8,128)(2,1)S(1)}, u32[]{:S(2)}, u32[]{:S(2)}) collective-permute-start(s16[8,400,128]{2,1,0:T(8,128)(2,1)} %shard_map.80.refs_1_), channel_id=1, source_target_pairs={{0,8},{8,0},{16,24},{24,16},{1,9},{9,1},{17,25},{25,17},{2,10},{10... | collective-permute-start | bytes 2457608 | tf_op jit(solution)/shard_map/ppermute | solution.py:263
  241.0 20.4 %collective-permute-start.33 = (s16[8,400,128]{2,1,0:T(8,128)(2,1)}, s16[8,400,128]{2,1,0:T(8,128)(2,1)}, u32[]{:S(2)}, u32[]{:S(2)}) collective-permute-start(s16[8,400,128]{2,1,0:T(8,128)(2,1)} %collective-permute-done.31.refs_1_), channel_id=1, source_target_pairs={{0,8},{8,0},{16,24},{24,16},{1,9},{9,1},{17,25},{25,17},{2,10},{10... | collective-permute-start | bytes 2457608 | tf_op jit(solution)/shard_map/ppermute | solution.py:263
  259.6 8.2 %collective-permute-start.36 = (s16[8,400,128]{2,1,0:T(8,128)(2,1)S(1)}, s16[8,400,128]{2,1,0:T(8,128)(2,1)S(1)}, u32[]{:S(2)}, u32[]{:S(2)}) collective-permute-start(s16[8,400,128]{2,1,0:T(8,128)(2,1)S(1)} %collective-permute-done.34.refs_2_), channel_id=1, source_target_pairs={{0,8},{8,0},{16,24},{24,16},{1,9},{9,1},{17,25},{25,17},{2,10},{10... | collective-permute-start | bytes 2457608 | tf_op jit(solution)/shard_map/ppermute | solution.py:263
  259.7 20.9 %collective-permute-start.37 = (s16[8,400,128]{2,1,0:T(8,128)(2,1)}, s16[8,400,128]{2,1,0:T(8,128)(2,1)S(1)}, u32[]{:S(2)}, u32[]{:S(2)}) collective-permute-start(s16[8,400,128]{2,1,0:T(8,128)(2,1)} %shard_map.83.refs_1_), channel_id=1, source_target_pairs={{0,16},{8,24},{16,0},{24,8},{1,17},{9,25},{17,1},{25,9},{2,18},{10... | collective-permute-start | bytes 2457608 | tf_op jit(solution)/shard_map/ppermute | solution.py:263
  261.2 19.3 %collective-permute-start.38 = (s16[8,400,128]{2,1,0:T(8,128)(2,1)}, s16[8,400,128]{2,1,0:T(8,128)(2,1)S(1)}, u32[]{:S(2)}, u32[]{:S(2)}) collective-permute-start(s16[8,400,128]{2,1,0:T(8,128)(2,1)} %shard_map.83.refs_1_), channel_id=1, source_target_pairs={{0,8},{8,0},{16,24},{24,16},{1,9},{9,1},{17,25},{25,17},{2,10},{10... | collective-permute-start | bytes 2457608 | tf_op jit(solution)/shard_map/ppermute | solution.py:263
  280.6 2.3 collective-permute-start.39
  (37 other events, 287.8 us)

commit v12 on v11

--- a/solution.py
+++ b/solution.py
@@ -288,7 +288,7 @@
     height = width + PAD + slab
 
     def pack(start, diagonal):
-        pair = 2 if groups % 2 == 0 else 1
+        pair = 4 if groups % 4 == 0 else 1
         pieces = pl.BlockSpec((rows, pair * width), lambda q: (0, q))
         return call(
             pack_kernel,

time: 292 us -> 292 us (level)
  transfers between devices with their start and end apart: 46 -> 46, of which waited for: 17 -> 18; matrix products, arithmetic and copies ran while one was open for 2% -> 2% of each run, Pallas kernels for 43% -> 42%
where the time goes in v12:
time: 292 us; the launch traced here: 290 us
  Pallas kernels  129 us (44%)
  waiting for transfers between devices  90 us (31%)
  starting transfers between devices  52.6 us (18%)
  local copies, waits for them, and re-layouts  16.7 us (6%)
    ppermute x33, waiting for transfers between devices, cross(): return have + [lax.ppermute(h, 'root', pairs) for h in have]  40.3 us
    all_to_all x6, waiting for transfers between devices, swap(): lax.all_to_all(pieces, 'col', split_axis=0, concat_axis=0, tiled=True)  35 us
    pallas_call x3, Pallas kernels, blocked_shards(): call(functools.partial(left_second_kernel, dims, masks), groups, [smem(),...  34.4 us
    all_to_all x6, starting transfers between devices, swap(): lax.all_to_all(pieces, 'col', split_axis=0, concat_axis=0, tiled=True)  26.2 us
    pallas_call x1, Pallas kernels, blocked_shards(): call(functools.partial(right_first_kernel, dims, groups, owners, masks),...  24.7 us
    pallas_call x1, Pallas kernels, blocked_shards(): call(functools.partial(right_second_kernel, dims), groups, [smem(), smem(...  19.1 us
    pallas_call x3, Pallas kernels, blocked_shards(): call(functools.partial(rotate_kernel, len(out)), groups, [smem()] + [pl.B...  19.1 us
    pallas_call x1, Pallas kernels, blocked_shards(): call(functools.partial(left_first_kernel, dims), groups, [smem(), all_cod...  17.6 us
  transfers between devices with their start and end apart: 46, of which 18 were waited for; matrix products, arithmetic and copies ran while one was open for 2% of the time, Pallas kernels for 42%

profile of v12, /device:TPU:0, one launch (start us, length us, event | category | flops | bytes accessed | tf_op | source)
XLA Modules:
  0.0 290.1 jit_solution(10184606350699379600)
XLA Ops:
  0.0 1.6 constant_dynamic-slice_fusion
  1.9 3.1 %collective-permute-start = (bf16[30,32,128]{2,1,0:T(8,128)(2,1)S(1)}, bf16[30,32,128]{2,1,0:T(8,128)(2,1)S(1)}, u32[]{:S(2)}, u32[]{:S(2)}) collective-permute-start(bf16[30,32,128]{2,1,0:T(8,128)(2,1)S(1)} %bitcast.25), channel_id=1, source_target_pairs={{0,2},{2,4},{4,6},{6,7},{7,5},{5,3},{3,1},{1,0},{8,10},{10,12},{12... | collective-permute-start | bytes 737288 | tf_op jit(solution)/shard_map/ppermute | solution.py:312
  5.0 5.9 %collective-permute-done.rest_0_ = bf16[30,32,128]{2,1,0:T(8,128)(2,1)S(1)} collective-permute-done((bf16[30,32,128]{2,1,0:T(8,128)(2,1)S(1)}, bf16[30,32,128]{2,1,0:T(8,128)(2,1)S(1)}, u32[]{:S(2)}, u32[]{:S(2)}) %collective-permute-start) | collective-permute-done | bytes 245792 | tf_op jit(solution)/shard_map/ppermute | solution.py:312
  10.9 1.7 collective-permute-start.1
  13.9 1.6 collective-permute-start.8
  16.6 6.0 %shard_map.73 = s16[8,496,384]{2,1,0:T(8,128)(2,1)} custom-call(s32[1,2]{1,0:T(1,128)} %add_bitcast_fusion.here.place, f32[384,3072]{1,0:T(8,128)} %bitcast.19, f32[384,3072]{1,0:T(8,128)} %d_ref.4), custom_call_target="tpu_custom_call" | custom-call | bytes 14155776 | tf_op jit(solution)/shard_map/pallas_call | solution.py:293
  23.3 1.5 collective-permute-start.16
  25.4 4.3 %collective-permute-done.16.rest_16_ = bf16[30,32,128]{2,1,0:T(8,128)(2,1)S(1)} collective-permute-done((bf16[30,32,128]{2,1,0:T(8,128)(2,1)S(1)}, bf16[30,32,128]{2,1,0:T(8,128)(2,1)S(1)}, u32[]{:S(2)}, u32[]{:S(2)}) %collective-permute-start.16) | collective-permute-done | bytes 245792 | tf_op jit(solution)/shard_map/ppermute | solution.py:312
  29.8 1.8 collective-permute-start.24
  31.5 4.4 %collective-permute-done.24.rest_24_ = bf16[30,32,128]{2,1,0:T(8,128)(2,1)S(1)} collective-permute-done((bf16[30,32,128]{2,1,0:T(8,128)(2,1)S(1)}, bf16[30,32,128]{2,1,0:T(8,128)(2,1)S(1)}, u32[]{:S(2)}, u32[]{:S(2)}) %collective-permute-start.24) | collective-permute-done | bytes 245792 | tf_op jit(solution)/shard_map/ppermute | solution.py:312
  36.6 6.0 %all-to-all-start = ((s16[8,496,384]{2,1,0:T(8,128)(2,1)}), s16[8,496,384]{2,1,0:T(8,128)(2,1)S(1)}, u32[]{:S(2)}, u32[]{:S(2)}) async-start(s16[8,496,384]{2,1,0:T(8,128)(2,1)} %shard_map.73), calls=%async_computation | async-start | bytes 6094848 | tf_op jit(solution)/shard_map/all_to_all | solution.py:247
  47.5 4.8 %collective-permute-done.9.rest_9_ = bf16[30,32,128]{2,1,0:T(8,128)(2,1)S(1)} collective-permute-done((bf16[30,32,128]{2,1,0:T(8,128)(2,1)}, bf16[30,32,128]{2,1,0:T(8,128)(2,1)S(1)}, u32[]{:S(2)}, u32[]{:S(2)}) %collective-permute-start.9) | collective-permute-done | bytes 245792 | tf_op jit(solution)/shard_map/ppermute | solution.py:263
  53.0 4.1 %collective-permute-done.13.rest_13_ = bf16[30,32,128]{2,1,0:T(8,128)(2,1)S(1)} collective-permute-done((bf16[30,32,128]{2,1,0:T(8,128)(2,1)}, bf16[30,32,128]{2,1,0:T(8,128)(2,1)S(1)}, u32[]{:S(2)}, u32[]{:S(2)}) %collective-permute-start.13) | collective-permute-done | bytes 245792 | tf_op jit(solution)/shard_map/ppermute | solution.py:263
  57.1 1.6 collective-permute-start.17
  59.4 1.6 collective-permute-start.25
  61.0 5.2 %collective-permute-done.17.rest_17_ = bf16[30,32,128]{2,1,0:T(8,128)(2,1)} collective-permute-done((bf16[30,32,128]{2,1,0:T(8,128)(2,1)}, bf16[30,32,128]{2,1,0:T(8,128)(2,1)}, u32[]{:S(2)}, u32[]{:S(2)}) %collective-permute-start.17) | collective-permute-done | bytes 245792 | tf_op jit(solution)/shard_map/ppermute | solution.py:263
  66.8 4.7 %collective-permute-done.21.rest_21_ = bf16[30,32,128]{2,1,0:T(8,128)(2,1)} collective-permute-done((bf16[30,32,128]{2,1,0:T(8,128)(2,1)}, bf16[30,32,128]{2,1,0:T(8,128)(2,1)}, u32[]{:S(2)}, u32[]{:S(2)}) %collective-permute-start.21) | collective-permute-done | bytes 245792 | tf_op jit(solution)/shard_map/ppermute | solution.py:263
  71.5 4.8 %collective-permute-done.25.rest_25_ = bf16[30,32,128]{2,1,0:T(8,128)(2,1)} collective-permute-done((bf16[30,32,128]{2,1,0:T(8,128)(2,1)}, bf16[30,32,128]{2,1,0:T(8,128)(2,1)}, u32[]{:S(2)}, u32[]{:S(2)}) %collective-permute-start.25) | collective-permute-done | bytes 245792 | tf_op jit(solution)/shard_map/ppermute | solution.py:263
  77.7 2.2 copy.16
  80.0 24.7 %shard_map.74 = (f32[384,3072]{1,0:T(8,128)}, s16[8,144,384]{2,1,0:T(8,128)(2,1)}, s16[8,272,384]{2,1,0:T(8,128)(2,1)}, bf16[30720,128]{1,0:T(8,128)(2,1)}) custom-call(s32[24,10]{1,0:T(8,128)} %copy.21.cols, f32[1,1]{1,0:T(1,128)} %bitcast.14.shift, s32[1,2]{1,0:T(1,128)} %add_bitcast_fusion.here.place, f32[384,3072]{1,0:T(8,128)} %bitcast.20, ...), custom_call_target="tpu_custom_call" | custom-call | flops 6039797760 | bytes 28311552 | tf_op jit(solution)/shard_map/pallas_call | solution.py:324
  104.6 2.8 all-to-all-done.tv_ref
  107.5 1.6 copy-done.8
  109.1 3.5 %all-to-all-start.1 = ((s16[8,144,384]{2,1,0:T(8,128)(2,1)}), s16[8,144,384]{2,1,0:T(8,128)(2,1)S(1)}, u32[]{:S(2)}, u32[]{:S(2)}) async-start(s16[8,144,384]{2,1,0:T(8,128)(2,1)} %get-tuple-element.30), calls=%async_computation.1 | async-start | bytes 1769472 | tf_op jit(solution)/shard_map/all_to_all | solution.py:247
  112.7 17.6 %shard_map.75.y_ref = f32[384,3072]{1,0:T(8,128)} custom-call(s32[24,10]{1,0:T(8,128)} %copy.21.cols, s16[8,496,384]{2,1,0:T(8,128)(2,1)} %copy-done.8, bf16[30720,128]{1,0:T(8,128)(2,1)} %get-tuple-element.31.tiles), custom_call_target="tpu_custom_call" | custom-call | flops 6039797760 | bytes 14155776 | tf_op jit(solution)/shard_map/pallas_call | solution.py:349
  130.3 4.9 %all-to-all-done.1.after.tu_ref.tail_ref = s16[8,144,384]{2,1,0:T(8,128)(2,1)S(1)} async-done(((s16[8,144,384]{2,1,0:T(8,128)(2,1)}), s16[8,144,384]{2,1,0:T(8,128)(2,1)S(1)}, u32[]{:S(2)}, u32[]{:S(2)}) %all-to-all-start.1) | async-done | bytes 884768 | tf_op jit(solution)/shard_map/all_to_all | solution.py:247
  135.2 3.8 %all-to-all-start.3 = ((s16[8,272,384]{2,1,0:T(8,128)(2,1)}), s16[8,272,384]{2,1,0:T(8,128)(2,1)S(1)}, u32[]{:S(2)}, u32[]{:S(2)}) async-start(s16[8,272,384]{2,1,0:T(8,128)(2,1)} %get-tuple-element.36), calls=%async_computation.3 | async-start | bytes 3342336 | tf_op jit(solution)/shard_map/all_to_all | solution.py:247
  140.1 1.6 collective-permute-start.28
  141.6 19.1 %shard_map.76 = (f32[384,1024]{1,0:T(8,128)}, f32[384,1024]{1,0:T(8,128)}, f32[384,1024]{1,0:T(8,128)}) custom-call(s32[24,10]{1,0:T(8,128)} %copy.21.cols, f32[1,1]{1,0:T(1,128)} %bitcast.15.shift, f32[384,3072]{1,0:T(8,128)} %get-tuple-element.32.w_ref, f32[384,3072]{1,0:T(8,128)} %bitcast.21, f32[384,3072]{1,0:T(8,128)} %d_ref.4, ...), custom_call_target="tpu_custom_call" | custom-call | flops 6039797760 | bytes 23592960 | tf_op jit(solution)/shard_map/pallas_call | solution.py:361
  161.3 1.6 collective-permute-done.30.rest_3_
  163.8 11.5 %shard_map.77 = s16[8,400,128]{2,1,0:T(8,128)(2,1)} custom-call(s32[24,10]{1,0:T(8,128)} %copy.21.cols, f32[1,1]{1,0:T(1,128)} %bitcast.16.shift, s32[1,2]{1,0:T(1,128)} %add_bitcast_fusion.here.place, s16[8,144,384]{2,1,0:T(8,128)(2,1)} %copy-done.2, s16[8,144,384]{2,1,0:T(8,128)(2,1)} %copy-done.2, f32[384,3072]{1,0:T(8,128)} %shard_map.75.y_ref, ...), custom_call_target="tpu_custom_call" | custom-call | flops 2013265920 | bytes 6291456 | tf_op jit(solution)/shard_map/pallas_call | solution.py:380
  175.3 2.9 all-to-all-done.3.tu_ref.tail_ref
  178.1 3.6 %all-to-all-start.2 = ((s16[8,400,128]{2,1,0:T(8,128)(2,1)}), s16[8,400,128]{2,1,0:T(8,128)(2,1)S(1)}, u32[]{:S(2)}, u32[]{:S(2)}) async-start(s16[8,400,128]{2,1,0:T(8,128)(2,1)} %shard_map.77), calls=%async_computation.2 | async-start | bytes 1638400 | tf_op jit(solution)/shard_map/all_to_all | solution.py:247
  181.7 11.5 %shard_map.79 = s16[8,400,128]{2,1,0:T(8,128)(2,1)} custom-call(s32[24,10]{1,0:T(8,128)} %copy.21.cols, f32[1,1]{1,0:T(1,128)} %bitcast.17.shift, s32[1,2]{1,0:T(1,128)} %add_bitcast_fusion.here.place, s16[8,272,384]{2,1,0:T(8,128)(2,1)} %copy-done.1, s16[8,272,384]{2,1,0:T(8,128)(2,1)} %copy-done.1, f32[384,3072]{1,0:T(8,128)} %shard_map.75.y_ref, ...), custom_call_target="tpu_custom_call" | custom-call | flops 2013265920 | bytes 6291456 | tf_op jit(solution)/shard_map/pallas_call | solution.py:380
  193.2 9.6 %all-to-all-done.2.z_ref = s16[8,400,128]{2,1,0:T(8,128)(2,1)S(1)} async-done(((s16[8,400,128]{2,1,0:T(8,128)(2,1)}), s16[8,400,128]{2,1,0:T(8,128)(2,1)S(1)}, u32[]{:S(2)}, u32[]{:S(2)}) %all-to-all-start.2) | async-done | bytes 819232 | tf_op jit(solution)/shard_map/all_to_all | solution.py:247
  202.8 3.6 %all-to-all-start.4 = ((s16[8,400,128]{2,1,0:T(8,128)(2,1)}), s16[8,400,128]{2,1,0:T(8,128)(2,1)S(1)}, u32[]{:S(2)}, u32[]{:S(2)}) async-start(s16[8,400,128]{2,1,0:T(8,128)(2,1)} %shard_map.79), calls=%async_computation.4 | async-start | bytes 1638400 | tf_op jit(solution)/shard_map/all_to_all | solution.py:247
  207.6 2.8 shard_map.78.refs_0_.rest_4_
  211.8 11.5 %shard_map.82 = s16[8,400,128]{2,1,0:T(8,128)(2,1)} custom-call(s32[24,10]{1,0:T(8,128)} %copy.21.cols, f32[1,1]{1,0:T(1,128)} %bitcast.18.shift, s32[1,2]{1,0:T(1,128)} %add_bitcast_fusion.here.place, s16[8,272,384]{2,1,0:T(8,128)(2,1)} %copy-done.1, s16[8,272,384]{2,1,0:T(8,128)(2,1)} %copy-done.1, f32[384,3072]{1,0:T(8,128)} %shard_map.75.y_ref, ...), custom_call_target="tpu_custom_call" | custom-call | flops 2013265920 | bytes 6291456 | tf_op jit(solution)/shard_map/pallas_call | solution.py:380
  223.3 7.2 %collective-permute-done.31.refs_1_ = s16[8,400,128]{2,1,0:T(8,128)(2,1)} collective-permute-done((s16[8,400,128]{2,1,0:T(8,128)(2,1)}, s16[8,400,128]{2,1,0:T(8,128)(2,1)}, u32[]{:S(2)}, u32[]{:S(2)}) %collective-permute-start.31) | collective-permute-done | bytes 819232 | tf_op jit(solution)/shard_map/ppermute | solution.py:263
  230.5 5.7 %all-to-all-start.5 = ((s16[8,400,128]{2,1,0:T(8,128)(2,1)}), s16[8,400,128]{2,1,0:T(8,128)(2,1)S(1)}, u32[]{:S(2)}, u32[]{:S(2)}) async-start(s16[8,400,128]{2,1,0:T(8,128)(2,1)} %shard_map.82), calls=%async_computation.5 | async-start | bytes 1638400 | tf_op jit(solution)/shard_map/all_to_all | solution.py:247
  236.3 2.8 shard_map.80.refs_1_
  241.0 14.9 %all-to-all-done.5.z_ref = s16[8,400,128]{2,1,0:T(8,128)(2,1)S(1)} async-done(((s16[8,400,128]{2,1,0:T(8,128)(2,1)}), s16[8,400,128]{2,1,0:T(8,128)(2,1)S(1)}, u32[]{:S(2)}, u32[]{:S(2)}) %all-to-all-start.5) | async-done | bytes 819232 | tf_op jit(solution)/shard_map/all_to_all | solution.py:247
  256.8 2.8 shard_map.83.refs_1_
  259.7 1.6 collective-permute-start.37
  261.4 6.4 %shard_map.81.refs_0_ = f32[1,384,3072]{2,1,0:T(8,128)} custom-call(f32[1,4]{1,0:T(1,128)} %bitcast.30, s16[8,400,128]{2,1,0:T(8,128)(2,1)} %shard_map.78.refs_0_.rest_4_, s16[8,400,128]{2,1,0:T(8,128)(2,1)} %collective-permute-done.31.refs_1_, s16[8,400,128]{2,1,0:T(8,128)(2,1)} %collective-permute-done.32.refs_2_, ...), custom_call_target="tpu_custom_call" | custom-call | bytes 1 | tf_op jit(solution)/shard_map/pallas_call | solution.py:419
  269.6 6.4 %shard_map.84.refs_0_ = f32[1,384,3072]{2,1,0:T(8,128)} custom-call(f32[1,4]{1,0:T(1,128)} %bitcast.31, f32[1,384,3072]{2,1,0:T(8,128)} %shard_map.81.refs_0_, s16[8,400,128]{2,1,0:T(8,128)(2,1)} %shard_map.80.refs_1_, s16[8,400,128]{2,1,0:T(8,128)(2,1)} %copy-done.12, s16[8,400,128]{2,1,0:T(8,128)(2,1)} %copy-done.13, ...), custom_call_target="tpu_custom_call", output_to_operand_aliasing={{}: (1, {})} | custom-call | bytes 1 | tf_op jit(solution)/shard_map/pallas_call | solution.py:419
  275.9 4.6 %collective-permute-done.37.refs_2_ = s16[8,400,128]{2,1,0:T(8,128)(2,1)S(1)} collective-permute-done((s16[8,400,128]{2,1,0:T(8,128)(2,1)}, s16[8,400,128]{2,1,0:T(8,128)(2,1)S(1)}, u32[]{:S(2)}, u32[]{:S(2)}) %collective-permute-start.37) | collective-permute-done | bytes 819232 | tf_op jit(solution)/shard_map/ppermute | solution.py:263
  280.6 2.3 collective-permute-done.39.refs_4_
  283.8 6.4 %shard_map.85 = f32[1,384,3072]{2,1,0:T(8,128)} custom-call(f32[1,4]{1,0:T(1,128)} %bitcast.32, f32[1,384,3072]{2,1,0:T(8,128)} %shard_map.84.refs_0_, s16[8,400,128]{2,1,0:T(8,128)(2,1)} %shard_map.83.refs_1_, s16[8,400,128]{2,1,0:T(8,128)(2,1)} %copy-done.14, s16[8,400,128]{2,1,0:T(8,128)(2,1)} %copy-done.15, ...), custom_call_target="tpu_custom_call", output_to_operand_aliasing={{}: (1, {})} | custom-call | bytes 1 | tf_op jit(solution)/shard_map/pallas_call | solution.py:419
  (145 shorter events, 23.3 us)
Async XLA Ops:
  0.0 206.4 %copy-start = (f32[4,4]{1,0:T(4,128)S(1)}, f32[4,4]{1,0:T(4,128)}, u32[]{:S(2)}) copy-start(f32[4,4]{1,0:T(4,128)} %param.10) | copy-start | bytes 196
  1.9 9.0 %collective-permute-start = (bf16[30,32,128]{2,1,0:T(8,128)(2,1)S(1)}, bf16[30,32,128]{2,1,0:T(8,128)(2,1)S(1)}, u32[]{:S(2)}, u32[]{:S(2)}) collective-permute-start(bf16[30,32,128]{2,1,0:T(8,128)(2,1)S(1)} %bitcast.25), channel_id=1, source_target_pairs={{0,2},{2,4},{4,6},{6,7},{7,5},{5,3},{3,1},{1,0},{8,10},{10,12},{12... | collective-permute-start | bytes 737288 | tf_op jit(solution)/shard_map/ppermute | solution.py:312
  5.0 7.6 %collective-permute-start.4 = (bf16[30,32,128]{2,1,0:T(8,128)(2,1)S(1)}, bf16[30,32,128]{2,1,0:T(8,128)(2,1)S(1)}, u32[]{:S(2)}, u32[]{:S(2)}) collective-permute-start(bf16[30,32,128]{2,1,0:T(8,128)(2,1)S(1)} %bitcast.26), channel_id=1, source_target_pairs={{0,1},{2,0},{4,2},{6,4},{7,6},{5,7},{3,5},{1,3},{8,9},{10,8},{12,1... | collective-permute-start | bytes 737288 | tf_op jit(solution)/shard_map/ppermute | solution.py:312
  10.9 11.6 %collective-permute-start.1 = (bf16[30,32,128]{2,1,0:T(8,128)(2,1)S(1)}, bf16[30,32,128]{2,1,0:T(8,128)(2,1)S(1)}, u32[]{:S(2)}, u32[]{:S(2)}) collective-permute-start(bf16[30,32,128]{2,1,0:T(8,128)(2,1)S(1)} %collective-permute-done.rest_0_), channel_id=1, source_target_pairs={{0,16},{8,24},{16,0},{24,8},{1,17},{9,25},{17,1},{25,9},{2,18},{10... | collective-permute-start | bytes 737288 | tf_op jit(solution)/shard_map/ppermute | solution.py:263
  12.6 10.7 %collective-permute-start.5 = (bf16[30,32,128]{2,1,0:T(8,128)(2,1)S(1)}, bf16[30,32,128]{2,1,0:T(8,128)(2,1)S(1)}, u32[]{:S(2)}, u32[]{:S(2)}) collective-permute-start(bf16[30,32,128]{2,1,0:T(8,128)(2,1)S(1)} %collective-permute-done.4.rest_4_), channel_id=1, source_target_pairs={{0,16},{8,24},{16,0},{24,8},{1,17},{9,25},{17,1},{25,9},{2,18},{10... | collective-permute-start | bytes 737288 | tf_op jit(solution)/shard_map/ppermute | solution.py:263
  13.9 9.4 %collective-permute-start.8 = (bf16[30,32,128]{2,1,0:T(8,128)(2,1)S(1)}, bf16[30,32,128]{2,1,0:T(8,128)(2,1)S(1)}, u32[]{:S(2)}, u32[]{:S(2)}) collective-permute-start(bf16[30,32,128]{2,1,0:T(8,128)(2,1)S(1)} %collective-permute-done.rest_0_), channel_id=1, source_target_pairs={{0,2},{2,4},{4,6},{6,7},{7,5},{5,3},{3,1},{1,0},{8,10},{10,12},{12... | collective-permute-start | bytes 737288 | tf_op jit(solution)/shard_map/ppermute | solution.py:312
  15.5 7.8 %collective-permute-start.12 = (bf16[30,32,128]{2,1,0:T(8,128)(2,1)S(1)}, bf16[30,32,128]{2,1,0:T(8,128)(2,1)S(1)}, u32[]{:S(2)}, u32[]{:S(2)}) collective-permute-start(bf16[30,32,128]{2,1,0:T(8,128)(2,1)S(1)} %collective-permute-done.4.rest_4_), channel_id=1, source_target_pairs={{0,1},{2,0},{4,2},{6,4},{7,6},{5,7},{3,5},{1,3},{8,9},{10,8},{12,1... | collective-permute-start | bytes 737288 | tf_op jit(solution)/shard_map/ppermute | solution.py:312
  22.5 53.8 %copy-start.18 = (s32[24,10]{0,1:T(8,128)S(1)}, s32[24,10]{0,1:T(8,128)}, u32[]{:S(2)}) copy-start(s32[24,10]{0,1:T(8,128)} %param.12) | copy-start | bytes 2884
  23.3 6.4 %collective-permute-start.16 = (bf16[30,32,128]{2,1,0:T(8,128)(2,1)S(1)}, bf16[30,32,128]{2,1,0:T(8,128)(2,1)S(1)}, u32[]{:S(2)}, u32[]{:S(2)}) collective-permute-start(bf16[30,32,128]{2,1,0:T(8,128)(2,1)S(1)} %collective-permute-done.8.rest_8_), channel_id=1, source_target_pairs={{0,2},{2,4},{4,6},{6,7},{7,5},{5,3},{3,1},{1,0},{8,10},{10,12},{12... | collective-permute-start | bytes 737288 | tf_op jit(solution)/shard_map/ppermute | solution.py:312
  24.9 6.6 %collective-permute-start.20 = (bf16[30,32,128]{2,1,0:T(8,128)(2,1)S(1)}, bf16[30,32,128]{2,1,0:T(8,128)(2,1)S(1)}, u32[]{:S(2)}, u32[]{:S(2)}) collective-permute-start(bf16[30,32,128]{2,1,0:T(8,128)(2,1)S(1)} %collective-permute-done.12.rest_12_), channel_id=1, source_target_pairs={{0,1},{2,0},{4,2},{6,4},{7,6},{5,7},{3,5},{1,3},{8,9},{10,8},{12,1... | collective-permute-start | bytes 737288 | tf_op jit(solution)/shard_map/ppermute | solution.py:312
  29.8 6.2 %collective-permute-start.24 = (bf16[30,32,128]{2,1,0:T(8,128)(2,1)S(1)}, bf16[30,32,128]{2,1,0:T(8,128)(2,1)S(1)}, u32[]{:S(2)}, u32[]{:S(2)}) collective-permute-start(bf16[30,32,128]{2,1,0:T(8,128)(2,1)S(1)} %collective-permute-done.16.rest_16_), channel_id=1, source_target_pairs={{0,2},{2,4},{4,6},{6,7},{7,5},{5,3},{3,1},{1,0},{8,10},{10,12},{12... | collective-permute-start | bytes 737288 | tf_op jit(solution)/shard_map/ppermute | solution.py:312
  36.6 70.8 %all-to-all-start = ((s16[8,496,384]{2,1,0:T(8,128)(2,1)}), s16[8,496,384]{2,1,0:T(8,128)(2,1)S(1)}, u32[]{:S(2)}, u32[]{:S(2)}) async-start(s16[8,496,384]{2,1,0:T(8,128)(2,1)} %shard_map.73), calls=%async_computation | async-start | bytes 6094848 | tf_op jit(solution)/shard_map/all_to_all | solution.py:247
  42.7 2.7 collective-permute-start.2
  42.7 2.6 collective-permute-start.6
  43.2 3.5 %collective-permute-start.3 = (bf16[30,32,128]{2,1,0:T(8,128)(2,1)}, bf16[30,32,128]{2,1,0:T(8,128)(2,1)S(1)}, u32[]{:S(2)}, u32[]{:S(2)}) collective-permute-start(bf16[30,32,128]{2,1,0:T(8,128)(2,1)} %copy-done.21), channel_id=1, source_target_pairs={{0,8},{8,0},{16,24},{24,16},{1,9},{9,1},{17,25},{25,17},{2,10},{10... | collective-permute-start | bytes 737288 | tf_op jit(solution)/shard_map/ppermute | solution.py:263
  43.3 9.0 %collective-permute-start.9 = (bf16[30,32,128]{2,1,0:T(8,128)(2,1)}, bf16[30,32,128]{2,1,0:T(8,128)(2,1)S(1)}, u32[]{:S(2)}, u32[]{:S(2)}) collective-permute-start(bf16[30,32,128]{2,1,0:T(8,128)(2,1)} %copy-done.23), channel_id=1, source_target_pairs={{0,16},{8,24},{16,0},{24,8},{1,17},{9,25},{17,1},{25,9},{2,18},{10... | collective-permute-start | bytes 737288 | tf_op jit(solution)/shard_map/ppermute | solution.py:263
  44.8 12.3 %collective-permute-start.13 = (bf16[30,32,128]{2,1,0:T(8,128)(2,1)}, bf16[30,32,128]{2,1,0:T(8,128)(2,1)S(1)}, u32[]{:S(2)}, u32[]{:S(2)}) collective-permute-start(bf16[30,32,128]{2,1,0:T(8,128)(2,1)} %copy-done.24), channel_id=1, source_target_pairs={{0,16},{8,24},{16,0},{24,8},{1,17},{9,25},{17,1},{25,9},{2,18},{10... | collective-permute-start | bytes 737288 | tf_op jit(solution)/shard_map/ppermute | solution.py:263
  45.4 11.8 %collective-permute-start.7 = (bf16[30,32,128]{2,1,0:T(8,128)(2,1)}, bf16[30,32,128]{2,1,0:T(8,128)(2,1)S(1)}, u32[]{:S(2)}, u32[]{:S(2)}) collective-permute-start(bf16[30,32,128]{2,1,0:T(8,128)(2,1)} %copy-done.22), channel_id=1, source_target_pairs={{0,8},{8,0},{16,24},{24,16},{1,9},{9,1},{17,25},{25,17},{2,10},{10... | collective-permute-start | bytes 737288 | tf_op jit(solution)/shard_map/ppermute | solution.py:263
  46.1 12.6 %collective-permute-start.10 = (bf16[30,32,128]{2,1,0:T(8,128)(2,1)}, bf16[30,32,128]{2,1,0:T(8,128)(2,1)S(1)}, u32[]{:S(2)}, u32[]{:S(2)}) collective-permute-start(bf16[30,32,128]{2,1,0:T(8,128)(2,1)} %copy-done.23), channel_id=1, source_target_pairs={{0,8},{8,0},{16,24},{24,16},{1,9},{9,1},{17,25},{25,17},{2,10},{10... | collective-permute-start | bytes 737288 | tf_op jit(solution)/shard_map/ppermute | solution.py:263
  47.5 11.4 %collective-permute-start.14 = (bf16[30,32,128]{2,1,0:T(8,128)(2,1)}, bf16[30,32,128]{2,1,0:T(8,128)(2,1)S(1)}, u32[]{:S(2)}, u32[]{:S(2)}) collective-permute-start(bf16[30,32,128]{2,1,0:T(8,128)(2,1)} %copy-done.24), channel_id=1, source_target_pairs={{0,8},{8,0},{16,24},{24,16},{1,9},{9,1},{17,25},{25,17},{2,10},{10... | collective-permute-start | bytes 737288 | tf_op jit(solution)/shard_map/ppermute | solution.py:263
  53.0 6.4 %collective-permute-start.11 = (bf16[30,32,128]{2,1,0:T(8,128)(2,1)S(1)}, bf16[30,32,128]{2,1,0:T(8,128)(2,1)S(1)}, u32[]{:S(2)}, u32[]{:S(2)}) collective-permute-start(bf16[30,32,128]{2,1,0:T(8,128)(2,1)S(1)} %collective-permute-done.9.rest_9_), channel_id=1, source_target_pairs={{0,8},{8,0},{16,24},{24,16},{1,9},{9,1},{17,25},{25,17},{2,10},{10... | collective-permute-start | bytes 737288 | tf_op jit(solution)/shard_map/ppermute | solution.py:263
  57.1 3.9 %collective-permute-start.15 = (bf16[30,32,128]{2,1,0:T(8,128)(2,1)S(1)}, bf16[30,32,128]{2,1,0:T(8,128)(2,1)S(1)}, u32[]{:S(2)}, u32[]{:S(2)}) collective-permute-start(bf16[30,32,128]{2,1,0:T(8,128)(2,1)S(1)} %collective-permute-done.13.rest_13_), channel_id=1, source_target_pairs={{0,8},{8,0},{16,24},{24,16},{1,9},{9,1},{17,25},{25,17},{2,10},{10... | collective-permute-start | bytes 737288 | tf_op jit(solution)/shard_map/ppermute | solution.py:263
  57.1 9.1 %collective-permute-start.17 = (bf16[30,32,128]{2,1,0:T(8,128)(2,1)}, bf16[30,32,128]{2,1,0:T(8,128)(2,1)}, u32[]{:S(2)}, u32[]{:S(2)}) collective-permute-start(bf16[30,32,128]{2,1,0:T(8,128)(2,1)} %copy-done.25), channel_id=1, source_target_pairs={{0,16},{8,24},{16,0},{24,8},{1,17},{9,25},{17,1},{25,9},{2,18},{10... | collective-permute-start | bytes 737288 | tf_op jit(solution)/shard_map/ppermute | solution.py:263
  58.7 7.6 %collective-permute-start.18 = (bf16[30,32,128]{2,1,0:T(8,128)(2,1)}, bf16[30,32,128]{2,1,0:T(8,128)(2,1)}, u32[]{:S(2)}, u32[]{:S(2)}) collective-permute-start(bf16[30,32,128]{2,1,0:T(8,128)(2,1)} %copy-done.25), channel_id=1, source_target_pairs={{0,8},{8,0},{16,24},{24,16},{1,9},{9,1},{17,25},{25,17},{2,10},{10... | collective-permute-start | bytes 737288 | tf_op jit(solution)/shard_map/ppermute | solution.py:263
  58.9 12.7 %collective-permute-start.21 = (bf16[30,32,128]{2,1,0:T(8,128)(2,1)}, bf16[30,32,128]{2,1,0:T(8,128)(2,1)}, u32[]{:S(2)}, u32[]{:S(2)}) collective-permute-start(bf16[30,32,128]{2,1,0:T(8,128)(2,1)} %copy-done.26), channel_id=1, source_target_pairs={{0,16},{8,24},{16,0},{24,8},{1,17},{9,25},{17,1},{25,9},{2,18},{10... | collective-permute-start | bytes 737288 | tf_op jit(solution)/shard_map/ppermute | solution.py:263
  59.4 16.9 %collective-permute-start.25 = (bf16[30,32,128]{2,1,0:T(8,128)(2,1)}, bf16[30,32,128]{2,1,0:T(8,128)(2,1)}, u32[]{:S(2)}, u32[]{:S(2)}) collective-permute-start(bf16[30,32,128]{2,1,0:T(8,128)(2,1)} %copy-done.27), channel_id=1, source_target_pairs={{0,16},{8,24},{16,0},{24,8},{1,17},{9,25},{17,1},{25,9},{2,18},{10... | collective-permute-start | bytes 737288 | tf_op jit(solution)/shard_map/ppermute | solution.py:263
  61.0 19.0 %collective-permute-start.22 = (bf16[30,32,128]{2,1,0:T(8,128)(2,1)}, bf16[30,32,128]{2,1,0:T(8,128)(2,1)}, u32[]{:S(2)}, u32[]{:S(2)}) collective-permute-start(bf16[30,32,128]{2,1,0:T(8,128)(2,1)} %copy-done.26), channel_id=1, source_target_pairs={{0,8},{8,0},{16,24},{24,16},{1,9},{9,1},{17,25},{25,17},{2,10},{10... | collective-permute-start | bytes 737288 | tf_op jit(solution)/shard_map/ppermute | solution.py:263
  66.3 13.7 %collective-permute-start.26 = (bf16[30,32,128]{2,1,0:T(8,128)(2,1)}, bf16[30,32,128]{2,1,0:T(8,128)(2,1)}, u32[]{:S(2)}, u32[]{:S(2)}) collective-permute-start(bf16[30,32,128]{2,1,0:T(8,128)(2,1)} %copy-done.27), channel_id=1, source_target_pairs={{0,8},{8,0},{16,24},{24,16},{1,9},{9,1},{17,25},{25,17},{2,10},{10... | collective-permute-start | bytes 737288 | tf_op jit(solution)/shard_map/ppermute | solution.py:263
  66.3 13.7 %collective-permute-start.19 = (bf16[30,32,128]{2,1,0:T(8,128)(2,1)}, bf16[30,32,128]{2,1,0:T(8,128)(2,1)}, u32[]{:S(2)}, u32[]{:S(2)}) collective-permute-start(bf16[30,32,128]{2,1,0:T(8,128)(2,1)} %collective-permute-done.17.rest_17_), channel_id=1, source_target_pairs={{0,8},{8,0},{16,24},{24,16},{1,9},{9,1},{17,25},{25,17},{2,10},{10... | collective-permute-start | bytes 737288 | tf_op jit(solution)/shard_map/ppermute | solution.py:263
  71.5 8.4 %collective-permute-start.23 = (bf16[30,32,128]{2,1,0:T(8,128)(2,1)}, bf16[30,32,128]{2,1,0:T(8,128)(2,1)}, u32[]{:S(2)}, u32[]{:S(2)}) collective-permute-start(bf16[30,32,128]{2,1,0:T(8,128)(2,1)} %collective-permute-done.21.rest_21_), channel_id=1, source_target_pairs={{0,8},{8,0},{16,24},{24,16},{1,9},{9,1},{17,25},{25,17},{2,10},{10... | collective-permute-start | bytes 737288 | tf_op jit(solution)/shard_map/ppermute | solution.py:263
  76.3 3.6 %collective-permute-start.27 = (bf16[30,32,128]{2,1,0:T(8,128)(2,1)}, bf16[30,32,128]{2,1,0:T(8,128)(2,1)}, u32[]{:S(2)}, u32[]{:S(2)}) collective-permute-start(bf16[30,32,128]{2,1,0:T(8,128)(2,1)} %collective-permute-done.25.rest_25_), channel_id=1, source_target_pairs={{0,8},{8,0},{16,24},{24,16},{1,9},{9,1},{17,25},{25,17},{2,10},{10... | collective-permute-start | bytes 737288 | tf_op jit(solution)/shard_map/ppermute | solution.py:263
  109.1 26.1 %all-to-all-start.1 = ((s16[8,144,384]{2,1,0:T(8,128)(2,1)}), s16[8,144,384]{2,1,0:T(8,128)(2,1)S(1)}, u32[]{:S(2)}, u32[]{:S(2)}) async-start(s16[8,144,384]{2,1,0:T(8,128)(2,1)} %get-tuple-element.30), calls=%async_computation.1 | async-start | bytes 1769472 | tf_op jit(solution)/shard_map/all_to_all | solution.py:247
  135.2 43.0 %all-to-all-start.3 = ((s16[8,272,384]{2,1,0:T(8,128)(2,1)}), s16[8,272,384]{2,1,0:T(8,128)(2,1)S(1)}, u32[]{:S(2)}, u32[]{:S(2)}) async-start(s16[8,272,384]{2,1,0:T(8,128)(2,1)} %get-tuple-element.36), calls=%async_computation.3 | async-start | bytes 3342336 | tf_op jit(solution)/shard_map/all_to_all | solution.py:247
  140.1 20.7 %collective-permute-start.28 = (s16[8,96,384]{2,1,0:T(8,128)(2,1)S(1)}, s16[8,96,384]{2,1,0:T(8,128)(2,1)S(1)}, u32[]{:S(2)}, u32[]{:S(2)}) collective-permute-start(s16[8,96,384]{2,1,0:T(8,128)(2,1)S(1)} %slice.6.rest_0_), channel_id=1, source_target_pairs={{0,16},{8,24},{16,0},{24,8},{1,17},{9,25},{17,1},{25,9},{2,18},{10... | collective-permute-start | bytes 1769480 | tf_op jit(solution)/shard_map/ppermute | solution.py:263
  141.6 19.7 %collective-permute-start.29 = (s16[8,96,384]{2,1,0:T(8,128)(2,1)S(1)}, s16[8,96,384]{2,1,0:T(8,128)(2,1)S(1)}, u32[]{:S(2)}, u32[]{:S(2)}) collective-permute-start(s16[8,96,384]{2,1,0:T(8,128)(2,1)S(1)} %slice.6.rest_0_), channel_id=1, source_target_pairs={{0,8},{8,0},{16,24},{24,16},{1,9},{9,1},{17,25},{25,17},{2,10},{10... | collective-permute-start | bytes 1769480 | tf_op jit(solution)/shard_map/ppermute | solution.py:263
  160.8 2.2 collective-permute-start.30
  178.1 24.7 %all-to-all-start.2 = ((s16[8,400,128]{2,1,0:T(8,128)(2,1)}), s16[8,400,128]{2,1,0:T(8,128)(2,1)S(1)}, u32[]{:S(2)}, u32[]{:S(2)}) async-start(s16[8,400,128]{2,1,0:T(8,128)(2,1)} %shard_map.77), calls=%async_computation.2 | async-start | bytes 1638400 | tf_op jit(solution)/shard_map/all_to_all | solution.py:247
  202.8 27.7 %all-to-all-start.4 = ((s16[8,400,128]{2,1,0:T(8,128)(2,1)}), s16[8,400,128]{2,1,0:T(8,128)(2,1)S(1)}, u32[]{:S(2)}, u32[]{:S(2)}) async-start(s16[8,400,128]{2,1,0:T(8,128)(2,1)} %shard_map.79), calls=%async_computation.4 | async-start | bytes 1638400 | tf_op jit(solution)/shard_map/all_to_all | solution.py:247
  210.3 20.2 %collective-permute-start.31 = (s16[8,400,128]{2,1,0:T(8,128)(2,1)}, s16[8,400,128]{2,1,0:T(8,128)(2,1)}, u32[]{:S(2)}, u32[]{:S(2)}) collective-permute-start(s16[8,400,128]{2,1,0:T(8,128)(2,1)} %shard_map.78.refs_0_.rest_4_), channel_id=1, source_target_pairs={{0,16},{8,24},{16,0},{24,8},{1,17},{9,25},{17,1},{25,9},{2,18},{10... | collective-permute-start | bytes 2457608 | tf_op jit(solution)/shard_map/ppermute | solution.py:263
  230.5 25.4 %all-to-all-start.5 = ((s16[8,400,128]{2,1,0:T(8,128)(2,1)}), s16[8,400,128]{2,1,0:T(8,128)(2,1)S(1)}, u32[]{:S(2)}, u32[]{:S(2)}) async-start(s16[8,400,128]{2,1,0:T(8,128)(2,1)} %shard_map.82), calls=%async_computation.5 | async-start | bytes 1638400 | tf_op jit(solution)/shard_map/all_to_all | solution.py:247
  239.0 20.6 %collective-permute-start.34 = (s16[8,400,128]{2,1,0:T(8,128)(2,1)}, s16[8,400,128]{2,1,0:T(8,128)(2,1)S(1)}, u32[]{:S(2)}, u32[]{:S(2)}) collective-permute-start(s16[8,400,128]{2,1,0:T(8,128)(2,1)} %shard_map.80.refs_1_), channel_id=1, source_target_pairs={{0,16},{8,24},{16,0},{24,8},{1,17},{9,25},{17,1},{25,9},{2,18},{10... | collective-permute-start | bytes 2457608 | tf_op jit(solution)/shard_map/ppermute | solution.py:263
  240.5 20.7 %collective-permute-start.32 = (s16[8,400,128]{2,1,0:T(8,128)(2,1)S(1)}, s16[8,400,128]{2,1,0:T(8,128)(2,1)}, u32[]{:S(2)}, u32[]{:S(2)}) collective-permute-start(s16[8,400,128]{2,1,0:T(8,128)(2,1)S(1)} %copy-done.4), channel_id=1, source_target_pairs={{0,8},{8,0},{16,24},{24,16},{1,9},{9,1},{17,25},{25,17},{2,10},{10... | collective-permute-start | bytes 2457608 | tf_op jit(solution)/shard_map/ppermute | solution.py:263
  240.5 27.3 %collective-permute-start.35 = (s16[8,400,128]{2,1,0:T(8,128)(2,1)}, s16[8,400,128]{2,1,0:T(8,128)(2,1)S(1)}, u32[]{:S(2)}, u32[]{:S(2)}) collective-permute-start(s16[8,400,128]{2,1,0:T(8,128)(2,1)} %shard_map.80.refs_1_), channel_id=1, source_target_pairs={{0,8},{8,0},{16,24},{24,16},{1,9},{9,1},{17,25},{25,17},{2,10},{10... | collective-permute-start | bytes 2457608 | tf_op jit(solution)/shard_map/ppermute | solution.py:263
  241.0 20.4 %collective-permute-start.33 = (s16[8,400,128]{2,1,0:T(8,128)(2,1)}, s16[8,400,128]{2,1,0:T(8,128)(2,1)}, u32[]{:S(2)}, u32[]{:S(2)}) collective-permute-start(s16[8,400,128]{2,1,0:T(8,128)(2,1)} %collective-permute-done.31.refs_1_), channel_id=1, source_target_pairs={{0,8},{8,0},{16,24},{24,16},{1,9},{9,1},{17,25},{25,17},{2,10},{10... | collective-permute-start | bytes 2457608 | tf_op jit(solution)/shard_map/ppermute | solution.py:263
  259.6 8.2 %collective-permute-start.36 = (s16[8,400,128]{2,1,0:T(8,128)(2,1)S(1)}, s16[8,400,128]{2,1,0:T(8,128)(2,1)S(1)}, u32[]{:S(2)}, u32[]{:S(2)}) collective-permute-start(s16[8,400,128]{2,1,0:T(8,128)(2,1)S(1)} %collective-permute-done.34.refs_2_), channel_id=1, source_target_pairs={{0,8},{8,0},{16,24},{24,16},{1,9},{9,1},{17,25},{25,17},{2,10},{10... | collective-permute-start | bytes 2457608 | tf_op jit(solution)/shard_map/ppermute | solution.py:263
  259.7 20.9 %collective-permute-start.37 = (s16[8,400,128]{2,1,0:T(8,128)(2,1)}, s16[8,400,128]{2,1,0:T(8,128)(2,1)S(1)}, u32[]{:S(2)}, u32[]{:S(2)}) collective-permute-start(s16[8,400,128]{2,1,0:T(8,128)(2,1)} %shard_map.83.refs_1_), channel_id=1, source_target_pairs={{0,16},{8,24},{16,0},{24,8},{1,17},{9,25},{17,1},{25,9},{2,18},{10... | collective-permute-start | bytes 2457608 | tf_op jit(solution)/shard_map/ppermute | solution.py:263
  261.2 19.3 %collective-permute-start.38 = (s16[8,400,128]{2,1,0:T(8,128)(2,1)}, s16[8,400,128]{2,1,0:T(8,128)(2,1)S(1)}, u32[]{:S(2)}, u32[]{:S(2)}) collective-permute-start(s16[8,400,128]{2,1,0:T(8,128)(2,1)} %shard_map.83.refs_1_), channel_id=1, source_target_pairs={{0,8},{8,0},{16,24},{24,16},{1,9},{9,1},{17,25},{25,17},{2,10},{10... | collective-permute-start | bytes 2457608 | tf_op jit(solution)/shard_map/ppermute | solution.py:263
  280.6 2.3 collective-permute-start.39
  (37 other events, 288.8 us)
